TPU v7x, 512 devices: a whole 4x4x16 slice. The times are simulated.
512 devices in a mesh: ctx: 32 (over z, y_hi), tp: 16 (over x, y_lo, core).
Axes of the slice: x: 4, y: 4 (y_hi: 2, y_lo: 2; y = y_hi * 2 + y_lo), z: 16, core: 2. Of those that a mesh axis runs over, the one named last changes fastest.
Arguments:
- queries: bfloat16 [192, 8192], P('ctx', 'tp')
- cache_keys: bfloat16 [16, 98304, 128], P('tp', 'ctx'), as said below
- cache_values: bfloat16 [16, 98304, 128], P('tp', 'ctx')
- seg_keys: bfloat16 [192, 2048], P('ctx', 'tp')
- seg_values: bfloat16 [192, 2048], P('ctx', 'tp')
- lengths: int32 [32], P('ctx'), may hold values from 1 to 3072, as said below
- residual_stream: bfloat16 [192, 8192], P('tp', 'ctx')
- out_weight: bfloat16 [8192, 8192], P('tp', 'ctx'), may hold values from -0.0625 to 0.0625
- norm_gain: float32 [8192], P('ctx'), may hold values from 0.1 to 1.9
- gate_weight: bfloat16 [8192, 29568], P('ctx', 'tp'), may hold values from -0.0625 to 0.0625
- up_weight: bfloat16 [8192, 29568], P('ctx', 'tp'), may hold values from -0.0625 to 0.0625
- down_weight: bfloat16 [29568, 8192], P('tp', 'ctx'), may hold values from -0.03125 to 0.03125
Outputs:
- attention: bfloat16 [192, 8192], P('ctx', 'tp')
- layer_out: bfloat16 [192, 8192], P('tp', 'ctx')
Inputs may be any that keep to these rules, and one draw needn't show every extreme that they name: Block c of the cache holds live entries at its first lengths[c] positions; the rest are unused. The last block is at most half live and at least one block is fully live. `cache_keys`: slots hold the 8 key-value heads in order, each repeated 16 / 8 times in a row; the same holds for the segment's keys and values.
All inputs are finite; a program needn't handle non-finite values.
Results may differ from a plain program's by a relative error of at most 0.02.
Values may be sent and summed in bfloat16 or wider, within the bound.
No kernel may reach another device: no remote copies, remote signals or barrier semaphores. Data moves between devices by JAX's collectives and lax.ppermute only.
A program may use at most 64 MiB of HBM per device.

v0:
```python
import math

import jax
import jax.numpy as jnp
from jax import lax
from jax.sharding import PartitionSpec as P

D = 8192


def from_behind(x, axis, by):
    count = lax.axis_size(axis)
    return lax.ppermute(x, axis, [(i, (i + by) % count) for i in range(count)])


def per_device(
    queries,
    cache_keys,
    cache_values,
    seg_keys,
    seg_values,
    lengths,
    residual_stream,
    out_weight,
    norm_gain,
    gate_weight,
    up_weight,
    down_weight,
):
    rows, width = queries.shape
    slots_dev, stretch, head_dim = cache_keys.shape
    heads_dev = width // head_dim
    group = heads_dev // slots_dev
    scale = 1.0 / math.sqrt(head_dim)
    length = lengths[0]
    ctx_size = lax.axis_size("ctx")
    here = lax.axis_index("ctx")
    span = min(512, stretch)

    def split_heads(block, count):
        return block.reshape(count, slots_dev, group, head_dim)

    def cache_pass(query4, state):

        def advance(step, carry):
            top_old, total, numer = carry
            start = step * span
            key_block = lax.dynamic_slice_in_dim(cache_keys, start, span, 1)
            val_block = lax.dynamic_slice_in_dim(cache_values, start, span, 1)
            score = (
                jnp.einsum("rsgd,sbd->rsgb", query4, key_block, preferred_element_type=jnp.float32)
                * scale
            )
            alive = start + jnp.arange(span) < length
            score = jnp.where(alive, score, -1e30)
            top_new = jnp.maximum(top_old, score.max(axis=-1))
            fade = jnp.exp(top_old - top_new)
            weight = jnp.exp(score - top_new[..., None])
            total = total * fade + weight.sum(axis=-1)
            numer = numer * fade[..., None] + jnp.einsum(
                "rsgb,sbd->rsgd",
                weight.astype(jnp.bfloat16),
                val_block,
                preferred_element_type=jnp.float32,
            )
            return (top_new, total, numer)

        blocks = (length + span - 1) // span
        return lax.fori_loop(0, blocks, advance, state)

    def turn(step, carry):
        block, top, total, numer = carry
        top, total, numer = cache_pass(split_heads(block, rows), (top, total, numer))
        block = from_behind(block, "ctx", 1)
        top, total, numer = from_behind((top, total, numer), "ctx", 1)
        return (block, top, total, numer)

    start_top = jnp.full((rows, slots_dev, group), -1e30, jnp.float32)
    start_total = jnp.zeros((rows, slots_dev, group), jnp.float32)
    start_numer = jnp.zeros((rows, slots_dev, group, head_dim), jnp.float32)
    _, top, total, numer = lax.fori_loop(
        0, ctx_size, turn, (queries, start_top, start_total, start_numer)
    )
    seg_all_keys, seg_all_vals = (
        lax.all_gather(seg_keys, "ctx", axis=0, tiled=True),
        lax.all_gather(seg_values, "ctx", axis=0, tiled=True),
    )
    seg_total = rows * ctx_size
    own_keys = seg_all_keys.reshape(seg_total, slots_dev, head_dim)
    own_vals = seg_all_vals.reshape(seg_total, slots_dev, head_dim)
    mine = split_heads(queries, rows)
    score = jnp.einsum("rsgd,bsd->rsgb", mine, own_keys, preferred_element_type=jnp.float32) * scale
    token_of = here * rows + jnp.arange(rows)
    visible = jnp.arange(seg_total)[None, :] <= token_of[:, None]
    score = jnp.where(visible[:, None, None, :], score, -1e30)
    top_new = jnp.maximum(top, score.max(axis=-1))
    fade = jnp.exp(top - top_new)
    weight = jnp.exp(score - top_new[..., None])
    total = total * fade + weight.sum(axis=-1)
    numer = numer * fade[..., None] + jnp.einsum(
        "rsgb,bsd->rsgd", weight.astype(jnp.bfloat16), own_vals, preferred_element_type=jnp.float32
    )
    attention = (numer / total[..., None]).astype(jnp.bfloat16).reshape(rows, width)
    heads_all = lax.all_gather(attention, "ctx", axis=0, tiled=True)
    picked = heads_all
    mixed = lax.psum_scatter(
        jnp.dot(picked, out_weight, preferred_element_type=jnp.float32).astype(jnp.bfloat16),
        "tp",
        scatter_dimension=0,
        tiled=True,
    ).astype(jnp.float32)
    stream = (residual_stream.astype(jnp.float32) + mixed).astype(jnp.bfloat16)
    wide = stream.astype(jnp.float32)
    power = lax.psum(jnp.sum(wide * wide, axis=1), "ctx") / D
    normed = (wide * lax.rsqrt(power + 1e-06)[:, None] * norm_gain).astype(jnp.bfloat16)
    rows_all = lax.all_gather(normed, "tp", axis=0, tiled=True)
    gate, upper = (
        lax.psum(
            jnp.dot(rows_all, gate_weight, preferred_element_type=jnp.float32).astype(jnp.bfloat16),
            "ctx",
        ).astype(jnp.float32),
        lax.psum(
            jnp.dot(rows_all, up_weight, preferred_element_type=jnp.float32).astype(jnp.bfloat16),
            "ctx",
        ).astype(jnp.float32),
    )
    hidden_all = (jax.nn.silu(gate) * upper).astype(jnp.bfloat16)
    picked = hidden_all
    lowered = lax.psum_scatter(
        jnp.dot(picked, down_weight, preferred_element_type=jnp.float32).astype(jnp.bfloat16),
        "tp",
        scatter_dimension=0,
        tiled=True,
    ).astype(jnp.float32)
    layer_out = (wide + lowered).astype(jnp.bfloat16)
    return (attention, layer_out)


def solution(mesh):
    return jax.shard_map(
        per_device,
        mesh=mesh,
        in_specs=(
            P("ctx", "tp"),
            P("tp", "ctx", None),
            P("tp", "ctx", None),
            P("ctx", "tp"),
            P("ctx", "tp"),
            P("ctx"),
            P("tp", "ctx"),
            P("tp", "ctx"),
            P("ctx"),
            P("ctx", "tp"),
            P("ctx", "tp"),
            P("tp", "ctx"),
        ),
        out_specs=(P("ctx", "tp"), P("tp", "ctx")),
        check_vma=False,
    )
```

profile of v0, /device:TPU:1, one launch (start us, length us, event | category | flops | bytes accessed | tf_op | source)
XLA Modules:
  0.0 1915.6 jit_solution(16168744179997844608)
XLA Ops:
  8.7 69.7 %all-gather = bf16[32,6,128]{2,1,0:T(8,128)(2,1)S(1)} all-gather(bf16[1,6,128]{2,1,0:T(8,128)(2,1)} %bitcast.133), channel_id=1, replica_groups=mesh['ctx'=32,'tp'=16] {'ctx'}, dimensions={0}, use_global_device_ids=true | all-gather | bytes 50688 | tf_op jit(solution)/shard_map/all_gather | solution.py:85
  78.5 57.1 %all-gather.1 = bf16[32,6,128]{2,1,0:T(8,128)(2,1)S(1)} all-gather(bf16[1,6,128]{2,1,0:T(8,128)(2,1)} %bitcast.134), channel_id=1, replica_groups=mesh['ctx'=32,'tp'=16] {'ctx'}, dimensions={0}, use_global_device_ids=true | all-gather | bytes 50688 | tf_op jit(solution)/shard_map/all_gather | solution.py:86
  135.9 1124.7 %while.49 = (s32[]{:T(128)}, bf16[6,512]{1,0:T(8,128)(2,1)S(1)}, f32[6,1,4]{0,2,1:T(4,128)S(1)}, f32[6,1,4]{0,2,1:T(4,128)S(1)}, f32[6,1,4,128]{3,0,2,1:T(8,128)...) while((s32[]{:T(128)}, bf16[6,512]{1,0:T(8,128)(2,1)S(1)}, ...), condition=%wide.region_5.6_spmd, body=%wide.region_0.5_spmd.sunk | while | flops 6384720 | bytes 555224 | solution.py:81
  135.9 19.0 while.50
  170.5 19.0 while.50
  203.2 19.0 while.50
  237.3 19.0 while.50
  273.8 19.0 while.50
  294.7 6.0 collective-permute-start
  310.7 19.0 while.50
  347.2 19.0 while.50
  381.3 19.0 while.50
  402.2 6.0 collective-permute-start
  418.2 19.0 while.50
  452.8 19.0 while.50
  486.6 19.0 while.50
  522.8 19.0 while.50
  557.5 19.0 while.50
  591.2 19.0 while.50
  624.2 19.0 while.50
  660.8 19.0 while.50
  681.7 6.0 collective-permute-start
  697.7 19.0 while.50
  718.6 5.8 collective-permute-start
  734.4 19.0 while.50
  768.5 19.0 while.50
  789.4 6.0 collective-permute-start
  805.3 19.0 while.50
  839.7 19.0 while.50
  873.5 19.0 while.50
  909.7 19.0 while.50
  944.4 19.0 while.50
  978.2 19.0 while.50
  1011.8 19.0 while.50
  1047.8 19.0 while.50
  1068.7 6.0 collective-permute-start
  1084.6 19.0 while.50
  1121.3 19.0 while.50
  1155.4 19.0 while.50
  1176.3 6.0 collective-permute-start
  1192.2 19.0 while.50
  1227.0 19.0 while.50
  1261.1 61.6 %all-gather.2 = bf16[32,6,512]{2,1,0:T(8,128)(2,1)S(1)} all-gather(bf16[1,6,512]{2,1,0:T(8,128)(2,1)S(1)} %bitcast.131), channel_id=1, replica_groups=mesh['ctx'=32,'tp'=16] {'ctx'}, dimensions={0}, use_global_device_ids=true | all-gather | bytes 202752 | tf_op jit(solution)/shard_map/all_gather | solution.py:104
  1323.0 128.4 %fusion = bf16[16,256]{1,0:T(8,128)(2,1)S(1)} fusion(bf16[192,256]{1,0:T(8,128)(2,1)S(1)} %convolution_convert_fusion.3), kind=kCustom, calls=%all-reduce-scatter | all-reduce-scatter fusion | flops 65537 | bytes 108544
  1461.9 60.4 %psum.21 = f32[12]{0:T(128)S(1)} all-reduce(f32[12]{0:T(128)S(1)} %get-tuple-element.280), channel_id=1, replica_groups=mesh['ctx'=32,'tp'=16] {'ctx'}, use_global_device_ids=true, to_apply=%region_10.11 | all-reduce | flops 12 | bytes 96 | tf_op jit(solution)/shard_map/psum | solution.py:114
  1522.4 35.0 %all-gather.3 = bf16[16,12,256]{2,1,0:T(8,128)(2,1)S(1)} all-gather(bf16[1,12,256]{2,1,0:T(8,128)(2,1)S(1)} %fusion.39), channel_id=1, replica_groups=mesh['ctx'=32,'tp'=16] {'tp'}, dimensions={0}, use_global_device_ids=true | all-gather | bytes 104448 | tf_op jit(solution)/shard_map/all_gather | solution.py:116
  1560.2 288.2 %all-reduce.7.cloned.1.call-done = (bf16[192,1848]{1,0:T(8,128)(2,1)}, bf16[192,1848]{1,0:T(8,128)(2,1)}) async-done(((bf16[192,1848]{1,0:T(8,128)(2,1)}, bf16[192,1848]{1,0:T(8,128)(2,1)}), (bf16[192,1848]{1,0:T(8,128)(2,1)}, bf16[192,1848]{1,0:T(8,128)(2,1)})) %all-reduce.7.cloned.1.call-update) | async-done | bytes 1419280 | tf_op jit(solution)/shard_map/psum | solution.py:122
  1850.3 48.5 %fusion.1 = bf16[16,256]{1,0:T(8,128)(2,1)S(1)} fusion(bf16[192,256]{1,0:T(8,128)(2,1)S(1)} %convolution_convert_fusion.2), kind=kCustom, calls=%all-reduce-scatter.1 | all-reduce-scatter fusion | flops 65537 | bytes 108544
  (1781 shorter events, 1098.3 us)
Async XLA Ops:
  7.2 1841.2 %all-reduce.7.cloned.1.call-start = ((), (), s32[]{:S(2)}) async-start(), calls=%async_computation | async-start | bytes 2949120 | tf_op jit(solution)/shard_map/psum | solution.py:122
  154.9 15.5 collective-permute-start.3
  222.2 15.1 collective-permute-start.3
  256.3 17.5 collective-permute-start.3
  258.2 15.6 collective-permute-start
  292.8 17.9 collective-permute-start.3
  294.7 16.0 collective-permute-start
  329.7 17.4 collective-permute-start.3
  331.6 15.5 collective-permute-start
  366.1 15.1 collective-permute-start.3
  400.2 17.9 collective-permute-start.3
  402.2 16.0 collective-permute-start
  437.1 15.7 collective-permute-start.3
  471.8 14.8 collective-permute-start.3
  505.6 17.2 collective-permute-start.3
  507.5 15.3 collective-permute-start
  541.8 15.7 collective-permute-start.3
  576.5 14.6 collective-permute-start.3
  610.2 14.0 collective-permute-start.3
  643.2 17.6 collective-permute-start.3
  645.1 15.7 collective-permute-start
  679.8 17.9 collective-permute-start.3
  681.7 16.0 collective-permute-start
  716.7 17.7 collective-permute-start.3
  718.6 15.7 collective-permute-start
  753.3 15.1 collective-permute-start.3
  787.4 17.8 collective-permute-start.3
  789.4 15.9 collective-permute-start
  824.3 15.4 collective-permute-start.3
  858.7 14.8 collective-permute-start.3
  892.5 17.2 collective-permute-start.3
  894.4 15.3 collective-permute-start
  928.7 15.7 collective-permute-start.3
  930.6 13.8 collective-permute-start
  963.4 14.7 collective-permute-start.3
  997.1 14.7 collective-permute-start.3
  1030.8 16.9 collective-permute-start.3
  1032.7 15.0 collective-permute-start
  1066.7 17.8 collective-permute-start.3
  1068.7 15.9 collective-permute-start
  1103.6 17.7 collective-permute-start.3
  1105.5 15.8 collective-permute-start
  1140.3 15.1 collective-permute-start.3
  1174.4 17.8 collective-permute-start.3
  1176.3 15.9 collective-permute-start
  1211.2 15.7 collective-permute-start.3
  1213.1 13.8 collective-permute-start
  1245.9 14.7 collective-permute-start.3
  (96 other events, 3446.4 us)
Sparse Core Ops, SparseCore 0:
  1560.3 287.9 all-reduce.6
where the time goes:
time: 1930 us; the launch traced here: 1920 us
  waiting for transfers between devices  482 us (25%)
  blocking collectives  461 us (24%)
  matrix products  439 us (23%)
  starting transfers between devices  339 us (18%)
  other arithmetic  165 us (9%)
    ppermute x128, starting transfers between devices, from_behind(): return lax.ppermute(x, axis, [(i, (i + by) % count) for i in range(count)])  323 us
    psum x1, waiting for transfers between devices, per_device(): lax.psum(jnp.dot(rows_all, up_weight, preferred_element_type=jnp.float32)...  288 us
    dot_general x192, matrix products, advance(): jnp.einsum('rsgd,sbd->rsgb', query4, key_block, preferred_element_type=jn...  221 us
    dot_general x192, matrix products, advance(): jnp.einsum('rsgb,sbd->rsgd', weight.astype(jnp.bfloat16), val_block, pref...  213 us
    ppermute x128, waiting for transfers between devices, from_behind(): return lax.ppermute(x, axis, [(i, (i + by) % count) for i in range(count)])  193 us
    unnamed x2, blocking collectives  177 us
    lt x192, other arithmetic, advance(): alive = start + jnp.arange(span) < length  125 us
    all_gather x1, blocking collectives, per_device(): lax.all_gather(seg_keys, 'ctx', axis=0, tiled=True)  69.7 us
  transfers between devices with their start and end apart: 137, of which 66 were waited for; matrix products, arithmetic and copies ran while one was open for 0% of the time, Pallas kernels for 0%

commit v1 on v0

v1 whole, which is shorter than its diff:
```python
import functools
import math

import jax
import jax.numpy as jnp
from jax import lax
from jax.experimental import pallas as pl
from jax.experimental.pallas import tpu as pltpu
from jax.sharding import PartitionSpec as P

D = 8192
F32 = jnp.float32
BF16 = jnp.bfloat16
LOW = -1e30
SPAN = 512


def three_parts(x):
    one = x.astype(BF16).astype(F32)
    rest = x - one
    two = rest.astype(BF16).astype(F32)
    return one, two, (rest - two).astype(BF16).astype(F32)


def attend_kernel(where, q_ref, k_ref, v_ref, sk_ref, sv_ref, out_ref, *, tokens, group, head, scale):
    length = where[0]
    first = where[1]
    rows = tokens * group
    own = sk_ref.shape[0]
    query = jnp.concatenate([q_ref[:, g * head : (g + 1) * head] for g in range(group)], axis=0)

    def scores(keys):
        return lax.dot_general(keys, query, (((1,), (1,)), ((), ())), preferred_element_type=F32) * scale

    def add(carry, s, values):
        top, total, numer = carry
        top_new = jnp.maximum(top, jnp.max(s, axis=0, keepdims=True))
        fade = jnp.exp(top - top_new)
        w = jnp.exp(s - top_new)
        total = total * fade + jnp.sum(w, axis=0, keepdims=True)
        numer = numer * fade + lax.dot_general(
            values, w.astype(BF16), (((0,), (0,)), ((), ())), preferred_element_type=F32
        )
        return top_new, total, numer

    s = scores(sk_ref[...])
    token = lax.broadcasted_iota(jnp.int32, (own, rows), 1) % tokens
    place = first + lax.broadcasted_iota(jnp.int32, (own, rows), 0)
    seen = place <= token
    s = jnp.where(seen, s, LOW)
    top = jnp.max(s, axis=0, keepdims=True)
    w = jnp.where(seen, jnp.exp(s - top), 0.0)
    total = jnp.sum(w, axis=0, keepdims=True)
    numer = lax.dot_general(sv_ref[...], w.astype(BF16), (((0,), (0,)), ((), ())), preferred_element_type=F32)

    def whole(step, carry):
        at = pl.ds(pl.multiple_of(step * SPAN, SPAN), SPAN)
        return add(carry, scores(k_ref[at, :]), v_ref[at, :])

    full = length // SPAN
    carry = lax.fori_loop(0, full, whole, (top, total, numer))

    def part(step, carry):
        at = pl.ds(pl.multiple_of(step * SPAN, SPAN), SPAN)
        s = scores(k_ref[at, :])
        live = step * SPAN + lax.broadcasted_iota(jnp.int32, s.shape, 0) < length
        return add(carry, jnp.where(live, s, LOW), v_ref[at, :])

    top, total, numer = lax.fori_loop(full, (length + SPAN - 1) // SPAN, part, carry)
    out = (numer / total).T
    stats = jnp.concatenate([*three_parts(top), *three_parts(total), jnp.zeros((2, rows), F32)], axis=0).T
    for g in range(group):
        mine = slice(g * tokens, (g + 1) * tokens)
        out_ref[:, g * head : (g + 1) * head] = out[mine].astype(BF16)
    tail = jnp.concatenate(
        [stats[g * tokens : (g + 1) * tokens] for g in range(group)] + [jnp.zeros((tokens, 128 - 8 * group), F32)],
        axis=1,
    )
    out_ref[:, group * head :] = tail.astype(BF16)


def merge_kernel(in_ref, out_ref, *, group, head):
    stats = in_ref[:, :, group * head :].astype(F32)
    for g in range(group):
        col = [stats[:, :, 8 * g + i : 8 * g + i + 1] for i in range(6)]
        top = col[0] + col[1] + col[2]
        total = col[3] + col[4] + col[5]
        best = jnp.max(top, axis=0, keepdims=True)
        w = jnp.exp(top - best) * total
        mine = slice(g * head, (g + 1) * head)
        numer = jnp.sum(in_ref[:, :, mine].astype(F32) * w, axis=0)
        out_ref[:, mine] = (numer / jnp.sum(w, axis=0)).astype(BF16)


def to_all(x, axis):
    n = lax.axis_size(axis)
    return lax.all_to_all(jnp.broadcast_to(x[None], (n, *x.shape)), axis, 0, 0, tiled=True)


def swap(x, axis, mask):
    n = lax.axis_size(axis)
    return lax.ppermute(x, axis, [(i, i ^ mask) for i in range(n)])


def per_device(
    queries,
    cache_keys,
    cache_values,
    seg_keys,
    seg_values,
    lengths,
    residual_stream,
    out_weight,
    norm_gain,
    gate_weight,
    up_weight,
    down_weight,
):
    rows, width = queries.shape
    _, stretch, head = cache_keys.shape
    group = width // head
    n_ctx, n_tp = lax.axis_size("ctx"), lax.axis_size("tp")
    tokens = rows * n_ctx
    c, t = lax.axis_index("ctx"), lax.axis_index("tp")
    trows = residual_stream.shape[0]
    feats = residual_stream.shape[1]
    units = gate_weight.shape[1]

    q_all = to_all(queries, "ctx").reshape(tokens, width)
    where = jnp.stack([lengths[0], c * rows])
    vmem = pl.BlockSpec(memory_space=pltpu.VMEM)
    partial = pl.pallas_call(
        functools.partial(attend_kernel, tokens=tokens, group=group, head=head, scale=1.0 / math.sqrt(head)),
        out_shape=jax.ShapeDtypeStruct((tokens, width + 128), BF16),
        in_specs=[pl.BlockSpec(memory_space=pltpu.SMEM)] + [vmem] * 5,
        out_specs=vmem,
        compiler_params=pltpu.CompilerParams(vmem_limit_bytes=40 * 2**20),
        cost_estimate=pl.CostEstimate(flops=4 * tokens * width * stretch, bytes_accessed=2**21, transcendentals=tokens * group * stretch),
        name="attend",
    )(where, q_all, cache_keys[0], cache_values[0], seg_keys, seg_values)
    parts = lax.all_to_all(partial.reshape(n_ctx, rows, width + 128), "ctx", 0, 0, tiled=True)
    attention = pl.pallas_call(
        functools.partial(merge_kernel, group=group, head=head),
        out_shape=jax.ShapeDtypeStruct((rows, width), BF16),
        in_specs=[vmem],
        out_specs=vmem,
        compiler_params=pltpu.CompilerParams(vmem_limit_bytes=40 * 2**20),
        name="merge",
    )(parts)

    heads_all = to_all(attention, "ctx").reshape(tokens, width)
    mixed = jnp.dot(heads_all, out_weight, preferred_element_type=F32)
    residual = jnp.where(
        (jnp.arange(n_tp) == t)[:, None, None], residual_stream.astype(F32)[None], 0.0
    ).reshape(tokens, feats)
    total = (mixed + residual).astype(BF16)
    for mask in (1, 2, 4, 8):
        got = swap(total, "tp", mask)
        total = (total.astype(F32) + got.astype(F32)).astype(BF16)
    stream = total
    wide = stream.astype(F32)
    squares = jnp.sum(wide * wide, axis=1, keepdims=True)
    scaled = (wide * norm_gain).astype(BF16)
    gate = jnp.dot(scaled, gate_weight, preferred_element_type=F32).astype(BF16)
    upper = jnp.dot(scaled, up_weight, preferred_element_type=F32).astype(BF16)
    pad = -(2 * units + 3) % 128
    sums = jnp.concatenate(
        [gate, upper] + [p.astype(BF16) for p in three_parts(squares)] + [jnp.zeros((tokens, pad), BF16)], axis=1
    )
    sums = lax.all_to_all(sums.reshape(n_ctx, rows, -1), "ctx", 0, 0, tiled=True)
    sums = jnp.sum(sums.astype(F32), axis=0)
    power = jnp.sum(sums[:, 2 * units : 2 * units + 3], axis=1, keepdims=True) / D
    inv = lax.rsqrt(power + 1e-06)
    gate, upper = sums[:, :units] * inv, sums[:, units : 2 * units] * inv
    hidden = (jax.nn.silu(gate) * upper).astype(BF16)
    hidden_all = to_all(hidden, "ctx").reshape(tokens, units)
    lowered = jnp.dot(hidden_all, down_weight, preferred_element_type=F32)

    keep = lowered.reshape(n_tp, trows, feats)
    for bit in range(4):
        both = keep.reshape(-1, 2, trows, feats)
        mine = (t >> bit) & 1
        send = lax.dynamic_index_in_dim(both, 1 - mine, 1, keepdims=False).astype(BF16)
        stay = lax.dynamic_index_in_dim(both, mine, 1, keepdims=False)
        keep = stay + swap(send, "tp", 1 << bit).astype(F32)
    own = lax.dynamic_slice_in_dim(wide, t * trows, trows, 0)
    layer_out = (own + keep[0]).astype(BF16)
    return (attention, layer_out)


def solution(mesh):
    return jax.shard_map(
        per_device,
        mesh=mesh,
        in_specs=(
            P("ctx", "tp"),
            P("tp", "ctx", None),
            P("tp", "ctx", None),
            P("ctx", "tp"),
            P("ctx", "tp"),
            P("ctx"),
            P("tp", "ctx"),
            P("tp", "ctx"),
            P("ctx"),
            P("ctx", "tp"),
            P("ctx", "tp"),
            P("tp", "ctx"),
        ),
        out_specs=(P("ctx", "tp"), P("tp", "ctx")),
        check_vma=False,
    )
```

time: 1930 us -> 319 us (0.17)
  matrix products: 439 us -> 2.84 us
  waiting for transfers between devices: 482 us -> 103 us
  blocking collectives: 461 us -> 122 us
  starting transfers between devices: 339 us -> 65.3 us
  other arithmetic: 165 us -> 1.63 us
    dot_general x390 -> x4, matrix products: 439 us -> 2.84 us  [the longest x1 1.64 us: per_device(): lowered = jnp.dot(hidden_all, down_weight, preferred_element_type=F32)]
    ppermute x128 -> x8, starting transfers between devices: 323 us -> 32.2 us  [swap(): return lax.ppermute(x, axis, [(i, i ^ mask) for i in range(n)])]
    psum x1 -> x0, waiting for transfers between devices: 288 us -> none  [per_device(): lax.psum(jnp.dot(rows_all, up_weight, preferred_element_type=jnp.float32)...]
    all_gather x4 -> x0, blocking collectives: 223 us -> none  [the longest x1 69.7 us: per_device(): lax.all_gather(seg_keys, 'ctx', axis=0, tiled=True)]
    ppermute x128 -> x8, waiting for transfers between devices: 193 us -> 14 us  [swap(): return lax.ppermute(x, axis, [(i, i ^ mask) for i in range(n)])]
    unnamed x2 -> x0, blocking collectives: 177 us -> none
    lt x192 -> x0, other arithmetic: 125 us -> none  [advance(): alive = start + jnp.arange(span) < length]
    all_to_all x0 -> x2, blocking collectives: none -> 122 us  [the longest x1 91.8 us: per_device(): lax.all_to_all(sums.reshape(n_ctx, rows, -1), 'ctx', 0, 0, tiled=True)]
  transfers between devices with their start and end apart: 137 -> 11, of which waited for: 66 -> 11; matrix products, arithmetic and copies ran while one was open for 0% -> 0% of each run, Pallas kernels for 0% -> 0%
where the time goes in v1:
time: 319 us; the launch traced here: 316 us
  blocking collectives  122 us (38%)
  waiting for transfers between devices  103 us (32%)
  starting transfers between devices  65.3 us (20%)
  local copies, waits for them, and re-layouts  14.8 us (5%)
  Pallas kernels  5.07 us (2%)
    all_to_all x1, blocking collectives, per_device(): lax.all_to_all(sums.reshape(n_ctx, rows, -1), 'ctx', 0, 0, tiled=True)  91.8 us
    all_to_all x3, waiting for transfers between devices, to_all(): lax.all_to_all(jnp.broadcast_to(x[None], (n, *x.shape)), axis, 0, 0, tile...  88.6 us
    all_to_all x3, starting transfers between devices, to_all(): lax.all_to_all(jnp.broadcast_to(x[None], (n, *x.shape)), axis, 0, 0, tile...  33.1 us
    ppermute x8, starting transfers between devices, swap(): return lax.ppermute(x, axis, [(i, i ^ mask) for i in range(n)])  32.2 us
    all_to_all x1, blocking collectives, per_device(): lax.all_to_all(partial.reshape(n_ctx, rows, width + 128), 'ctx', 0, 0, ti...  29.9 us
    ppermute x8, waiting for transfers between devices, swap(): return lax.ppermute(x, axis, [(i, i ^ mask) for i in range(n)])  14 us
  transfers between devices with their start and end apart: 11, of which 11 were waited for; matrix products, arithmetic and copies ran while one was open for 0% of the time, Pallas kernels for 0%

profile of v1, /device:TPU:1, one launch (start us, length us, event | category | flops | bytes accessed | tf_op | source)
XLA Modules:
  0.0 315.7 jit_solution(15156304765032531607)
XLA Ops:
  0.6 1.5 broadcast_in_dim.52
  2.1 18.7 %all-to-all-start = ((bf16[32,6,512]{2,1,0:T(8,128)(2,1)}), bf16[32,6,512]{2,1,0:T(8,128)(2,1)S(1)}, u32[]{:S(2)}, u32[]{:S(2)}) async-start(bf16[32,6,512]{2,1,0:T(8,128)(2,1)} %broadcast_in_dim.52), calls=%async_computation | async-start | bytes 524288 | tf_op jit(solution)/shard_map/all_to_all | solution.py:97
  21.5 20.0 %all-to-all-done = bf16[32,6,512]{2,1,0:T(8,128)(2,1)S(1)} async-done(((bf16[32,6,512]{2,1,0:T(8,128)(2,1)}), bf16[32,6,512]{2,1,0:T(8,128)(2,1)S(1)}, u32[]{:S(2)}, u32[]{:S(2)}) %all-to-all-start) | async-done | bytes 196640 | tf_op jit(solution)/shard_map/all_to_all | solution.py:97
  41.6 1.1 copy-done.1
  42.7 1.1 copy-done.2
  43.9 0.7 copy-done.3
  44.6 0.7 copy-done.4
  45.2 4.1 %attend.1 = bf16[192,640]{1,0:T(8,128)(2,1)S(1)} custom-call(s32[2]{0:T(128)S(1)} %pad_add_fusion.where, bf16[192,512]{1,0:T(8,128)(2,1)S(1)} %reshape.114.q_ref, bf16[3072,128]{1,0:T(8,128)(2,1)S(1)} %bitcast.34, bf16[3072,128]{1,0:T(8,128)(2,1)S(1)} %bitcast.35, bf16[6,128]{1,0:T(8,128)(2,1)S(1)} %copy-done.3, bf16[6,128]{1,0:T(8,128)(2,1)S(1)} %copy-done.4), custom_call_target="tpu_custom_call" | custom-call | flops 1207959552 | bytes 2097152 | tf_op jit(solution)/shard_map/attend/pallas_call | solution.py:132
  49.4 29.9 %all_to_all.25.in_ref = bf16[32,6,640]{2,1,0:T(8,128)(2,1)S(1)} all-to-all(bf16[32,6,640]{2,1,0:T(8,128)(2,1)S(1)} %reshape.115), channel_id=1, replica_groups=mesh['ctx'=32,'tp'=16] {'ctx'}, dimensions={0} | all-to-all | bytes 491520 | tf_op jit(solution)/shard_map/all_to_all | solution.py:141
  79.3 1.0 merge.1
  80.3 1.4 broadcast_in_dim.53
  81.7 6.6 %all-to-all-start.2 = ((bf16[32,6,512]{2,1,0:T(8,128)(2,1)}), bf16[32,6,512]{2,1,0:T(8,128)(2,1)S(1)}, u32[]{:S(2)}, u32[]{:S(2)}) async-start(bf16[32,6,512]{2,1,0:T(8,128)(2,1)} %broadcast_in_dim.53), calls=%async_computation.2 | async-start | bytes 524288 | tf_op jit(solution)/shard_map/all_to_all | solution.py:97
  88.6 19.1 %all-to-all-done.2 = bf16[32,6,512]{2,1,0:T(8,128)(2,1)S(1)} async-done(((bf16[32,6,512]{2,1,0:T(8,128)(2,1)}), bf16[32,6,512]{2,1,0:T(8,128)(2,1)S(1)}, u32[]{:S(2)}, u32[]{:S(2)}) %all-to-all-start.2) | async-done | bytes 196640 | tf_op jit(solution)/shard_map/all_to_all | solution.py:97
  107.8 0.2 fusion
  108.0 5.4 %collective-permute-start = (bf16[192,256]{1,0:T(8,128)(2,1)S(1)}, bf16[192,256]{1,0:T(8,128)(2,1)S(1)}, u32[]{:S(2)}, u32[]{:S(2)}) collective-permute-start(bf16[192,256]{1,0:T(8,128)(2,1)S(1)} %fusion), channel_id=1, source_target_pairs={{0,1},{1,0},{2,3},{3,2},{4,5},{5,4},{6,7},{7,6},{8,9},{9,8},{10,11... | collective-permute-start | bytes 294920 | tf_op jit(solution)/shard_map/ppermute | solution.py:102
  113.4 0.9 collective-permute-done
  114.3 2.5 collective-permute-start.1
  116.8 3.4 %collective-permute-done.1 = bf16[192,256]{1,0:T(8,128)(2,1)S(1)} collective-permute-done((bf16[192,256]{1,0:T(8,128)(2,1)S(1)}, bf16[192,256]{1,0:T(8,128)(2,1)S(1)}, u32[]{:S(2)}, u32[]{:S(2)}) %collective-permute-start.1) | collective-permute-done | bytes 98336 | tf_op jit(solution)/shard_map/ppermute | solution.py:102
  120.3 3.2 %collective-permute-start.2 = (bf16[192,256]{1,0:T(8,128)(2,1)S(1)}, bf16[192,256]{1,0:T(8,128)(2,1)S(1)}, u32[]{:S(2)}, u32[]{:S(2)}) collective-permute-start(bf16[192,256]{1,0:T(8,128)(2,1)S(1)} %add_convert_fusion.2), channel_id=1, source_target_pairs={{0,4},{1,5},{2,6},{3,7},{4,0},{5,1},{6,2},{7,3},{8,12},{9,13},{10,... | collective-permute-start | bytes 294920 | tf_op jit(solution)/shard_map/ppermute | solution.py:102
  123.4 2.2 collective-permute-done.2
  125.7 4.9 %collective-permute-start.3 = (bf16[192,256]{1,0:T(8,128)(2,1)S(1)}, bf16[192,256]{1,0:T(8,128)(2,1)S(1)}, u32[]{:S(2)}, u32[]{:S(2)}) collective-permute-start(bf16[192,256]{1,0:T(8,128)(2,1)S(1)} %add_convert_fusion.1), channel_id=1, source_target_pairs={{0,8},{1,9},{2,10},{3,11},{4,12},{5,13},{6,14},{7,15},{8,0},{9,1},... | collective-permute-start | bytes 294920 | tf_op jit(solution)/shard_map/ppermute | solution.py:102
  130.5 2.1 collective-permute-done.3
  132.7 0.5 convolution_convert_fusion
  133.2 1.3 concatenate.9
  134.4 0.1 fusion.3
  134.7 0.2 copy.22
  134.9 0.2 copy.23
  135.1 0.2 copy.24
  135.2 0.5 convolution_convert_fusion.1
  135.7 1.2 concatenate.8
  137.0 3.0 concatenate.10
  140.0 91.8 %all_to_all.26 = bf16[32,6,3712]{2,1,0:T(8,128)(2,1)S(1)} all-to-all(bf16[32,6,3712]{2,1,0:T(8,128)(2,1)S(1)} %concatenate.10), channel_id=1, replica_groups=mesh['ctx'=32,'tp'=16] {'ctx'}, dimensions={0} | all-to-all | bytes 2850816 | tf_op jit(solution)/shard_map/all_to_all | solution.py:170
  231.8 0.4 convert_reduce_fusion
  232.2 0.2 slice_reduce_fusion
  232.5 1.0 broadcast_in_dim.61
  233.5 7.9 %all-to-all-start.4 = ((bf16[32,6,1848]{2,1,0:T(8,128)(2,1)}), bf16[32,6,1848]{2,1,0:T(8,128)(2,1)S(1)}, u32[]{:S(2)}, u32[]{:S(2)}) async-start(bf16[32,6,1848]{2,1,0:T(8,128)(2,1)} %broadcast_in_dim.61), calls=%async_computation.4 | async-start | bytes 1966080 | tf_op jit(solution)/shard_map/all_to_all | solution.py:97
  241.5 49.4 %all-to-all-done.4 = bf16[32,6,1848]{2,1,0:T(8,128)(2,1)S(1)} async-done(((bf16[32,6,1848]{2,1,0:T(8,128)(2,1)}), bf16[32,6,1848]{2,1,0:T(8,128)(2,1)S(1)}, u32[]{:S(2)}, u32[]{:S(2)}) %all-to-all-start.4) | async-done | bytes 709664 | tf_op jit(solution)/shard_map/all_to_all | solution.py:97
  290.9 0.5 dot_general.17
  291.4 1.6 fusion.1
  293.0 6.0 %collective-permute-start.4 = (bf16[8,12,256]{2,1,0:T(8,128)(2,1)S(1)}, bf16[8,12,256]{2,1,0:T(8,128)(2,1)S(1)}, u32[]{:S(2)}, u32[]{:S(2)}) collective-permute-start(bf16[8,12,256]{2,1,0:T(8,128)(2,1)S(1)} %fusion.4), channel_id=1, source_target_pairs={{0,1},{1,0},{2,3},{3,2},{4,5},{5,4},{6,7},{7,6},{8,9},{9,8},{10,11... | collective-permute-start | bytes 147464 | tf_op jit(solution)/shard_map/ppermute | solution.py:102
  299.0 0.9 collective-permute-done.4
  300.0 2.5 collective-permute-start.5
  302.5 2.0 collective-permute-done.5
  304.7 3.2 %collective-permute-start.6 = (bf16[2,12,256]{2,1,0:T(8,128)(2,1)S(1)}, bf16[2,12,256]{2,1,0:T(8,128)(2,1)S(1)}, u32[]{:S(2)}, u32[]{:S(2)}) collective-permute-start(bf16[2,12,256]{2,1,0:T(8,128)(2,1)S(1)} %bitcast.39), channel_id=1, source_target_pairs={{0,4},{1,5},{2,6},{3,7},{4,0},{5,1},{6,2},{7,3},{8,12},{9,13},{10,... | collective-permute-start | bytes 36872 | tf_op jit(solution)/shard_map/ppermute | solution.py:102
  307.9 1.3 collective-permute-done.6
  309.2 4.7 %collective-permute-start.7 = (bf16[1,12,256]{2,1,0:T(8,128)(2,1)S(1)}, bf16[1,12,256]{2,1,0:T(8,128)(2,1)S(1)}, u32[]{:S(2)}, u32[]{:S(2)}) collective-permute-start(bf16[1,12,256]{2,1,0:T(8,128)(2,1)S(1)} %dynamic-slice_convert_fusion.2), channel_id=1, source_target_pairs={{0,8},{1,9},{2,10},{3,11},{4,12},{5,13},{6,14},{7,15},{8,0},{9,1},... | collective-permute-start | bytes 18440 | tf_op jit(solution)/shard_map/ppermute | solution.py:102
  313.9 1.2 collective-permute-done.7
  315.1 0.6 fusion.8
  (44 shorter events, 1.2 us)
Async XLA Ops:
  0.6 132.0 %copy-start = (bf16[256,1848]{0,1:T(8,128)(2,1)S(1)}, bf16[256,1848]{0,1:T(8,128)(2,1)}, u32[]{:S(2)}) copy-start(bf16[256,1848]{0,1:T(8,128)(2,1)} %param.22) | copy-start | bytes 2838532
  2.1 39.4 %all-to-all-start = ((bf16[32,6,512]{2,1,0:T(8,128)(2,1)}), bf16[32,6,512]{2,1,0:T(8,128)(2,1)S(1)}, u32[]{:S(2)}, u32[]{:S(2)}) async-start(bf16[32,6,512]{2,1,0:T(8,128)(2,1)} %broadcast_in_dim.52), calls=%async_computation | async-start | bytes 524288 | tf_op jit(solution)/shard_map/all_to_all | solution.py:97
  41.6 1.1 copy-start.1
  42.7 1.1 copy-start.2
  43.9 0.7 copy-start.3
  44.6 0.7 copy-start.4
  49.3 39.2 %copy-start.7 = (bf16[12,256]{1,0:T(8,128)(2,1)S(1)}, bf16[12,256]{1,0:T(8,128)(2,1)}, u32[]{:S(2)}) copy-start(bf16[12,256]{1,0:T(8,128)(2,1)} %param.18) | copy-start | bytes 18436
  49.3 58.4 %copy-start.6 = (bf16[512,256]{1,0:T(8,128)(2,1)S(1)}, bf16[512,256]{1,0:T(8,128)(2,1)}, u32[]{:S(2)}) copy-start(bf16[512,256]{1,0:T(8,128)(2,1)} %param.19) | copy-start | bytes 786436
  79.3 53.3 %copy-start.8 = (f32[256]{0:T(256)S(1)}, f32[256]{0:T(256)}, u32[]{:S(2)}) copy-start(f32[256]{0:T(256)} %param.20) | copy-start | bytes 3076
  81.7 26.0 %all-to-all-start.2 = ((bf16[32,6,512]{2,1,0:T(8,128)(2,1)}), bf16[32,6,512]{2,1,0:T(8,128)(2,1)S(1)}, u32[]{:S(2)}, u32[]{:S(2)}) async-start(bf16[32,6,512]{2,1,0:T(8,128)(2,1)} %broadcast_in_dim.53), calls=%async_computation.2 | async-start | bytes 524288 | tf_op jit(solution)/shard_map/all_to_all | solution.py:97
  108.0 6.3 %collective-permute-start = (bf16[192,256]{1,0:T(8,128)(2,1)S(1)}, bf16[192,256]{1,0:T(8,128)(2,1)S(1)}, u32[]{:S(2)}, u32[]{:S(2)}) collective-permute-start(bf16[192,256]{1,0:T(8,128)(2,1)S(1)} %fusion), channel_id=1, source_target_pairs={{0,1},{1,0},{2,3},{3,2},{4,5},{5,4},{6,7},{7,6},{8,9},{9,8},{10,11... | collective-permute-start | bytes 294920 | tf_op jit(solution)/shard_map/ppermute | solution.py:102
  114.3 5.9 %collective-permute-start.1 = (bf16[192,256]{1,0:T(8,128)(2,1)S(1)}, bf16[192,256]{1,0:T(8,128)(2,1)S(1)}, u32[]{:S(2)}, u32[]{:S(2)}) collective-permute-start(bf16[192,256]{1,0:T(8,128)(2,1)S(1)} %add_convert_fusion.3), channel_id=1, source_target_pairs={{0,2},{1,3},{2,0},{3,1},{4,6},{5,7},{6,4},{7,5},{8,10},{9,11},{10,... | collective-permute-start | bytes 294920 | tf_op jit(solution)/shard_map/ppermute | solution.py:102
  120.3 5.4 %collective-permute-start.2 = (bf16[192,256]{1,0:T(8,128)(2,1)S(1)}, bf16[192,256]{1,0:T(8,128)(2,1)S(1)}, u32[]{:S(2)}, u32[]{:S(2)}) collective-permute-start(bf16[192,256]{1,0:T(8,128)(2,1)S(1)} %add_convert_fusion.2), channel_id=1, source_target_pairs={{0,4},{1,5},{2,6},{3,7},{4,0},{5,1},{6,2},{7,3},{8,12},{9,13},{10,... | collective-permute-start | bytes 294920 | tf_op jit(solution)/shard_map/ppermute | solution.py:102
  125.7 9.6 %copy-start.5 = (bf16[256,1848]{0,1:T(8,128)(2,1)S(1)}, bf16[256,1848]{0,1:T(8,128)(2,1)}, u32[]{:S(2)}) copy-start(bf16[256,1848]{0,1:T(8,128)(2,1)} %param.21) | copy-start | bytes 2838532
  125.7 7.0 %collective-permute-start.3 = (bf16[192,256]{1,0:T(8,128)(2,1)S(1)}, bf16[192,256]{1,0:T(8,128)(2,1)S(1)}, u32[]{:S(2)}, u32[]{:S(2)}) collective-permute-start(bf16[192,256]{1,0:T(8,128)(2,1)S(1)} %add_convert_fusion.1), channel_id=1, source_target_pairs={{0,8},{1,9},{2,10},{3,11},{4,12},{5,13},{6,14},{7,15},{8,0},{9,1},... | collective-permute-start | bytes 294920 | tf_op jit(solution)/shard_map/ppermute | solution.py:102
  233.5 57.3 %all-to-all-start.4 = ((bf16[32,6,1848]{2,1,0:T(8,128)(2,1)}), bf16[32,6,1848]{2,1,0:T(8,128)(2,1)S(1)}, u32[]{:S(2)}, u32[]{:S(2)}) async-start(bf16[32,6,1848]{2,1,0:T(8,128)(2,1)} %broadcast_in_dim.61), calls=%async_computation.4 | async-start | bytes 1966080 | tf_op jit(solution)/shard_map/all_to_all | solution.py:97
  293.0 6.9 %collective-permute-start.4 = (bf16[8,12,256]{2,1,0:T(8,128)(2,1)S(1)}, bf16[8,12,256]{2,1,0:T(8,128)(2,1)S(1)}, u32[]{:S(2)}, u32[]{:S(2)}) collective-permute-start(bf16[8,12,256]{2,1,0:T(8,128)(2,1)S(1)} %fusion.4), channel_id=1, source_target_pairs={{0,1},{1,0},{2,3},{3,2},{4,5},{5,4},{6,7},{7,6},{8,9},{9,8},{10,11... | collective-permute-start | bytes 147464 | tf_op jit(solution)/shard_map/ppermute | solution.py:102
  300.0 4.6 %collective-permute-start.5 = (bf16[4,12,256]{2,0,1:T(4,128)(2,1)S(1)}, bf16[4,12,256]{2,0,1:T(4,128)(2,1)S(1)}, u32[]{:S(2)}, u32[]{:S(2)}) collective-permute-start(bf16[4,12,256]{2,0,1:T(4,128)(2,1)S(1)} %bitcast.38), channel_id=1, source_target_pairs={{0,2},{1,3},{2,0},{3,1},{4,6},{5,7},{6,4},{7,5},{8,10},{9,11},{10,... | collective-permute-start | bytes 73736 | tf_op jit(solution)/shard_map/ppermute | solution.py:102
  304.7 4.5 %collective-permute-start.6 = (bf16[2,12,256]{2,1,0:T(8,128)(2,1)S(1)}, bf16[2,12,256]{2,1,0:T(8,128)(2,1)S(1)}, u32[]{:S(2)}, u32[]{:S(2)}) collective-permute-start(bf16[2,12,256]{2,1,0:T(8,128)(2,1)S(1)} %bitcast.39), channel_id=1, source_target_pairs={{0,4},{1,5},{2,6},{3,7},{4,0},{5,1},{6,2},{7,3},{8,12},{9,13},{10,... | collective-permute-start | bytes 36872 | tf_op jit(solution)/shard_map/ppermute | solution.py:102
  309.2 5.9 %collective-permute-start.7 = (bf16[1,12,256]{2,1,0:T(8,128)(2,1)S(1)}, bf16[1,12,256]{2,1,0:T(8,128)(2,1)S(1)}, u32[]{:S(2)}, u32[]{:S(2)}) collective-permute-start(bf16[1,12,256]{2,1,0:T(8,128)(2,1)S(1)} %dynamic-slice_convert_fusion.2), channel_id=1, source_target_pairs={{0,8},{1,9},{2,10},{3,11},{4,12},{5,13},{6,14},{7,15},{8,0},{9,1},... | collective-permute-start | bytes 18440 | tf_op jit(solution)/shard_map/ppermute | solution.py:102

commit v2 on v1

--- a/solution.py
+++ b/solution.py
@@ -22,7 +22,13 @@
     return one, two, (rest - two).astype(BF16).astype(F32)
 
 
-def attend_kernel(where, q_ref, k_ref, v_ref, sk_ref, sv_ref, out_ref, *, tokens, group, head, scale):
+def attend_kernel(
+    where, q_ref, k_hbm, v_hbm, sk_ref, sv_ref, out_ref, k_ref, v_ref, sems, *, tokens, group, head, scale
+):
+    k_copy = pltpu.make_async_copy(k_hbm, k_ref, sems.at[0])
+    v_copy = pltpu.make_async_copy(v_hbm, v_ref, sems.at[1])
+    k_copy.start()
+    v_copy.start()
     length = where[0]
     first = where[1]
     rows = tokens * group
@@ -52,6 +58,9 @@
     w = jnp.where(seen, jnp.exp(s - top), 0.0)
     total = jnp.sum(w, axis=0, keepdims=True)
     numer = lax.dot_general(sv_ref[...], w.astype(BF16), (((0,), (0,)), ((), ())), preferred_element_type=F32)
+
+    k_copy.wait()
+    v_copy.wait()
 
     def whole(step, carry):
         at = pl.ds(pl.multiple_of(step * SPAN, SPAN), SPAN)
@@ -92,14 +101,83 @@
         out_ref[:, mine] = (numer / jnp.sum(w, axis=0)).astype(BF16)
 
 
-def to_all(x, axis):
-    n = lax.axis_size(axis)
-    return lax.all_to_all(jnp.broadcast_to(x[None], (n, *x.shape)), axis, 0, 0, tiled=True)
+def project_kernel(sel, x_ref, gain_ref, w_ref, send_ref, stay_ref, *, bit, power):
+    quarter = send_ref.shape[1]
+    units = w_ref.shape[0]
+    stride = (2, 1)[bit]
+    mine = sel[bit]
+
+    def rows(which, other):
+        block = which * stride + other * (3 - stride)
+        return x_ref[pl.ds(pl.multiple_of(block * quarter, quarter), quarter), :]
+
+    x = jnp.concatenate([rows(1 - mine, 0), rows(1 - mine, 1), rows(mine, 0), rows(mine, 1)], axis=0).astype(F32)
+    y = lax.dot_general(
+        (x * gain_ref[...]).astype(BF16), w_ref[...], (((1,), (1,)), ((), ())), preferred_element_type=F32
+    )
+    if power:
+        parts = three_parts(jnp.sum(x * x, axis=1, keepdims=True))
+        cut = units // 128 * 128
+        spare = jnp.zeros((x.shape[0], send_ref.shape[2] - units - 3), F32)
+        y = jnp.concatenate([y[:, :cut], jnp.concatenate([y[:, cut:], *parts, spare], axis=1)], axis=1)
+    for other in range(2):
+        send_ref[other] = y[other * quarter : (other + 1) * quarter].astype(BF16)
+        stay_ref[other] = y[(2 + other) * quarter : (3 + other) * quarter]
+
+
+def resplit(x, units):
+    cut = units // 128 * 128
+    tail = x[:, cut:]
+    at = units - cut
+    one, two, three = three_parts(jnp.sum(tail[:, at : at + 3], axis=1, keepdims=True))
+    column = lax.broadcasted_iota(jnp.int32, tail.shape, 1) - at
+    tail = jnp.where(column == 0, one, jnp.where(column == 1, two, jnp.where(column == 2, three, tail)))
+    return jnp.concatenate([x[:, :cut], tail], axis=1)
+
+
+def halve_kernel(sel, stay_ref, got_ref, send_ref, keep_ref, *, bit, units):
+    mine = sel[bit]
+    send = stay_ref[1 - mine] + got_ref[1 - mine].astype(F32)
+    send_ref[...] = (resplit(send, units) if units else send).astype(BF16)
+    keep_ref[...] = stay_ref[mine] + got_ref[mine].astype(F32)
+
+
+def join_kernel(g_ref, g_got_ref, u_ref, u_got_ref, out_ref, *, units):
+    g = resplit(g_ref[...] + g_got_ref[...].astype(F32), units)
+    u = u_ref[...] + u_got_ref[...].astype(F32)
+    rows = out_ref.shape[1]
+    width = g.shape[1]
+    for i in range(out_ref.shape[0]):
+        out_ref[i, :, :width] = g[i * rows : (i + 1) * rows].astype(BF16)
+        out_ref[i, :, width:] = u[i * rows : (i + 1) * rows].astype(BF16)
+
+
+def hidden_kernel(in_ref, out_ref, *, units, width):
+    sums = jnp.sum(in_ref[...].astype(F32), axis=0)
+    power = jnp.sum(sums[:, units : units + 3], axis=1, keepdims=True) / D
+    inv = lax.rsqrt(power + 1e-06)
+    gate, upper = sums[:, :units] * inv, sums[:, width:] * inv
+    out_ref[...] = (gate / (1.0 + jnp.exp(-gate)) * upper).astype(BF16)
 
 
 def swap(x, axis, mask):
     n = lax.axis_size(axis)
     return lax.ppermute(x, axis, [(i, i ^ mask) for i in range(n)])
+
+
+def doubled(x, axis, bits):
+    here = lax.axis_index(axis)
+    for bit in bits:
+        got = swap(x, axis, 1 << bit)
+        first = ((here >> bit) & 1) == 0
+        x = jnp.where(first, jnp.concatenate([x, got]), jnp.concatenate([got, x]))
+    return x
+
+
+def all_tokens(x, axis):
+    x = doubled(x[None], axis, (4, 3, 2, 1, 0))
+    x = x.reshape(2, 2, 2, 2, 2, *x.shape[1:]).transpose(4, 3, 2, 1, 0, 5, 6)
+    return x.reshape(-1, x.shape[-1])
 
 
 def per_device(
@@ -126,16 +204,27 @@
     feats = residual_stream.shape[1]
     units = gate_weight.shape[1]
 
-    q_all = to_all(queries, "ctx").reshape(tokens, width)
+    q_all = all_tokens(queries, "ctx")
     where = jnp.stack([lengths[0], c * rows])
     vmem = pl.BlockSpec(memory_space=pltpu.VMEM)
+    smem = pl.BlockSpec(memory_space=pltpu.SMEM)
+    anywhere = pl.BlockSpec(memory_space=pl.ANY)
+    params = pltpu.CompilerParams(vmem_limit_bytes=60 * 2**20)
+    small = pltpu.CompilerParams(vmem_limit_bytes=24 * 2**20)
     partial = pl.pallas_call(
         functools.partial(attend_kernel, tokens=tokens, group=group, head=head, scale=1.0 / math.sqrt(head)),
         out_shape=jax.ShapeDtypeStruct((tokens, width + 128), BF16),
-        in_specs=[pl.BlockSpec(memory_space=pltpu.SMEM)] + [vmem] * 5,
+        in_specs=[smem, vmem, anywhere, anywhere, vmem, vmem],
         out_specs=vmem,
-        compiler_params=pltpu.CompilerParams(vmem_limit_bytes=40 * 2**20),
-        cost_estimate=pl.CostEstimate(flops=4 * tokens * width * stretch, bytes_accessed=2**21, transcendentals=tokens * group * stretch),
+        scratch_shapes=[
+            pltpu.VMEM((stretch, head), BF16),
+            pltpu.VMEM((stretch, head), BF16),
+            pltpu.SemaphoreType.DMA((2,)),
+        ],
+        compiler_params=params,
+        cost_estimate=pl.CostEstimate(
+            flops=4 * tokens * width * stretch, bytes_accessed=2**21, transcendentals=tokens * group * stretch
+        ),
         name="attend",
     )(where, q_all, cache_keys[0], cache_values[0], seg_keys, seg_values)
     parts = lax.all_to_all(partial.reshape(n_ctx, rows, width + 128), "ctx", 0, 0, tiled=True)
@@ -144,11 +233,11 @@
         out_shape=jax.ShapeDtypeStruct((rows, width), BF16),
         in_specs=[vmem],
         out_specs=vmem,
-        compiler_params=pltpu.CompilerParams(vmem_limit_bytes=40 * 2**20),
+        compiler_params=small,
         name="merge",
     )(parts)
 
-    heads_all = to_all(attention, "ctx").reshape(tokens, width)
+    heads_all = all_tokens(attention, "ctx")
     mixed = jnp.dot(heads_all, out_weight, preferred_element_type=F32)
     residual = jnp.where(
         (jnp.arange(n_tp) == t)[:, None, None], residual_stream.astype(F32)[None], 0.0
@@ -158,33 +247,78 @@
         got = swap(total, "tp", mask)
         total = (total.astype(F32) + got.astype(F32)).astype(BF16)
     stream = total
-    wide = stream.astype(F32)
-    squares = jnp.sum(wide * wide, axis=1, keepdims=True)
-    scaled = (wide * norm_gain).astype(BF16)
-    gate = jnp.dot(scaled, gate_weight, preferred_element_type=F32).astype(BF16)
-    upper = jnp.dot(scaled, up_weight, preferred_element_type=F32).astype(BF16)
-    pad = -(2 * units + 3) % 128
-    sums = jnp.concatenate(
-        [gate, upper] + [p.astype(BF16) for p in three_parts(squares)] + [jnp.zeros((tokens, pad), BF16)], axis=1
-    )
-    sums = lax.all_to_all(sums.reshape(n_ctx, rows, -1), "ctx", 0, 0, tiled=True)
-    sums = jnp.sum(sums.astype(F32), axis=0)
-    power = jnp.sum(sums[:, 2 * units : 2 * units + 3], axis=1, keepdims=True) / D
-    inv = lax.rsqrt(power + 1e-06)
-    gate, upper = sums[:, :units] * inv, sums[:, units : 2 * units] * inv
-    hidden = (jax.nn.silu(gate) * upper).astype(BF16)
-    hidden_all = to_all(hidden, "ctx").reshape(tokens, units)
-    lowered = jnp.dot(hidden_all, down_weight, preferred_element_type=F32)
-
-    keep = lowered.reshape(n_tp, trows, feats)
-    for bit in range(4):
-        both = keep.reshape(-1, 2, trows, feats)
+
+    y_hi, z_lo = c & 1, (c >> 1) & 1
+    sel = jnp.stack([y_hi, z_lo])
+    quarter = tokens // 4
+    wide_units = -(-(units + 3) // 128) * 128
+
+    def project(weight, bit, power):
+        out = wide_units if power else units
+        return pl.pallas_call(
+            functools.partial(project_kernel, bit=bit, power=power),
+            out_shape=(
+                jax.ShapeDtypeStruct((2, quarter, out), BF16),
+                jax.ShapeDtypeStruct((2, quarter, out), F32),
+            ),
+            in_specs=[smem, vmem, vmem, vmem],
+            out_specs=(vmem, vmem),
+            compiler_params=small,
+            cost_estimate=pl.CostEstimate(flops=2 * tokens * feats * units, bytes_accessed=2**21, transcendentals=0),
+            name="gate" if power else "up",
+        )(sel, stream, norm_gain[None], weight.T)
+
+    def halve(stay, got, bit, power):
+        out = stay.shape[2]
+        return pl.pallas_call(
+            functools.partial(halve_kernel, bit=bit, units=units if power else 0),
+            out_shape=(jax.ShapeDtypeStruct((quarter, out), BF16), jax.ShapeDtypeStruct((quarter, out), F32)),
+            in_specs=[smem, vmem, vmem],
+            out_specs=(vmem, vmem),
+            compiler_params=small,
+            name="halve_gate" if power else "halve_up",
+        )(sel, stay, got)
+
+    g_send, g_stay = project(gate_weight, 1, True)
+    g_got = swap(g_send, "ctx", 2)
+    u_send, u_stay = project(up_weight, 0, False)
+    u_got = swap(u_send, "ctx", 1)
+    g_send, g_stay = halve(g_stay, g_got, 0, True)
+    g_got = swap(g_send, "ctx", 1)
+    u_send, u_stay = halve(u_stay, u_got, 1, False)
+    u_got = swap(u_send, "ctx", 2)
+    far = n_ctx // 4
+    sums = pl.pallas_call(
+        functools.partial(join_kernel, units=units),
+        out_shape=jax.ShapeDtypeStruct((far, rows, wide_units + units), BF16),
+        in_specs=[vmem] * 4,
+        out_specs=vmem,
+        compiler_params=small,
+        name="join",
+    )(g_stay, g_got, u_stay, u_got)
+    turned = [sum(((i >> k) & 1) << (2 - k) for k in range(3)) for i in range(far)]
+    groups = [[j * 4 + q for j in turned] for q in range(4)]
+    sums = lax.all_to_all(sums, "ctx", 0, 0, axis_index_groups=groups, tiled=True)
+    hidden = pl.pallas_call(
+        functools.partial(hidden_kernel, units=units, width=wide_units),
+        out_shape=jax.ShapeDtypeStruct((rows, units), BF16),
+        in_specs=[vmem],
+        out_specs=vmem,
+        compiler_params=small,
+        name="hidden",
+    )(sums)
+    hidden = doubled(hidden[None], "ctx", (4, 3, 2)).reshape(quarter, units)
+    hidden = doubled(hidden, "ctx", (1, 0))
+    keep = jnp.dot(hidden, down_weight, preferred_element_type=F32)
+
+    for bit in (3, 2, 1, 0):
+        half = keep.shape[0] // 2
         mine = (t >> bit) & 1
-        send = lax.dynamic_index_in_dim(both, 1 - mine, 1, keepdims=False).astype(BF16)
-        stay = lax.dynamic_index_in_dim(both, mine, 1, keepdims=False)
+        send = lax.dynamic_slice_in_dim(keep, (1 - mine) * half, half, 0).astype(BF16)
+        stay = lax.dynamic_slice_in_dim(keep, mine * half, half, 0)
         keep = stay + swap(send, "tp", 1 << bit).astype(F32)
-    own = lax.dynamic_slice_in_dim(wide, t * trows, trows, 0)
-    layer_out = (own + keep[0]).astype(BF16)
+    own = lax.dynamic_slice_in_dim(stream, t * trows, trows, 0).astype(F32)
+    layer_out = (own + keep).astype(BF16)
     return (attention, layer_out)
 
 

time: 319 us -> 299 us (0.937)
  starting transfers between devices: 65.3 us -> 148 us
  blocking collectives: 122 us -> 56.8 us
  waiting for transfers between devices: 103 us -> 73.9 us
  local copies, waits for them, and re-layouts: 14.8 us -> 2.31 us
  Pallas kernels: 5.07 us -> 11.1 us
    ppermute x8 -> x27, starting transfers between devices: 32.2 us -> 148 us  [swap(): return lax.ppermute(x, axis, [(i, i ^ mask) for i in range(n)])]
    all_to_all x3 -> x0, waiting for transfers between devices: 88.6 us -> none  [to_all(): lax.all_to_all(jnp.broadcast_to(x[None], (n, *x.shape)), axis, 0, 0, tile...]
    all_to_all x1, blocking collectives: 91.8 us -> 22.6 us  [per_device(): lax.all_to_all(sums, 'ctx', 0, 0, axis_index_groups=groups, tiled=True)]
    ppermute x8 -> x27, waiting for transfers between devices: 14 us -> 73.9 us  [swap(): return lax.ppermute(x, axis, [(i, i ^ mask) for i in range(n)])]
    all_to_all x3 -> x0, starting transfers between devices: 33.1 us -> none  [to_all(): lax.all_to_all(jnp.broadcast_to(x[None], (n, *x.shape)), axis, 0, 0, tile...]
    concatenate x3 -> x0, local copies, waits for them, and re-layouts: 5.49 us -> none  [per_device(): jnp.concatenate([gate, upper] + [p.astype(BF16) for p in three_parts(squa...]
    all_to_all x1, blocking collectives: 29.9 us -> 34.2 us  [per_device(): lax.all_to_all(partial.reshape(n_ctx, rows, width + 128), 'ctx', 0, 0, ti...]
    broadcast_in_dim x4 -> x0, local copies, waits for them, and re-layouts: 3.93 us -> none  [the longest x3 3.92 us: to_all(): jnp.broadcast_to(x[None], (n, *x.shape))]
  transfers between devices with their start and end apart: 11 -> 27, of which waited for: 11 -> 26; matrix products, arithmetic and copies ran while one was open for 0% -> 0% of each run, Pallas kernels for 0% -> 1%
where the time goes in v2:
time: 299 us; the launch traced here: 298 us
  starting transfers between devices  148 us (49%)
  waiting for transfers between devices  73.9 us (25%)
  blocking collectives  56.8 us (19%)
  Pallas kernels  11.1 us (4%)
  other arithmetic  3.72 us (1%)
    ppermute x27, starting transfers between devices, swap(): return lax.ppermute(x, axis, [(i, i ^ mask) for i in range(n)])  148 us
    ppermute x27, waiting for transfers between devices, swap(): return lax.ppermute(x, axis, [(i, i ^ mask) for i in range(n)])  73.9 us
    all_to_all x1, blocking collectives, per_device(): lax.all_to_all(partial.reshape(n_ctx, rows, width + 128), 'ctx', 0, 0, ti...  34.2 us
    all_to_all x1, blocking collectives, per_device(): lax.all_to_all(sums, 'ctx', 0, 0, axis_index_groups=groups, tiled=True)  22.6 us
    pallas_call x1, Pallas kernels, per_device(): pl.pallas_call(functools.partial(attend_kernel, tokens=tokens, group=grou...  6.23 us
  transfers between devices with their start and end apart: 27, of which 26 were waited for; matrix products, arithmetic and copies ran while one was open for 0% of the time, Pallas kernels for 1%

profile of v2, /device:TPU:1, one launch (start us, length us, event | category | flops | bytes accessed | tf_op | source)
XLA Modules:
  0.0 297.8 jit_solution(14775606876375499728)
XLA Ops:
  0.6 16.4 %collective-permute-start = (bf16[1,6,512]{2,1,0:T(8,128)(2,1)}, bf16[1,6,512]{2,1,0:T(8,128)(2,1)S(1)}, u32[]{:S(2)}, u32[]{:S(2)}) collective-permute-start(bf16[1,6,512]{2,1,0:T(8,128)(2,1)} %bitcast.34), channel_id=1, source_target_pairs={{0,256},{16,272},{32,288},{48,304},{64,320},{80,336},{96,352},{112... | collective-permute-start | bytes 18440 | tf_op jit(solution)/shard_map/ppermute | solution.py:165
  19.1 5.4 %collective-permute-start.1 = (bf16[2,6,512]{2,1,0:T(8,128)(2,1)S(1)}, bf16[2,6,512]{2,1,0:T(8,128)(2,1)S(1)}, u32[]{:S(2)}, u32[]{:S(2)}) collective-permute-start(bf16[2,6,512]{2,1,0:T(8,128)(2,1)S(1)} %maximum_select_fusion.14), channel_id=1, source_target_pairs={{0,128},{16,144},{32,160},{48,176},{64,192},{80,208},{96,224},{112... | collective-permute-start | bytes 36872 | tf_op jit(solution)/shard_map/ppermute | solution.py:165
  24.5 3.0 %collective-permute-done.1 = bf16[2,6,512]{2,1,0:T(8,128)(2,1)S(1)} collective-permute-done((bf16[2,6,512]{2,1,0:T(8,128)(2,1)S(1)}, bf16[2,6,512]{2,1,0:T(8,128)(2,1)S(1)}, u32[]{:S(2)}, u32[]{:S(2)}) %collective-permute-start.1) | collective-permute-done | bytes 12320 | tf_op jit(solution)/shard_map/ppermute | solution.py:165
  27.5 3.0 %collective-permute-start.2 = (bf16[4,6,512]{2,1,0:T(8,128)(2,1)S(1)}, bf16[4,6,512]{2,1,0:T(8,128)(2,1)S(1)}, u32[]{:S(2)}, u32[]{:S(2)}) collective-permute-start(bf16[4,6,512]{2,1,0:T(8,128)(2,1)S(1)} %maximum_select_fusion.12), channel_id=1, source_target_pairs={{0,64},{16,80},{32,96},{48,112},{64,0},{80,16},{96,32},{112,48},{1... | collective-permute-start | bytes 73736 | tf_op jit(solution)/shard_map/ppermute | solution.py:165
  30.6 2.5 collective-permute-done.2
  33.1 2.6 collective-permute-start.3
  38.2 4.8 %collective-permute-start.4 = (bf16[16,6,512]{2,1,0:T(8,128)(2,1)S(1)}, bf16[16,6,512]{2,1,0:T(8,128)(2,1)S(1)}, u32[]{:S(2)}, u32[]{:S(2)}) collective-permute-start(bf16[16,6,512]{2,1,0:T(8,128)(2,1)S(1)} %maximum_select_fusion.6), channel_id=1, source_target_pairs={{0,16},{16,0},{32,48},{48,32},{64,80},{80,64},{96,112},{112,96},{1... | collective-permute-start | bytes 294920 | tf_op jit(solution)/shard_map/ppermute | solution.py:165
  43.6 1.8 collective-permute-done.4
  46.3 6.2 %attend.1 = bf16[192,640]{1,0:T(8,128)(2,1)} custom-call(s32[2]{0:T(128)} %pad_add_fusion.where, bf16[192,512]{1,0:T(8,128)(2,1)} %reshape.36.q_ref, bf16[3072,128]{1,0:T(8,128)(2,1)} %bitcast.36, bf16[3072,128]{1,0:T(8,128)(2,1)} %bitcast.37, bf16[6,128]{1,0:T(8,128)(2,1)} %sk_ref.1, bf16[6,128]{1,0:T(8,128)(2,1)} %sv_ref.1), custom_call_target="tpu_custom_call" | custom-call | flops 1207959552 | bytes 2097152 | tf_op jit(solution)/shard_map/attend/pallas_call | solution.py:214
  53.6 34.2 %all_to_all.10.in_ref = bf16[32,6,640]{2,1,0:T(8,128)(2,1)S(1)} all-to-all(bf16[32,6,640]{2,1,0:T(8,128)(2,1)S(1)} %reshape.37), channel_id=1, replica_groups=mesh['ctx'=32,'tp'=16] {'ctx'}, dimensions={0} | all-to-all | bytes 491520 | tf_op jit(solution)/shard_map/all_to_all | solution.py:230
  88.8 4.6 %collective-permute-start.5 = (bf16[1,6,512]{2,1,0:T(8,128)(2,1)}, bf16[1,6,512]{2,1,0:T(8,128)(2,1)S(1)}, u32[]{:S(2)}, u32[]{:S(2)}) collective-permute-start(bf16[1,6,512]{2,1,0:T(8,128)(2,1)} %bitcast.32), channel_id=1, source_target_pairs={{0,256},{16,272},{32,288},{48,304},{64,320},{80,336},{96,352},{112... | collective-permute-start | bytes 18440 | tf_op jit(solution)/shard_map/ppermute | solution.py:165
  93.5 8.7 %collective-permute-done.5 = bf16[1,6,512]{2,1,0:T(8,128)(2,1)S(1)} collective-permute-done((bf16[1,6,512]{2,1,0:T(8,128)(2,1)}, bf16[1,6,512]{2,1,0:T(8,128)(2,1)S(1)}, u32[]{:S(2)}, u32[]{:S(2)}) %collective-permute-start.5) | collective-permute-done | bytes 6176 | tf_op jit(solution)/shard_map/ppermute | solution.py:165
  102.9 3.3 %collective-permute-start.6 = (bf16[2,6,512]{2,1,0:T(8,128)(2,1)S(1)}, bf16[2,6,512]{2,1,0:T(8,128)(2,1)S(1)}, u32[]{:S(2)}, u32[]{:S(2)}) collective-permute-start(bf16[2,6,512]{2,1,0:T(8,128)(2,1)S(1)} %maximum_select_fusion.15), channel_id=1, source_target_pairs={{0,128},{16,144},{32,160},{48,176},{64,192},{80,208},{96,224},{112... | collective-permute-start | bytes 36872 | tf_op jit(solution)/shard_map/ppermute | solution.py:165
  106.2 5.1 %collective-permute-done.6 = bf16[2,6,512]{2,1,0:T(8,128)(2,1)S(1)} collective-permute-done((bf16[2,6,512]{2,1,0:T(8,128)(2,1)S(1)}, bf16[2,6,512]{2,1,0:T(8,128)(2,1)S(1)}, u32[]{:S(2)}, u32[]{:S(2)}) %collective-permute-start.6) | collective-permute-done | bytes 12320 | tf_op jit(solution)/shard_map/ppermute | solution.py:165
  111.3 1.9 collective-permute-start.7
  113.2 3.6 %collective-permute-done.7 = bf16[4,6,512]{2,1,0:T(8,128)(2,1)S(1)} collective-permute-done((bf16[4,6,512]{2,1,0:T(8,128)(2,1)S(1)}, bf16[4,6,512]{2,1,0:T(8,128)(2,1)S(1)}, u32[]{:S(2)}, u32[]{:S(2)}) %collective-permute-start.7) | collective-permute-done | bytes 24608 | tf_op jit(solution)/shard_map/ppermute | solution.py:165
  116.9 2.5 collective-permute-start.8
  119.5 2.5 collective-permute-done.8
  122.0 4.6 %collective-permute-start.9 = (bf16[16,6,512]{2,1,0:T(8,128)(2,1)S(1)}, bf16[16,6,512]{2,1,0:T(8,128)(2,1)S(1)}, u32[]{:S(2)}, u32[]{:S(2)}) collective-permute-start(bf16[16,6,512]{2,1,0:T(8,128)(2,1)S(1)} %maximum_select_fusion.7), channel_id=1, source_target_pairs={{0,16},{16,0},{32,48},{48,32},{64,80},{80,64},{96,112},{112,96},{1... | collective-permute-start | bytes 294920 | tf_op jit(solution)/shard_map/ppermute | solution.py:165
  126.9 2.3 collective-permute-done.9
  129.7 16.0 %collective-permute-start.10 = (bf16[192,256]{1,0:T(8,128)(2,1)S(1)}, bf16[192,256]{1,0:T(8,128)(2,1)S(1)}, u32[]{:S(2)}, u32[]{:S(2)}) collective-permute-start(bf16[192,256]{1,0:T(8,128)(2,1)S(1)} %fusion), channel_id=1, source_target_pairs={{0,1},{1,0},{2,3},{3,2},{4,5},{5,4},{6,7},{7,6},{8,9},{9,8},{10,11... | collective-permute-start | bytes 294920 | tf_op jit(solution)/shard_map/ppermute | solution.py:165
  146.6 2.4 collective-permute-start.11
  149.1 3.6 %collective-permute-done.11 = bf16[192,256]{1,0:T(8,128)(2,1)S(1)} collective-permute-done((bf16[192,256]{1,0:T(8,128)(2,1)S(1)}, bf16[192,256]{1,0:T(8,128)(2,1)S(1)}, u32[]{:S(2)}, u32[]{:S(2)}) %collective-permute-start.11) | collective-permute-done | bytes 98336 | tf_op jit(solution)/shard_map/ppermute | solution.py:165
  152.7 3.1 %collective-permute-start.12 = (bf16[192,256]{1,0:T(8,128)(2,1)S(1)}, bf16[192,256]{1,0:T(8,128)(2,1)S(1)}, u32[]{:S(2)}, u32[]{:S(2)}) collective-permute-start(bf16[192,256]{1,0:T(8,128)(2,1)S(1)} %add_convert_fusion.2), channel_id=1, source_target_pairs={{0,4},{1,5},{2,6},{3,7},{4,0},{5,1},{6,2},{7,3},{8,12},{9,13},{10,... | collective-permute-start | bytes 294920 | tf_op jit(solution)/shard_map/ppermute | solution.py:165
  155.8 2.2 collective-permute-done.12
  158.1 4.6 %collective-permute-start.13 = (bf16[192,256]{1,0:T(8,128)(2,1)S(1)}, bf16[192,256]{1,0:T(8,128)(2,1)S(1)}, u32[]{:S(2)}, u32[]{:S(2)}) collective-permute-start(bf16[192,256]{1,0:T(8,128)(2,1)S(1)} %add_convert_fusion.1), channel_id=1, source_target_pairs={{0,8},{1,9},{2,10},{3,11},{4,12},{5,13},{6,14},{7,15},{8,0},{9,1},... | collective-permute-start | bytes 294920 | tf_op jit(solution)/shard_map/ppermute | solution.py:165
  162.8 2.2 collective-permute-done.13
  166.1 1.9 collective-permute-start.14
  169.0 4.4 %collective-permute-start.16 = (bf16[2,48,1848]{2,1,0:T(8,128)(2,1)S(1)}, bf16[2,48,1848]{2,1,0:T(8,128)(2,1)S(1)}, u32[]{:S(2)}, u32[]{:S(2)}) collective-permute-start(bf16[2,48,1848]{2,1,0:T(8,128)(2,1)S(1)} %get-tuple-element.15), channel_id=1, source_target_pairs={{0,16},{16,0},{32,48},{48,32},{64,80},{80,64},{96,112},{112,96},{1... | collective-permute-start | bytes 1064456 | tf_op jit(solution)/shard_map/ppermute | solution.py:165
  175.1 3.5 %collective-permute-start.15 = (bf16[48,1920]{1,0:T(8,128)(2,1)S(1)}, bf16[48,1920]{1,0:T(8,128)(2,1)S(1)}, u32[]{:S(2)}, u32[]{:S(2)}) collective-permute-start(bf16[48,1920]{1,0:T(8,128)(2,1)S(1)} %get-tuple-element.13), channel_id=1, source_target_pairs={{0,16},{16,0},{32,48},{48,32},{64,80},{80,64},{96,112},{112,96},{1... | collective-permute-start | bytes 552968 | tf_op jit(solution)/shard_map/ppermute | solution.py:165
  179.4 3.4 %collective-permute-start.17 = (bf16[48,1848]{1,0:T(8,128)(2,1)S(1)}, bf16[48,1848]{1,0:T(8,128)(2,1)S(1)}, u32[]{:S(2)}, u32[]{:S(2)}) collective-permute-start(bf16[48,1848]{1,0:T(8,128)(2,1)S(1)} %get-tuple-element.17), channel_id=1, source_target_pairs={{0,32},{16,48},{32,0},{48,16},{64,96},{80,112},{96,64},{112,80},{1... | collective-permute-start | bytes 532232 | tf_op jit(solution)/shard_map/ppermute | solution.py:165
  182.8 2.9 collective-permute-done.17.u_got_ref
  185.9 22.6 %all_to_all.11.in_ref = bf16[8,6,3768]{2,1,0:T(8,128)(2,1)S(1)} all-to-all(bf16[8,6,3768]{2,1,0:T(8,128)(2,1)S(1)} %join.1), channel_id=1, replica_groups={{0,256,128,384,64,320,192,448},{16,272,144,400,80,336,208,464},{32,288,..., dimensions={0} | all-to-all | bytes 723456 | tf_op jit(solution)/shard_map/all_to_all | solution.py:301
  208.7 7.0 %collective-permute-start.18 = (bf16[1,6,1848]{2,1,0:T(8,128)(2,1)S(1)}, bf16[1,6,1848]{2,1,0:T(8,128)(2,1)S(1)}, u32[]{:S(2)}, u32[]{:S(2)}) collective-permute-start(bf16[1,6,1848]{2,1,0:T(8,128)(2,1)S(1)} %bitcast.24), channel_id=1, source_target_pairs={{0,256},{16,272},{32,288},{48,304},{64,320},{80,336},{96,352},{112... | collective-permute-start | bytes 66536 | tf_op jit(solution)/shard_map/ppermute | solution.py:165
  215.7 7.1 %collective-permute-done.18 = bf16[1,6,1848]{2,1,0:T(8,128)(2,1)S(1)} collective-permute-done((bf16[1,6,1848]{2,1,0:T(8,128)(2,1)S(1)}, bf16[1,6,1848]{2,1,0:T(8,128)(2,1)S(1)}, u32[]{:S(2)}, u32[]{:S(2)}) %collective-permute-start.18) | collective-permute-done | bytes 22208 | tf_op jit(solution)/shard_map/ppermute | solution.py:165
  222.9 7.4 %collective-permute-start.19 = (bf16[2,6,1848]{2,1,0:T(8,128)(2,1)S(1)}, bf16[2,6,1848]{2,1,0:T(8,128)(2,1)S(1)}, u32[]{:S(2)}, u32[]{:S(2)}) collective-permute-start(bf16[2,6,1848]{2,1,0:T(8,128)(2,1)S(1)} %maximum_select_fusion.11), channel_id=1, source_target_pairs={{0,128},{16,144},{32,160},{48,176},{64,192},{80,208},{96,224},{112... | collective-permute-start | bytes 133064 | tf_op jit(solution)/shard_map/ppermute | solution.py:165
  230.2 2.3 collective-permute-done.19
  232.5 4.3 %collective-permute-start.20 = (bf16[4,6,1848]{2,1,0:T(8,128)(2,1)S(1)}, bf16[4,6,1848]{2,1,0:T(8,128)(2,1)S(1)}, u32[]{:S(2)}, u32[]{:S(2)}) collective-permute-start(bf16[4,6,1848]{2,1,0:T(8,128)(2,1)S(1)} %maximum_select_fusion.8), channel_id=1, source_target_pairs={{0,64},{16,80},{32,96},{48,112},{64,0},{80,16},{96,32},{112,48},{1... | collective-permute-start | bytes 266120 | tf_op jit(solution)/shard_map/ppermute | solution.py:165
  236.8 3.6 %collective-permute-done.20 = bf16[4,6,1848]{2,1,0:T(8,128)(2,1)S(1)} collective-permute-done((bf16[4,6,1848]{2,1,0:T(8,128)(2,1)S(1)}, bf16[4,6,1848]{2,1,0:T(8,128)(2,1)S(1)}, u32[]{:S(2)}, u32[]{:S(2)}) %collective-permute-start.20) | collective-permute-done | bytes 88736 | tf_op jit(solution)/shard_map/ppermute | solution.py:165
  240.6 1.9 collective-permute-start.21
  242.6 4.4 %collective-permute-done.21 = bf16[48,1848]{1,0:T(8,128)(2,1)S(1)} collective-permute-done((bf16[48,1848]{1,0:T(8,128)(2,1)S(1)}, bf16[48,1848]{1,0:T(8,128)(2,1)S(1)}, u32[]{:S(2)}, u32[]{:S(2)}) %collective-permute-start.21) | collective-permute-done | bytes 177440 | tf_op jit(solution)/shard_map/ppermute | solution.py:165
  247.0 5.2 %collective-permute-start.22 = (bf16[96,1848]{1,0:T(8,128)(2,1)S(1)}, bf16[96,1848]{1,0:T(8,128)(2,1)S(1)}, u32[]{:S(2)}, u32[]{:S(2)}) collective-permute-start(bf16[96,1848]{1,0:T(8,128)(2,1)S(1)} %maximum_select_fusion.2), channel_id=1, source_target_pairs={{0,16},{16,0},{32,48},{48,32},{64,80},{80,64},{96,112},{112,96},{1... | collective-permute-start | bytes 1064456 | tf_op jit(solution)/shard_map/ppermute | solution.py:165
  252.2 4.9 %collective-permute-done.22 = bf16[96,1848]{1,0:T(8,128)(2,1)S(1)} collective-permute-done((bf16[96,1848]{1,0:T(8,128)(2,1)S(1)}, bf16[96,1848]{1,0:T(8,128)(2,1)S(1)}, u32[]{:S(2)}, u32[]{:S(2)}) %collective-permute-start.22) | collective-permute-done | bytes 354848 | tf_op jit(solution)/shard_map/ppermute | solution.py:165
  257.5 5.3 %collective-permute-start.23 = (bf16[96,256]{1,0:T(8,128)(2,1)S(1)}, bf16[96,256]{1,0:T(8,128)(2,1)S(1)}, u32[]{:S(2)}, u32[]{:S(2)}) collective-permute-start(bf16[96,256]{1,0:T(8,128)(2,1)S(1)} %dynamic-slice_convert_fusion), channel_id=1, source_target_pairs={{0,8},{1,9},{2,10},{3,11},{4,12},{5,13},{6,14},{7,15},{8,0},{9,1},... | collective-permute-start | bytes 147464 | tf_op jit(solution)/shard_map/ppermute | solution.py:165
  264.4 3.1 %collective-permute-start.24 = (bf16[48,256]{1,0:T(8,128)(2,1)S(1)}, bf16[48,256]{1,0:T(8,128)(2,1)S(1)}, u32[]{:S(2)}, u32[]{:S(2)}) collective-permute-start(bf16[48,256]{1,0:T(8,128)(2,1)S(1)} %dynamic-slice_convert_fusion.1), channel_id=1, source_target_pairs={{0,4},{1,5},{2,6},{3,7},{4,0},{5,1},{6,2},{7,3},{8,12},{9,13},{10,... | collective-permute-start | bytes 73736 | tf_op jit(solution)/shard_map/ppermute | solution.py:165
  269.0 2.3 collective-permute-start.25
  271.3 2.6 collective-permute-done.25
  273.9 22.4 %collective-permute-start.26 = (bf16[12,256]{1,0:T(8,128)(2,1)S(1)}, bf16[12,256]{1,0:T(8,128)(2,1)S(1)}, u32[]{:S(2)}, u32[]{:S(2)}) collective-permute-start(bf16[12,256]{1,0:T(8,128)(2,1)S(1)} %dynamic-slice_convert_fusion.3), channel_id=1, source_target_pairs={{0,1},{1,0},{2,3},{3,2},{4,5},{5,4},{6,7},{7,6},{8,9},{9,8},{10,11... | collective-permute-start | bytes 18440 | tf_op jit(solution)/shard_map/ppermute | solution.py:165
  (69 shorter events, 20.2 us)
Async XLA Ops:
  0.6 256.5 %copy-start = (bf16[1848,256]{1,0:T(8,128)(2,1)S(1)}, bf16[1848,256]{1,0:T(8,128)(2,1)}, u32[]{:S(2)}) copy-start(bf16[1848,256]{1,0:T(8,128)(2,1)} %param.23) | copy-start | bytes 2838532
  0.6 17.7 %collective-permute-start = (bf16[1,6,512]{2,1,0:T(8,128)(2,1)}, bf16[1,6,512]{2,1,0:T(8,128)(2,1)S(1)}, u32[]{:S(2)}, u32[]{:S(2)}) collective-permute-start(bf16[1,6,512]{2,1,0:T(8,128)(2,1)} %bitcast.34), channel_id=1, source_target_pairs={{0,256},{16,272},{32,288},{48,304},{64,320},{80,336},{96,352},{112... | collective-permute-start | bytes 18440 | tf_op jit(solution)/shard_map/ppermute | solution.py:165
  19.1 8.4 %collective-permute-start.1 = (bf16[2,6,512]{2,1,0:T(8,128)(2,1)S(1)}, bf16[2,6,512]{2,1,0:T(8,128)(2,1)S(1)}, u32[]{:S(2)}, u32[]{:S(2)}) collective-permute-start(bf16[2,6,512]{2,1,0:T(8,128)(2,1)S(1)} %maximum_select_fusion.14), channel_id=1, source_target_pairs={{0,128},{16,144},{32,160},{48,176},{64,192},{80,208},{96,224},{112... | collective-permute-start | bytes 36872 | tf_op jit(solution)/shard_map/ppermute | solution.py:165
  27.5 5.6 %collective-permute-start.2 = (bf16[4,6,512]{2,1,0:T(8,128)(2,1)S(1)}, bf16[4,6,512]{2,1,0:T(8,128)(2,1)S(1)}, u32[]{:S(2)}, u32[]{:S(2)}) collective-permute-start(bf16[4,6,512]{2,1,0:T(8,128)(2,1)S(1)} %maximum_select_fusion.12), channel_id=1, source_target_pairs={{0,64},{16,80},{32,96},{48,112},{64,0},{80,16},{96,32},{112,48},{1... | collective-permute-start | bytes 73736 | tf_op jit(solution)/shard_map/ppermute | solution.py:165
  33.1 5.0 %collective-permute-start.3 = (bf16[8,6,512]{2,1,0:T(8,128)(2,1)S(1)}, bf16[8,6,512]{2,1,0:T(8,128)(2,1)S(1)}, u32[]{:S(2)}, u32[]{:S(2)}) collective-permute-start(bf16[8,6,512]{2,1,0:T(8,128)(2,1)S(1)} %maximum_select_fusion.9), channel_id=1, source_target_pairs={{0,32},{16,48},{32,0},{48,16},{64,96},{80,112},{96,64},{112,80},{1... | collective-permute-start | bytes 147464 | tf_op jit(solution)/shard_map/ppermute | solution.py:165
  38.2 7.2 %collective-permute-start.4 = (bf16[16,6,512]{2,1,0:T(8,128)(2,1)S(1)}, bf16[16,6,512]{2,1,0:T(8,128)(2,1)S(1)}, u32[]{:S(2)}, u32[]{:S(2)}) collective-permute-start(bf16[16,6,512]{2,1,0:T(8,128)(2,1)S(1)} %maximum_select_fusion.6), channel_id=1, source_target_pairs={{0,16},{16,0},{32,48},{48,32},{64,80},{80,64},{96,112},{112,96},{1... | collective-permute-start | bytes 294920 | tf_op jit(solution)/shard_map/ppermute | solution.py:165
  52.6 74.3 %copy-start.5 = (bf16[12,256]{1,0:T(8,128)(2,1)S(1)}, bf16[12,256]{1,0:T(8,128)(2,1)}, u32[]{:S(2)}) copy-start(bf16[12,256]{1,0:T(8,128)(2,1)} %param.18) | copy-start | bytes 18436
  88.8 13.3 %collective-permute-start.5 = (bf16[1,6,512]{2,1,0:T(8,128)(2,1)}, bf16[1,6,512]{2,1,0:T(8,128)(2,1)S(1)}, u32[]{:S(2)}, u32[]{:S(2)}) collective-permute-start(bf16[1,6,512]{2,1,0:T(8,128)(2,1)} %bitcast.32), channel_id=1, source_target_pairs={{0,256},{16,272},{32,288},{48,304},{64,320},{80,336},{96,352},{112... | collective-permute-start | bytes 18440 | tf_op jit(solution)/shard_map/ppermute | solution.py:165
  102.9 8.4 %collective-permute-start.6 = (bf16[2,6,512]{2,1,0:T(8,128)(2,1)S(1)}, bf16[2,6,512]{2,1,0:T(8,128)(2,1)S(1)}, u32[]{:S(2)}, u32[]{:S(2)}) collective-permute-start(bf16[2,6,512]{2,1,0:T(8,128)(2,1)S(1)} %maximum_select_fusion.15), channel_id=1, source_target_pairs={{0,128},{16,144},{32,160},{48,176},{64,192},{80,208},{96,224},{112... | collective-permute-start | bytes 36872 | tf_op jit(solution)/shard_map/ppermute | solution.py:165
  111.3 5.6 %collective-permute-start.7 = (bf16[4,6,512]{2,1,0:T(8,128)(2,1)S(1)}, bf16[4,6,512]{2,1,0:T(8,128)(2,1)S(1)}, u32[]{:S(2)}, u32[]{:S(2)}) collective-permute-start(bf16[4,6,512]{2,1,0:T(8,128)(2,1)S(1)} %maximum_select_fusion.13), channel_id=1, source_target_pairs={{0,64},{16,80},{32,96},{48,112},{64,0},{80,16},{96,32},{112,48},{1... | collective-permute-start | bytes 73736 | tf_op jit(solution)/shard_map/ppermute | solution.py:165
  116.9 5.0 %collective-permute-start.8 = (bf16[8,6,512]{2,1,0:T(8,128)(2,1)S(1)}, bf16[8,6,512]{2,1,0:T(8,128)(2,1)S(1)}, u32[]{:S(2)}, u32[]{:S(2)}) collective-permute-start(bf16[8,6,512]{2,1,0:T(8,128)(2,1)S(1)} %maximum_select_fusion.10), channel_id=1, source_target_pairs={{0,32},{16,48},{32,0},{48,16},{64,96},{80,112},{96,64},{112,80},{1... | collective-permute-start | bytes 147464 | tf_op jit(solution)/shard_map/ppermute | solution.py:165
  122.0 7.2 %collective-permute-start.9 = (bf16[16,6,512]{2,1,0:T(8,128)(2,1)S(1)}, bf16[16,6,512]{2,1,0:T(8,128)(2,1)S(1)}, u32[]{:S(2)}, u32[]{:S(2)}) collective-permute-start(bf16[16,6,512]{2,1,0:T(8,128)(2,1)S(1)} %maximum_select_fusion.7), channel_id=1, source_target_pairs={{0,16},{16,0},{32,48},{48,32},{64,80},{80,64},{96,112},{112,96},{1... | collective-permute-start | bytes 294920 | tf_op jit(solution)/shard_map/ppermute | solution.py:165
  126.9 2.6 copy-start.4
  129.4 35.6 %copy-start.1 = (bf16[256,1848]{0,1:T(8,128)(2,1)S(1)}, bf16[256,1848]{0,1:T(8,128)(2,1)}, u32[]{:S(2)}) copy-start(bf16[256,1848]{0,1:T(8,128)(2,1)} %param.21) | copy-start | bytes 2838532
  129.5 35.6 %copy-start.3 = (f32[256]{0:T(256)S(1)}, f32[256]{0:T(256)}, u32[]{:S(2)}) copy-start(f32[256]{0:T(256)} %param.20) | copy-start | bytes 3076
  129.7 16.9 %collective-permute-start.10 = (bf16[192,256]{1,0:T(8,128)(2,1)S(1)}, bf16[192,256]{1,0:T(8,128)(2,1)S(1)}, u32[]{:S(2)}, u32[]{:S(2)}) collective-permute-start(bf16[192,256]{1,0:T(8,128)(2,1)S(1)} %fusion), channel_id=1, source_target_pairs={{0,1},{1,0},{2,3},{3,2},{4,5},{5,4},{6,7},{7,6},{8,9},{9,8},{10,11... | collective-permute-start | bytes 294920 | tf_op jit(solution)/shard_map/ppermute | solution.py:165
  146.6 21.4 %copy-start.2 = (bf16[256,1848]{0,1:T(8,128)(2,1)S(1)}, bf16[256,1848]{0,1:T(8,128)(2,1)}, u32[]{:S(2)}) copy-start(bf16[256,1848]{0,1:T(8,128)(2,1)} %param.22) | copy-start | bytes 2838532
  146.6 6.1 %collective-permute-start.11 = (bf16[192,256]{1,0:T(8,128)(2,1)S(1)}, bf16[192,256]{1,0:T(8,128)(2,1)S(1)}, u32[]{:S(2)}, u32[]{:S(2)}) collective-permute-start(bf16[192,256]{1,0:T(8,128)(2,1)S(1)} %add_convert_fusion.3), channel_id=1, source_target_pairs={{0,2},{1,3},{2,0},{3,1},{4,6},{5,7},{6,4},{7,5},{8,10},{9,11},{10,... | collective-permute-start | bytes 294920 | tf_op jit(solution)/shard_map/ppermute | solution.py:165
  152.7 5.4 %collective-permute-start.12 = (bf16[192,256]{1,0:T(8,128)(2,1)S(1)}, bf16[192,256]{1,0:T(8,128)(2,1)S(1)}, u32[]{:S(2)}, u32[]{:S(2)}) collective-permute-start(bf16[192,256]{1,0:T(8,128)(2,1)S(1)} %add_convert_fusion.2), channel_id=1, source_target_pairs={{0,4},{1,5},{2,6},{3,7},{4,0},{5,1},{6,2},{7,3},{8,12},{9,13},{10,... | collective-permute-start | bytes 294920 | tf_op jit(solution)/shard_map/ppermute | solution.py:165
  158.1 6.9 %collective-permute-start.13 = (bf16[192,256]{1,0:T(8,128)(2,1)S(1)}, bf16[192,256]{1,0:T(8,128)(2,1)S(1)}, u32[]{:S(2)}, u32[]{:S(2)}) collective-permute-start(bf16[192,256]{1,0:T(8,128)(2,1)S(1)} %add_convert_fusion.1), channel_id=1, source_target_pairs={{0,8},{1,9},{2,10},{3,11},{4,12},{5,13},{6,14},{7,15},{8,0},{9,1},... | collective-permute-start | bytes 294920 | tf_op jit(solution)/shard_map/ppermute | solution.py:165
  166.1 8.3 %collective-permute-start.14 = (bf16[2,48,1920]{2,1,0:T(8,128)(2,1)S(1)}, bf16[2,48,1920]{2,1,0:T(8,128)(2,1)S(1)}, u32[]{:S(2)}, u32[]{:S(2)}) collective-permute-start(bf16[2,48,1920]{2,1,0:T(8,128)(2,1)S(1)} %get-tuple-element.11), channel_id=1, source_target_pairs={{0,32},{16,48},{32,0},{48,16},{64,96},{80,112},{96,64},{112,80},{1... | collective-permute-start | bytes 1105928 | tf_op jit(solution)/shard_map/ppermute | solution.py:165
  169.0 9.8 %collective-permute-start.16 = (bf16[2,48,1848]{2,1,0:T(8,128)(2,1)S(1)}, bf16[2,48,1848]{2,1,0:T(8,128)(2,1)S(1)}, u32[]{:S(2)}, u32[]{:S(2)}) collective-permute-start(bf16[2,48,1848]{2,1,0:T(8,128)(2,1)S(1)} %get-tuple-element.15), channel_id=1, source_target_pairs={{0,16},{16,0},{32,48},{48,32},{64,80},{80,64},{96,112},{112,96},{1... | collective-permute-start | bytes 1064456 | tf_op jit(solution)/shard_map/ppermute | solution.py:165
  175.1 10.6 %collective-permute-start.15 = (bf16[48,1920]{1,0:T(8,128)(2,1)S(1)}, bf16[48,1920]{1,0:T(8,128)(2,1)S(1)}, u32[]{:S(2)}, u32[]{:S(2)}) collective-permute-start(bf16[48,1920]{1,0:T(8,128)(2,1)S(1)} %get-tuple-element.13), channel_id=1, source_target_pairs={{0,16},{16,0},{32,48},{48,32},{64,80},{80,64},{96,112},{112,96},{1... | collective-permute-start | bytes 552968 | tf_op jit(solution)/shard_map/ppermute | solution.py:165
  179.4 6.3 %collective-permute-start.17 = (bf16[48,1848]{1,0:T(8,128)(2,1)S(1)}, bf16[48,1848]{1,0:T(8,128)(2,1)S(1)}, u32[]{:S(2)}, u32[]{:S(2)}) collective-permute-start(bf16[48,1848]{1,0:T(8,128)(2,1)S(1)} %get-tuple-element.17), channel_id=1, source_target_pairs={{0,32},{16,48},{32,0},{48,16},{64,96},{80,112},{96,64},{112,80},{1... | collective-permute-start | bytes 532232 | tf_op jit(solution)/shard_map/ppermute | solution.py:165
  208.7 14.1 %collective-permute-start.18 = (bf16[1,6,1848]{2,1,0:T(8,128)(2,1)S(1)}, bf16[1,6,1848]{2,1,0:T(8,128)(2,1)S(1)}, u32[]{:S(2)}, u32[]{:S(2)}) collective-permute-start(bf16[1,6,1848]{2,1,0:T(8,128)(2,1)S(1)} %bitcast.24), channel_id=1, source_target_pairs={{0,256},{16,272},{32,288},{48,304},{64,320},{80,336},{96,352},{112... | collective-permute-start | bytes 66536 | tf_op jit(solution)/shard_map/ppermute | solution.py:165
  222.9 9.6 %collective-permute-start.19 = (bf16[2,6,1848]{2,1,0:T(8,128)(2,1)S(1)}, bf16[2,6,1848]{2,1,0:T(8,128)(2,1)S(1)}, u32[]{:S(2)}, u32[]{:S(2)}) collective-permute-start(bf16[2,6,1848]{2,1,0:T(8,128)(2,1)S(1)} %maximum_select_fusion.11), channel_id=1, source_target_pairs={{0,128},{16,144},{32,160},{48,176},{64,192},{80,208},{96,224},{112... | collective-permute-start | bytes 133064 | tf_op jit(solution)/shard_map/ppermute | solution.py:165
  232.5 7.9 %collective-permute-start.20 = (bf16[4,6,1848]{2,1,0:T(8,128)(2,1)S(1)}, bf16[4,6,1848]{2,1,0:T(8,128)(2,1)S(1)}, u32[]{:S(2)}, u32[]{:S(2)}) collective-permute-start(bf16[4,6,1848]{2,1,0:T(8,128)(2,1)S(1)} %maximum_select_fusion.8), channel_id=1, source_target_pairs={{0,64},{16,80},{32,96},{48,112},{64,0},{80,16},{96,32},{112,48},{1... | collective-permute-start | bytes 266120 | tf_op jit(solution)/shard_map/ppermute | solution.py:165
  240.6 6.3 %collective-permute-start.21 = (bf16[48,1848]{1,0:T(8,128)(2,1)S(1)}, bf16[48,1848]{1,0:T(8,128)(2,1)S(1)}, u32[]{:S(2)}, u32[]{:S(2)}) collective-permute-start(bf16[48,1848]{1,0:T(8,128)(2,1)S(1)} %select_n.171), channel_id=1, source_target_pairs={{0,32},{16,48},{32,0},{48,16},{64,96},{80,112},{96,64},{112,80},{1... | collective-permute-start | bytes 532232 | tf_op jit(solution)/shard_map/ppermute | solution.py:165
  247.0 10.1 %collective-permute-start.22 = (bf16[96,1848]{1,0:T(8,128)(2,1)S(1)}, bf16[96,1848]{1,0:T(8,128)(2,1)S(1)}, u32[]{:S(2)}, u32[]{:S(2)}) collective-permute-start(bf16[96,1848]{1,0:T(8,128)(2,1)S(1)} %maximum_select_fusion.2), channel_id=1, source_target_pairs={{0,16},{16,0},{32,48},{48,32},{64,80},{80,64},{96,112},{112,96},{1... | collective-permute-start | bytes 1064456 | tf_op jit(solution)/shard_map/ppermute | solution.py:165
  257.5 6.8 %collective-permute-start.23 = (bf16[96,256]{1,0:T(8,128)(2,1)S(1)}, bf16[96,256]{1,0:T(8,128)(2,1)S(1)}, u32[]{:S(2)}, u32[]{:S(2)}) collective-permute-start(bf16[96,256]{1,0:T(8,128)(2,1)S(1)} %dynamic-slice_convert_fusion), channel_id=1, source_target_pairs={{0,8},{1,9},{2,10},{3,11},{4,12},{5,13},{6,14},{7,15},{8,0},{9,1},... | collective-permute-start | bytes 147464 | tf_op jit(solution)/shard_map/ppermute | solution.py:165
  264.4 4.6 %collective-permute-start.24 = (bf16[48,256]{1,0:T(8,128)(2,1)S(1)}, bf16[48,256]{1,0:T(8,128)(2,1)S(1)}, u32[]{:S(2)}, u32[]{:S(2)}) collective-permute-start(bf16[48,256]{1,0:T(8,128)(2,1)S(1)} %dynamic-slice_convert_fusion.1), channel_id=1, source_target_pairs={{0,4},{1,5},{2,6},{3,7},{4,0},{5,1},{6,2},{7,3},{8,12},{9,13},{10,... | collective-permute-start | bytes 73736 | tf_op jit(solution)/shard_map/ppermute | solution.py:165
  269.0 4.9 %collective-permute-start.25 = (bf16[24,256]{1,0:T(8,128)(2,1)S(1)}, bf16[24,256]{1,0:T(8,128)(2,1)S(1)}, u32[]{:S(2)}, u32[]{:S(2)}) collective-permute-start(bf16[24,256]{1,0:T(8,128)(2,1)S(1)} %dynamic-slice_convert_fusion.2), channel_id=1, source_target_pairs={{0,2},{1,3},{2,0},{3,1},{4,6},{5,7},{6,4},{7,5},{8,10},{9,11},{10,... | collective-permute-start | bytes 36872 | tf_op jit(solution)/shard_map/ppermute | solution.py:165
  273.9 23.2 %collective-permute-start.26 = (bf16[12,256]{1,0:T(8,128)(2,1)S(1)}, bf16[12,256]{1,0:T(8,128)(2,1)S(1)}, u32[]{:S(2)}, u32[]{:S(2)}) collective-permute-start(bf16[12,256]{1,0:T(8,128)(2,1)S(1)} %dynamic-slice_convert_fusion.3), channel_id=1, source_target_pairs={{0,1},{1,0},{2,3},{3,2},{4,5},{5,4},{6,7},{7,6},{8,9},{9,8},{10,11... | collective-permute-start | bytes 18440 | tf_op jit(solution)/shard_map/ppermute | solution.py:165

commit v3 on v2

--- a/solution.py
+++ b/solution.py
@@ -33,32 +33,31 @@
     first = where[1]
     rows = tokens * group
     own = sk_ref.shape[0]
-    query = jnp.concatenate([q_ref[:, g * head : (g + 1) * head] for g in range(group)], axis=0)
+    query = q_ref[...].reshape(rows, head)
+    unit = scale / math.log(2.0)
 
     def scores(keys):
-        return lax.dot_general(keys, query, (((1,), (1,)), ((), ())), preferred_element_type=F32) * scale
+        return lax.dot_general(keys, query, (((1,), (1,)), ((), ())), preferred_element_type=F32)
+
+    def weigh(values, w):
+        return lax.dot_general(values, w.astype(BF16), (((0,), (0,)), ((), ())), preferred_element_type=F32)
 
     def add(carry, s, values):
         top, total, numer = carry
         top_new = jnp.maximum(top, jnp.max(s, axis=0, keepdims=True))
-        fade = jnp.exp(top - top_new)
-        w = jnp.exp(s - top_new)
-        total = total * fade + jnp.sum(w, axis=0, keepdims=True)
-        numer = numer * fade + lax.dot_general(
-            values, w.astype(BF16), (((0,), (0,)), ((), ())), preferred_element_type=F32
-        )
-        return top_new, total, numer
+        fade = jnp.exp2((top - top_new) * unit)
+        w = jnp.exp2((s - top_new) * unit)
+        return top_new, total * fade + jnp.sum(w, axis=0, keepdims=True), numer * fade + weigh(values, w)
 
     s = scores(sk_ref[...])
-    token = lax.broadcasted_iota(jnp.int32, (own, rows), 1) % tokens
+    token = lax.broadcasted_iota(jnp.int32, (own, rows), 1) // group
     place = first + lax.broadcasted_iota(jnp.int32, (own, rows), 0)
     seen = place <= token
     s = jnp.where(seen, s, LOW)
     top = jnp.max(s, axis=0, keepdims=True)
-    w = jnp.where(seen, jnp.exp(s - top), 0.0)
+    w = jnp.where(seen, jnp.exp2((s - top) * unit), 0.0)
     total = jnp.sum(w, axis=0, keepdims=True)
-    numer = lax.dot_general(sv_ref[...], w.astype(BF16), (((0,), (0,)), ((), ())), preferred_element_type=F32)
-
+    numer = weigh(sv_ref[...], w)
     k_copy.wait()
     v_copy.wait()
 
@@ -76,29 +75,31 @@
         return add(carry, jnp.where(live, s, LOW), v_ref[at, :])
 
     top, total, numer = lax.fori_loop(full, (length + SPAN - 1) // SPAN, part, carry)
-    out = (numer / total).T
-    stats = jnp.concatenate([*three_parts(top), *three_parts(total), jnp.zeros((2, rows), F32)], axis=0).T
-    for g in range(group):
-        mine = slice(g * tokens, (g + 1) * tokens)
-        out_ref[:, g * head : (g + 1) * head] = out[mine].astype(BF16)
-    tail = jnp.concatenate(
-        [stats[g * tokens : (g + 1) * tokens] for g in range(group)] + [jnp.zeros((tokens, 128 - 8 * group), F32)],
-        axis=1,
-    )
-    out_ref[:, group * head :] = tail.astype(BF16)
-
-
-def merge_kernel(in_ref, out_ref, *, group, head):
-    stats = in_ref[:, :, group * head :].astype(F32)
-    for g in range(group):
-        col = [stats[:, :, 8 * g + i : 8 * g + i + 1] for i in range(6)]
-        top = col[0] + col[1] + col[2]
-        total = col[3] + col[4] + col[5]
-        best = jnp.max(top, axis=0, keepdims=True)
-        w = jnp.exp(top - best) * total
-        mine = slice(g * head, (g + 1) * head)
-        numer = jnp.sum(in_ref[:, :, mine].astype(F32) * w, axis=0)
-        out_ref[:, mine] = (numer / jnp.sum(w, axis=0)).astype(BF16)
+    blocks = out_ref.shape[0]
+    each = rows // blocks
+    out_ref[:, :each, :] = (numer / total).T.astype(BF16).reshape(blocks, each, head)
+    stats = jnp.concatenate([*three_parts(top * unit), *three_parts(total), jnp.zeros((2, rows), F32)], axis=0)
+    stats = jnp.concatenate([stats, jnp.zeros((8, rows), F32)], axis=0)
+    spare = jnp.zeros((out_ref.shape[1] - each, head - each), F32)
+    for i in range(blocks):
+        tail = stats[: out_ref.shape[1] - each, i * each : (i + 1) * each]
+        out_ref[i, each:, :] = jnp.concatenate([tail, spare], axis=1).astype(BF16)
+
+
+def merge_kernel(in_ref, out_ref, copies_ref):
+    blocks, rows, head = copies_ref.shape
+    stat = [in_ref[:, rows + i, :].astype(F32) for i in range(6)]
+    top = stat[0] + stat[1] + stat[2]
+    total = stat[3] + stat[4] + stat[5]
+    w = jnp.exp2(top - jnp.max(top, axis=0, keepdims=True)) * total
+    w = (w / jnp.sum(w, axis=0, keepdims=True)).T
+    out = jnp.zeros((rows, head), F32)
+    for i in range(blocks):
+        out = out + in_ref[i, :rows, :].astype(F32) * w[:rows, i : i + 1]
+    out = out.astype(BF16)
+    out_ref[...] = out
+    for i in range(blocks):
+        copies_ref[i] = out
 
 
 def project_kernel(sel, x_ref, gain_ref, w_ref, send_ref, stay_ref, *, bit, power):
@@ -157,7 +158,9 @@
     power = jnp.sum(sums[:, units : units + 3], axis=1, keepdims=True) / D
     inv = lax.rsqrt(power + 1e-06)
     gate, upper = sums[:, :units] * inv, sums[:, width:] * inv
-    out_ref[...] = (gate / (1.0 + jnp.exp(-gate)) * upper).astype(BF16)
+    out = (gate / (1.0 + jnp.exp(-gate)) * upper).astype(BF16)
+    for i in range(out_ref.shape[0]):
+        out_ref[i] = out
 
 
 def swap(x, axis, mask):
@@ -172,12 +175,6 @@
         first = ((here >> bit) & 1) == 0
         x = jnp.where(first, jnp.concatenate([x, got]), jnp.concatenate([got, x]))
     return x
-
-
-def all_tokens(x, axis):
-    x = doubled(x[None], axis, (4, 3, 2, 1, 0))
-    x = x.reshape(2, 2, 2, 2, 2, *x.shape[1:]).transpose(4, 3, 2, 1, 0, 5, 6)
-    return x.reshape(-1, x.shape[-1])
 
 
 def per_device(
@@ -204,7 +201,9 @@
     feats = residual_stream.shape[1]
     units = gate_weight.shape[1]
 
-    q_all = all_tokens(queries, "ctx")
+    each = rows * group
+    q_all = jnp.broadcast_to(queries.reshape(1, each, head), (n_ctx, each, head))
+    q_all = lax.all_to_all(q_all, "ctx", 0, 0, tiled=True)
     where = jnp.stack([lengths[0], c * rows])
     vmem = pl.BlockSpec(memory_space=pltpu.VMEM)
     smem = pl.BlockSpec(memory_space=pltpu.SMEM)
@@ -213,7 +212,7 @@
     small = pltpu.CompilerParams(vmem_limit_bytes=24 * 2**20)
     partial = pl.pallas_call(
         functools.partial(attend_kernel, tokens=tokens, group=group, head=head, scale=1.0 / math.sqrt(head)),
-        out_shape=jax.ShapeDtypeStruct((tokens, width + 128), BF16),
+        out_shape=jax.ShapeDtypeStruct((n_ctx, each + 8, head), BF16),
         in_specs=[smem, vmem, anywhere, anywhere, vmem, vmem],
         out_specs=vmem,
         scratch_shapes=[
@@ -227,17 +226,17 @@
         ),
         name="attend",
     )(where, q_all, cache_keys[0], cache_values[0], seg_keys, seg_values)
-    parts = lax.all_to_all(partial.reshape(n_ctx, rows, width + 128), "ctx", 0, 0, tiled=True)
-    attention = pl.pallas_call(
-        functools.partial(merge_kernel, group=group, head=head),
-        out_shape=jax.ShapeDtypeStruct((rows, width), BF16),
+    parts = lax.all_to_all(partial, "ctx", 0, 0, tiled=True)
+    attention, copies = pl.pallas_call(
+        merge_kernel,
+        out_shape=(jax.ShapeDtypeStruct((each, head), BF16), jax.ShapeDtypeStruct((n_ctx, each, head), BF16)),
         in_specs=[vmem],
-        out_specs=vmem,
+        out_specs=(vmem, vmem),
         compiler_params=small,
         name="merge",
     )(parts)
-
-    heads_all = all_tokens(attention, "ctx")
+    attention = attention.reshape(rows, width)
+    heads_all = lax.all_to_all(copies, "ctx", 0, 0, tiled=True).reshape(tokens, width)
     mixed = jnp.dot(heads_all, out_weight, preferred_element_type=F32)
     residual = jnp.where(
         (jnp.arange(n_tp) == t)[:, None, None], residual_stream.astype(F32)[None], 0.0
@@ -296,18 +295,17 @@
         compiler_params=small,
         name="join",
     )(g_stay, g_got, u_stay, u_got)
-    turned = [sum(((i >> k) & 1) << (2 - k) for k in range(3)) for i in range(far)]
-    groups = [[j * 4 + q for j in turned] for q in range(4)]
+    groups = [[j * 4 + q for j in range(far)] for q in range(4)]
     sums = lax.all_to_all(sums, "ctx", 0, 0, axis_index_groups=groups, tiled=True)
     hidden = pl.pallas_call(
         functools.partial(hidden_kernel, units=units, width=wide_units),
-        out_shape=jax.ShapeDtypeStruct((rows, units), BF16),
+        out_shape=jax.ShapeDtypeStruct((far, rows, units), BF16),
         in_specs=[vmem],
         out_specs=vmem,
         compiler_params=small,
         name="hidden",
     )(sums)
-    hidden = doubled(hidden[None], "ctx", (4, 3, 2)).reshape(quarter, units)
+    hidden = lax.all_to_all(hidden, "ctx", 0, 0, axis_index_groups=groups, tiled=True).reshape(quarter, units)
     hidden = doubled(hidden, "ctx", (1, 0))
     keep = jnp.dot(hidden, down_weight, preferred_element_type=F32)
 

time: 299 us -> 247 us (0.83)
  starting transfers between devices: 148 us -> 95.5 us
  waiting for transfers between devices: 73.9 us -> 60.5 us
  blocking collectives: 56.8 us -> 69 us
    ppermute x27 -> x14, starting transfers between devices: 148 us -> 70.5 us  [swap(): return lax.ppermute(x, axis, [(i, i ^ mask) for i in range(n)])]
    ppermute x27 -> x14, waiting for transfers between devices: 73.9 us -> 28.8 us  [swap(): return lax.ppermute(x, axis, [(i, i ^ mask) for i in range(n)])]
    all_to_all x0 -> x2, waiting for transfers between devices: none -> 31.7 us  [the longest x1 15.9 us: per_device(): q_all = lax.all_to_all(q_all, 'ctx', 0, 0, tiled=True)]
    all_to_all x0 -> x2, starting transfers between devices: none -> 25 us  [the longest x1 18.7 us: per_device(): q_all = lax.all_to_all(q_all, 'ctx', 0, 0, tiled=True)]
    all_to_all x1 -> x2, blocking collectives: 34.2 us -> 44.4 us  [the longest x1 24.7 us: per_device(): parts = lax.all_to_all(partial, 'ctx', 0, 0, tiled=True)]
  transfers between devices with their start and end apart: 27 -> 16, of which waited for: 26 -> 14; matrix products, arithmetic and copies ran while one was open for 0% -> 1% of each run, Pallas kernels for 1% -> 1%
where the time goes in v3:
time: 247 us; the launch traced here: 246 us
  starting transfers between devices  95.5 us (39%)
  blocking collectives  69 us (28%)
  waiting for transfers between devices  60.5 us (24%)
  Pallas kernels  13.6 us (6%)
  local copies, waits for them, and re-layouts  3.33 us (1%)
    ppermute x14, starting transfers between devices, swap(): return lax.ppermute(x, axis, [(i, i ^ mask) for i in range(n)])  70.5 us
    ppermute x14, waiting for transfers between devices, swap(): return lax.ppermute(x, axis, [(i, i ^ mask) for i in range(n)])  28.8 us
    all_to_all x1, blocking collectives, per_device(): parts = lax.all_to_all(partial, 'ctx', 0, 0, tiled=True)  24.7 us
    all_to_all x1, blocking collectives, per_device(): lax.all_to_all(sums, 'ctx', 0, 0, axis_index_groups=groups, tiled=True)  24.6 us
    all_to_all x1, blocking collectives, per_device(): lax.all_to_all(hidden, 'ctx', 0, 0, axis_index_groups=groups, tiled=True)  19.7 us
    all_to_all x1, starting transfers between devices, per_device(): q_all = lax.all_to_all(q_all, 'ctx', 0, 0, tiled=True)  18.7 us
    all_to_all x1, waiting for transfers between devices, per_device(): q_all = lax.all_to_all(q_all, 'ctx', 0, 0, tiled=True)  15.9 us
    all_to_all x1, waiting for transfers between devices, per_device(): lax.all_to_all(copies, 'ctx', 0, 0, tiled=True).reshape(tokens, width)  15.8 us
  transfers between devices with their start and end apart: 16, of which 14 were waited for; matrix products, arithmetic and copies ran while one was open for 1% of the time, Pallas kernels for 1%

profile of v3, /device:TPU:1, one launch (start us, length us, event | category | flops | bytes accessed | tf_op | source)
XLA Modules:
  0.0 245.7 jit_solution(1413206735367924897)
XLA Ops:
  0.6 0.8 broadcast_in_dim.39
  1.4 0.7 broadcast_in_dim.40
  2.2 18.7 %all-to-all-start = ((bf16[32,24,128]{2,1,0:T(8,128)(2,1)}), bf16[32,24,128]{2,1,0:T(8,128)(2,1)S(1)}, u32[]{:S(2)}, u32[]{:S(2)}) async-start(bf16[32,24,128]{2,1,0:T(8,128)(2,1)} %broadcast_in_dim.40), calls=%async_computation | async-start | bytes 393216 | tf_op jit(solution)/shard_map/all_to_all | solution.py:206
  21.5 0.6 pad_add_fusion.where
  22.1 15.9 %all-to-all-done.q_ref = bf16[32,24,128]{2,1,0:T(8,128)(2,1)S(1)} async-done(((bf16[32,24,128]{2,1,0:T(8,128)(2,1)}), bf16[32,24,128]{2,1,0:T(8,128)(2,1)S(1)}, u32[]{:S(2)}, u32[]{:S(2)}) %all-to-all-start) | async-done | bytes 196640 | tf_op jit(solution)/shard_map/all_to_all | solution.py:206
  38.0 0.7 copy-done.5
  38.7 8.6 %attend.1 = bf16[32,32,128]{2,1,0:T(8,128)(2,1)} custom-call(s32[2]{0:T(128)} %pad_add_fusion.where, bf16[32,24,128]{2,1,0:T(8,128)(2,1)} %copy-done.5, bf16[3072,128]{1,0:T(8,128)(2,1)} %bitcast.15, bf16[3072,128]{1,0:T(8,128)(2,1)} %bitcast.16, bf16[6,128]{1,0:T(8,128)(2,1)} %sk_ref.1, bf16[6,128]{1,0:T(8,128)(2,1)} %sv_ref.1), custom_call_target="tpu_custom_call" | custom-call | flops 1207959552 | bytes 2097152 | tf_op jit(solution)/shard_map/attend/pallas_call | solution.py:213
  47.2 24.7 %all_to_all.25.in_ref = bf16[32,32,128]{2,1,0:T(8,128)(2,1)S(1)} all-to-all(bf16[32,32,128]{2,1,0:T(8,128)(2,1)} %attend.1), channel_id=1, replica_groups=mesh['ctx'=32,'tp'=16] {'ctx'}, dimensions={0} | all-to-all | bytes 524288 | tf_op jit(solution)/shard_map/all_to_all | solution.py:229
  71.9 1.1 merge.1
  73.0 6.3 %all-to-all-start.2 = ((bf16[32,24,128]{2,1,0:T(8,128)(2,1)}), bf16[32,24,128]{2,1,0:T(8,128)(2,1)S(1)}, u32[]{:S(2)}, u32[]{:S(2)}) async-start(bf16[32,24,128]{2,1,0:T(8,128)(2,1)} %get-tuple-element.13), calls=%async_computation.2 | async-start | bytes 393216 | tf_op jit(solution)/shard_map/all_to_all | solution.py:239
  79.7 15.8 %all-to-all-done.2 = bf16[32,24,128]{2,1,0:T(8,128)(2,1)S(1)} async-done(((bf16[32,24,128]{2,1,0:T(8,128)(2,1)}), bf16[32,24,128]{2,1,0:T(8,128)(2,1)S(1)}, u32[]{:S(2)}, u32[]{:S(2)}) %all-to-all-start.2) | async-done | bytes 196640 | tf_op jit(solution)/shard_map/all_to_all | solution.py:239
  95.6 0.2 fusion
  95.8 6.5 %collective-permute-start = (bf16[192,256]{1,0:T(8,128)(2,1)S(1)}, bf16[192,256]{1,0:T(8,128)(2,1)S(1)}, u32[]{:S(2)}, u32[]{:S(2)}) collective-permute-start(bf16[192,256]{1,0:T(8,128)(2,1)S(1)} %fusion), channel_id=1, source_target_pairs={{0,1},{1,0},{2,3},{3,2},{4,5},{5,4},{6,7},{7,6},{8,9},{9,8},{10,11... | collective-permute-start | bytes 294920 | tf_op jit(solution)/shard_map/ppermute | solution.py:168
  102.3 0.9 collective-permute-done
  103.3 2.4 collective-permute-start.1
  105.7 3.6 %collective-permute-done.1 = bf16[192,256]{1,0:T(8,128)(2,1)S(1)} collective-permute-done((bf16[192,256]{1,0:T(8,128)(2,1)S(1)}, bf16[192,256]{1,0:T(8,128)(2,1)S(1)}, u32[]{:S(2)}, u32[]{:S(2)}) %collective-permute-start.1) | collective-permute-done | bytes 98336 | tf_op jit(solution)/shard_map/ppermute | solution.py:168
  109.3 3.1 %collective-permute-start.2 = (bf16[192,256]{1,0:T(8,128)(2,1)S(1)}, bf16[192,256]{1,0:T(8,128)(2,1)S(1)}, u32[]{:S(2)}, u32[]{:S(2)}) collective-permute-start(bf16[192,256]{1,0:T(8,128)(2,1)S(1)} %add_convert_fusion.2), channel_id=1, source_target_pairs={{0,4},{1,5},{2,6},{3,7},{4,0},{5,1},{6,2},{7,3},{8,12},{9,13},{10,... | collective-permute-start | bytes 294920 | tf_op jit(solution)/shard_map/ppermute | solution.py:168
  112.5 2.2 collective-permute-done.2
  114.7 4.6 %collective-permute-start.3 = (bf16[192,256]{1,0:T(8,128)(2,1)S(1)}, bf16[192,256]{1,0:T(8,128)(2,1)S(1)}, u32[]{:S(2)}, u32[]{:S(2)}) collective-permute-start(bf16[192,256]{1,0:T(8,128)(2,1)S(1)} %add_convert_fusion.1), channel_id=1, source_target_pairs={{0,8},{1,9},{2,10},{3,11},{4,12},{5,13},{6,14},{7,15},{8,0},{9,1},... | collective-permute-start | bytes 294920 | tf_op jit(solution)/shard_map/ppermute | solution.py:168
  119.5 2.1 collective-permute-done.3
  121.6 1.0 gate.1
  122.7 2.1 collective-permute-start.4
  124.8 1.0 up.1
  125.8 4.0 %collective-permute-start.6 = (bf16[2,48,1848]{2,1,0:T(8,128)(2,1)S(1)}, bf16[2,48,1848]{2,1,0:T(8,128)(2,1)S(1)}, u32[]{:S(2)}, u32[]{:S(2)}) collective-permute-start(bf16[2,48,1848]{2,1,0:T(8,128)(2,1)S(1)} %get-tuple-element.19), channel_id=1, source_target_pairs={{0,16},{16,0},{32,48},{48,32},{64,80},{80,64},{96,112},{112,96},{1... | collective-permute-start | bytes 1064456 | tf_op jit(solution)/shard_map/ppermute | solution.py:168
  129.8 1.1 collective-permute-done.4.got_ref
  130.9 0.8 halve_gate.1
  131.7 4.2 %collective-permute-start.5 = (bf16[48,1920]{1,0:T(8,128)(2,1)S(1)}, bf16[48,1920]{1,0:T(8,128)(2,1)S(1)}, u32[]{:S(2)}, u32[]{:S(2)}) collective-permute-start(bf16[48,1920]{1,0:T(8,128)(2,1)S(1)} %get-tuple-element.17), channel_id=1, source_target_pairs={{0,16},{16,0},{32,48},{48,32},{64,80},{80,64},{96,112},{112,96},{1... | collective-permute-start | bytes 552968 | tf_op jit(solution)/shard_map/ppermute | solution.py:168
  135.9 0.6 halve_up.1
  136.5 2.9 %collective-permute-start.7 = (bf16[48,1848]{1,0:T(8,128)(2,1)S(1)}, bf16[48,1848]{1,0:T(8,128)(2,1)S(1)}, u32[]{:S(2)}, u32[]{:S(2)}) collective-permute-start(bf16[48,1848]{1,0:T(8,128)(2,1)S(1)} %get-tuple-element.21), channel_id=1, source_target_pairs={{0,32},{16,48},{32,0},{48,16},{64,96},{80,112},{96,64},{112,80},{1... | collective-permute-start | bytes 532232 | tf_op jit(solution)/shard_map/ppermute | solution.py:168
  139.4 3.7 %collective-permute-done.7.u_got_ref = bf16[48,1848]{1,0:T(8,128)(2,1)S(1)} collective-permute-done((bf16[48,1848]{1,0:T(8,128)(2,1)S(1)}, bf16[48,1848]{1,0:T(8,128)(2,1)S(1)}, u32[]{:S(2)}, u32[]{:S(2)}) %collective-permute-start.7) | collective-permute-done | bytes 177440 | tf_op jit(solution)/shard_map/ppermute | solution.py:168
  143.1 0.2 join.1
  143.3 24.6 %all_to_all.26.in_ref = bf16[8,6,3768]{2,1,0:T(8,128)(2,1)S(1)} all-to-all(bf16[8,6,3768]{2,1,0:T(8,128)(2,1)S(1)} %join.1), channel_id=1, replica_groups={{0,64,128,192,256,320,384,448},{16,80,144,208,272,336,400,464},{32,96,1..., dimensions={0} | all-to-all | bytes 723456 | tf_op jit(solution)/shard_map/all_to_all | solution.py:299
  167.9 0.2 hidden.1
  168.1 19.7 %all_to_all.27 = bf16[8,6,1848]{2,1,0:T(8,128)(2,1)S(1)} all-to-all(bf16[8,6,1848]{2,1,0:T(8,128)(2,1)S(1)} %hidden.1), channel_id=1, replica_groups={{0,64,128,192,256,320,384,448},{16,80,144,208,272,336,400,464},{32,96,1..., dimensions={0} | all-to-all | bytes 354816 | tf_op jit(solution)/shard_map/all_to_all | solution.py:308
  188.0 2.0 collective-permute-start.8
  190.0 4.4 %collective-permute-done.8 = bf16[48,1848]{1,0:T(8,128)(2,1)S(1)} collective-permute-done((bf16[48,1848]{1,0:T(8,128)(2,1)S(1)}, bf16[48,1848]{1,0:T(8,128)(2,1)S(1)}, u32[]{:S(2)}, u32[]{:S(2)}) %collective-permute-start.8) | collective-permute-done | bytes 177440 | tf_op jit(solution)/shard_map/ppermute | solution.py:168
  194.4 6.7 %collective-permute-start.9 = (bf16[96,1848]{1,0:T(8,128)(2,1)S(1)}, bf16[96,1848]{1,0:T(8,128)(2,1)S(1)}, u32[]{:S(2)}, u32[]{:S(2)}) collective-permute-start(bf16[96,1848]{1,0:T(8,128)(2,1)S(1)} %maximum_select_fusion.2), channel_id=1, source_target_pairs={{0,16},{16,0},{32,48},{48,32},{64,80},{80,64},{96,112},{112,96},{1... | collective-permute-start | bytes 1064456 | tf_op jit(solution)/shard_map/ppermute | solution.py:168
  201.2 4.9 %collective-permute-done.9 = bf16[96,1848]{1,0:T(8,128)(2,1)S(1)} collective-permute-done((bf16[96,1848]{1,0:T(8,128)(2,1)S(1)}, bf16[96,1848]{1,0:T(8,128)(2,1)S(1)}, u32[]{:S(2)}, u32[]{:S(2)}) %collective-permute-start.9) | collective-permute-done | bytes 354848 | tf_op jit(solution)/shard_map/ppermute | solution.py:168
  206.1 0.4 fusion.1
  206.5 4.6 %collective-permute-start.10 = (bf16[96,256]{1,0:T(8,128)(2,1)S(1)}, bf16[96,256]{1,0:T(8,128)(2,1)S(1)}, u32[]{:S(2)}, u32[]{:S(2)}) collective-permute-start(bf16[96,256]{1,0:T(8,128)(2,1)S(1)} %dynamic-slice_convert_fusion), channel_id=1, source_target_pairs={{0,8},{1,9},{2,10},{3,11},{4,12},{5,13},{6,14},{7,15},{8,0},{9,1},... | collective-permute-start | bytes 147464 | tf_op jit(solution)/shard_map/ppermute | solution.py:168
  211.1 1.7 collective-permute-done.10
  212.8 3.1 %collective-permute-start.11 = (bf16[48,256]{1,0:T(8,128)(2,1)S(1)}, bf16[48,256]{1,0:T(8,128)(2,1)S(1)}, u32[]{:S(2)}, u32[]{:S(2)}) collective-permute-start(bf16[48,256]{1,0:T(8,128)(2,1)S(1)} %dynamic-slice_convert_fusion.1), channel_id=1, source_target_pairs={{0,4},{1,5},{2,6},{3,7},{4,0},{5,1},{6,2},{7,3},{8,12},{9,13},{10,... | collective-permute-start | bytes 73736 | tf_op jit(solution)/shard_map/ppermute | solution.py:168
  216.0 1.4 collective-permute-done.11
  217.4 2.3 collective-permute-start.12
  219.8 2.6 %collective-permute-done.12 = bf16[24,256]{1,0:T(8,128)(2,1)S(1)} collective-permute-done((bf16[24,256]{1,0:T(8,128)(2,1)S(1)}, bf16[24,256]{1,0:T(8,128)(2,1)S(1)}, u32[]{:S(2)}, u32[]{:S(2)}) %collective-permute-start.12) | collective-permute-done | bytes 12320 | tf_op jit(solution)/shard_map/ppermute | solution.py:168
  222.4 21.9 %collective-permute-start.13 = (bf16[12,256]{1,0:T(8,128)(2,1)S(1)}, bf16[12,256]{1,0:T(8,128)(2,1)S(1)}, u32[]{:S(2)}, u32[]{:S(2)}) collective-permute-start(bf16[12,256]{1,0:T(8,128)(2,1)S(1)} %dynamic-slice_convert_fusion.3), channel_id=1, source_target_pairs={{0,1},{1,0},{2,3},{3,2},{4,5},{5,4},{6,7},{7,6},{8,9},{9,8},{10,11... | collective-permute-start | bytes 18440 | tf_op jit(solution)/shard_map/ppermute | solution.py:168
  244.3 0.6 reshape.23
  245.1 0.6 add_convert_fusion.4
  (36 shorter events, 1.0 us)
Async XLA Ops:
  0.6 205.4 %copy-start = (bf16[1848,256]{1,0:T(8,128)(2,1)S(1)}, bf16[1848,256]{1,0:T(8,128)(2,1)}, u32[]{:S(2)}) copy-start(bf16[1848,256]{1,0:T(8,128)(2,1)} %param.23) | copy-start | bytes 2838532
  2.2 35.8 %all-to-all-start = ((bf16[32,24,128]{2,1,0:T(8,128)(2,1)}), bf16[32,24,128]{2,1,0:T(8,128)(2,1)S(1)}, u32[]{:S(2)}, u32[]{:S(2)}) async-start(bf16[32,24,128]{2,1,0:T(8,128)(2,1)} %broadcast_in_dim.40), calls=%async_computation | async-start | bytes 393216 | tf_op jit(solution)/shard_map/all_to_all | solution.py:206
  38.0 0.7 copy-start.5
  47.2 32.4 %copy-start.6 = (bf16[12,256]{1,0:T(8,128)(2,1)S(1)}, bf16[12,256]{1,0:T(8,128)(2,1)}, u32[]{:S(2)}) copy-start(bf16[12,256]{1,0:T(8,128)(2,1)} %param.18) | copy-start | bytes 18436
  71.9 23.6 %copy-start.4 = (bf16[512,256]{1,0:T(8,128)(2,1)S(1)}, bf16[512,256]{1,0:T(8,128)(2,1)}, u32[]{:S(2)}) copy-start(bf16[512,256]{1,0:T(8,128)(2,1)} %param.19) | copy-start | bytes 786436
  73.0 22.4 %all-to-all-start.2 = ((bf16[32,24,128]{2,1,0:T(8,128)(2,1)}), bf16[32,24,128]{2,1,0:T(8,128)(2,1)S(1)}, u32[]{:S(2)}, u32[]{:S(2)}) async-start(bf16[32,24,128]{2,1,0:T(8,128)(2,1)} %get-tuple-element.13), calls=%async_computation.2 | async-start | bytes 393216 | tf_op jit(solution)/shard_map/all_to_all | solution.py:239
  95.6 26.1 %copy-start.1 = (bf16[256,1848]{0,1:T(8,128)(2,1)S(1)}, bf16[256,1848]{0,1:T(8,128)(2,1)}, u32[]{:S(2)}) copy-start(bf16[256,1848]{0,1:T(8,128)(2,1)} %param.21) | copy-start | bytes 2838532
  95.6 26.1 %copy-start.3 = (f32[256]{0:T(256)S(1)}, f32[256]{0:T(256)}, u32[]{:S(2)}) copy-start(f32[256]{0:T(256)} %param.20) | copy-start | bytes 3076
  95.8 7.4 %collective-permute-start = (bf16[192,256]{1,0:T(8,128)(2,1)S(1)}, bf16[192,256]{1,0:T(8,128)(2,1)S(1)}, u32[]{:S(2)}, u32[]{:S(2)}) collective-permute-start(bf16[192,256]{1,0:T(8,128)(2,1)S(1)} %fusion), channel_id=1, source_target_pairs={{0,1},{1,0},{2,3},{3,2},{4,5},{5,4},{6,7},{7,6},{8,9},{9,8},{10,11... | collective-permute-start | bytes 294920 | tf_op jit(solution)/shard_map/ppermute | solution.py:168
  103.2 21.6 %copy-start.2 = (bf16[256,1848]{0,1:T(8,128)(2,1)S(1)}, bf16[256,1848]{0,1:T(8,128)(2,1)}, u32[]{:S(2)}) copy-start(bf16[256,1848]{0,1:T(8,128)(2,1)} %param.22) | copy-start | bytes 2838532
  103.3 6.1 %collective-permute-start.1 = (bf16[192,256]{1,0:T(8,128)(2,1)S(1)}, bf16[192,256]{1,0:T(8,128)(2,1)S(1)}, u32[]{:S(2)}, u32[]{:S(2)}) collective-permute-start(bf16[192,256]{1,0:T(8,128)(2,1)S(1)} %add_convert_fusion.3), channel_id=1, source_target_pairs={{0,2},{1,3},{2,0},{3,1},{4,6},{5,7},{6,4},{7,5},{8,10},{9,11},{10,... | collective-permute-start | bytes 294920 | tf_op jit(solution)/shard_map/ppermute | solution.py:168
  109.3 5.4 %collective-permute-start.2 = (bf16[192,256]{1,0:T(8,128)(2,1)S(1)}, bf16[192,256]{1,0:T(8,128)(2,1)S(1)}, u32[]{:S(2)}, u32[]{:S(2)}) collective-permute-start(bf16[192,256]{1,0:T(8,128)(2,1)S(1)} %add_convert_fusion.2), channel_id=1, source_target_pairs={{0,4},{1,5},{2,6},{3,7},{4,0},{5,1},{6,2},{7,3},{8,12},{9,13},{10,... | collective-permute-start | bytes 294920 | tf_op jit(solution)/shard_map/ppermute | solution.py:168
  114.7 6.9 %collective-permute-start.3 = (bf16[192,256]{1,0:T(8,128)(2,1)S(1)}, bf16[192,256]{1,0:T(8,128)(2,1)S(1)}, u32[]{:S(2)}, u32[]{:S(2)}) collective-permute-start(bf16[192,256]{1,0:T(8,128)(2,1)S(1)} %add_convert_fusion.1), channel_id=1, source_target_pairs={{0,8},{1,9},{2,10},{3,11},{4,12},{5,13},{6,14},{7,15},{8,0},{9,1},... | collective-permute-start | bytes 294920 | tf_op jit(solution)/shard_map/ppermute | solution.py:168
  122.7 8.3 %collective-permute-start.4 = (bf16[2,48,1920]{2,1,0:T(8,128)(2,1)S(1)}, bf16[2,48,1920]{2,1,0:T(8,128)(2,1)S(1)}, u32[]{:S(2)}, u32[]{:S(2)}) collective-permute-start(bf16[2,48,1920]{2,1,0:T(8,128)(2,1)S(1)} %get-tuple-element.15), channel_id=1, source_target_pairs={{0,32},{16,48},{32,0},{48,16},{64,96},{80,112},{96,64},{112,80},{1... | collective-permute-start | bytes 1105928 | tf_op jit(solution)/shard_map/ppermute | solution.py:168
  125.8 10.1 %collective-permute-start.6 = (bf16[2,48,1848]{2,1,0:T(8,128)(2,1)S(1)}, bf16[2,48,1848]{2,1,0:T(8,128)(2,1)S(1)}, u32[]{:S(2)}, u32[]{:S(2)}) collective-permute-start(bf16[2,48,1848]{2,1,0:T(8,128)(2,1)S(1)} %get-tuple-element.19), channel_id=1, source_target_pairs={{0,16},{16,0},{32,48},{48,32},{64,80},{80,64},{96,112},{112,96},{1... | collective-permute-start | bytes 1064456 | tf_op jit(solution)/shard_map/ppermute | solution.py:168
  131.7 11.4 %collective-permute-start.5 = (bf16[48,1920]{1,0:T(8,128)(2,1)S(1)}, bf16[48,1920]{1,0:T(8,128)(2,1)S(1)}, u32[]{:S(2)}, u32[]{:S(2)}) collective-permute-start(bf16[48,1920]{1,0:T(8,128)(2,1)S(1)} %get-tuple-element.17), channel_id=1, source_target_pairs={{0,16},{16,0},{32,48},{48,32},{64,80},{80,64},{96,112},{112,96},{1... | collective-permute-start | bytes 552968 | tf_op jit(solution)/shard_map/ppermute | solution.py:168
  136.5 6.6 %collective-permute-start.7 = (bf16[48,1848]{1,0:T(8,128)(2,1)S(1)}, bf16[48,1848]{1,0:T(8,128)(2,1)S(1)}, u32[]{:S(2)}, u32[]{:S(2)}) collective-permute-start(bf16[48,1848]{1,0:T(8,128)(2,1)S(1)} %get-tuple-element.21), channel_id=1, source_target_pairs={{0,32},{16,48},{32,0},{48,16},{64,96},{80,112},{96,64},{112,80},{1... | collective-permute-start | bytes 532232 | tf_op jit(solution)/shard_map/ppermute | solution.py:168
  188.0 6.4 %collective-permute-start.8 = (bf16[48,1848]{1,0:T(8,128)(2,1)S(1)}, bf16[48,1848]{1,0:T(8,128)(2,1)S(1)}, u32[]{:S(2)}, u32[]{:S(2)}) collective-permute-start(bf16[48,1848]{1,0:T(8,128)(2,1)S(1)} %reshape.25), channel_id=1, source_target_pairs={{0,32},{16,48},{32,0},{48,16},{64,96},{80,112},{96,64},{112,80},{1... | collective-permute-start | bytes 532232 | tf_op jit(solution)/shard_map/ppermute | solution.py:168
  194.4 11.6 %collective-permute-start.9 = (bf16[96,1848]{1,0:T(8,128)(2,1)S(1)}, bf16[96,1848]{1,0:T(8,128)(2,1)S(1)}, u32[]{:S(2)}, u32[]{:S(2)}) collective-permute-start(bf16[96,1848]{1,0:T(8,128)(2,1)S(1)} %maximum_select_fusion.2), channel_id=1, source_target_pairs={{0,16},{16,0},{32,48},{48,32},{64,80},{80,64},{96,112},{112,96},{1... | collective-permute-start | bytes 1064456 | tf_op jit(solution)/shard_map/ppermute | solution.py:168
  206.5 6.3 %collective-permute-start.10 = (bf16[96,256]{1,0:T(8,128)(2,1)S(1)}, bf16[96,256]{1,0:T(8,128)(2,1)S(1)}, u32[]{:S(2)}, u32[]{:S(2)}) collective-permute-start(bf16[96,256]{1,0:T(8,128)(2,1)S(1)} %dynamic-slice_convert_fusion), channel_id=1, source_target_pairs={{0,8},{1,9},{2,10},{3,11},{4,12},{5,13},{6,14},{7,15},{8,0},{9,1},... | collective-permute-start | bytes 147464 | tf_op jit(solution)/shard_map/ppermute | solution.py:168
  212.8 4.6 %collective-permute-start.11 = (bf16[48,256]{1,0:T(8,128)(2,1)S(1)}, bf16[48,256]{1,0:T(8,128)(2,1)S(1)}, u32[]{:S(2)}, u32[]{:S(2)}) collective-permute-start(bf16[48,256]{1,0:T(8,128)(2,1)S(1)} %dynamic-slice_convert_fusion.1), channel_id=1, source_target_pairs={{0,4},{1,5},{2,6},{3,7},{4,0},{5,1},{6,2},{7,3},{8,12},{9,13},{10,... | collective-permute-start | bytes 73736 | tf_op jit(solution)/shard_map/ppermute | solution.py:168
  217.4 4.9 %collective-permute-start.12 = (bf16[24,256]{1,0:T(8,128)(2,1)S(1)}, bf16[24,256]{1,0:T(8,128)(2,1)S(1)}, u32[]{:S(2)}, u32[]{:S(2)}) collective-permute-start(bf16[24,256]{1,0:T(8,128)(2,1)S(1)} %dynamic-slice_convert_fusion.2), channel_id=1, source_target_pairs={{0,2},{1,3},{2,0},{3,1},{4,6},{5,7},{6,4},{7,5},{8,10},{9,11},{10,... | collective-permute-start | bytes 36872 | tf_op jit(solution)/shard_map/ppermute | solution.py:168
  222.4 22.7 %collective-permute-start.13 = (bf16[12,256]{1,0:T(8,128)(2,1)S(1)}, bf16[12,256]{1,0:T(8,128)(2,1)S(1)}, u32[]{:S(2)}, u32[]{:S(2)}) collective-permute-start(bf16[12,256]{1,0:T(8,128)(2,1)S(1)} %dynamic-slice_convert_fusion.3), channel_id=1, source_target_pairs={{0,1},{1,0},{2,3},{3,2},{4,5},{5,4},{6,7},{7,6},{8,9},{9,8},{10,11... | collective-permute-start | bytes 18440 | tf_op jit(solution)/shard_map/ppermute | solution.py:168

commit v4 on v3

--- a/solution.py
+++ b/solution.py
@@ -196,7 +196,7 @@
     group = width // head
     n_ctx, n_tp = lax.axis_size("ctx"), lax.axis_size("tp")
     tokens = rows * n_ctx
-    c, t = lax.axis_index("ctx"), lax.axis_index("tp")
+    c = lax.axis_index("ctx")
     trows = residual_stream.shape[0]
     feats = residual_stream.shape[1]
     units = gate_weight.shape[1]
@@ -238,14 +238,14 @@
     attention = attention.reshape(rows, width)
     heads_all = lax.all_to_all(copies, "ctx", 0, 0, tiled=True).reshape(tokens, width)
     mixed = jnp.dot(heads_all, out_weight, preferred_element_type=F32)
-    residual = jnp.where(
-        (jnp.arange(n_tp) == t)[:, None, None], residual_stream.astype(F32)[None], 0.0
-    ).reshape(tokens, feats)
-    total = (mixed + residual).astype(BF16)
-    for mask in (1, 2, 4, 8):
-        got = swap(total, "tp", mask)
-        total = (total.astype(F32) + got.astype(F32)).astype(BF16)
-    stream = total
+
+    def sum_tp(x):
+        x = x.astype(BF16).reshape(n_tp, trows, feats)
+        return jnp.sum(lax.all_to_all(x, "tp", 0, 0, tiled=True).astype(F32), axis=0)
+
+    own = (residual_stream.astype(F32) + sum_tp(mixed)).astype(BF16)
+    stream = jnp.broadcast_to(own[None], (n_tp, trows, feats))
+    stream = lax.all_to_all(stream, "tp", 0, 0, tiled=True).reshape(tokens, feats)
 
     y_hi, z_lo = c & 1, (c >> 1) & 1
     sel = jnp.stack([y_hi, z_lo])
@@ -307,16 +307,8 @@
     )(sums)
     hidden = lax.all_to_all(hidden, "ctx", 0, 0, axis_index_groups=groups, tiled=True).reshape(quarter, units)
     hidden = doubled(hidden, "ctx", (1, 0))
-    keep = jnp.dot(hidden, down_weight, preferred_element_type=F32)
-
-    for bit in (3, 2, 1, 0):
-        half = keep.shape[0] // 2
-        mine = (t >> bit) & 1
-        send = lax.dynamic_slice_in_dim(keep, (1 - mine) * half, half, 0).astype(BF16)
-        stay = lax.dynamic_slice_in_dim(keep, mine * half, half, 0)
-        keep = stay + swap(send, "tp", 1 << bit).astype(F32)
-    own = lax.dynamic_slice_in_dim(stream, t * trows, trows, 0).astype(F32)
-    layer_out = (own + keep).astype(BF16)
+    lowered = jnp.dot(hidden, down_weight, preferred_element_type=F32)
+    layer_out = (own.astype(F32) + sum_tp(lowered)).astype(BF16)
     return (attention, layer_out)
 
 

time: 247 us -> 236 us (0.955)
  starting transfers between devices: 95.5 us -> 61.2 us
  blocking collectives: 69 us -> 99.3 us
  waiting for transfers between devices: 60.5 us -> 52.8 us
    ppermute x14 -> x6, starting transfers between devices: 70.5 us -> 20.9 us  [swap(): return lax.ppermute(x, axis, [(i, i ^ mask) for i in range(n)])]
    all_to_all x0 -> x1, blocking collectives: none -> 22.6 us  [per_device(): lax.all_to_all(copies, 'ctx', 0, 0, tiled=True).reshape(tokens, width)]
    all_to_all x1 -> x3, starting transfers between devices: 6.34 us -> 21.6 us  [the longest x2 17.9 us: sum_tp(): lax.all_to_all(x, 'tp', 0, 0, tiled=True).astype(F32)]
    ppermute x14 -> x6, waiting for transfers between devices: 28.8 us -> 18.9 us  [swap(): return lax.ppermute(x, axis, [(i, i ^ mask) for i in range(n)])]
    all_to_all x1, blocking collectives: 19.7 us -> 25.8 us  [per_device(): lax.all_to_all(hidden, 'ctx', 0, 0, axis_index_groups=groups, tiled=True)]
    all_to_all x1 -> x3, waiting for transfers between devices: 15.8 us -> 17.9 us  [the longest x2 11.8 us: sum_tp(): lax.all_to_all(x, 'tp', 0, 0, tiled=True).astype(F32)]
  transfers between devices with their start and end apart: 16 -> 10, of which waited for: 14 -> 8; matrix products, arithmetic and copies ran while one was open for 1% -> 1% of each run, Pallas kernels for 1% -> 1%
where the time goes in v4:
time: 236 us; the launch traced here: 235 us
  blocking collectives  99.3 us (42%)
  starting transfers between devices  61.2 us (26%)
  waiting for transfers between devices  52.8 us (22%)
  Pallas kernels  12.9 us (5%)
  local copies, waits for them, and re-layouts  5.08 us (2%)
    all_to_all x1, blocking collectives, per_device(): lax.all_to_all(sums, 'ctx', 0, 0, axis_index_groups=groups, tiled=True)  26.5 us
    all_to_all x1, blocking collectives, per_device(): lax.all_to_all(hidden, 'ctx', 0, 0, axis_index_groups=groups, tiled=True)  25.8 us
    all_to_all x1, blocking collectives, per_device(): parts = lax.all_to_all(partial, 'ctx', 0, 0, tiled=True)  24.2 us
    all_to_all x1, blocking collectives, per_device(): lax.all_to_all(copies, 'ctx', 0, 0, tiled=True).reshape(tokens, width)  22.6 us
    ppermute x6, starting transfers between devices, swap(): return lax.ppermute(x, axis, [(i, i ^ mask) for i in range(n)])  20.9 us
    ppermute x6, waiting for transfers between devices, swap(): return lax.ppermute(x, axis, [(i, i ^ mask) for i in range(n)])  18.9 us
    all_to_all x1, starting transfers between devices, per_device(): q_all = lax.all_to_all(q_all, 'ctx', 0, 0, tiled=True)  18.7 us
    all_to_all x2, starting transfers between devices, sum_tp(): lax.all_to_all(x, 'tp', 0, 0, tiled=True).astype(F32)  17.9 us
  transfers between devices with their start and end apart: 10, of which 8 were waited for; matrix products, arithmetic and copies ran while one was open for 1% of the time, Pallas kernels for 1%

profile of v4, /device:TPU:1, one launch (start us, length us, event | category | flops | bytes accessed | tf_op | source)
XLA Modules:
  0.0 234.7 jit_solution(10020080337655482521)
XLA Ops:
  0.6 0.0 copy-start
  0.6 0.8 broadcast_in_dim.8
  1.4 0.7 broadcast_in_dim.18
  2.1 18.7 %all-to-all-start = ((bf16[32,24,128]{2,1,0:T(8,128)(2,1)}), bf16[32,24,128]{2,1,0:T(8,128)(2,1)S(1)}, u32[]{:S(2)}, u32[]{:S(2)}) async-start(bf16[32,24,128]{2,1,0:T(8,128)(2,1)} %broadcast_in_dim.18), calls=%async_computation | async-start | bytes 393216 | tf_op jit(solution)/shard_map/all_to_all | solution.py:206
  21.5 0.6 pad_add_fusion.where
  22.0 15.9 %all-to-all-done.q_ref = bf16[32,24,128]{2,1,0:T(8,128)(2,1)S(1)} async-done(((bf16[32,24,128]{2,1,0:T(8,128)(2,1)}), bf16[32,24,128]{2,1,0:T(8,128)(2,1)S(1)}, u32[]{:S(2)}, u32[]{:S(2)}) %all-to-all-start) | async-done | bytes 196640 | tf_op jit(solution)/shard_map/all_to_all | solution.py:206
  38.0 0.7 copy-done.5
  38.6 8.6 %attend.1 = bf16[32,32,128]{2,1,0:T(8,128)(2,1)} custom-call(s32[2]{0:T(128)} %pad_add_fusion.where, bf16[32,24,128]{2,1,0:T(8,128)(2,1)} %copy-done.5, bf16[3072,128]{1,0:T(8,128)(2,1)} %bitcast.15, bf16[3072,128]{1,0:T(8,128)(2,1)} %bitcast.16, bf16[6,128]{1,0:T(8,128)(2,1)} %sk_ref.1, bf16[6,128]{1,0:T(8,128)(2,1)} %sv_ref.1), custom_call_target="tpu_custom_call" | custom-call | flops 1207959552 | bytes 2097152 | tf_op jit(solution)/shard_map/attend/pallas_call | solution.py:213
  47.2 0.0 copy-start.4
  47.2 24.2 %all_to_all.40.in_ref = bf16[32,32,128]{2,1,0:T(8,128)(2,1)S(1)} all-to-all(bf16[32,32,128]{2,1,0:T(8,128)(2,1)} %attend.1), channel_id=1, replica_groups=mesh['ctx'=32,'tp'=16] {'ctx'}, dimensions={0} | all-to-all | bytes 524288 | tf_op jit(solution)/shard_map/all_to_all | solution.py:229
  71.4 0.4 merge.1
  71.9 0.0 copy-start.6
  71.9 22.6 %all_to_all.41 = bf16[32,24,128]{2,1,0:T(8,128)(2,1)S(1)} all-to-all(bf16[32,24,128]{2,1,0:T(8,128)(2,1)S(1)} %get-tuple-element.13), channel_id=1, replica_groups=mesh['ctx'=32,'tp'=16] {'ctx'}, dimensions={0} | all-to-all | bytes 393216 | tf_op jit(solution)/shard_map/all_to_all | solution.py:239
  94.6 0.1 reshape.26
  94.7 0.2 convolution_convert_fusion.1
  94.9 0.7 reshape.27
  95.6 9.1 %all-to-all-start.3 = ((bf16[16,12,256]{2,1,0:T(8,128)(2,1)}), bf16[16,12,256]{2,1,0:T(8,128)(2,1)S(1)}, u32[]{:S(2)}, u32[]{:S(2)}) async-start(bf16[16,12,256]{2,1,0:T(8,128)(2,1)} %reshape.27), calls=%async_computation.3 | async-start | bytes 262144 | tf_op jit(solution)/shard_map/all_to_all | solution.py:244
  104.8 6.2 %all-to-all-done.3 = bf16[16,12,256]{2,1,0:T(8,128)(2,1)S(1)} async-done(((bf16[16,12,256]{2,1,0:T(8,128)(2,1)}), bf16[16,12,256]{2,1,0:T(8,128)(2,1)S(1)}, u32[]{:S(2)}, u32[]{:S(2)}) %all-to-all-start.3) | async-done | bytes 98336 | tf_op jit(solution)/shard_map/all_to_all | solution.py:244
  111.0 0.7 broadcast_in_dim.19
  111.6 3.7 %all-to-all-start.4 = ((bf16[16,12,256]{2,1,0:T(8,128)(2,1)}), bf16[16,12,256]{2,1,0:T(8,128)(2,1)S(1)}, u32[]{:S(2)}, u32[]{:S(2)}) async-start(bf16[16,12,256]{2,1,0:T(8,128)(2,1)} %broadcast_in_dim.19), calls=%async_computation.4 | async-start | bytes 262144 | tf_op jit(solution)/shard_map/all_to_all | solution.py:248
  115.3 0.1 pad_add_fusion.1.sel
  115.4 6.2 %all-to-all-done.4 = bf16[16,12,256]{2,1,0:T(8,128)(2,1)S(1)} async-done(((bf16[16,12,256]{2,1,0:T(8,128)(2,1)}), bf16[16,12,256]{2,1,0:T(8,128)(2,1)S(1)}, u32[]{:S(2)}, u32[]{:S(2)}) %all-to-all-start.4) | async-done | bytes 98336 | tf_op jit(solution)/shard_map/all_to_all | solution.py:248
  121.6 1.0 gate.1
  122.6 1.9 collective-permute-start
  124.6 1.0 up.1
  125.6 4.5 %collective-permute-start.2 = (bf16[2,48,1848]{2,1,0:T(8,128)(2,1)S(1)}, bf16[2,48,1848]{2,1,0:T(8,128)(2,1)S(1)}, u32[]{:S(2)}, u32[]{:S(2)}) collective-permute-start(bf16[2,48,1848]{2,1,0:T(8,128)(2,1)S(1)} %get-tuple-element.19), channel_id=1, source_target_pairs={{0,16},{16,0},{32,48},{48,32},{64,80},{80,64},{96,112},{112,96},{1... | collective-permute-start | bytes 1064456 | tf_op jit(solution)/shard_map/ppermute | solution.py:168
  130.1 4.2 %collective-permute-done.got_ref = bf16[2,48,1920]{2,1,0:T(8,128)(2,1)S(1)} collective-permute-done((bf16[2,48,1920]{2,1,0:T(8,128)(2,1)S(1)}, bf16[2,48,1920]{2,1,0:T(8,128)(2,1)S(1)}, u32[]{:S(2)}, u32[]{:S(2)}) %collective-permute-start) | collective-permute-done | bytes 368672 | tf_op jit(solution)/shard_map/ppermute | solution.py:168
  134.3 0.8 halve_gate.1
  135.1 4.4 %collective-permute-start.1 = (bf16[48,1920]{1,0:T(8,128)(2,1)S(1)}, bf16[48,1920]{1,0:T(8,128)(2,1)S(1)}, u32[]{:S(2)}, u32[]{:S(2)}) collective-permute-start(bf16[48,1920]{1,0:T(8,128)(2,1)S(1)} %get-tuple-element.17), channel_id=1, source_target_pairs={{0,16},{16,0},{32,48},{48,32},{64,80},{80,64},{96,112},{112,96},{1... | collective-permute-start | bytes 552968 | tf_op jit(solution)/shard_map/ppermute | solution.py:168
  139.5 0.6 halve_up.1
  140.1 2.3 collective-permute-start.3
  142.4 4.0 %collective-permute-done.3.u_got_ref = bf16[48,1848]{1,0:T(8,128)(2,1)S(1)} collective-permute-done((bf16[48,1848]{1,0:T(8,128)(2,1)S(1)}, bf16[48,1848]{1,0:T(8,128)(2,1)S(1)}, u32[]{:S(2)}, u32[]{:S(2)}) %collective-permute-start.3) | collective-permute-done | bytes 177440 | tf_op jit(solution)/shard_map/ppermute | solution.py:168
  146.4 0.2 join.1
  146.6 26.5 %all_to_all.42.in_ref = bf16[8,6,3768]{2,1,0:T(8,128)(2,1)S(1)} all-to-all(bf16[8,6,3768]{2,1,0:T(8,128)(2,1)S(1)} %join.1), channel_id=1, replica_groups={{0,64,128,192,256,320,384,448},{16,80,144,208,272,336,400,464},{32,96,1..., dimensions={0} | all-to-all | bytes 723456 | tf_op jit(solution)/shard_map/all_to_all | solution.py:299
  173.2 0.2 hidden.1
  173.4 25.8 %all_to_all.43 = bf16[8,6,1848]{2,1,0:T(8,128)(2,1)S(1)} all-to-all(bf16[8,6,1848]{2,1,0:T(8,128)(2,1)S(1)} %hidden.1), channel_id=1, replica_groups={{0,64,128,192,256,320,384,448},{16,80,144,208,272,336,400,464},{32,96,1..., dimensions={0} | all-to-all | bytes 354816 | tf_op jit(solution)/shard_map/all_to_all | solution.py:308
  199.2 0.1 reshape.29
  199.3 5.9 %collective-permute-start.4 = (bf16[48,1848]{1,0:T(8,128)(2,1)S(1)}, bf16[48,1848]{1,0:T(8,128)(2,1)S(1)}, u32[]{:S(2)}, u32[]{:S(2)}) collective-permute-start(bf16[48,1848]{1,0:T(8,128)(2,1)S(1)} %reshape.29), channel_id=1, source_target_pairs={{0,32},{16,48},{32,0},{48,16},{64,96},{80,112},{96,64},{112,80},{1... | collective-permute-start | bytes 532232 | tf_op jit(solution)/shard_map/ppermute | solution.py:168
  205.3 2.9 %collective-permute-done.4 = bf16[48,1848]{1,0:T(8,128)(2,1)S(1)} collective-permute-done((bf16[48,1848]{1,0:T(8,128)(2,1)S(1)}, bf16[48,1848]{1,0:T(8,128)(2,1)S(1)}, u32[]{:S(2)}, u32[]{:S(2)}) %collective-permute-start.4) | collective-permute-done | bytes 177440 | tf_op jit(solution)/shard_map/ppermute | solution.py:168
  208.2 0.1 maximum_select_fusion.2
  208.3 1.9 collective-permute-start.5
  210.2 7.8 %collective-permute-done.5 = bf16[96,1848]{1,0:T(8,128)(2,1)S(1)} collective-permute-done((bf16[96,1848]{1,0:T(8,128)(2,1)S(1)}, bf16[96,1848]{1,0:T(8,128)(2,1)S(1)}, u32[]{:S(2)}, u32[]{:S(2)}) %collective-permute-start.5) | collective-permute-done | bytes 354848 | tf_op jit(solution)/shard_map/ppermute | solution.py:168
  218.0 0.4 convolution_convert_fusion
  218.4 0.7 reshape.30
  219.1 8.8 %all-to-all-start.7 = ((bf16[16,12,256]{2,1,0:T(8,128)(2,1)}), bf16[16,12,256]{2,1,0:T(8,128)(2,1)S(1)}, u32[]{:S(2)}, u32[]{:S(2)}) async-start(bf16[16,12,256]{2,1,0:T(8,128)(2,1)} %reshape.30), calls=%async_computation.7 | async-start | bytes 262144 | tf_op jit(solution)/shard_map/all_to_all | solution.py:244
  227.9 0.6 reshape.25
  228.5 5.6 %all-to-all-done.7 = bf16[16,12,256]{2,1,0:T(8,128)(2,1)S(1)} async-done(((bf16[16,12,256]{2,1,0:T(8,128)(2,1)}), bf16[16,12,256]{2,1,0:T(8,128)(2,1)S(1)}, u32[]{:S(2)}, u32[]{:S(2)}) %all-to-all-start.7) | async-done | bytes 98336 | tf_op jit(solution)/shard_map/all_to_all | solution.py:244
  234.1 0.6 add_convert_fusion
  (16 shorter events, 0.1 us)
Async XLA Ops:
  0.6 217.4 %copy-start = (bf16[1848,256]{1,0:T(8,128)(2,1)S(1)}, bf16[1848,256]{1,0:T(8,128)(2,1)}, u32[]{:S(2)}) copy-start(bf16[1848,256]{1,0:T(8,128)(2,1)} %param.23) | copy-start | bytes 2838532
  2.1 35.8 %all-to-all-start = ((bf16[32,24,128]{2,1,0:T(8,128)(2,1)}), bf16[32,24,128]{2,1,0:T(8,128)(2,1)S(1)}, u32[]{:S(2)}, u32[]{:S(2)}) async-start(bf16[32,24,128]{2,1,0:T(8,128)(2,1)} %broadcast_in_dim.18), calls=%async_computation | async-start | bytes 393216 | tf_op jit(solution)/shard_map/all_to_all | solution.py:206
  38.0 0.7 copy-start.5
  47.2 47.5 %copy-start.4 = (bf16[512,256]{1,0:T(8,128)(2,1)S(1)}, bf16[512,256]{1,0:T(8,128)(2,1)}, u32[]{:S(2)}) copy-start(bf16[512,256]{1,0:T(8,128)(2,1)} %param.19) | copy-start | bytes 786436
  71.9 39.1 %copy-start.6 = (bf16[12,256]{1,0:T(8,128)(2,1)S(1)}, bf16[12,256]{1,0:T(8,128)(2,1)}, u32[]{:S(2)}) copy-start(bf16[12,256]{1,0:T(8,128)(2,1)} %param.18) | copy-start | bytes 18436
  94.7 26.9 %copy-start.1 = (bf16[256,1848]{0,1:T(8,128)(2,1)S(1)}, bf16[256,1848]{0,1:T(8,128)(2,1)}, u32[]{:S(2)}) copy-start(bf16[256,1848]{0,1:T(8,128)(2,1)} %param.21) | copy-start | bytes 2838532
  94.7 26.9 %copy-start.3 = (f32[256]{0:T(256)S(1)}, f32[256]{0:T(256)}, u32[]{:S(2)}) copy-start(f32[256]{0:T(256)} %param.20) | copy-start | bytes 3076
  95.6 15.3 %all-to-all-start.3 = ((bf16[16,12,256]{2,1,0:T(8,128)(2,1)}), bf16[16,12,256]{2,1,0:T(8,128)(2,1)S(1)}, u32[]{:S(2)}, u32[]{:S(2)}) async-start(bf16[16,12,256]{2,1,0:T(8,128)(2,1)} %reshape.27), calls=%async_computation.3 | async-start | bytes 262144 | tf_op jit(solution)/shard_map/all_to_all | solution.py:244
  104.8 19.8 %copy-start.2 = (bf16[256,1848]{0,1:T(8,128)(2,1)S(1)}, bf16[256,1848]{0,1:T(8,128)(2,1)}, u32[]{:S(2)}) copy-start(bf16[256,1848]{0,1:T(8,128)(2,1)} %param.22) | copy-start | bytes 2838532
  111.6 9.9 %all-to-all-start.4 = ((bf16[16,12,256]{2,1,0:T(8,128)(2,1)}), bf16[16,12,256]{2,1,0:T(8,128)(2,1)S(1)}, u32[]{:S(2)}, u32[]{:S(2)}) async-start(bf16[16,12,256]{2,1,0:T(8,128)(2,1)} %broadcast_in_dim.19), calls=%async_computation.4 | async-start | bytes 262144 | tf_op jit(solution)/shard_map/all_to_all | solution.py:248
  122.6 11.6 %collective-permute-start = (bf16[2,48,1920]{2,1,0:T(8,128)(2,1)S(1)}, bf16[2,48,1920]{2,1,0:T(8,128)(2,1)S(1)}, u32[]{:S(2)}, u32[]{:S(2)}) collective-permute-start(bf16[2,48,1920]{2,1,0:T(8,128)(2,1)S(1)} %get-tuple-element.15), channel_id=1, source_target_pairs={{0,32},{16,48},{32,0},{48,16},{64,96},{80,112},{96,64},{112,80},{1... | collective-permute-start | bytes 1105928 | tf_op jit(solution)/shard_map/ppermute | solution.py:168
  125.6 13.9 %collective-permute-start.2 = (bf16[2,48,1848]{2,1,0:T(8,128)(2,1)S(1)}, bf16[2,48,1848]{2,1,0:T(8,128)(2,1)S(1)}, u32[]{:S(2)}, u32[]{:S(2)}) collective-permute-start(bf16[2,48,1848]{2,1,0:T(8,128)(2,1)S(1)} %get-tuple-element.19), channel_id=1, source_target_pairs={{0,16},{16,0},{32,48},{48,32},{64,80},{80,64},{96,112},{112,96},{1... | collective-permute-start | bytes 1064456 | tf_op jit(solution)/shard_map/ppermute | solution.py:168
  135.1 11.4 %collective-permute-start.1 = (bf16[48,1920]{1,0:T(8,128)(2,1)S(1)}, bf16[48,1920]{1,0:T(8,128)(2,1)S(1)}, u32[]{:S(2)}, u32[]{:S(2)}) collective-permute-start(bf16[48,1920]{1,0:T(8,128)(2,1)S(1)} %get-tuple-element.17), channel_id=1, source_target_pairs={{0,16},{16,0},{32,48},{48,32},{64,80},{80,64},{96,112},{112,96},{1... | collective-permute-start | bytes 552968 | tf_op jit(solution)/shard_map/ppermute | solution.py:168
  140.1 6.3 %collective-permute-start.3 = (bf16[48,1848]{1,0:T(8,128)(2,1)S(1)}, bf16[48,1848]{1,0:T(8,128)(2,1)S(1)}, u32[]{:S(2)}, u32[]{:S(2)}) collective-permute-start(bf16[48,1848]{1,0:T(8,128)(2,1)S(1)} %get-tuple-element.21), channel_id=1, source_target_pairs={{0,32},{16,48},{32,0},{48,16},{64,96},{80,112},{96,64},{112,80},{1... | collective-permute-start | bytes 532232 | tf_op jit(solution)/shard_map/ppermute | solution.py:168
  199.3 8.9 %collective-permute-start.4 = (bf16[48,1848]{1,0:T(8,128)(2,1)S(1)}, bf16[48,1848]{1,0:T(8,128)(2,1)S(1)}, u32[]{:S(2)}, u32[]{:S(2)}) collective-permute-start(bf16[48,1848]{1,0:T(8,128)(2,1)S(1)} %reshape.29), channel_id=1, source_target_pairs={{0,32},{16,48},{32,0},{48,16},{64,96},{80,112},{96,64},{112,80},{1... | collective-permute-start | bytes 532232 | tf_op jit(solution)/shard_map/ppermute | solution.py:168
  208.3 9.8 %collective-permute-start.5 = (bf16[96,1848]{1,0:T(8,128)(2,1)S(1)}, bf16[96,1848]{1,0:T(8,128)(2,1)S(1)}, u32[]{:S(2)}, u32[]{:S(2)}) collective-permute-start(bf16[96,1848]{1,0:T(8,128)(2,1)S(1)} %maximum_select_fusion.2), channel_id=1, source_target_pairs={{0,16},{16,0},{32,48},{48,32},{64,80},{80,64},{96,112},{112,96},{1... | collective-permute-start | bytes 1064456 | tf_op jit(solution)/shard_map/ppermute | solution.py:168
  219.1 15.0 %all-to-all-start.7 = ((bf16[16,12,256]{2,1,0:T(8,128)(2,1)}), bf16[16,12,256]{2,1,0:T(8,128)(2,1)S(1)}, u32[]{:S(2)}, u32[]{:S(2)}) async-start(bf16[16,12,256]{2,1,0:T(8,128)(2,1)} %reshape.30), calls=%async_computation.7 | async-start | bytes 262144 | tf_op jit(solution)/shard_map/all_to_all | solution.py:244

commit v5 on v4

v5 whole, which is shorter than its diff:
```python
import functools
import math

import jax
import jax.numpy as jnp
from jax import lax
from jax.experimental import pallas as pl
from jax.experimental.pallas import tpu as pltpu
from jax.sharding import PartitionSpec as P

D = 8192
F32 = jnp.float32
BF16 = jnp.bfloat16
LOW = -1e30
SPAN = 512


def three_parts(x):
    one = x.astype(BF16).astype(F32)
    rest = x - one
    two = rest.astype(BF16).astype(F32)
    return one, two, (rest - two).astype(BF16).astype(F32)


def attend_kernel(
    where, q_ref, k_hbm, v_hbm, sk_ref, sv_ref, out_ref, k_ref, v_ref, sems, *, tokens, group, head, scale
):
    k_copy = pltpu.make_async_copy(k_hbm, k_ref, sems.at[0])
    v_copy = pltpu.make_async_copy(v_hbm, v_ref, sems.at[1])
    k_copy.start()
    v_copy.start()
    length = where[0]
    first = where[1]
    rows = tokens * group
    own = sk_ref.shape[0]
    query = q_ref[...].reshape(rows, head)
    unit = scale / math.log(2.0)

    def scores(keys):
        return lax.dot_general(keys, query, (((1,), (1,)), ((), ())), preferred_element_type=F32)

    def weigh(values, w):
        return lax.dot_general(values, w.astype(BF16), (((0,), (0,)), ((), ())), preferred_element_type=F32)

    def add(carry, s, values):
        top, total, numer = carry
        top_new = jnp.maximum(top, jnp.max(s, axis=0, keepdims=True))
        fade = jnp.exp2((top - top_new) * unit)
        w = jnp.exp2((s - top_new) * unit)
        return top_new, total * fade + jnp.sum(w, axis=0, keepdims=True), numer * fade + weigh(values, w)

    s = scores(sk_ref[...])
    token = lax.broadcasted_iota(jnp.int32, (own, rows), 1) // group
    place = first + lax.broadcasted_iota(jnp.int32, (own, rows), 0)
    seen = place <= token
    s = jnp.where(seen, s, LOW)
    top = jnp.max(s, axis=0, keepdims=True)
    w = jnp.where(seen, jnp.exp2((s - top) * unit), 0.0)
    total = jnp.sum(w, axis=0, keepdims=True)
    numer = weigh(sv_ref[...], w)
    k_copy.wait()
    v_copy.wait()

    def whole(step, carry):
        at = pl.ds(pl.multiple_of(step * SPAN, SPAN), SPAN)
        return add(carry, scores(k_ref[at, :]), v_ref[at, :])

    full = length // SPAN
    carry = lax.fori_loop(0, full, whole, (top, total, numer))

    def part(step, carry):
        at = pl.ds(pl.multiple_of(step * SPAN, SPAN), SPAN)
        s = scores(k_ref[at, :])
        live = step * SPAN + lax.broadcasted_iota(jnp.int32, s.shape, 0) < length
        return add(carry, jnp.where(live, s, LOW), v_ref[at, :])

    top, total, numer = lax.fori_loop(full, (length + SPAN - 1) // SPAN, part, carry)
    blocks = out_ref.shape[0]
    each = rows // blocks
    out_ref[:, :each, :] = (numer / total).T.astype(BF16).reshape(blocks, each, head)
    stats = jnp.concatenate([*three_parts(top * unit), *three_parts(total), jnp.zeros((2, rows), F32)], axis=0)
    stats = jnp.concatenate([stats, jnp.zeros((8, rows), F32)], axis=0)
    spare = jnp.zeros((out_ref.shape[1] - each, head - each), F32)
    for i in range(blocks):
        tail = stats[: out_ref.shape[1] - each, i * each : (i + 1) * each]
        out_ref[i, each:, :] = jnp.concatenate([tail, spare], axis=1).astype(BF16)


def merge_kernel(in_ref, out_ref, copies_ref):
    blocks, rows, head = copies_ref.shape
    stat = [in_ref[:, rows + i, :].astype(F32) for i in range(6)]
    top = stat[0] + stat[1] + stat[2]
    total = stat[3] + stat[4] + stat[5]
    w = jnp.exp2(top - jnp.max(top, axis=0, keepdims=True)) * total
    w = (w / jnp.sum(w, axis=0, keepdims=True)).T
    out = jnp.zeros((rows, head), F32)
    for i in range(blocks):
        out = out + in_ref[i, :rows, :].astype(F32) * w[:rows, i : i + 1]
    out = out.astype(BF16)
    out_ref[...] = out
    for i in range(blocks):
        copies_ref[i] = out


def project_kernel(place, x_ref, *refs):
    out_ref = refs[-1]
    w_refs = refs[:-1]
    _, units, _ = w_refs[0].shape
    blocks, rows, width = out_ref.shape
    half = width // 2
    near = place[0]

    def product(kind):
        y = 0.0
        for m, w_ref in enumerate(w_refs):
            y = y + lax.dot_general(x_ref[near ^ m], w_ref[kind], (((1,), (1,)), ((), ())), preferred_element_type=F32)
        return y

    squares = 0.0
    for i in range(x_ref.shape[0]):
        x = x_ref[i].astype(F32)
        squares = squares + jnp.sum(x * x, axis=1, keepdims=True)
    tokens = squares.shape[0]
    spare = jnp.zeros((tokens, half - units - 3), F32)
    gate = jnp.concatenate([product(0), *three_parts(squares), spare], axis=1).astype(BF16)
    up = product(1).astype(BF16)
    for i in range(blocks):
        out_ref[i, :, :half] = gate[i * rows : (i + 1) * rows]
        out_ref[i, :, half : half + units] = up[i * rows : (i + 1) * rows]
        out_ref[i, :, half + units :] = jnp.zeros((rows, half - units), BF16)


def hidden_kernel(in_ref, out_ref):
    blocks, _, units = out_ref.shape
    half = in_ref.shape[2] // 2
    sums = jnp.sum(in_ref[...].astype(F32), axis=0)
    power = jnp.sum(sums[:, units : units + 3], axis=1, keepdims=True) / D
    inv = lax.rsqrt(power + 1e-06)
    gate, upper = sums[:, :units] * inv, sums[:, half : half + units] * inv
    out = (gate / (1.0 + jnp.exp(-gate)) * upper).astype(BF16)
    for i in range(blocks):
        out_ref[i] = out


def down_kernel(place, h_ref, *refs):
    out_ref = refs[-1]
    w_refs = refs[:-1]
    rows = out_ref.shape[1]
    each = out_ref.shape[0] // len(w_refs)
    near = place[0]
    for m, w_ref in enumerate(w_refs):
        y = jnp.dot(h_ref[...], w_ref[2], preferred_element_type=F32)
        for k in range(each):
            out_ref[(near ^ m) * each + k] = y[k * rows : (k + 1) * rows].astype(BF16)


def per_device(
    queries,
    cache_keys,
    cache_values,
    seg_keys,
    seg_values,
    lengths,
    residual_stream,
    out_weight,
    norm_gain,
    gate_weight,
    up_weight,
    down_weight,
):
    rows, width = queries.shape
    _, stretch, head = cache_keys.shape
    group = width // head
    n_far, n_near, n_tp = lax.axis_size("far"), lax.axis_size("near"), lax.axis_size("tp")
    n_ctx = n_far * n_near
    ctx = ("far", "near")
    tokens = rows * n_ctx
    c = lax.axis_index(ctx)
    trows = residual_stream.shape[0]
    feats = residual_stream.shape[1]
    units = gate_weight.shape[1] // n_near

    near = lax.axis_index("near")

    def chunk(place):
        def part(w):
            return lax.dynamic_slice_in_dim(w, place * units, units, 0)

        gate, upper = part(gate_weight.T).astype(F32) * norm_gain, part(up_weight.T).astype(F32) * norm_gain
        return jnp.stack([gate.astype(BF16), upper.astype(BF16), part(down_weight)])

    def trade(m, place):
        return lax.ppermute(chunk(place ^ m), "near", [(i, i ^ m) for i in range(4)])

    weights = [chunk(near)]
    each = rows * group
    q_all = jnp.broadcast_to(queries.reshape(1, each, head), (n_ctx, each, head))
    q_all = lax.all_to_all(q_all, ctx, 0, 0, tiled=True)
    q_all, w, place = lax.optimization_barrier((q_all, trade(1, near), near))
    weights.append(w)
    where = jnp.stack([lengths[0], c * rows])
    vmem = pl.BlockSpec(memory_space=pltpu.VMEM)
    smem = pl.BlockSpec(memory_space=pltpu.SMEM)
    anywhere = pl.BlockSpec(memory_space=pl.ANY)
    params = pltpu.CompilerParams(vmem_limit_bytes=60 * 2**20)
    small = pltpu.CompilerParams(vmem_limit_bytes=24 * 2**20)
    partial = pl.pallas_call(
        functools.partial(attend_kernel, tokens=tokens, group=group, head=head, scale=1.0 / math.sqrt(head)),
        out_shape=jax.ShapeDtypeStruct((n_ctx, each + 8, head), BF16),
        in_specs=[smem, vmem, anywhere, anywhere, vmem, vmem],
        out_specs=vmem,
        scratch_shapes=[
            pltpu.VMEM((stretch, head), BF16),
            pltpu.VMEM((stretch, head), BF16),
            pltpu.SemaphoreType.DMA((2,)),
        ],
        compiler_params=params,
        cost_estimate=pl.CostEstimate(
            flops=4 * tokens * width * stretch, bytes_accessed=2**21, transcendentals=tokens * group * stretch
        ),
        name="attend",
    )(where, q_all, cache_keys[0], cache_values[0], seg_keys, seg_values)
    parts = lax.all_to_all(partial, ctx, 0, 0, tiled=True)
    parts, w, place = lax.optimization_barrier((parts, trade(2, place), place))
    weights.append(w)
    attention, copies = pl.pallas_call(
        merge_kernel,
        out_shape=(jax.ShapeDtypeStruct((each, head), BF16), jax.ShapeDtypeStruct((n_ctx, each, head), BF16)),
        in_specs=[vmem],
        out_specs=(vmem, vmem),
        compiler_params=small,
        name="merge",
    )(parts)
    attention = attention.reshape(rows, width)
    heads_all = lax.all_to_all(copies, ctx, 0, 0, tiled=True)
    heads_all, w = lax.optimization_barrier((heads_all, trade(3, place)))
    heads_all = heads_all.reshape(tokens, width)
    weights.append(w)
    mixed = jnp.dot(heads_all, out_weight, preferred_element_type=F32)

    mixed = mixed.astype(BF16).reshape(n_tp, trows, feats)
    mixed = jnp.sum(lax.all_to_all(mixed, "tp", 0, 0, tiled=True).astype(F32), axis=0)
    own = (residual_stream.astype(F32) + mixed).astype(BF16)
    stream = jnp.broadcast_to(own[None], (n_near * n_tp, trows, feats))
    stream = lax.all_to_all(stream, ("near", "tp"), 0, 0, tiled=True).reshape(n_near, tokens, feats)

    half = -(-(units + 3) // 128) * 128
    block = tokens // n_far
    sums = pl.pallas_call(
        project_kernel,
        out_shape=jax.ShapeDtypeStruct((n_far, block, 2 * half), BF16),
        in_specs=[smem] + [vmem] * 5,
        out_specs=vmem,
        compiler_params=small,
        name="project",
    )(near[None], stream, *weights)
    sums = lax.all_to_all(sums, "far", 0, 0, tiled=True)
    hidden = pl.pallas_call(
        hidden_kernel,
        out_shape=jax.ShapeDtypeStruct((n_far, block, units), BF16),
        in_specs=[vmem],
        out_specs=vmem,
        compiler_params=small,
        name="hidden",
    )(sums)
    hidden = lax.all_to_all(hidden, "far", 0, 0, tiled=True).reshape(tokens, units)
    lowered = pl.pallas_call(
        down_kernel,
        out_shape=jax.ShapeDtypeStruct((n_near * n_tp, trows, feats), BF16),
        in_specs=[smem] + [vmem] * 5,
        out_specs=vmem,
        compiler_params=small,
        name="down",
    )(near[None], hidden, *weights)
    lowered = lax.all_to_all(lowered, ("near", "tp"), 0, 0, tiled=True)
    layer_out = (own.astype(F32) + jnp.sum(lowered.astype(F32), axis=0)).astype(BF16)
    return (attention, layer_out)


def solution(mesh):
    fine = jax.sharding.Mesh(mesh.devices.reshape(-1, 4, mesh.shape["tp"]), ("far", "near", "tp"))
    ctx = ("far", "near")
    return jax.shard_map(
        per_device,
        mesh=fine,
        in_specs=(
            P(ctx, "tp"),
            P("tp", ctx, None),
            P("tp", ctx, None),
            P(ctx, "tp"),
            P(ctx, "tp"),
            P(ctx),
            P("tp", ctx),
            P("tp", ctx),
            P(ctx),
            P(ctx, "tp"),
            P(ctx, "tp"),
            P("tp", ctx),
        ),
        out_specs=(P(ctx, "tp"), P("tp", ctx)),
        check_vma=False,
    )
```

time: 236 us -> 250 us (1.059)
  blocking collectives: 99.3 us -> 67.5 us
  waiting for transfers between devices: 52.8 us -> 81.9 us
  starting transfers between devices: 61.2 us -> 69.2 us
  other arithmetic: 1.4 us -> 9.27 us
  local copies, waits for them, and re-layouts: 5.08 us -> 8.22 us
    ppermute x6 -> x3, waiting for transfers between devices: 18.9 us -> 59.3 us  [trade(): lax.ppermute(chunk(place ^ m), 'near', [(i, i ^ m) for i in range(4)])]
    all_to_all x4 -> x3, blocking collectives: 99.3 us -> 67.5 us  [the longest x1 33.6 us: per_device(): sums = lax.all_to_all(sums, 'far', 0, 0, tiled=True)]
    all_to_all x4 -> x5, starting transfers between devices: 40.3 us -> 55.9 us  [the longest x1 18.7 us: per_device(): q_all = lax.all_to_all(q_all, ctx, 0, 0, tiled=True)]
    all_to_all x4 -> x5, waiting for transfers between devices: 33.8 us -> 22.6 us  [the longest x1 11.5 us: per_device(): lowered = lax.all_to_all(lowered, ('near', 'tp'), 0, 0, tiled=True)]
    another operation x1 -> x7, other arithmetic: 0.07 us -> 7.96 us  [chunk(): return jnp.stack([gate.astype(BF16), upper.astype(BF16), part(down_weight)])]
    ppermute x6 -> x3, starting transfers between devices: 20.9 us -> 13.3 us  [trade(): lax.ppermute(chunk(place ^ m), 'near', [(i, i ^ m) for i in range(4)])]
    pallas_call x6 -> x3, Pallas kernels: 3.89 us -> 1.27 us  [the longest x1 0.7 us: per_device(): pl.pallas_call(project_kernel, out_shape=jax.ShapeDtypeStruct((n_far, blo...]
  transfers between devices with their start and end apart: 10 -> 8, of which waited for: 8 -> 5; matrix products, arithmetic and copies ran while one was open for 1% -> 3% of each run, Pallas kernels for 1% -> 0%
where the time goes in v5:
time: 250 us; the launch traced here: 249 us
  waiting for transfers between devices  81.9 us (33%)
  starting transfers between devices  69.2 us (28%)
  blocking collectives  67.5 us (27%)
  Pallas kernels  11 us (4%)
  other arithmetic  9.27 us (4%)
  local copies, waits for them, and re-layouts  8.22 us (3%)
    ppermute x3, waiting for transfers between devices, trade(): lax.ppermute(chunk(place ^ m), 'near', [(i, i ^ m) for i in range(4)])  59.3 us
    all_to_all x1, blocking collectives, per_device(): sums = lax.all_to_all(sums, 'far', 0, 0, tiled=True)  33.6 us
    all_to_all x1, blocking collectives, per_device(): lax.all_to_all(hidden, 'far', 0, 0, tiled=True).reshape(tokens, units)  22.2 us
    all_to_all x1, starting transfers between devices, per_device(): q_all = lax.all_to_all(q_all, ctx, 0, 0, tiled=True)  18.7 us
    all_to_all x1, starting transfers between devices, per_device(): heads_all = lax.all_to_all(copies, ctx, 0, 0, tiled=True)  13.6 us
    ppermute x3, starting transfers between devices, trade(): lax.ppermute(chunk(place ^ m), 'near', [(i, i ^ m) for i in range(4)])  13.3 us
    all_to_all x1, starting transfers between devices, per_device(): parts = lax.all_to_all(partial, ctx, 0, 0, tiled=True)  12 us
    all_to_all x1, blocking collectives, per_device(): lax.all_to_all(mixed, 'tp', 0, 0, tiled=True).astype(F32)  11.6 us
  transfers between devices with their start and end apart: 8, of which 5 were waited for; matrix products, arithmetic and copies ran while one was open for 3% of the time, Pallas kernels for 0%

profile of v5, /device:TPU:1, one launch (start us, length us, event | category | flops | bytes accessed | tf_op | source)
XLA Modules:
  0.0 248.7 jit_solution(10478987050534316204)
XLA Ops:
  0.6 0.0 copy-start
  0.6 0.8 broadcast_in_dim.8
  1.4 0.7 broadcast_in_dim.9
  2.1 18.7 %all-to-all-start = ((bf16[32,24,128]{2,1,0:T(8,128)(2,1)}), bf16[32,24,128]{2,1,0:T(8,128)(2,1)S(1)}, u32[]{:S(2)}, u32[]{:S(2)}) async-start(bf16[32,24,128]{2,1,0:T(8,128)(2,1)} %broadcast_in_dim.9), calls=%async_computation | async-start | bytes 393216 | tf_op jit(solution)/shard_map/all_to_all | solution.py:198
  20.8 0.0 copy-start.6
  20.8 1.0 dynamic-slice_bitcast_fusion.3
  21.8 1.2 fusion
  23.0 0.1 pad_maximum_fusion
  23.1 4.6 %collective-permute-start = (bf16[3,462,256]{2,1,0:T(8,128)(2,1)S(1)}, bf16[3,462,256]{2,1,0:T(8,128)(2,1)S(1)}, u32[]{:S(2)}, u32[]{:S(2)}) collective-permute-start(bf16[3,462,256]{2,1,0:T(8,128)(2,1)S(1)} %pad_maximum_fusion), channel_id=1, source_target_pairs={{0,16},{16,0},{32,48},{48,32},{1,17},{17,1},{33,49},{49,33},{2,18}... | collective-permute-start | bytes 2128904 | tf_op jit(solution)/shard_map/ppermute | solution.py:193
  28.4 0.6 pad_add_fusion.where
  29.0 15.9 %collective-permute-done.refs_1_ = bf16[3,462,256]{2,1,0:T(8,128)(2,1)S(1)} collective-permute-done((bf16[3,462,256]{2,1,0:T(8,128)(2,1)S(1)}, bf16[3,462,256]{2,1,0:T(8,128)(2,1)S(1)}, u32[]{:S(2)}, u32[]{:S(2)}) %collective-permute-start) | collective-permute-done | bytes 709664 | tf_op jit(solution)/shard_map/ppermute | solution.py:193
  44.9 0.0 all-to-all-done.q_ref
  44.9 0.7 copy-done.5
  45.5 8.6 %attend.1 = bf16[32,32,128]{2,1,0:T(8,128)(2,1)} custom-call(s32[2]{0:T(128)} %pad_add_fusion.where, bf16[32,24,128]{2,1,0:T(8,128)(2,1)} %copy-done.5, bf16[3072,128]{1,0:T(8,128)(2,1)} %bitcast.48, bf16[3072,128]{1,0:T(8,128)(2,1)} %bitcast.49, bf16[6,128]{1,0:T(8,128)(2,1)} %sk_ref.1, bf16[6,128]{1,0:T(8,128)(2,1)} %sv_ref.1), custom_call_target="tpu_custom_call" | custom-call | flops 1207959552 | bytes 2097152 | tf_op jit(solution)/shard_map/attend/pallas_call | solution.py:207
  54.1 12.0 %all-to-all-start.1 = ((bf16[32,32,128]{2,1,0:T(8,128)(2,1)}), bf16[32,32,128]{2,1,0:T(8,128)(2,1)S(1)}, u32[]{:S(2)}, u32[]{:S(2)}) async-start(bf16[32,32,128]{2,1,0:T(8,128)(2,1)} %attend.1), calls=%async_computation.1 | async-start | bytes 524288 | tf_op jit(solution)/shard_map/all_to_all | solution.py:223
  66.1 0.0 copy-start.2
  66.1 2.4 fusion.6
  68.6 0.1 dynamic-slice_bitcast_fusion
  68.7 0.1 pad_maximum_fusion.1
  68.8 3.1 %collective-permute-start.1 = (bf16[3,462,256]{2,1,0:T(8,128)(2,1)S(1)}, bf16[3,462,256]{2,1,0:T(8,128)(2,1)S(1)}, u32[]{:S(2)}, u32[]{:S(2)}) collective-permute-start(bf16[3,462,256]{2,1,0:T(8,128)(2,1)S(1)} %pad_maximum_fusion.1), channel_id=1, source_target_pairs={{0,32},{16,48},{32,0},{48,16},{1,33},{17,49},{33,1},{49,17},{2,34}... | collective-permute-start | bytes 2128904 | tf_op jit(solution)/shard_map/ppermute | solution.py:193
  71.9 22.1 %collective-permute-done.1.refs_2_ = bf16[3,462,256]{2,1,0:T(8,128)(2,1)S(1)} collective-permute-done((bf16[3,462,256]{2,1,0:T(8,128)(2,1)S(1)}, bf16[3,462,256]{2,1,0:T(8,128)(2,1)S(1)}, u32[]{:S(2)}, u32[]{:S(2)}) %collective-permute-start.1) | collective-permute-done | bytes 709664 | tf_op jit(solution)/shard_map/ppermute | solution.py:193
  94.0 2.0 fusion.4
  96.0 0.8 dynamic-slice_bitcast_fusion.1
  96.7 1.1 merge.1
  97.9 13.6 %all-to-all-start.2 = ((bf16[32,24,128]{2,1,0:T(8,128)(2,1)}), bf16[32,24,128]{2,1,0:T(8,128)(2,1)S(1)}, u32[]{:S(2)}, u32[]{:S(2)}) async-start(bf16[32,24,128]{2,1,0:T(8,128)(2,1)} %get-tuple-element.16), calls=%async_computation.2 | async-start | bytes 393216 | tf_op jit(solution)/shard_map/all_to_all | solution.py:235
  111.5 1.0 pad_maximum_fusion.2
  112.6 5.5 %collective-permute-start.2 = (bf16[3,462,256]{2,1,0:T(8,128)(2,1)S(1)}, bf16[3,462,256]{2,1,0:T(8,128)(2,1)S(1)}, u32[]{:S(2)}, u32[]{:S(2)}) collective-permute-start(bf16[3,462,256]{2,1,0:T(8,128)(2,1)S(1)} %pad_maximum_fusion.2), channel_id=1, source_target_pairs={{0,48},{16,32},{32,16},{48,0},{1,49},{17,33},{33,17},{49,1},{2,50}... | collective-permute-start | bytes 2128904 | tf_op jit(solution)/shard_map/ppermute | solution.py:193
  118.1 21.3 %collective-permute-done.2.refs_3_ = bf16[3,462,256]{2,1,0:T(8,128)(2,1)S(1)} collective-permute-done((bf16[3,462,256]{2,1,0:T(8,128)(2,1)S(1)}, bf16[3,462,256]{2,1,0:T(8,128)(2,1)S(1)}, u32[]{:S(2)}, u32[]{:S(2)}) %collective-permute-start.2) | collective-permute-done | bytes 709664 | tf_op jit(solution)/shard_map/ppermute | solution.py:193
  139.4 0.1 reshape.24
  139.6 0.2 convolution_convert_fusion
  139.8 11.6 %all_to_all.40 = bf16[16,12,256]{2,1,0:T(8,128)(2,1)S(1)} all-to-all(bf16[16,12,256]{2,1,0:T(8,128)(2,1)S(1)} %reshape.25), channel_id=1, replica_groups=mesh['far'=8,'near'=4,'tp'=16] {'tp'}, dimensions={0} | all-to-all | bytes 196608 | tf_op jit(solution)/shard_map/all_to_all | solution.py:242
  151.5 0.7 copy-done.7
  152.2 0.8 broadcast_in_dim.11
  153.0 5.2 %all-to-all-start.4 = ((bf16[64,12,256]{2,1,0:T(8,128)(2,1)}), bf16[64,12,256]{2,1,0:T(8,128)(2,1)}, u32[]{:S(2)}, u32[]{:S(2)}) async-start(bf16[64,12,256]{2,1,0:T(8,128)(2,1)} %broadcast_in_dim.11), calls=%async_computation.4 | async-start | bytes 1048576 | tf_op jit(solution)/shard_map/all_to_all | solution.py:245
  158.2 1.1 pad_maximum_fusion.3.refs_0_
  159.4 11.0 %all-to-all-done.4 = bf16[64,12,256]{2,1,0:T(8,128)(2,1)} async-done(((bf16[64,12,256]{2,1,0:T(8,128)(2,1)}), bf16[64,12,256]{2,1,0:T(8,128)(2,1)}, u32[]{:S(2)}, u32[]{:S(2)}) %all-to-all-start.4) | async-done | bytes 393248 | tf_op jit(solution)/shard_map/all_to_all | solution.py:245
  170.4 1.1 reshape.26.x_ref
  171.6 0.7 project.1
  172.3 33.6 %all_to_all.41.in_ref = bf16[8,24,1024]{2,1,0:T(8,128)(2,1)S(1)} all-to-all(bf16[8,24,1024]{2,1,0:T(8,128)(2,1)S(1)} %project.1), channel_id=1, replica_groups=mesh['far'=8,'near'=4,'tp'=16] {'far'}, dimensions={0} | all-to-all | bytes 786432 | tf_op jit(solution)/shard_map/all_to_all | solution.py:257
  205.8 0.2 hidden.1
  206.0 22.2 %all_to_all.42 = bf16[8,24,462]{2,1,0:T(8,128)(2,1)S(1)} all-to-all(bf16[8,24,462]{2,1,0:T(8,128)(2,1)S(1)} %hidden.1), channel_id=1, replica_groups=mesh['far'=8,'near'=4,'tp'=16] {'far'}, dimensions={0} | all-to-all | bytes 354816 | tf_op jit(solution)/shard_map/all_to_all | solution.py:266
  228.3 0.4 down.1
  228.7 0.8 copy-done.1
  229.5 6.4 %all-to-all-start.7 = ((bf16[64,12,256]{2,1,0:T(8,128)(2,1)}), bf16[64,12,256]{2,1,0:T(8,128)(2,1)S(1)}, u32[]{:S(2)}, u32[]{:S(2)}) async-start(bf16[64,12,256]{2,1,0:T(8,128)(2,1)} %copy-done.1), calls=%async_computation.7 | async-start | bytes 1048576 | tf_op jit(solution)/shard_map/all_to_all | solution.py:275
  235.9 0.6 reshape.23
  236.5 11.5 %all-to-all-done.7 = bf16[64,12,256]{2,1,0:T(8,128)(2,1)S(1)} async-done(((bf16[64,12,256]{2,1,0:T(8,128)(2,1)}), bf16[64,12,256]{2,1,0:T(8,128)(2,1)S(1)}, u32[]{:S(2)}, u32[]{:S(2)}) %all-to-all-start.7) | async-done | bytes 393248 | tf_op jit(solution)/shard_map/all_to_all | solution.py:275
  248.0 0.1 convert_reduce_fusion
  248.1 0.6 add_convert_fusion
  (15 shorter events, 0.1 us)
Async XLA Ops:
  0.6 138.9 %copy-start = (bf16[512,256]{1,0:T(8,128)(2,1)S(1)}, bf16[512,256]{1,0:T(8,128)(2,1)}, u32[]{:S(2)}) copy-start(bf16[512,256]{1,0:T(8,128)(2,1)} %param.19) | copy-start | bytes 786436
  2.1 42.8 %all-to-all-start = ((bf16[32,24,128]{2,1,0:T(8,128)(2,1)}), bf16[32,24,128]{2,1,0:T(8,128)(2,1)S(1)}, u32[]{:S(2)}, u32[]{:S(2)}) async-start(bf16[32,24,128]{2,1,0:T(8,128)(2,1)} %broadcast_in_dim.9), calls=%async_computation | async-start | bytes 393216 | tf_op jit(solution)/shard_map/all_to_all | solution.py:198
  20.8 1.0 copy-start.6
  23.1 21.8 %collective-permute-start = (bf16[3,462,256]{2,1,0:T(8,128)(2,1)S(1)}, bf16[3,462,256]{2,1,0:T(8,128)(2,1)S(1)}, u32[]{:S(2)}, u32[]{:S(2)}) collective-permute-start(bf16[3,462,256]{2,1,0:T(8,128)(2,1)S(1)} %pad_maximum_fusion), channel_id=1, source_target_pairs={{0,16},{16,0},{32,48},{48,32},{1,17},{17,1},{33,49},{49,33},{2,18}... | collective-permute-start | bytes 2128904 | tf_op jit(solution)/shard_map/ppermute | solution.py:193
  44.9 0.7 copy-start.5
  54.1 39.9 %all-to-all-start.1 = ((bf16[32,32,128]{2,1,0:T(8,128)(2,1)}), bf16[32,32,128]{2,1,0:T(8,128)(2,1)S(1)}, u32[]{:S(2)}, u32[]{:S(2)}) async-start(bf16[32,32,128]{2,1,0:T(8,128)(2,1)} %attend.1), calls=%async_computation.1 | async-start | bytes 524288 | tf_op jit(solution)/shard_map/all_to_all | solution.py:223
  66.1 2.5 copy-start.2
  68.8 25.2 %collective-permute-start.1 = (bf16[3,462,256]{2,1,0:T(8,128)(2,1)S(1)}, bf16[3,462,256]{2,1,0:T(8,128)(2,1)S(1)}, u32[]{:S(2)}, u32[]{:S(2)}) collective-permute-start(bf16[3,462,256]{2,1,0:T(8,128)(2,1)S(1)} %pad_maximum_fusion.1), channel_id=1, source_target_pairs={{0,32},{16,48},{32,0},{48,16},{1,33},{17,49},{33,1},{49,17},{2,34}... | collective-permute-start | bytes 2128904 | tf_op jit(solution)/shard_map/ppermute | solution.py:193
  96.7 14.8 %copy-start.4 = (bf16[1,462,256]{2,1,0:T(8,128)(2,1)S(1)}, bf16[1,462,256]{2,1,0:T(8,128)(2,1)}, u32[]{:S(2)}) copy-start(bf16[1,462,256]{2,1,0:T(8,128)(2,1)} %get-tuple-element.30) | copy-start | bytes 709636
  97.9 13.7 %copy-start.3 = (bf16[1,462,256]{2,1,0:T(8,128)(2,1)S(1)}, bf16[1,462,256]{2,1,0:T(8,128)(2,1)}, u32[]{:S(2)}) copy-start(bf16[1,462,256]{2,1,0:T(8,128)(2,1)} %dynamic-slice_bitcast_fusion.1) | copy-start | bytes 709636
  97.9 41.6 %all-to-all-start.2 = ((bf16[32,24,128]{2,1,0:T(8,128)(2,1)}), bf16[32,24,128]{2,1,0:T(8,128)(2,1)S(1)}, u32[]{:S(2)}, u32[]{:S(2)}) async-start(bf16[32,24,128]{2,1,0:T(8,128)(2,1)} %get-tuple-element.16), calls=%async_computation.2 | async-start | bytes 393216 | tf_op jit(solution)/shard_map/all_to_all | solution.py:235
  112.6 26.9 %collective-permute-start.2 = (bf16[3,462,256]{2,1,0:T(8,128)(2,1)S(1)}, bf16[3,462,256]{2,1,0:T(8,128)(2,1)S(1)}, u32[]{:S(2)}, u32[]{:S(2)}) collective-permute-start(bf16[3,462,256]{2,1,0:T(8,128)(2,1)S(1)} %pad_maximum_fusion.2), channel_id=1, source_target_pairs={{0,48},{16,32},{32,16},{48,0},{1,49},{17,33},{33,17},{49,1},{2,50}... | collective-permute-start | bytes 2128904 | tf_op jit(solution)/shard_map/ppermute | solution.py:193
  151.4 0.7 copy-start.7
  153.0 17.4 %all-to-all-start.4 = ((bf16[64,12,256]{2,1,0:T(8,128)(2,1)}), bf16[64,12,256]{2,1,0:T(8,128)(2,1)}, u32[]{:S(2)}, u32[]{:S(2)}) async-start(bf16[64,12,256]{2,1,0:T(8,128)(2,1)} %broadcast_in_dim.11), calls=%async_computation.4 | async-start | bytes 1048576 | tf_op jit(solution)/shard_map/all_to_all | solution.py:245
  228.7 0.8 copy-start.1
  229.5 18.6 %all-to-all-start.7 = ((bf16[64,12,256]{2,1,0:T(8,128)(2,1)}), bf16[64,12,256]{2,1,0:T(8,128)(2,1)S(1)}, u32[]{:S(2)}, u32[]{:S(2)}) async-start(bf16[64,12,256]{2,1,0:T(8,128)(2,1)} %copy-done.1), calls=%async_computation.7 | async-start | bytes 1048576 | tf_op jit(solution)/shard_map/all_to_all | solution.py:275

commit v6 on v5

--- a/solution.py
+++ b/solution.py
@@ -23,16 +23,16 @@
 
 
 def attend_kernel(
-    where, q_ref, k_hbm, v_hbm, sk_ref, sv_ref, out_ref, k_ref, v_ref, sems, *, tokens, group, head, scale
+    lengths, q_ref, k_hbm, v_hbm, sk_ref, sv_ref, out_ref, k_ref, v_ref, sems, *, tokens, group, head, scale
 ):
     k_copy = pltpu.make_async_copy(k_hbm, k_ref, sems.at[0])
     v_copy = pltpu.make_async_copy(v_hbm, v_ref, sems.at[1])
     k_copy.start()
     v_copy.start()
-    length = where[0]
-    first = where[1]
+    length = lengths[0]
     rows = tokens * group
     own = sk_ref.shape[0]
+    first = lax.axis_index(("far", "near")) * own
     query = q_ref[...].reshape(rows, head)
     unit = scale / math.log(2.0)
 
@@ -102,28 +102,61 @@
         copies_ref[i] = out
 
 
-def project_kernel(place, x_ref, *refs):
+def out_kernel(h_ref, w_ref, out_ref, wide_ref):
+    blocks, rows, _ = out_ref.shape
+    tokens = blocks * rows
+    head = h_ref.shape[2]
+    group = w_ref.shape[0] // head
+    wide_ref[...] = h_ref[...].astype(F32).reshape(tokens * group, head)
+    y = 0.0
+    for g in range(group):
+        x = wide_ref[pl.ds(g, tokens, stride=group), :].astype(BF16)
+        y = y + jnp.dot(x, w_ref[g * head : (g + 1) * head, :], preferred_element_type=F32)
+    for i in range(blocks):
+        out_ref[i] = y[i * rows : (i + 1) * rows].astype(BF16)
+
+
+def stream_kernel(in_ref, residual_ref, own_ref, copies_ref):
+    own = jnp.sum(in_ref[...].astype(F32), axis=0) + residual_ref[...].astype(F32)
+    own = own.astype(BF16)
+    own_ref[...] = own
+    for i in range(copies_ref.shape[0]):
+        copies_ref[i] = own
+
+
+def last_kernel(in_ref, own_ref, out_ref):
+    out_ref[...] = (own_ref[...].astype(F32) + jnp.sum(in_ref[...].astype(F32), axis=0)).astype(BF16)
+
+
+def project_kernel(x_ref, *refs):
     out_ref = refs[-1]
-    w_refs = refs[:-1]
-    _, units, _ = w_refs[0].shape
+    gates, ups = refs[: len(refs) // 2], refs[len(refs) // 2 : -1]
+    units = gates[0].shape[0]
+    slices = len(gates)
+    each = x_ref.shape[0] // slices
     blocks, rows, width = out_ref.shape
     half = width // 2
-    near = place[0]
-
-    def product(kind):
+    near = lax.axis_index("near")
+    xs = []
+    for m in range(slices):
+        at = (near ^ m) * each
+        xs.append(jnp.concatenate([x_ref[at + i].astype(F32) for i in range(each)], axis=0))
+
+    def product(w_refs):
         y = 0.0
-        for m, w_ref in enumerate(w_refs):
-            y = y + lax.dot_general(x_ref[near ^ m], w_ref[kind], (((1,), (1,)), ((), ())), preferred_element_type=F32)
+        for x, w_ref in zip(xs, w_refs):
+            y = y + lax.dot_general(
+                x.astype(BF16), w_ref[...], (((1,), (1,)), ((), ())), preferred_element_type=F32
+            )
         return y
 
     squares = 0.0
-    for i in range(x_ref.shape[0]):
-        x = x_ref[i].astype(F32)
+    for x in xs:
         squares = squares + jnp.sum(x * x, axis=1, keepdims=True)
     tokens = squares.shape[0]
     spare = jnp.zeros((tokens, half - units - 3), F32)
-    gate = jnp.concatenate([product(0), *three_parts(squares), spare], axis=1).astype(BF16)
-    up = product(1).astype(BF16)
+    gate = jnp.concatenate([product(gates), *three_parts(squares), spare], axis=1).astype(BF16)
+    up = product(ups).astype(BF16)
     for i in range(blocks):
         out_ref[i, :, :half] = gate[i * rows : (i + 1) * rows]
         out_ref[i, :, half : half + units] = up[i * rows : (i + 1) * rows]
@@ -142,14 +175,14 @@
         out_ref[i] = out
 
 
-def down_kernel(place, h_ref, *refs):
+def down_kernel(h_ref, *refs):
     out_ref = refs[-1]
     w_refs = refs[:-1]
     rows = out_ref.shape[1]
     each = out_ref.shape[0] // len(w_refs)
-    near = place[0]
+    near = lax.axis_index("near")
     for m, w_ref in enumerate(w_refs):
-        y = jnp.dot(h_ref[...], w_ref[2], preferred_element_type=F32)
+        y = jnp.dot(h_ref[...], w_ref[...], preferred_element_type=F32)
         for k in range(each):
             out_ref[(near ^ m) * each + k] = y[k * rows : (k + 1) * rows].astype(BF16)
 
@@ -175,30 +208,34 @@
     n_ctx = n_far * n_near
     ctx = ("far", "near")
     tokens = rows * n_ctx
-    c = lax.axis_index(ctx)
     trows = residual_stream.shape[0]
     feats = residual_stream.shape[1]
     units = gate_weight.shape[1] // n_near
 
     near = lax.axis_index("near")
 
-    def chunk(place):
-        def part(w):
-            return lax.dynamic_slice_in_dim(w, place * units, units, 0)
-
-        gate, upper = part(gate_weight.T).astype(F32) * norm_gain, part(up_weight.T).astype(F32) * norm_gain
-        return jnp.stack([gate.astype(BF16), upper.astype(BF16), part(down_weight)])
-
-    def trade(m, place):
-        return lax.ppermute(chunk(place ^ m), "near", [(i, i ^ m) for i in range(4)])
-
-    weights = [chunk(near)]
+    def chunk(kind, place):
+        w = (gate_weight.T, up_weight.T, down_weight)[kind]
+        w = lax.dynamic_slice_in_dim(w, place * units, units, 0)
+        return w if kind == 2 else (w.astype(F32) * norm_gain).astype(BF16)
+
+    weights = [[chunk(kind, near)] + [None] * 3 for kind in range(3)]
+    place = near
+
+    def beside(x, *trades):
+        nonlocal place
+        sent = [
+            lax.ppermute(chunk(kind, place ^ m), "near", [(i, i ^ m) for i in range(4)]) for kind, m in trades
+        ]
+        x, place, *sent = lax.optimization_barrier((x, place, *sent))
+        for (kind, m), w in zip(trades, sent):
+            weights[kind][m] = w
+        return x
+
     each = rows * group
     q_all = jnp.broadcast_to(queries.reshape(1, each, head), (n_ctx, each, head))
     q_all = lax.all_to_all(q_all, ctx, 0, 0, tiled=True)
-    q_all, w, place = lax.optimization_barrier((q_all, trade(1, near), near))
-    weights.append(w)
-    where = jnp.stack([lengths[0], c * rows])
+    q_all = beside(q_all, (0, 1), (0, 2))
     vmem = pl.BlockSpec(memory_space=pltpu.VMEM)
     smem = pl.BlockSpec(memory_space=pltpu.SMEM)
     anywhere = pl.BlockSpec(memory_space=pl.ANY)
@@ -219,10 +256,9 @@
             flops=4 * tokens * width * stretch, bytes_accessed=2**21, transcendentals=tokens * group * stretch
         ),
         name="attend",
-    )(where, q_all, cache_keys[0], cache_values[0], seg_keys, seg_values)
+    )(lengths, q_all, cache_keys[0], cache_values[0], seg_keys, seg_values)
     parts = lax.all_to_all(partial, ctx, 0, 0, tiled=True)
-    parts, w, place = lax.optimization_barrier((parts, trade(2, place), place))
-    weights.append(w)
+    parts = beside(parts, (1, 1), (1, 2))
     attention, copies = pl.pallas_call(
         merge_kernel,
         out_shape=(jax.ShapeDtypeStruct((each, head), BF16), jax.ShapeDtypeStruct((n_ctx, each, head), BF16)),
@@ -233,28 +269,41 @@
     )(parts)
     attention = attention.reshape(rows, width)
     heads_all = lax.all_to_all(copies, ctx, 0, 0, tiled=True)
-    heads_all, w = lax.optimization_barrier((heads_all, trade(3, place)))
-    heads_all = heads_all.reshape(tokens, width)
-    weights.append(w)
-    mixed = jnp.dot(heads_all, out_weight, preferred_element_type=F32)
-
-    mixed = mixed.astype(BF16).reshape(n_tp, trows, feats)
-    mixed = jnp.sum(lax.all_to_all(mixed, "tp", 0, 0, tiled=True).astype(F32), axis=0)
-    own = (residual_stream.astype(F32) + mixed).astype(BF16)
-    stream = jnp.broadcast_to(own[None], (n_near * n_tp, trows, feats))
-    stream = lax.all_to_all(stream, ("near", "tp"), 0, 0, tiled=True).reshape(n_near, tokens, feats)
+    heads_all = beside(heads_all, (0, 3), (1, 3))
+    mixed = pl.pallas_call(
+        out_kernel,
+        out_shape=jax.ShapeDtypeStruct((n_tp, trows, feats), BF16),
+        in_specs=[vmem] * 2,
+        out_specs=vmem,
+        scratch_shapes=[pltpu.VMEM((tokens * group, head), F32)],
+        compiler_params=small,
+        name="out",
+    )(heads_all, out_weight)
+    mixed = lax.all_to_all(mixed, "tp", 0, 0, tiled=True)
+    own, stream = pl.pallas_call(
+        stream_kernel,
+        out_shape=(
+            jax.ShapeDtypeStruct((trows, feats), BF16),
+            jax.ShapeDtypeStruct((n_near * n_tp, trows, feats), BF16),
+        ),
+        in_specs=[vmem] * 2,
+        out_specs=(vmem, vmem),
+        compiler_params=small,
+        name="stream",
+    )(mixed, residual_stream)
+    stream = lax.all_to_all(stream, ("near", "tp"), 0, 0, tiled=True)
 
     half = -(-(units + 3) // 128) * 128
     block = tokens // n_far
     sums = pl.pallas_call(
         project_kernel,
         out_shape=jax.ShapeDtypeStruct((n_far, block, 2 * half), BF16),
-        in_specs=[smem] + [vmem] * 5,
+        in_specs=[vmem] * 9,
         out_specs=vmem,
         compiler_params=small,
         name="project",
-    )(near[None], stream, *weights)
-    sums = lax.all_to_all(sums, "far", 0, 0, tiled=True)
+    )(stream, *weights[0], *weights[1])
+    sums = beside(lax.all_to_all(sums, "far", 0, 0, tiled=True), (2, 1), (2, 2))
     hidden = pl.pallas_call(
         hidden_kernel,
         out_shape=jax.ShapeDtypeStruct((n_far, block, units), BF16),
@@ -263,17 +312,24 @@
         compiler_params=small,
         name="hidden",
     )(sums)
-    hidden = lax.all_to_all(hidden, "far", 0, 0, tiled=True).reshape(tokens, units)
+    hidden = beside(lax.all_to_all(hidden, "far", 0, 0, tiled=True), (2, 3)).reshape(tokens, units)
     lowered = pl.pallas_call(
         down_kernel,
         out_shape=jax.ShapeDtypeStruct((n_near * n_tp, trows, feats), BF16),
-        in_specs=[smem] + [vmem] * 5,
+        in_specs=[vmem] * 5,
         out_specs=vmem,
         compiler_params=small,
         name="down",
-    )(near[None], hidden, *weights)
+    )(hidden, *weights[2])
     lowered = lax.all_to_all(lowered, ("near", "tp"), 0, 0, tiled=True)
-    layer_out = (own.astype(F32) + jnp.sum(lowered.astype(F32), axis=0)).astype(BF16)
+    layer_out = pl.pallas_call(
+        last_kernel,
+        out_shape=jax.ShapeDtypeStruct((trows, feats), BF16),
+        in_specs=[vmem] * 2,
+        out_specs=vmem,
+        compiler_params=small,
+        name="last",
+    )(lowered, own)
     return (attention, layer_out)
 
 

time: 250 us -> 229 us (0.916)
  blocking collectives: 67.5 us -> 28.3 us
  starting transfers between devices: 69.2 us -> 103 us
  other arithmetic: 9.27 us -> 2.75 us
  waiting for transfers between devices: 81.9 us -> 77.3 us
  local copies, waits for them, and re-layouts: 8.22 us -> 3.63 us
    all_to_all x3 -> x2, blocking collectives: 67.5 us -> 28.3 us  [the longest x1 16.7 us: per_device(): stream = lax.all_to_all(stream, ('near', 'tp'), 0, 0, tiled=True)]
    ppermute x3 -> x9, starting transfers between devices: 13.3 us -> 32.5 us  [beside(): lax.ppermute(chunk(kind, place ^ m), 'near', [(i, i ^ m) for i in range(4)])]
    all_to_all x1 -> x2, starting transfers between devices: 5.24 us -> 18.6 us  [the longest x1 10.4 us: per_device(): sums = beside(lax.all_to_all(sums, 'far', 0, 0, tiled=True), (2, 1), (2, 2))]
    another operation x8 -> x0, other arithmetic: 8.52 us -> none  [the longest x7 7.96 us: chunk(): return jnp.stack([gate.astype(BF16), upper.astype(BF16), part(down_weight)])]
    all_to_all x1 -> x2, waiting for transfers between devices: 11 us -> 2.56 us  [the longest x1 2.56 us: per_device(): sums = beside(lax.all_to_all(sums, 'far', 0, 0, tiled=True), (2, 1), (2, 2))]
    pallas_call x1, Pallas kernels: 8.56 us -> 6.03 us  [per_device(): pl.pallas_call(functools.partial(attend_kernel, tokens=tokens, group=grou...]
    ppermute x3 -> x9, waiting for transfers between devices: 59.3 us -> 60.2 us  [beside(): lax.ppermute(chunk(kind, place ^ m), 'near', [(i, i ^ m) for i in range(4)])]
  transfers between devices with their start and end apart: 8 -> 15, of which waited for: 5 -> 13; matrix products, arithmetic and copies ran while one was open for 3% -> 2% of each run, Pallas kernels for 0% -> 0%
where the time goes in v6:
time: 229 us; the launch traced here: 228 us
  starting transfers between devices  103 us (45%)
  waiting for transfers between devices  77.3 us (34%)
  blocking collectives  28.3 us (12%)
  Pallas kernels  11.7 us (5%)
  local copies, waits for them, and re-layouts  3.63 us (2%)
  other arithmetic  2.75 us (1%)
    ppermute x9, waiting for transfers between devices, beside(): lax.ppermute(chunk(kind, place ^ m), 'near', [(i, i ^ m) for i in range(4)])  60.2 us
    ppermute x9, starting transfers between devices, beside(): lax.ppermute(chunk(kind, place ^ m), 'near', [(i, i ^ m) for i in range(4)])  32.5 us
    all_to_all x1, starting transfers between devices, per_device(): q_all = lax.all_to_all(q_all, ctx, 0, 0, tiled=True)  18.7 us
    all_to_all x1, blocking collectives, per_device(): stream = lax.all_to_all(stream, ('near', 'tp'), 0, 0, tiled=True)  16.7 us
    all_to_all x1, starting transfers between devices, per_device(): parts = lax.all_to_all(partial, ctx, 0, 0, tiled=True)  13.4 us
    all_to_all x1, blocking collectives, per_device(): mixed = lax.all_to_all(mixed, 'tp', 0, 0, tiled=True)  11.6 us
    all_to_all x1, waiting for transfers between devices, per_device(): lowered = lax.all_to_all(lowered, ('near', 'tp'), 0, 0, tiled=True)  11.5 us
    all_to_all x1, starting transfers between devices, per_device(): heads_all = lax.all_to_all(copies, ctx, 0, 0, tiled=True)  11.3 us
  transfers between devices with their start and end apart: 15, of which 13 were waited for; matrix products, arithmetic and copies ran while one was open for 2% of the time, Pallas kernels for 0%

profile of v6, /device:TPU:1, one launch (start us, length us, event | category | flops | bytes accessed | tf_op | source)
XLA Modules:
  0.0 228.2 jit_solution(4505739593931427869)
XLA Ops:
  0.6 0.7 broadcast_in_dim.4
  1.3 0.7 broadcast_in_dim.5
  2.0 18.7 %all-to-all-start = ((bf16[32,24,128]{2,1,0:T(8,128)(2,1)}), bf16[32,24,128]{2,1,0:T(8,128)(2,1)S(1)}, u32[]{:S(2)}, u32[]{:S(2)}) async-start(bf16[32,24,128]{2,1,0:T(8,128)(2,1)} %broadcast_in_dim.5), calls=%async_computation | async-start | bytes 393216 | tf_op jit(solution)/shard_map/all_to_all | solution.py:237
  20.7 0.7 copy-done.5
  21.4 1.4 fusion.6
  22.8 4.6 %collective-permute-start = (bf16[462,256]{1,0:T(8,128)(2,1)S(1)}, bf16[462,256]{1,0:T(8,128)(2,1)S(1)}, u32[]{:S(2)}, u32[]{:S(2)}) collective-permute-start(bf16[462,256]{1,0:T(8,128)(2,1)S(1)} %get-tuple-element.51), channel_id=1, source_target_pairs={{0,16},{16,0},{32,48},{48,32},{1,17},{17,1},{33,49},{49,33},{2,18}... | collective-permute-start | bytes 709640 | tf_op jit(solution)/shard_map/ppermute | solution.py:228
  27.5 3.1 %collective-permute-start.1 = (bf16[462,256]{1,0:T(8,128)(2,1)S(1)}, bf16[462,256]{1,0:T(8,128)(2,1)S(1)}, u32[]{:S(2)}, u32[]{:S(2)}) collective-permute-start(bf16[462,256]{1,0:T(8,128)(2,1)S(1)} %get-tuple-element.50), channel_id=1, source_target_pairs={{0,32},{16,48},{32,0},{48,16},{1,33},{17,49},{33,1},{49,17},{2,34}... | collective-permute-start | bytes 709640 | tf_op jit(solution)/shard_map/ppermute | solution.py:228
  31.2 2.5 %collective-permute-done.refs_1_ = bf16[462,256]{1,0:T(8,128)(2,1)S(1)} collective-permute-done((bf16[462,256]{1,0:T(8,128)(2,1)S(1)}, bf16[462,256]{1,0:T(8,128)(2,1)S(1)}, u32[]{:S(2)}, u32[]{:S(2)}) %collective-permute-start) | collective-permute-done | bytes 236576 | tf_op jit(solution)/shard_map/ppermute | solution.py:228
  33.7 3.2 %collective-permute-done.1.refs_2_ = bf16[462,256]{1,0:T(8,128)(2,1)S(1)} collective-permute-done((bf16[462,256]{1,0:T(8,128)(2,1)S(1)}, bf16[462,256]{1,0:T(8,128)(2,1)S(1)}, u32[]{:S(2)}, u32[]{:S(2)}) %collective-permute-start.1) | collective-permute-done | bytes 236576 | tf_op jit(solution)/shard_map/ppermute | solution.py:228
  36.9 1.0 all-to-all-done.q_ref
  37.9 0.7 copy-done.4
  38.5 6.0 %attend.1 = bf16[32,32,128]{2,1,0:T(8,128)(2,1)} custom-call(s32[1]{0:T(128)S(6)} %copy.14.lengths, bf16[32,24,128]{2,1,0:T(8,128)(2,1)} %copy-done.4, bf16[3072,128]{1,0:T(8,128)(2,1)} %bitcast.20, bf16[3072,128]{1,0:T(8,128)(2,1)} %bitcast.21, bf16[6,128]{1,0:T(8,128)(2,1)} %sk_ref.1, bf16[6,128]{1,0:T(8,128)(2,1)} %sv_ref.1), custom_call_target="tpu_custom_call" | custom-call | flops 1207959552 | bytes 2097152 | tf_op jit(solution)/shard_map/attend/pallas_call | solution.py:244
  44.6 13.4 %all-to-all-start.1 = ((bf16[32,32,128]{2,1,0:T(8,128)(2,1)}), bf16[32,32,128]{2,1,0:T(8,128)(2,1)S(1)}, u32[]{:S(2)}, u32[]{:S(2)}) async-start(bf16[32,32,128]{2,1,0:T(8,128)(2,1)} %attend.1), calls=%async_computation.1 | async-start | bytes 524288 | tf_op jit(solution)/shard_map/all_to_all | solution.py:260
  58.0 0.2 fusion.7
  58.3 4.6 %collective-permute-start.2 = (bf16[462,256]{1,0:T(8,128)(2,1)S(1)}, bf16[462,256]{1,0:T(8,128)(2,1)S(1)}, u32[]{:S(2)}, u32[]{:S(2)}) collective-permute-start(bf16[462,256]{1,0:T(8,128)(2,1)S(1)} %get-tuple-element.48), channel_id=1, source_target_pairs={{0,16},{16,0},{32,48},{48,32},{1,17},{17,1},{33,49},{49,33},{2,18}... | collective-permute-start | bytes 709640 | tf_op jit(solution)/shard_map/ppermute | solution.py:228
  62.9 3.1 %collective-permute-start.3 = (bf16[462,256]{1,0:T(8,128)(2,1)S(1)}, bf16[462,256]{1,0:T(8,128)(2,1)S(1)}, u32[]{:S(2)}, u32[]{:S(2)}) collective-permute-start(bf16[462,256]{1,0:T(8,128)(2,1)S(1)} %get-tuple-element.47), channel_id=1, source_target_pairs={{0,32},{16,48},{32,0},{48,16},{1,33},{17,49},{33,1},{49,17},{2,34}... | collective-permute-start | bytes 709640 | tf_op jit(solution)/shard_map/ppermute | solution.py:228
  66.0 2.9 %collective-permute-done.2.refs_5_ = bf16[462,256]{1,0:T(8,128)(2,1)S(1)} collective-permute-done((bf16[462,256]{1,0:T(8,128)(2,1)S(1)}, bf16[462,256]{1,0:T(8,128)(2,1)S(1)}, u32[]{:S(2)}, u32[]{:S(2)}) %collective-permute-start.2) | collective-permute-done | bytes 236576 | tf_op jit(solution)/shard_map/ppermute | solution.py:228
  68.9 7.3 %collective-permute-done.3.refs_6_ = bf16[462,256]{1,0:T(8,128)(2,1)S(1)} collective-permute-done((bf16[462,256]{1,0:T(8,128)(2,1)S(1)}, bf16[462,256]{1,0:T(8,128)(2,1)S(1)}, u32[]{:S(2)}, u32[]{:S(2)}) %collective-permute-start.3) | collective-permute-done | bytes 236576 | tf_op jit(solution)/shard_map/ppermute | solution.py:228
  76.2 2.0 all-to-all-done.1.in_ref
  78.2 1.1 merge.1
  79.3 11.3 %all-to-all-start.2 = ((bf16[32,24,128]{2,1,0:T(8,128)(2,1)}), bf16[32,24,128]{2,1,0:T(8,128)(2,1)S(1)}, u32[]{:S(2)}, u32[]{:S(2)}) async-start(bf16[32,24,128]{2,1,0:T(8,128)(2,1)} %get-tuple-element.28), calls=%async_computation.2 | async-start | bytes 393216 | tf_op jit(solution)/shard_map/all_to_all | solution.py:271
  90.6 1.1 fusion.5
  91.8 5.5 %collective-permute-start.4 = (bf16[462,256]{1,0:T(8,128)(2,1)S(1)}, bf16[462,256]{1,0:T(8,128)(2,1)S(1)}, u32[]{:S(2)}, u32[]{:S(2)}) collective-permute-start(bf16[462,256]{1,0:T(8,128)(2,1)S(1)} %get-tuple-element.56), channel_id=1, source_target_pairs={{0,48},{16,32},{32,16},{48,0},{1,49},{17,33},{33,17},{49,1},{2,50}... | collective-permute-start | bytes 709640 | tf_op jit(solution)/shard_map/ppermute | solution.py:228
  97.3 2.1 collective-permute-start.5
  99.5 8.9 %collective-permute-done.4.refs_3_ = bf16[462,256]{1,0:T(8,128)(2,1)S(1)} collective-permute-done((bf16[462,256]{1,0:T(8,128)(2,1)S(1)}, bf16[462,256]{1,0:T(8,128)(2,1)S(1)}, u32[]{:S(2)}, u32[]{:S(2)}) %collective-permute-start.4) | collective-permute-done | bytes 236576 | tf_op jit(solution)/shard_map/ppermute | solution.py:228
  108.3 5.2 %collective-permute-done.5.refs_7_ = bf16[462,256]{1,0:T(8,128)(2,1)S(1)} collective-permute-done((bf16[462,256]{1,0:T(8,128)(2,1)S(1)}, bf16[462,256]{1,0:T(8,128)(2,1)S(1)}, u32[]{:S(2)}, u32[]{:S(2)}) %collective-permute-start.5) | collective-permute-done | bytes 236576 | tf_op jit(solution)/shard_map/ppermute | solution.py:228
  113.5 0.3 out.1
  113.8 11.6 %all_to_all.40.in_ref = bf16[16,12,256]{2,1,0:T(8,128)(2,1)S(1)} all-to-all(bf16[16,12,256]{2,1,0:T(8,128)(2,1)S(1)} %out.1), channel_id=1, replica_groups=mesh['far'=8,'near'=4,'tp'=16] {'tp'}, dimensions={0} | all-to-all | bytes 196608 | tf_op jit(solution)/shard_map/all_to_all | solution.py:282
  125.4 0.1 stream.1
  125.4 16.7 %all_to_all.41.x_ref = bf16[64,12,256]{2,1,0:T(8,128)(2,1)S(1)} all-to-all(bf16[64,12,256]{2,1,0:T(8,128)(2,1)S(1)} %get-tuple-element.31), channel_id=1, replica_groups=mesh['far'=8,'near'=4,'tp'=16] {'near','tp'}, dimensions={0} | all-to-all | bytes 786432 | tf_op jit(solution)/shard_map/all_to_all | solution.py:294
  142.1 1.5 project.1
  143.6 10.4 %all-to-all-start.5 = ((bf16[8,24,1024]{2,1,0:T(8,128)(2,1)}), bf16[8,24,1024]{2,1,0:T(8,128)(2,1)S(1)}, u32[]{:S(2)}, u32[]{:S(2)}) async-start(bf16[8,24,1024]{2,1,0:T(8,128)(2,1)} %project.1), calls=%async_computation.5 | async-start | bytes 786432 | tf_op jit(solution)/shard_map/all_to_all | solution.py:306
  154.0 0.2 constant_dynamic-slice_fusion
  154.2 3.2 %collective-permute-start.6 = (bf16[462,256]{1,0:T(8,128)(2,1)S(1)}, bf16[462,256]{1,0:T(8,128)(2,1)S(1)}, u32[]{:S(2)}, u32[]{:S(2)}) collective-permute-start(bf16[462,256]{1,0:T(8,128)(2,1)S(1)} %get-tuple-element.54), channel_id=1, source_target_pairs={{0,16},{16,0},{32,48},{48,32},{1,17},{17,1},{33,49},{49,33},{2,18}... | collective-permute-start | bytes 709640 | tf_op jit(solution)/shard_map/ppermute | solution.py:228
  157.4 2.0 collective-permute-start.7
  159.4 4.3 %collective-permute-done.6.refs_1_ = bf16[462,256]{1,0:T(8,128)(2,1)S(1)} collective-permute-done((bf16[462,256]{1,0:T(8,128)(2,1)S(1)}, bf16[462,256]{1,0:T(8,128)(2,1)S(1)}, u32[]{:S(2)}, u32[]{:S(2)}) %collective-permute-start.6) | collective-permute-done | bytes 236576 | tf_op jit(solution)/shard_map/ppermute | solution.py:228
  163.6 13.4 %collective-permute-done.7.refs_2_ = bf16[462,256]{1,0:T(8,128)(2,1)S(1)} collective-permute-done((bf16[462,256]{1,0:T(8,128)(2,1)S(1)}, bf16[462,256]{1,0:T(8,128)(2,1)S(1)}, u32[]{:S(2)}, u32[]{:S(2)}) %collective-permute-start.7) | collective-permute-done | bytes 236576 | tf_op jit(solution)/shard_map/ppermute | solution.py:228
  177.0 2.6 %all-to-all-done.5.in_ref = bf16[8,24,1024]{2,1,0:T(8,128)(2,1)S(1)} async-done(((bf16[8,24,1024]{2,1,0:T(8,128)(2,1)}), bf16[8,24,1024]{2,1,0:T(8,128)(2,1)S(1)}, u32[]{:S(2)}, u32[]{:S(2)}) %all-to-all-start.5) | async-done | bytes 393248 | tf_op jit(solution)/shard_map/all_to_all | solution.py:306
  179.5 0.9 hidden.1
  180.4 8.3 %all-to-all-start.6 = ((bf16[8,24,462]{2,1,0:T(8,128)(2,1)}), bf16[8,24,462]{2,1,0:T(8,128)(2,1)S(1)}, u32[]{:S(2)}, u32[]{:S(2)}) async-start(bf16[8,24,462]{2,1,0:T(8,128)(2,1)} %hidden.1), calls=%async_computation.6 | async-start | bytes 393216 | tf_op jit(solution)/shard_map/all_to_all | solution.py:315
  188.7 0.1 constant_dynamic-slice_fusion.1
  188.7 4.2 %collective-permute-start.8 = (bf16[462,256]{1,0:T(8,128)(2,1)S(1)}, bf16[462,256]{1,0:T(8,128)(2,1)S(1)}, u32[]{:S(2)}, u32[]{:S(2)}) collective-permute-start(bf16[462,256]{1,0:T(8,128)(2,1)S(1)} %constant_dynamic-slice_fusion.1), channel_id=1, source_target_pairs={{0,48},{16,32},{32,16},{48,0},{1,49},{17,33},{33,17},{49,1},{2,50}... | collective-permute-start | bytes 709640 | tf_op jit(solution)/shard_map/ppermute | solution.py:228
  192.9 12.7 %collective-permute-done.8.refs_3_ = bf16[462,256]{1,0:T(8,128)(2,1)S(1)} collective-permute-done((bf16[462,256]{1,0:T(8,128)(2,1)S(1)}, bf16[462,256]{1,0:T(8,128)(2,1)S(1)}, u32[]{:S(2)}, u32[]{:S(2)}) %collective-permute-start.8) | collective-permute-done | bytes 236576 | tf_op jit(solution)/shard_map/ppermute | solution.py:228
  205.6 1.2 down.1
  206.8 8.5 %all-to-all-start.7 = ((bf16[64,12,256]{2,1,0:T(8,128)(2,1)}), bf16[64,12,256]{2,1,0:T(8,128)(2,1)S(1)}, u32[]{:S(2)}, u32[]{:S(2)}) async-start(bf16[64,12,256]{2,1,0:T(8,128)(2,1)} %down.1), calls=%async_computation.7 | async-start | bytes 1048576 | tf_op jit(solution)/shard_map/all_to_all | solution.py:324
  215.3 0.6 reshape.13
  215.9 11.5 %all-to-all-done.7.in_ref = bf16[64,12,256]{2,1,0:T(8,128)(2,1)S(1)} async-done(((bf16[64,12,256]{2,1,0:T(8,128)(2,1)}), bf16[64,12,256]{2,1,0:T(8,128)(2,1)S(1)}, u32[]{:S(2)}, u32[]{:S(2)}) %all-to-all-start.7) | async-done | bytes 393248 | tf_op jit(solution)/shard_map/all_to_all | solution.py:324
  227.5 0.7 last.1
  (12 shorter events, 0.0 us)
Async XLA Ops:
  2.0 35.8 %all-to-all-start = ((bf16[32,24,128]{2,1,0:T(8,128)(2,1)}), bf16[32,24,128]{2,1,0:T(8,128)(2,1)S(1)}, u32[]{:S(2)}, u32[]{:S(2)}) async-start(bf16[32,24,128]{2,1,0:T(8,128)(2,1)} %broadcast_in_dim.5), calls=%async_computation | async-start | bytes 393216 | tf_op jit(solution)/shard_map/all_to_all | solution.py:237
  20.7 0.7 copy-start.5
  22.8 10.9 %collective-permute-start = (bf16[462,256]{1,0:T(8,128)(2,1)S(1)}, bf16[462,256]{1,0:T(8,128)(2,1)S(1)}, u32[]{:S(2)}, u32[]{:S(2)}) collective-permute-start(bf16[462,256]{1,0:T(8,128)(2,1)S(1)} %get-tuple-element.51), channel_id=1, source_target_pairs={{0,16},{16,0},{32,48},{48,32},{1,17},{17,1},{33,49},{49,33},{2,18}... | collective-permute-start | bytes 709640 | tf_op jit(solution)/shard_map/ppermute | solution.py:228
  27.5 9.5 %collective-permute-start.1 = (bf16[462,256]{1,0:T(8,128)(2,1)S(1)}, bf16[462,256]{1,0:T(8,128)(2,1)S(1)}, u32[]{:S(2)}, u32[]{:S(2)}) collective-permute-start(bf16[462,256]{1,0:T(8,128)(2,1)S(1)} %get-tuple-element.50), channel_id=1, source_target_pairs={{0,32},{16,48},{32,0},{48,16},{1,33},{17,49},{33,1},{49,17},{2,34}... | collective-permute-start | bytes 709640 | tf_op jit(solution)/shard_map/ppermute | solution.py:228
  37.9 0.7 copy-start.4
  38.5 19.5 %copy-start.3 = (bf16[256,1848]{0,1:T(8,128)(2,1)S(1)}, bf16[256,1848]{0,1:T(8,128)(2,1)}, u32[]{:S(2)}) copy-start(bf16[256,1848]{0,1:T(8,128)(2,1)} %param.22) | copy-start | bytes 2838532
  44.6 33.6 %all-to-all-start.1 = ((bf16[32,32,128]{2,1,0:T(8,128)(2,1)}), bf16[32,32,128]{2,1,0:T(8,128)(2,1)S(1)}, u32[]{:S(2)}, u32[]{:S(2)}) async-start(bf16[32,32,128]{2,1,0:T(8,128)(2,1)} %attend.1), calls=%async_computation.1 | async-start | bytes 524288 | tf_op jit(solution)/shard_map/all_to_all | solution.py:260
  58.3 10.6 %collective-permute-start.2 = (bf16[462,256]{1,0:T(8,128)(2,1)S(1)}, bf16[462,256]{1,0:T(8,128)(2,1)S(1)}, u32[]{:S(2)}, u32[]{:S(2)}) collective-permute-start(bf16[462,256]{1,0:T(8,128)(2,1)S(1)} %get-tuple-element.48), channel_id=1, source_target_pairs={{0,16},{16,0},{32,48},{48,32},{1,17},{17,1},{33,49},{49,33},{2,18}... | collective-permute-start | bytes 709640 | tf_op jit(solution)/shard_map/ppermute | solution.py:228
  62.9 13.3 %collective-permute-start.3 = (bf16[462,256]{1,0:T(8,128)(2,1)S(1)}, bf16[462,256]{1,0:T(8,128)(2,1)S(1)}, u32[]{:S(2)}, u32[]{:S(2)}) collective-permute-start(bf16[462,256]{1,0:T(8,128)(2,1)S(1)} %get-tuple-element.47), channel_id=1, source_target_pairs={{0,32},{16,48},{32,0},{48,16},{1,33},{17,49},{33,1},{49,17},{2,34}... | collective-permute-start | bytes 709640 | tf_op jit(solution)/shard_map/ppermute | solution.py:228
  79.3 34.2 %all-to-all-start.2 = ((bf16[32,24,128]{2,1,0:T(8,128)(2,1)}), bf16[32,24,128]{2,1,0:T(8,128)(2,1)S(1)}, u32[]{:S(2)}, u32[]{:S(2)}) async-start(bf16[32,24,128]{2,1,0:T(8,128)(2,1)} %get-tuple-element.28), calls=%async_computation.2 | async-start | bytes 393216 | tf_op jit(solution)/shard_map/all_to_all | solution.py:271
  90.6 22.9 %copy-start = (bf16[512,256]{1,0:T(8,128)(2,1)S(1)}, bf16[512,256]{1,0:T(8,128)(2,1)}, u32[]{:S(2)}) copy-start(bf16[512,256]{1,0:T(8,128)(2,1)} %w_ref.1) | copy-start | bytes 786436
  91.8 16.6 %collective-permute-start.4 = (bf16[462,256]{1,0:T(8,128)(2,1)S(1)}, bf16[462,256]{1,0:T(8,128)(2,1)S(1)}, u32[]{:S(2)}, u32[]{:S(2)}) collective-permute-start(bf16[462,256]{1,0:T(8,128)(2,1)S(1)} %get-tuple-element.56), channel_id=1, source_target_pairs={{0,48},{16,32},{32,16},{48,0},{1,49},{17,33},{33,17},{49,1},{2,50}... | collective-permute-start | bytes 709640 | tf_op jit(solution)/shard_map/ppermute | solution.py:228
  97.3 16.2 %collective-permute-start.5 = (bf16[462,256]{1,0:T(8,128)(2,1)S(1)}, bf16[462,256]{1,0:T(8,128)(2,1)S(1)}, u32[]{:S(2)}, u32[]{:S(2)}) collective-permute-start(bf16[462,256]{1,0:T(8,128)(2,1)S(1)} %get-tuple-element.55), channel_id=1, source_target_pairs={{0,48},{16,32},{32,16},{48,0},{1,49},{17,33},{33,17},{49,1},{2,50}... | collective-permute-start | bytes 709640 | tf_op jit(solution)/shard_map/ppermute | solution.py:228
  113.8 11.6 %copy-start.1 = (bf16[12,256]{1,0:T(8,128)(2,1)S(1)}, bf16[12,256]{1,0:T(8,128)(2,1)}, u32[]{:S(2)}) copy-start(bf16[12,256]{1,0:T(8,128)(2,1)} %residual_ref.1) | copy-start | bytes 18436
  142.1 11.8 %copy-start.2 = (bf16[1848,256]{1,0:T(8,128)(2,1)S(1)}, bf16[1848,256]{1,0:T(8,128)(2,1)}, u32[]{:S(2)}) copy-start(bf16[1848,256]{1,0:T(8,128)(2,1)} %param.23) | copy-start | bytes 2838532
  143.6 35.9 %all-to-all-start.5 = ((bf16[8,24,1024]{2,1,0:T(8,128)(2,1)}), bf16[8,24,1024]{2,1,0:T(8,128)(2,1)S(1)}, u32[]{:S(2)}, u32[]{:S(2)}) async-start(bf16[8,24,1024]{2,1,0:T(8,128)(2,1)} %project.1), calls=%async_computation.5 | async-start | bytes 786432 | tf_op jit(solution)/shard_map/all_to_all | solution.py:306
  154.2 9.5 %collective-permute-start.6 = (bf16[462,256]{1,0:T(8,128)(2,1)S(1)}, bf16[462,256]{1,0:T(8,128)(2,1)S(1)}, u32[]{:S(2)}, u32[]{:S(2)}) collective-permute-start(bf16[462,256]{1,0:T(8,128)(2,1)S(1)} %get-tuple-element.54), channel_id=1, source_target_pairs={{0,16},{16,0},{32,48},{48,32},{1,17},{17,1},{33,49},{49,33},{2,18}... | collective-permute-start | bytes 709640 | tf_op jit(solution)/shard_map/ppermute | solution.py:228
  157.4 19.6 %collective-permute-start.7 = (bf16[462,256]{1,0:T(8,128)(2,1)S(1)}, bf16[462,256]{1,0:T(8,128)(2,1)S(1)}, u32[]{:S(2)}, u32[]{:S(2)}) collective-permute-start(bf16[462,256]{1,0:T(8,128)(2,1)S(1)} %get-tuple-element.53), channel_id=1, source_target_pairs={{0,32},{16,48},{32,0},{48,16},{1,33},{17,49},{33,1},{49,17},{2,34}... | collective-permute-start | bytes 709640 | tf_op jit(solution)/shard_map/ppermute | solution.py:228
  180.4 25.2 %all-to-all-start.6 = ((bf16[8,24,462]{2,1,0:T(8,128)(2,1)}), bf16[8,24,462]{2,1,0:T(8,128)(2,1)S(1)}, u32[]{:S(2)}, u32[]{:S(2)}) async-start(bf16[8,24,462]{2,1,0:T(8,128)(2,1)} %hidden.1), calls=%async_computation.6 | async-start | bytes 393216 | tf_op jit(solution)/shard_map/all_to_all | solution.py:315
  188.7 16.9 %collective-permute-start.8 = (bf16[462,256]{1,0:T(8,128)(2,1)S(1)}, bf16[462,256]{1,0:T(8,128)(2,1)S(1)}, u32[]{:S(2)}, u32[]{:S(2)}) collective-permute-start(bf16[462,256]{1,0:T(8,128)(2,1)S(1)} %constant_dynamic-slice_fusion.1), channel_id=1, source_target_pairs={{0,48},{16,32},{32,16},{48,0},{1,49},{17,33},{33,17},{49,1},{2,50}... | collective-permute-start | bytes 709640 | tf_op jit(solution)/shard_map/ppermute | solution.py:228
  206.8 20.7 %all-to-all-start.7 = ((bf16[64,12,256]{2,1,0:T(8,128)(2,1)}), bf16[64,12,256]{2,1,0:T(8,128)(2,1)S(1)}, u32[]{:S(2)}, u32[]{:S(2)}) async-start(bf16[64,12,256]{2,1,0:T(8,128)(2,1)} %down.1), calls=%async_computation.7 | async-start | bytes 1048576 | tf_op jit(solution)/shard_map/all_to_all | solution.py:324

commit v7 on v6

--- a/solution.py
+++ b/solution.py
@@ -23,16 +23,21 @@
 
 
 def attend_kernel(
-    lengths, q_ref, k_hbm, v_hbm, sk_ref, sv_ref, out_ref, k_ref, v_ref, sems, *, tokens, group, head, scale
+    lengths, q_ref, k_hbm, v_hbm, sk_hbm, sv_hbm, out_ref, k_ref, v_ref, sk_ref, sv_ref, sems,
+    *, tokens, group, head, scale
 ):
     k_copy = pltpu.make_async_copy(k_hbm, k_ref, sems.at[0])
     v_copy = pltpu.make_async_copy(v_hbm, v_ref, sems.at[1])
+    sk_copy = pltpu.make_async_copy(sk_hbm, sk_ref, sems.at[2])
+    sv_copy = pltpu.make_async_copy(sv_hbm, sv_ref, sems.at[3])
+    sk_copy.start()
+    sv_copy.start()
     k_copy.start()
     v_copy.start()
     length = lengths[0]
     rows = tokens * group
     own = sk_ref.shape[0]
-    first = lax.axis_index(("far", "near")) * own
+    first = lax.axis_index(("far", "lo", "hi")) * own
     query = q_ref[...].reshape(rows, head)
     unit = scale / math.log(2.0)
 
@@ -49,6 +54,8 @@
         w = jnp.exp2((s - top_new) * unit)
         return top_new, total * fade + jnp.sum(w, axis=0, keepdims=True), numer * fade + weigh(values, w)
 
+    sk_copy.wait()
+    sv_copy.wait()
     s = scores(sk_ref[...])
     token = lax.broadcasted_iota(jnp.int32, (own, rows), 1) // group
     place = first + lax.broadcasted_iota(jnp.int32, (own, rows), 0)
@@ -136,7 +143,7 @@
     each = x_ref.shape[0] // slices
     blocks, rows, width = out_ref.shape
     half = width // 2
-    near = lax.axis_index("near")
+    near = lax.axis_index(("lo", "hi"))
     xs = []
     for m in range(slices):
         at = (near ^ m) * each
@@ -175,16 +182,15 @@
         out_ref[i] = out
 
 
-def down_kernel(h_ref, *refs):
-    out_ref = refs[-1]
-    w_refs = refs[:-1]
+def down_kernel(mine_ref, other_ref, w_ref, wy_ref, out_ref):
     rows = out_ref.shape[1]
-    each = out_ref.shape[0] // len(w_refs)
-    near = lax.axis_index("near")
-    for m, w_ref in enumerate(w_refs):
-        y = jnp.dot(h_ref[...], w_ref[...], preferred_element_type=F32)
+    each = out_ref.shape[0] // 2
+    lo, hi = lax.axis_index("lo"), lax.axis_index("hi")
+    for at, ref in ((hi, w_ref), (1 - hi, wy_ref)):
+        y = jnp.dot(mine_ref[...], ref[lo], preferred_element_type=F32)
+        y = y + jnp.dot(other_ref[...], ref[1 - lo], preferred_element_type=F32)
         for k in range(each):
-            out_ref[(near ^ m) * each + k] = y[k * rows : (k + 1) * rows].astype(BF16)
+            out_ref[at * each + k] = y[k * rows : (k + 1) * rows].astype(BF16)
 
 
 def per_device(
@@ -204,38 +210,44 @@
     rows, width = queries.shape
     _, stretch, head = cache_keys.shape
     group = width // head
-    n_far, n_near, n_tp = lax.axis_size("far"), lax.axis_size("near"), lax.axis_size("tp")
+    near_axes = ("lo", "hi")
+    n_far, n_near, n_tp = lax.axis_size("far"), lax.axis_size(near_axes), lax.axis_size("tp")
     n_ctx = n_far * n_near
-    ctx = ("far", "near")
+    ctx = ("far", *near_axes)
     tokens = rows * n_ctx
     trows = residual_stream.shape[0]
     feats = residual_stream.shape[1]
     units = gate_weight.shape[1] // n_near
 
-    near = lax.axis_index("near")
-
-    def chunk(kind, place):
-        w = (gate_weight.T, up_weight.T, down_weight)[kind]
-        w = lax.dynamic_slice_in_dim(w, place * units, units, 0)
-        return w if kind == 2 else (w.astype(F32) * norm_gain).astype(BF16)
-
-    weights = [[chunk(kind, near)] + [None] * 3 for kind in range(3)]
+    near = lax.axis_index(near_axes)
+
+    def chunk(w, place):
+        w = lax.dynamic_slice_in_dim(w.T, place * units, units, 0)
+        return (w.astype(F32) * norm_gain).astype(BF16)
+
+    def trade(w, m):
+        return lambda place: lax.ppermute(chunk(w, place ^ m), near_axes, [(i, i ^ m) for i in range(4)])
+
+    def down_chunk(place):
+        lows = [
+            lax.dynamic_slice_in_dim(down_weight, (2 * lo + (place & 1)) * units, units, 0) for lo in range(2)
+        ]
+        return jnp.stack(lows)
+
+    def down_trade(place):
+        return lax.ppermute(down_chunk(place ^ 1), "hi", [(0, 1), (1, 0)])
+
     place = near
 
     def beside(x, *trades):
         nonlocal place
-        sent = [
-            lax.ppermute(chunk(kind, place ^ m), "near", [(i, i ^ m) for i in range(4)]) for kind, m in trades
-        ]
-        x, place, *sent = lax.optimization_barrier((x, place, *sent))
-        for (kind, m), w in zip(trades, sent):
-            weights[kind][m] = w
-        return x
+        x, place, *sent = lax.optimization_barrier((x, place, *[t(place) for t in trades]))
+        return x, *sent
 
     each = rows * group
     q_all = jnp.broadcast_to(queries.reshape(1, each, head), (n_ctx, each, head))
     q_all = lax.all_to_all(q_all, ctx, 0, 0, tiled=True)
-    q_all = beside(q_all, (0, 1), (0, 2))
+    q_all, gate_1, gate_2 = beside(q_all, trade(gate_weight, 1), trade(gate_weight, 2))
     vmem = pl.BlockSpec(memory_space=pltpu.VMEM)
     smem = pl.BlockSpec(memory_space=pltpu.SMEM)
     anywhere = pl.BlockSpec(memory_space=pl.ANY)
@@ -244,12 +256,14 @@
     partial = pl.pallas_call(
         functools.partial(attend_kernel, tokens=tokens, group=group, head=head, scale=1.0 / math.sqrt(head)),
         out_shape=jax.ShapeDtypeStruct((n_ctx, each + 8, head), BF16),
-        in_specs=[smem, vmem, anywhere, anywhere, vmem, vmem],
+        in_specs=[smem, vmem] + [anywhere] * 4,
         out_specs=vmem,
         scratch_shapes=[
             pltpu.VMEM((stretch, head), BF16),
             pltpu.VMEM((stretch, head), BF16),
-            pltpu.SemaphoreType.DMA((2,)),
+            pltpu.VMEM(seg_keys.shape, BF16),
+            pltpu.VMEM(seg_values.shape, BF16),
+            pltpu.SemaphoreType.DMA((4,)),
         ],
         compiler_params=params,
         cost_estimate=pl.CostEstimate(
@@ -258,7 +272,7 @@
         name="attend",
     )(lengths, q_all, cache_keys[0], cache_values[0], seg_keys, seg_values)
     parts = lax.all_to_all(partial, ctx, 0, 0, tiled=True)
-    parts = beside(parts, (1, 1), (1, 2))
+    parts, up_1, up_2 = beside(parts, trade(up_weight, 1), trade(up_weight, 2))
     attention, copies = pl.pallas_call(
         merge_kernel,
         out_shape=(jax.ShapeDtypeStruct((each, head), BF16), jax.ShapeDtypeStruct((n_ctx, each, head), BF16)),
@@ -269,7 +283,7 @@
     )(parts)
     attention = attention.reshape(rows, width)
     heads_all = lax.all_to_all(copies, ctx, 0, 0, tiled=True)
-    heads_all = beside(heads_all, (0, 3), (1, 3))
+    heads_all, gate_3 = beside(heads_all, trade(gate_weight, 3))
     mixed = pl.pallas_call(
         out_kernel,
         out_shape=jax.ShapeDtypeStruct((n_tp, trows, feats), BF16),
@@ -291,7 +305,8 @@
         compiler_params=small,
         name="stream",
     )(mixed, residual_stream)
-    stream = lax.all_to_all(stream, ("near", "tp"), 0, 0, tiled=True)
+    stream = lax.all_to_all(stream, (*near_axes, "tp"), 0, 0, tiled=True)
+    stream, up_3 = beside(stream, trade(up_weight, 3))
 
     half = -(-(units + 3) // 128) * 128
     block = tokens // n_far
@@ -302,8 +317,8 @@
         out_specs=vmem,
         compiler_params=small,
         name="project",
-    )(stream, *weights[0], *weights[1])
-    sums = beside(lax.all_to_all(sums, "far", 0, 0, tiled=True), (2, 1), (2, 2))
+    )(stream, chunk(gate_weight, near), gate_1, gate_2, gate_3, chunk(up_weight, near), up_1, up_2, up_3)
+    sums, down_y = beside(lax.all_to_all(sums, "far", 0, 0, tiled=True), down_trade)
     hidden = pl.pallas_call(
         hidden_kernel,
         out_shape=jax.ShapeDtypeStruct((n_far, block, units), BF16),
@@ -312,16 +327,17 @@
         compiler_params=small,
         name="hidden",
     )(sums)
-    hidden = beside(lax.all_to_all(hidden, "far", 0, 0, tiled=True), (2, 3)).reshape(tokens, units)
+    hidden = lax.all_to_all(hidden, "far", 0, 0, tiled=True).reshape(tokens, units)
+    other = lax.ppermute(hidden, "lo", [(0, 1), (1, 0)])
     lowered = pl.pallas_call(
         down_kernel,
-        out_shape=jax.ShapeDtypeStruct((n_near * n_tp, trows, feats), BF16),
-        in_specs=[vmem] * 5,
+        out_shape=jax.ShapeDtypeStruct((2 * n_tp, trows, feats), BF16),
+        in_specs=[vmem] * 4,
         out_specs=vmem,
         compiler_params=small,
         name="down",
-    )(hidden, *weights[2])
-    lowered = lax.all_to_all(lowered, ("near", "tp"), 0, 0, tiled=True)
+    )(hidden, other, down_chunk(near), down_y)
+    lowered = lax.all_to_all(lowered, ("hi", "tp"), 0, 0, tiled=True)
     layer_out = pl.pallas_call(
         last_kernel,
         out_shape=jax.ShapeDtypeStruct((trows, feats), BF16),
@@ -334,8 +350,8 @@
 
 
 def solution(mesh):
-    fine = jax.sharding.Mesh(mesh.devices.reshape(-1, 4, mesh.shape["tp"]), ("far", "near", "tp"))
-    ctx = ("far", "near")
+    fine = jax.sharding.Mesh(mesh.devices.reshape(-1, 2, 2, mesh.shape["tp"]), ("far", "lo", "hi", "tp"))
+    ctx = ("far", "lo", "hi")
     return jax.shard_map(
         per_device,
         mesh=fine,

time: 229 us -> 226 us (0.987)
  waiting for transfers between devices: 77.3 us -> 66.6 us
  blocking collectives: 28.3 us -> 38.8 us
    all_to_all x1, blocking collectives: 16.7 us -> 25.2 us  [per_device(): lax.all_to_all(hidden, 'far', 0, 0, tiled=True).reshape(tokens, units)]
    ppermute x9 -> x8, waiting for transfers between devices: 60.2 us -> 52 us  [the longest x6 36.8 us: trade(): lax.ppermute(chunk(w, place ^ m), near_axes, [(i, i ^ m) for i in range(4)])]
    all_to_all x3, starting transfers between devices: 27.1 us -> 21.6 us  [the longest x1 8.43 us: per_device(): lowered = lax.all_to_all(lowered, ('hi', 'tp'), 0, 0, tiled=True)]
    ppermute x9 -> x8, starting transfers between devices: 32.5 us -> 34.8 us  [the longest x6 26.9 us: trade(): lax.ppermute(chunk(w, place ^ m), near_axes, [(i, i ^ m) for i in range(4)])]
  transfers between devices with their start and end apart: 15 -> 14, of which waited for: 13 -> 12; matrix products, arithmetic and copies ran while one was open for 2% -> 2% of each run, Pallas kernels for 0% -> 0%
where the time goes in v7:
time: 226 us; the launch traced here: 225 us
  starting transfers between devices  101 us (45%)
  waiting for transfers between devices  66.6 us (29%)
  blocking collectives  38.8 us (17%)
  Pallas kernels  10.9 us (5%)
  local copies, waits for them, and re-layouts  3.65 us (2%)
  other arithmetic  2.86 us (1%)
    ppermute x6, waiting for transfers between devices, trade(): lax.ppermute(chunk(w, place ^ m), near_axes, [(i, i ^ m) for i in range(4)])  36.8 us
    ppermute x6, starting transfers between devices, trade(): lax.ppermute(chunk(w, place ^ m), near_axes, [(i, i ^ m) for i in range(4)])  26.9 us
    all_to_all x1, blocking collectives, per_device(): lax.all_to_all(hidden, 'far', 0, 0, tiled=True).reshape(tokens, units)  25.2 us
    all_to_all x1, starting transfers between devices, per_device(): q_all = lax.all_to_all(q_all, ctx, 0, 0, tiled=True)  18.7 us
    all_to_all x1, starting transfers between devices, per_device(): parts = lax.all_to_all(partial, ctx, 0, 0, tiled=True)  13.7 us
    all_to_all x1, blocking collectives, per_device(): mixed = lax.all_to_all(mixed, 'tp', 0, 0, tiled=True)  13.6 us
    ppermute x1, waiting for transfers between devices, down_trade(): return lax.ppermute(down_chunk(place ^ 1), 'hi', [(0, 1), (1, 0)])  12.3 us
    all_to_all x1, starting transfers between devices, per_device(): heads_all = lax.all_to_all(copies, ctx, 0, 0, tiled=True)  11.8 us
  transfers between devices with their start and end apart: 14, of which 12 were waited for; matrix products, arithmetic and copies ran while one was open for 2% of the time, Pallas kernels for 0%

profile of v7, /device:TPU:1, one launch (start us, length us, event | category | flops | bytes accessed | tf_op | source)
XLA Modules:
  0.0 224.8 jit_solution(10645230406009826963)
XLA Ops:
  0.6 0.7 broadcast_in_dim.4
  1.3 0.7 broadcast_in_dim.5
  2.1 18.7 %all-to-all-start = ((bf16[32,24,128]{2,1,0:T(8,128)(2,1)}), bf16[32,24,128]{2,1,0:T(8,128)(2,1)S(1)}, u32[]{:S(2)}, u32[]{:S(2)}) async-start(bf16[32,24,128]{2,1,0:T(8,128)(2,1)} %broadcast_in_dim.5), calls=%async_computation | async-start | bytes 393216 | tf_op jit(solution)/shard_map/all_to_all | solution.py:249
  20.7 0.0 copy-start.5
  20.8 0.7 copy-done.5
  21.4 1.4 fusion.6
  22.8 4.6 %collective-permute-start = (bf16[462,256]{1,0:T(8,128)(2,1)S(1)}, bf16[462,256]{1,0:T(8,128)(2,1)S(1)}, u32[]{:S(2)}, u32[]{:S(2)}) collective-permute-start(bf16[462,256]{1,0:T(8,128)(2,1)S(1)} %get-tuple-element.47), channel_id=1, source_target_pairs={{0,16},{16,0},{32,48},{48,32},{1,17},{17,1},{33,49},{49,33},{2,18}... | collective-permute-start | bytes 709640 | tf_op jit(solution)/shard_map/ppermute | solution.py:229
  27.5 3.1 %collective-permute-start.1 = (bf16[462,256]{1,0:T(8,128)(2,1)S(1)}, bf16[462,256]{1,0:T(8,128)(2,1)S(1)}, u32[]{:S(2)}, u32[]{:S(2)}) collective-permute-start(bf16[462,256]{1,0:T(8,128)(2,1)S(1)} %get-tuple-element.46), channel_id=1, source_target_pairs={{0,32},{16,48},{32,0},{48,16},{1,33},{17,49},{33,1},{49,17},{2,34}... | collective-permute-start | bytes 709640 | tf_op jit(solution)/shard_map/ppermute | solution.py:229
  31.2 2.5 %collective-permute-done.refs_1_ = bf16[462,256]{1,0:T(8,128)(2,1)S(1)} collective-permute-done((bf16[462,256]{1,0:T(8,128)(2,1)S(1)}, bf16[462,256]{1,0:T(8,128)(2,1)S(1)}, u32[]{:S(2)}, u32[]{:S(2)}) %collective-permute-start) | collective-permute-done | bytes 236576 | tf_op jit(solution)/shard_map/ppermute | solution.py:229
  33.7 3.2 %collective-permute-done.1.refs_2_ = bf16[462,256]{1,0:T(8,128)(2,1)S(1)} collective-permute-done((bf16[462,256]{1,0:T(8,128)(2,1)S(1)}, bf16[462,256]{1,0:T(8,128)(2,1)S(1)}, u32[]{:S(2)}, u32[]{:S(2)}) %collective-permute-start.1) | collective-permute-done | bytes 236576 | tf_op jit(solution)/shard_map/ppermute | solution.py:229
  36.9 1.0 all-to-all-done.q_ref
  37.9 0.7 copy-done.4
  38.6 5.2 %attend.1 = bf16[32,32,128]{2,1,0:T(8,128)(2,1)} custom-call(s32[1]{0:T(128)S(6)} %copy.14.lengths, bf16[32,24,128]{2,1,0:T(8,128)(2,1)} %copy-done.4, bf16[3072,128]{1,0:T(8,128)(2,1)} %bitcast.29, bf16[3072,128]{1,0:T(8,128)(2,1)} %bitcast.30, bf16[6,128]{1,0:T(8,128)(2,1)} %sk_hbm.1, bf16[6,128]{1,0:T(8,128)(2,1)} %sv_hbm.1), custom_call_target="tpu_custom_call" | custom-call | flops 1207959552 | bytes 2097152 | tf_op jit(solution)/shard_map/attend/pallas_call | solution.py:256
  43.8 13.7 %all-to-all-start.1 = ((bf16[32,32,128]{2,1,0:T(8,128)(2,1)}), bf16[32,32,128]{2,1,0:T(8,128)(2,1)S(1)}, u32[]{:S(2)}, u32[]{:S(2)}) async-start(bf16[32,32,128]{2,1,0:T(8,128)(2,1)} %attend.1), calls=%async_computation.1 | async-start | bytes 524288 | tf_op jit(solution)/shard_map/all_to_all | solution.py:274
  57.5 0.2 fusion.7
  57.8 4.6 %collective-permute-start.2 = (bf16[462,256]{1,0:T(8,128)(2,1)S(1)}, bf16[462,256]{1,0:T(8,128)(2,1)S(1)}, u32[]{:S(2)}, u32[]{:S(2)}) collective-permute-start(bf16[462,256]{1,0:T(8,128)(2,1)S(1)} %get-tuple-element.44), channel_id=1, source_target_pairs={{0,16},{16,0},{32,48},{48,32},{1,17},{17,1},{33,49},{49,33},{2,18}... | collective-permute-start | bytes 709640 | tf_op jit(solution)/shard_map/ppermute | solution.py:229
  62.4 3.1 %collective-permute-start.3 = (bf16[462,256]{1,0:T(8,128)(2,1)S(1)}, bf16[462,256]{1,0:T(8,128)(2,1)S(1)}, u32[]{:S(2)}, u32[]{:S(2)}) collective-permute-start(bf16[462,256]{1,0:T(8,128)(2,1)S(1)} %get-tuple-element.43), channel_id=1, source_target_pairs={{0,32},{16,48},{32,0},{48,16},{1,33},{17,49},{33,1},{49,17},{2,34}... | collective-permute-start | bytes 709640 | tf_op jit(solution)/shard_map/ppermute | solution.py:229
  65.5 2.2 collective-permute-done.2.refs_5_
  67.8 7.9 %collective-permute-done.3.refs_6_ = bf16[462,256]{1,0:T(8,128)(2,1)S(1)} collective-permute-done((bf16[462,256]{1,0:T(8,128)(2,1)S(1)}, bf16[462,256]{1,0:T(8,128)(2,1)S(1)}, u32[]{:S(2)}, u32[]{:S(2)}) %collective-permute-start.3) | collective-permute-done | bytes 236576 | tf_op jit(solution)/shard_map/ppermute | solution.py:229
  75.7 1.5 all-to-all-done.1.in_ref
  77.1 1.1 merge.1
  78.3 11.8 %all-to-all-start.2 = ((bf16[32,24,128]{2,1,0:T(8,128)(2,1)}), bf16[32,24,128]{2,1,0:T(8,128)(2,1)S(1)}, u32[]{:S(2)}, u32[]{:S(2)}) async-start(bf16[32,24,128]{2,1,0:T(8,128)(2,1)} %get-tuple-element.26), calls=%async_computation.2 | async-start | bytes 393216 | tf_op jit(solution)/shard_map/all_to_all | solution.py:285
  90.0 0.0 copy-start
  90.0 1.1 fusion.4
  91.1 5.5 %collective-permute-start.4 = (bf16[462,256]{1,0:T(8,128)(2,1)S(1)}, bf16[462,256]{1,0:T(8,128)(2,1)S(1)}, u32[]{:S(2)}, u32[]{:S(2)}) collective-permute-start(bf16[462,256]{1,0:T(8,128)(2,1)S(1)} %fusion.4), channel_id=1, source_target_pairs={{0,48},{16,32},{32,16},{48,0},{1,49},{17,33},{33,17},{49,1},{2,50}... | collective-permute-start | bytes 709640 | tf_op jit(solution)/shard_map/ppermute | solution.py:229
  96.7 11.1 %collective-permute-done.4.refs_3_ = bf16[462,256]{1,0:T(8,128)(2,1)S(1)} collective-permute-done((bf16[462,256]{1,0:T(8,128)(2,1)S(1)}, bf16[462,256]{1,0:T(8,128)(2,1)S(1)}, u32[]{:S(2)}, u32[]{:S(2)}) %collective-permute-start.4) | collective-permute-done | bytes 236576 | tf_op jit(solution)/shard_map/ppermute | solution.py:229
  107.8 0.3 out.1
  108.0 13.6 %all_to_all.40.in_ref = bf16[16,12,256]{2,1,0:T(8,128)(2,1)S(1)} all-to-all(bf16[16,12,256]{2,1,0:T(8,128)(2,1)S(1)} %out.1), channel_id=1, replica_groups=mesh['far'=8,'lo'=2,'hi'=2,'tp'=16] {'tp'}, dimensions={0} | all-to-all | bytes 196608 | tf_op jit(solution)/shard_map/all_to_all | solution.py:296
  121.6 0.9 stream.1
  122.5 6.2 %all-to-all-start.4 = ((bf16[64,12,256]{2,1,0:T(8,128)(2,1)}), bf16[64,12,256]{2,1,0:T(8,128)(2,1)S(1)}, u32[]{:S(2)}, u32[]{:S(2)}) async-start(bf16[64,12,256]{2,1,0:T(8,128)(2,1)} %get-tuple-element.29), calls=%async_computation.4 | async-start | bytes 1048576 | tf_op jit(solution)/shard_map/all_to_all | solution.py:308
  128.7 0.1 fusion.5
  128.8 5.9 %collective-permute-start.5 = (bf16[462,256]{1,0:T(8,128)(2,1)S(1)}, bf16[462,256]{1,0:T(8,128)(2,1)S(1)}, u32[]{:S(2)}, u32[]{:S(2)}) collective-permute-start(bf16[462,256]{1,0:T(8,128)(2,1)S(1)} %fusion.5), channel_id=1, source_target_pairs={{0,48},{16,32},{32,16},{48,0},{1,49},{17,33},{33,17},{49,1},{2,50}... | collective-permute-start | bytes 709640 | tf_op jit(solution)/shard_map/ppermute | solution.py:229
  134.7 9.8 %collective-permute-done.5.refs_7_ = bf16[462,256]{1,0:T(8,128)(2,1)S(1)} collective-permute-done((bf16[462,256]{1,0:T(8,128)(2,1)S(1)}, bf16[462,256]{1,0:T(8,128)(2,1)S(1)}, u32[]{:S(2)}, u32[]{:S(2)}) %collective-permute-start.5) | collective-permute-done | bytes 236576 | tf_op jit(solution)/shard_map/ppermute | solution.py:229
  144.6 1.5 project.1
  146.0 6.9 %all-to-all-start.5 = ((bf16[8,24,1024]{2,1,0:T(8,128)(2,1)}), bf16[8,24,1024]{2,1,0:T(8,128)(2,1)S(1)}, u32[]{:S(2)}, u32[]{:S(2)}) async-start(bf16[8,24,1024]{2,1,0:T(8,128)(2,1)} %project.1), calls=%async_computation.5 | async-start | bytes 786432 | tf_op jit(solution)/shard_map/all_to_all | solution.py:321
  153.0 0.2 dynamic-slice_bitcast_fusion.1
  153.3 2.2 collective-permute-start.6
  155.5 12.3 %collective-permute-done.6.wy_ref = bf16[2,462,256]{2,1,0:T(8,128)(2,1)S(1)} collective-permute-done((bf16[2,462,256]{2,1,0:T(8,128)(2,1)S(1)}, bf16[2,462,256]{2,1,0:T(8,128)(2,1)S(1)}, u32[]{:S(2)}, u32[]{:S(2)}) %collective-permute-start.6) | collective-permute-done | bytes 473120 | tf_op jit(solution)/shard_map/ppermute | solution.py:238
  167.8 3.9 %all-to-all-done.5.in_ref = bf16[8,24,1024]{2,1,0:T(8,128)(2,1)S(1)} async-done(((bf16[8,24,1024]{2,1,0:T(8,128)(2,1)}), bf16[8,24,1024]{2,1,0:T(8,128)(2,1)S(1)}, u32[]{:S(2)}, u32[]{:S(2)}) %all-to-all-start.5) | async-done | bytes 393248 | tf_op jit(solution)/shard_map/all_to_all | solution.py:321
  171.7 0.2 hidden.1
  171.9 25.2 %all_to_all.41 = bf16[8,24,462]{2,1,0:T(8,128)(2,1)S(1)} all-to-all(bf16[8,24,462]{2,1,0:T(8,128)(2,1)S(1)} %hidden.1), channel_id=1, replica_groups=mesh['far'=8,'lo'=2,'hi'=2,'tp'=16] {'far'}, dimensions={0} | all-to-all | bytes 354816 | tf_op jit(solution)/shard_map/all_to_all | solution.py:330
  197.1 5.7 %collective-permute-start.7 = (bf16[192,462]{1,0:T(8,128)(2,1)S(1)}, bf16[192,462]{1,0:T(8,128)(2,1)S(1)}, u32[]{:S(2)}, u32[]{:S(2)}) collective-permute-start(bf16[192,462]{1,0:T(8,128)(2,1)S(1)} %bitcast.27), channel_id=1, source_target_pairs={{0,32},{32,0},{1,33},{33,1},{2,34},{34,2},{3,35},{35,3},{4,36},{36... | collective-permute-start | bytes 532232 | tf_op jit(solution)/shard_map/ppermute | solution.py:331
  202.8 3.0 %collective-permute-done.7.other_ref = bf16[192,462]{1,0:T(8,128)(2,1)S(1)} collective-permute-done((bf16[192,462]{1,0:T(8,128)(2,1)S(1)}, bf16[192,462]{1,0:T(8,128)(2,1)S(1)}, u32[]{:S(2)}, u32[]{:S(2)}) %collective-permute-start.7) | collective-permute-done | bytes 177440 | tf_op jit(solution)/shard_map/ppermute | solution.py:331
  205.8 1.1 down.1
  206.9 8.4 %all-to-all-start.7 = ((bf16[32,12,256]{2,1,0:T(8,128)(2,1)}), bf16[32,12,256]{2,1,0:T(8,128)(2,1)S(1)}, u32[]{:S(2)}, u32[]{:S(2)}) async-start(bf16[32,12,256]{2,1,0:T(8,128)(2,1)} %down.1), calls=%async_computation.7 | async-start | bytes 524288 | tf_op jit(solution)/shard_map/all_to_all | solution.py:340
  215.3 0.6 reshape.13
  216.0 8.2 %all-to-all-done.7.in_ref = bf16[32,12,256]{2,1,0:T(8,128)(2,1)S(1)} async-done(((bf16[32,12,256]{2,1,0:T(8,128)(2,1)}), bf16[32,12,256]{2,1,0:T(8,128)(2,1)S(1)}, u32[]{:S(2)}, u32[]{:S(2)}) %all-to-all-start.7) | async-done | bytes 196640 | tf_op jit(solution)/shard_map/all_to_all | solution.py:340
  224.2 0.7 last.1
  (12 shorter events, 0.1 us)
Async XLA Ops:
  2.1 35.8 %all-to-all-start = ((bf16[32,24,128]{2,1,0:T(8,128)(2,1)}), bf16[32,24,128]{2,1,0:T(8,128)(2,1)S(1)}, u32[]{:S(2)}, u32[]{:S(2)}) async-start(bf16[32,24,128]{2,1,0:T(8,128)(2,1)} %broadcast_in_dim.5), calls=%async_computation | async-start | bytes 393216 | tf_op jit(solution)/shard_map/all_to_all | solution.py:249
  20.7 0.7 copy-start.5
  22.8 10.9 %collective-permute-start = (bf16[462,256]{1,0:T(8,128)(2,1)S(1)}, bf16[462,256]{1,0:T(8,128)(2,1)S(1)}, u32[]{:S(2)}, u32[]{:S(2)}) collective-permute-start(bf16[462,256]{1,0:T(8,128)(2,1)S(1)} %get-tuple-element.47), channel_id=1, source_target_pairs={{0,16},{16,0},{32,48},{48,32},{1,17},{17,1},{33,49},{49,33},{2,18}... | collective-permute-start | bytes 709640 | tf_op jit(solution)/shard_map/ppermute | solution.py:229
  27.5 9.5 %collective-permute-start.1 = (bf16[462,256]{1,0:T(8,128)(2,1)S(1)}, bf16[462,256]{1,0:T(8,128)(2,1)S(1)}, u32[]{:S(2)}, u32[]{:S(2)}) collective-permute-start(bf16[462,256]{1,0:T(8,128)(2,1)S(1)} %get-tuple-element.46), channel_id=1, source_target_pairs={{0,32},{16,48},{32,0},{48,16},{1,33},{17,49},{33,1},{49,17},{2,34}... | collective-permute-start | bytes 709640 | tf_op jit(solution)/shard_map/ppermute | solution.py:229
  37.9 0.7 copy-start.4
  38.6 19.0 %copy-start.3 = (bf16[256,1848]{0,1:T(8,128)(2,1)S(1)}, bf16[256,1848]{0,1:T(8,128)(2,1)}, u32[]{:S(2)}) copy-start(bf16[256,1848]{0,1:T(8,128)(2,1)} %param.22) | copy-start | bytes 2838532
  43.8 33.4 %all-to-all-start.1 = ((bf16[32,32,128]{2,1,0:T(8,128)(2,1)}), bf16[32,32,128]{2,1,0:T(8,128)(2,1)S(1)}, u32[]{:S(2)}, u32[]{:S(2)}) async-start(bf16[32,32,128]{2,1,0:T(8,128)(2,1)} %attend.1), calls=%async_computation.1 | async-start | bytes 524288 | tf_op jit(solution)/shard_map/all_to_all | solution.py:274
  57.8 10.0 %collective-permute-start.2 = (bf16[462,256]{1,0:T(8,128)(2,1)S(1)}, bf16[462,256]{1,0:T(8,128)(2,1)S(1)}, u32[]{:S(2)}, u32[]{:S(2)}) collective-permute-start(bf16[462,256]{1,0:T(8,128)(2,1)S(1)} %get-tuple-element.44), channel_id=1, source_target_pairs={{0,16},{16,0},{32,48},{48,32},{1,17},{17,1},{33,49},{49,33},{2,18}... | collective-permute-start | bytes 709640 | tf_op jit(solution)/shard_map/ppermute | solution.py:229
  62.4 13.3 %collective-permute-start.3 = (bf16[462,256]{1,0:T(8,128)(2,1)S(1)}, bf16[462,256]{1,0:T(8,128)(2,1)S(1)}, u32[]{:S(2)}, u32[]{:S(2)}) collective-permute-start(bf16[462,256]{1,0:T(8,128)(2,1)S(1)} %get-tuple-element.43), channel_id=1, source_target_pairs={{0,32},{16,48},{32,0},{48,16},{1,33},{17,49},{33,1},{49,17},{2,34}... | collective-permute-start | bytes 709640 | tf_op jit(solution)/shard_map/ppermute | solution.py:229
  78.3 29.5 %all-to-all-start.2 = ((bf16[32,24,128]{2,1,0:T(8,128)(2,1)}), bf16[32,24,128]{2,1,0:T(8,128)(2,1)S(1)}, u32[]{:S(2)}, u32[]{:S(2)}) async-start(bf16[32,24,128]{2,1,0:T(8,128)(2,1)} %get-tuple-element.26), calls=%async_computation.2 | async-start | bytes 393216 | tf_op jit(solution)/shard_map/all_to_all | solution.py:285
  90.0 17.7 %copy-start = (bf16[512,256]{1,0:T(8,128)(2,1)S(1)}, bf16[512,256]{1,0:T(8,128)(2,1)}, u32[]{:S(2)}) copy-start(bf16[512,256]{1,0:T(8,128)(2,1)} %w_ref.1) | copy-start | bytes 786436
  91.1 16.6 %collective-permute-start.4 = (bf16[462,256]{1,0:T(8,128)(2,1)S(1)}, bf16[462,256]{1,0:T(8,128)(2,1)S(1)}, u32[]{:S(2)}, u32[]{:S(2)}) collective-permute-start(bf16[462,256]{1,0:T(8,128)(2,1)S(1)} %fusion.4), channel_id=1, source_target_pairs={{0,48},{16,32},{32,16},{48,0},{1,49},{17,33},{33,17},{49,1},{2,50}... | collective-permute-start | bytes 709640 | tf_op jit(solution)/shard_map/ppermute | solution.py:229
  108.0 13.6 %copy-start.1 = (bf16[12,256]{1,0:T(8,128)(2,1)S(1)}, bf16[12,256]{1,0:T(8,128)(2,1)}, u32[]{:S(2)}) copy-start(bf16[12,256]{1,0:T(8,128)(2,1)} %residual_ref.1) | copy-start | bytes 18436
  122.5 22.1 %all-to-all-start.4 = ((bf16[64,12,256]{2,1,0:T(8,128)(2,1)}), bf16[64,12,256]{2,1,0:T(8,128)(2,1)S(1)}, u32[]{:S(2)}, u32[]{:S(2)}) async-start(bf16[64,12,256]{2,1,0:T(8,128)(2,1)} %get-tuple-element.29), calls=%async_computation.4 | async-start | bytes 1048576 | tf_op jit(solution)/shard_map/all_to_all | solution.py:308
  128.8 15.7 %collective-permute-start.5 = (bf16[462,256]{1,0:T(8,128)(2,1)S(1)}, bf16[462,256]{1,0:T(8,128)(2,1)S(1)}, u32[]{:S(2)}, u32[]{:S(2)}) collective-permute-start(bf16[462,256]{1,0:T(8,128)(2,1)S(1)} %fusion.5), channel_id=1, source_target_pairs={{0,48},{16,32},{32,16},{48,0},{1,49},{17,33},{33,17},{49,1},{2,50}... | collective-permute-start | bytes 709640 | tf_op jit(solution)/shard_map/ppermute | solution.py:229
  144.6 8.4 %copy-start.2 = (bf16[1848,256]{1,0:T(8,128)(2,1)S(1)}, bf16[1848,256]{1,0:T(8,128)(2,1)}, u32[]{:S(2)}) copy-start(bf16[1848,256]{1,0:T(8,128)(2,1)} %param.23) | copy-start | bytes 2838532
  146.0 25.6 %all-to-all-start.5 = ((bf16[8,24,1024]{2,1,0:T(8,128)(2,1)}), bf16[8,24,1024]{2,1,0:T(8,128)(2,1)S(1)}, u32[]{:S(2)}, u32[]{:S(2)}) async-start(bf16[8,24,1024]{2,1,0:T(8,128)(2,1)} %project.1), calls=%async_computation.5 | async-start | bytes 786432 | tf_op jit(solution)/shard_map/all_to_all | solution.py:321
  153.3 14.5 %collective-permute-start.6 = (bf16[2,462,256]{2,1,0:T(8,128)(2,1)S(1)}, bf16[2,462,256]{2,1,0:T(8,128)(2,1)S(1)}, u32[]{:S(2)}, u32[]{:S(2)}) collective-permute-start(bf16[2,462,256]{2,1,0:T(8,128)(2,1)S(1)} %pad_maximum_fusion), channel_id=1, source_target_pairs={{0,16},{16,0},{1,17},{17,1},{2,18},{18,2},{3,19},{19,3},{4,20},{20... | collective-permute-start | bytes 1419272 | tf_op jit(solution)/shard_map/ppermute | solution.py:238
  197.1 8.8 %collective-permute-start.7 = (bf16[192,462]{1,0:T(8,128)(2,1)S(1)}, bf16[192,462]{1,0:T(8,128)(2,1)S(1)}, u32[]{:S(2)}, u32[]{:S(2)}) collective-permute-start(bf16[192,462]{1,0:T(8,128)(2,1)S(1)} %bitcast.27), channel_id=1, source_target_pairs={{0,32},{32,0},{1,33},{33,1},{2,34},{34,2},{3,35},{35,3},{4,36},{36... | collective-permute-start | bytes 532232 | tf_op jit(solution)/shard_map/ppermute | solution.py:331
  206.9 17.3 %all-to-all-start.7 = ((bf16[32,12,256]{2,1,0:T(8,128)(2,1)}), bf16[32,12,256]{2,1,0:T(8,128)(2,1)S(1)}, u32[]{:S(2)}, u32[]{:S(2)}) async-start(bf16[32,12,256]{2,1,0:T(8,128)(2,1)} %down.1), calls=%async_computation.7 | async-start | bytes 524288 | tf_op jit(solution)/shard_map/all_to_all | solution.py:340

commit v8 on v7

--- a/solution.py
+++ b/solution.py
@@ -135,39 +135,44 @@
     out_ref[...] = (own_ref[...].astype(F32) + jnp.sum(in_ref[...].astype(F32), axis=0)).astype(BF16)
 
 
-def project_kernel(x_ref, *refs):
-    out_ref = refs[-1]
-    gates, ups = refs[: len(refs) // 2], refs[len(refs) // 2 : -1]
-    units = gates[0].shape[0]
-    slices = len(gates)
-    each = x_ref.shape[0] // slices
-    blocks, rows, width = out_ref.shape
-    half = width // 2
-    near = lax.axis_index(("lo", "hi"))
-    xs = []
-    for m in range(slices):
-        at = (near ^ m) * each
-        xs.append(jnp.concatenate([x_ref[at + i].astype(F32) for i in range(each)], axis=0))
-
-    def product(w_refs):
-        y = 0.0
-        for x, w_ref in zip(xs, w_refs):
-            y = y + lax.dot_general(
-                x.astype(BF16), w_ref[...], (((1,), (1,)), ((), ())), preferred_element_type=F32
-            )
-        return y
-
-    squares = 0.0
-    for x in xs:
-        squares = squares + jnp.sum(x * x, axis=1, keepdims=True)
+def project_kernel(x_ref, gate_ref, gate_y_ref, up_ref, up_y_ref, send_ref, keep_ref):
+    units = gate_ref.shape[1]
+    each = x_ref.shape[0] // 2
+    half = keep_ref.shape[1] // 2
+    lo, hi = lax.axis_index("lo"), lax.axis_index("hi")
+    own, other = (
+        jnp.concatenate([x_ref[at * each + i].astype(F32) for i in range(each)], axis=0) for at in (hi, 1 - hi)
+    )
+    squares = jnp.sum(own * own, axis=1, keepdims=True) + jnp.sum(other * other, axis=1, keepdims=True)
+    parts = three_parts(squares)
+    own, other = own.astype(BF16), other.astype(BF16)
+
+    def product(w_ref, w_y_ref, at):
+        y = lax.dot_general(own, w_ref[at], (((1,), (1,)), ((), ())), preferred_element_type=F32)
+        return y + lax.dot_general(other, w_y_ref[at], (((1,), (1,)), ((), ())), preferred_element_type=F32)
+
     tokens = squares.shape[0]
-    spare = jnp.zeros((tokens, half - units - 3), F32)
-    gate = jnp.concatenate([product(gates), *three_parts(squares), spare], axis=1).astype(BF16)
-    up = product(ups).astype(BF16)
-    for i in range(blocks):
-        out_ref[i, :, :half] = gate[i * rows : (i + 1) * rows]
-        out_ref[i, :, half : half + units] = up[i * rows : (i + 1) * rows]
-        out_ref[i, :, half + units :] = jnp.zeros((rows, half - units), BF16)
+    spare = half - units
+    for at, ref in ((1 - lo, send_ref), (lo, keep_ref)):
+        gate = product(gate_ref, gate_y_ref, at)
+        up = product(up_ref, up_y_ref, at)
+        ref[:, :half] = jnp.concatenate([gate, *parts, jnp.zeros((tokens, spare - 3), F32)], axis=1).astype(ref.dtype)
+        ref[:, half:] = jnp.concatenate([up, jnp.zeros((tokens, spare), F32)], axis=1).astype(ref.dtype)
+
+
+def join_kernel(keep_ref, got_ref, out_ref, *, units):
+    total = keep_ref[...] + got_ref[...].astype(F32)
+    cut = units // 128 * 128
+    at = units - cut
+    tail = total[:, cut : cut + 128]
+    one, two, three = three_parts(jnp.sum(tail[:, at : at + 3], axis=1, keepdims=True))
+    column = lax.broadcasted_iota(jnp.int32, tail.shape, 1) - at
+    tail = jnp.where(column == 0, one, jnp.where(column == 1, two, jnp.where(column == 2, three, tail)))
+    blocks, rows, _ = out_ref.shape
+    for i in range(blocks):
+        mine = slice(i * rows, (i + 1) * rows)
+        out_ref[i] = total[mine].astype(BF16)
+        out_ref[i, :, cut : cut + 128] = tail[mine].astype(BF16)
 
 
 def hidden_kernel(in_ref, out_ref):
@@ -222,20 +227,19 @@
     near = lax.axis_index(near_axes)
 
     def chunk(w, place):
-        w = lax.dynamic_slice_in_dim(w.T, place * units, units, 0)
-        return (w.astype(F32) * norm_gain).astype(BF16)
-
-    def trade(w, m):
-        return lambda place: lax.ppermute(chunk(w, place ^ m), near_axes, [(i, i ^ m) for i in range(4)])
+        lows = [lax.dynamic_slice_in_dim(w, (2 * lo + (place & 1)) * units, units, 0) for lo in range(2)]
+        return jnp.stack(lows)
+
+    def scaled(w):
+        return lambda place: (chunk(w.T, place).astype(F32) * norm_gain).astype(BF16)
+
+    gate_chunk, up_chunk = scaled(gate_weight), scaled(up_weight)
 
     def down_chunk(place):
-        lows = [
-            lax.dynamic_slice_in_dim(down_weight, (2 * lo + (place & 1)) * units, units, 0) for lo in range(2)
-        ]
-        return jnp.stack(lows)
-
-    def down_trade(place):
-        return lax.ppermute(down_chunk(place ^ 1), "hi", [(0, 1), (1, 0)])
+        return chunk(down_weight, place)
+
+    def trade(part):
+        return lambda place: lax.ppermute(part(place ^ 1), "hi", [(0, 1), (1, 0)])
 
     place = near
 
@@ -247,7 +251,7 @@
     each = rows * group
     q_all = jnp.broadcast_to(queries.reshape(1, each, head), (n_ctx, each, head))
     q_all = lax.all_to_all(q_all, ctx, 0, 0, tiled=True)
-    q_all, gate_1, gate_2 = beside(q_all, trade(gate_weight, 1), trade(gate_weight, 2))
+    q_all, gate_y = beside(q_all, trade(gate_chunk))
     vmem = pl.BlockSpec(memory_space=pltpu.VMEM)
     smem = pl.BlockSpec(memory_space=pltpu.SMEM)
     anywhere = pl.BlockSpec(memory_space=pl.ANY)
@@ -272,7 +276,7 @@
         name="attend",
     )(lengths, q_all, cache_keys[0], cache_values[0], seg_keys, seg_values)
     parts = lax.all_to_all(partial, ctx, 0, 0, tiled=True)
-    parts, up_1, up_2 = beside(parts, trade(up_weight, 1), trade(up_weight, 2))
+    parts, up_y = beside(parts, trade(up_chunk))
     attention, copies = pl.pallas_call(
         merge_kernel,
         out_shape=(jax.ShapeDtypeStruct((each, head), BF16), jax.ShapeDtypeStruct((n_ctx, each, head), BF16)),
@@ -283,7 +287,7 @@
     )(parts)
     attention = attention.reshape(rows, width)
     heads_all = lax.all_to_all(copies, ctx, 0, 0, tiled=True)
-    heads_all, gate_3 = beside(heads_all, trade(gate_weight, 3))
+    heads_all, down_y = beside(heads_all, trade(down_chunk))
     mixed = pl.pallas_call(
         out_kernel,
         out_shape=jax.ShapeDtypeStruct((n_tp, trows, feats), BF16),
@@ -298,27 +302,38 @@
         stream_kernel,
         out_shape=(
             jax.ShapeDtypeStruct((trows, feats), BF16),
-            jax.ShapeDtypeStruct((n_near * n_tp, trows, feats), BF16),
+            jax.ShapeDtypeStruct((2 * n_tp, trows, feats), BF16),
         ),
         in_specs=[vmem] * 2,
         out_specs=(vmem, vmem),
         compiler_params=small,
         name="stream",
     )(mixed, residual_stream)
-    stream = lax.all_to_all(stream, (*near_axes, "tp"), 0, 0, tiled=True)
-    stream, up_3 = beside(stream, trade(up_weight, 3))
+    stream = lax.all_to_all(stream, ("hi", "tp"), 0, 0, tiled=True)
 
     half = -(-(units + 3) // 128) * 128
     block = tokens // n_far
+    send, keep = pl.pallas_call(
+        project_kernel,
+        out_shape=(
+            jax.ShapeDtypeStruct((tokens, 2 * half), BF16),
+            jax.ShapeDtypeStruct((tokens, 2 * half), F32),
+        ),
+        in_specs=[vmem] * 5,
+        out_specs=(vmem, vmem),
+        compiler_params=small,
+        name="project",
+    )(stream, gate_chunk(near), gate_y, up_chunk(near), up_y)
+    got = lax.ppermute(send, "lo", [(0, 1), (1, 0)])
     sums = pl.pallas_call(
-        project_kernel,
+        functools.partial(join_kernel, units=units),
         out_shape=jax.ShapeDtypeStruct((n_far, block, 2 * half), BF16),
-        in_specs=[vmem] * 9,
-        out_specs=vmem,
-        compiler_params=small,
-        name="project",
-    )(stream, chunk(gate_weight, near), gate_1, gate_2, gate_3, chunk(up_weight, near), up_1, up_2, up_3)
-    sums, down_y = beside(lax.all_to_all(sums, "far", 0, 0, tiled=True), down_trade)
+        in_specs=[vmem] * 2,
+        out_specs=vmem,
+        compiler_params=small,
+        name="join",
+    )(keep, got)
+    sums = lax.all_to_all(sums, "far", 0, 0, tiled=True)
     hidden = pl.pallas_call(
         hidden_kernel,
         out_shape=jax.ShapeDtypeStruct((n_far, block, units), BF16),

time: 226 us -> 230 us (1.018)
  blocking collectives: 38.8 us -> 83.7 us
  starting transfers between devices: 101 us -> 67.9 us
  waiting for transfers between devices: 66.6 us -> 57.4 us
  local copies, waits for them, and re-layouts: 3.65 us -> 6.22 us
  other arithmetic: 2.86 us -> 0.47 us
    all_to_all x0 -> x2, blocking collectives: none -> 45.5 us  [the longest x1 31.5 us: per_device(): sums = lax.all_to_all(sums, 'far', 0, 0, tiled=True)]
    all_to_all x2 -> x0, starting transfers between devices: 13.1 us -> none  [the longest x1 6.94 us: per_device(): lax.all_to_all(sums, 'far', 0, 0, tiled=True)]
    ppermute x7 -> x4, starting transfers between devices: 29.1 us -> 16.4 us  [the longest x3 14.1 us: trade(): return lambda place: lax.ppermute(part(place ^ 1), 'hi', [(0, 1), (1, 0)])]
    ppermute x7 -> x4, waiting for transfers between devices: 49.1 us -> 42.4 us  [the longest x3 33.2 us: trade(): return lambda place: lax.ppermute(part(place ^ 1), 'hi', [(0, 1), (1, 0)])]
    all_to_all x2 -> x0, waiting for transfers between devices: 3.9 us -> none  [the longest x1 3.89 us: per_device(): lax.all_to_all(sums, 'far', 0, 0, tiled=True)]
    ppermute x1, starting transfers between devices: 5.71 us -> 1.91 us  [per_device(): other = lax.ppermute(hidden, 'lo', [(0, 1), (1, 0)])]
    pallas_call x1, Pallas kernels: 5.21 us -> 7.79 us  [per_device(): pl.pallas_call(functools.partial(attend_kernel, tokens=tokens, group=grou...]
    another operation x1 -> x3, local copies, waits for them, and re-layouts: 0.25 us -> 2.82 us  [chunk(): return jnp.stack(lows)]
  transfers between devices with their start and end apart: 14 -> 9, of which waited for: 12 -> 7; matrix products, arithmetic and copies ran while one was open for 2% -> 2% of each run, Pallas kernels for 0% -> 0%
where the time goes in v8:
time: 230 us; the launch traced here: 229 us
  blocking collectives  83.7 us (36%)
  starting transfers between devices  67.9 us (30%)
  waiting for transfers between devices  57.4 us (25%)
  Pallas kernels  12.1 us (5%)
  local copies, waits for them, and re-layouts  6.22 us (3%)
    ppermute x3, waiting for transfers between devices, trade(): return lambda place: lax.ppermute(part(place ^ 1), 'hi', [(0, 1), (1, 0)])  33.2 us
    all_to_all x1, blocking collectives, per_device(): sums = lax.all_to_all(sums, 'far', 0, 0, tiled=True)  31.5 us
    all_to_all x1, blocking collectives, per_device(): lax.all_to_all(hidden, 'far', 0, 0, tiled=True).reshape(tokens, units)  23.3 us
    all_to_all x1, starting transfers between devices, per_device(): q_all = lax.all_to_all(q_all, ctx, 0, 0, tiled=True)  18.7 us
    all_to_all x1, blocking collectives, per_device(): mixed = lax.all_to_all(mixed, 'tp', 0, 0, tiled=True)  14.9 us
    ppermute x3, starting transfers between devices, trade(): return lambda place: lax.ppermute(part(place ^ 1), 'hi', [(0, 1), (1, 0)])  14.1 us
    all_to_all x1, blocking collectives, per_device(): stream = lax.all_to_all(stream, ('hi', 'tp'), 0, 0, tiled=True)  14 us
    all_to_all x1, starting transfers between devices, per_device(): parts = lax.all_to_all(partial, ctx, 0, 0, tiled=True)  11.9 us
  transfers between devices with their start and end apart: 9, of which 7 were waited for; matrix products, arithmetic and copies ran while one was open for 2% of the time, Pallas kernels for 0%

profile of v8, /device:TPU:1, one launch (start us, length us, event | category | flops | bytes accessed | tf_op | source)
XLA Modules:
  0.0 229.4 jit_solution(6326948907150216300)
XLA Ops:
  0.6 0.7 broadcast_in_dim.4
  1.3 0.7 broadcast_in_dim.5
  2.0 18.7 %all-to-all-start = ((bf16[32,24,128]{2,1,0:T(8,128)(2,1)}), bf16[32,24,128]{2,1,0:T(8,128)(2,1)S(1)}, u32[]{:S(2)}, u32[]{:S(2)}) async-start(bf16[32,24,128]{2,1,0:T(8,128)(2,1)} %broadcast_in_dim.5), calls=%async_computation | async-start | bytes 393216 | tf_op jit(solution)/shard_map/all_to_all | solution.py:253
  20.7 1.5 dynamic-slice_bitcast_fusion.5
  22.3 0.0 copy-start.7
  22.3 0.7 copy-done.7
  23.0 0.1 multiply_convert_fusion.3
  23.1 4.6 %collective-permute-start = (bf16[2,462,256]{2,1,0:T(8,128)(2,1)S(1)}, bf16[2,462,256]{2,1,0:T(8,128)(2,1)S(1)}, u32[]{:S(2)}, u32[]{:S(2)}) collective-permute-start(bf16[2,462,256]{2,1,0:T(8,128)(2,1)S(1)} %multiply_convert_fusion.3), channel_id=1, source_target_pairs={{0,16},{16,0},{1,17},{17,1},{2,18},{18,2},{3,19},{19,3},{4,20},{20... | collective-permute-start | bytes 1419272 | tf_op jit(solution)/shard_map/ppermute | solution.py:242
  28.4 11.3 %collective-permute-done.gate_y_ref = bf16[2,462,256]{2,1,0:T(8,128)(2,1)S(1)} collective-permute-done((bf16[2,462,256]{2,1,0:T(8,128)(2,1)S(1)}, bf16[2,462,256]{2,1,0:T(8,128)(2,1)S(1)}, u32[]{:S(2)}, u32[]{:S(2)}) %collective-permute-start) | collective-permute-done | bytes 473120 | tf_op jit(solution)/shard_map/ppermute | solution.py:242
  39.7 0.0 all-to-all-done.q_ref
  39.7 0.7 copy-done.6
  40.3 7.8 %attend.1 = bf16[32,32,128]{2,1,0:T(8,128)(2,1)} custom-call(s32[1]{0:T(128)S(6)} %copy.14.lengths, bf16[32,24,128]{2,1,0:T(8,128)(2,1)} %copy-done.6, bf16[3072,128]{1,0:T(8,128)(2,1)} %bitcast.45, bf16[3072,128]{1,0:T(8,128)(2,1)} %bitcast.46, bf16[6,128]{1,0:T(8,128)(2,1)} %sk_hbm.1, bf16[6,128]{1,0:T(8,128)(2,1)} %sv_hbm.1), custom_call_target="tpu_custom_call" | custom-call | flops 1207959552 | bytes 2097152 | tf_op jit(solution)/shard_map/attend/pallas_call | solution.py:260
  48.1 11.9 %all-to-all-start.1 = ((bf16[32,32,128]{2,1,0:T(8,128)(2,1)}), bf16[32,32,128]{2,1,0:T(8,128)(2,1)S(1)}, u32[]{:S(2)}, u32[]{:S(2)}) async-start(bf16[32,32,128]{2,1,0:T(8,128)(2,1)} %attend.1), calls=%async_computation.1 | async-start | bytes 524288 | tf_op jit(solution)/shard_map/all_to_all | solution.py:278
  60.1 0.0 copy-done.2
  60.1 0.2 dynamic-slice_bitcast_fusion.3
  60.3 0.0 copy-start.3
  60.3 0.3 multiply_convert_fusion
  60.6 4.6 %collective-permute-start.1 = (bf16[2,462,256]{2,1,0:T(8,128)(2,1)S(1)}, bf16[2,462,256]{2,1,0:T(8,128)(2,1)S(1)}, u32[]{:S(2)}, u32[]{:S(2)}) collective-permute-start(bf16[2,462,256]{2,1,0:T(8,128)(2,1)S(1)} %get-tuple-element.43), channel_id=1, source_target_pairs={{0,16},{16,0},{1,17},{17,1},{2,18},{18,2},{3,19},{19,3},{4,20},{20... | collective-permute-start | bytes 1419272 | tf_op jit(solution)/shard_map/ppermute | solution.py:242
  65.3 11.6 %collective-permute-done.1.up_y_ref = bf16[2,462,256]{2,1,0:T(8,128)(2,1)S(1)} collective-permute-done((bf16[2,462,256]{2,1,0:T(8,128)(2,1)S(1)}, bf16[2,462,256]{2,1,0:T(8,128)(2,1)S(1)}, u32[]{:S(2)}, u32[]{:S(2)}) %collective-permute-start.1) | collective-permute-done | bytes 473120 | tf_op jit(solution)/shard_map/ppermute | solution.py:242
  76.8 2.4 %all-to-all-done.1.in_ref = bf16[32,32,128]{2,1,0:T(8,128)(2,1)S(1)} async-done(((bf16[32,32,128]{2,1,0:T(8,128)(2,1)}), bf16[32,32,128]{2,1,0:T(8,128)(2,1)S(1)}, u32[]{:S(2)}, u32[]{:S(2)}) %all-to-all-start.1) | async-done | bytes 262176 | tf_op jit(solution)/shard_map/all_to_all | solution.py:278
  79.2 1.1 merge.1
  80.3 11.0 %all-to-all-start.2 = ((bf16[32,24,128]{2,1,0:T(8,128)(2,1)}), bf16[32,24,128]{2,1,0:T(8,128)(2,1)S(1)}, u32[]{:S(2)}, u32[]{:S(2)}) async-start(bf16[32,24,128]{2,1,0:T(8,128)(2,1)} %get-tuple-element.20), calls=%async_computation.2 | async-start | bytes 393216 | tf_op jit(solution)/shard_map/all_to_all | solution.py:289
  91.3 0.0 copy-done.3
  91.3 1.0 dynamic-slice_bitcast_fusion.1
  92.4 4.8 %collective-permute-start.2 = (bf16[2,462,256]{2,1,0:T(8,128)(2,1)S(1)}, bf16[2,462,256]{2,1,0:T(8,128)(2,1)S(1)}, u32[]{:S(2)}, u32[]{:S(2)}) collective-permute-start(bf16[2,462,256]{2,1,0:T(8,128)(2,1)S(1)} %pad_maximum_fusion), channel_id=1, source_target_pairs={{0,16},{16,0},{1,17},{17,1},{2,18},{18,2},{3,19},{19,3},{4,20},{20... | collective-permute-start | bytes 1419272 | tf_op jit(solution)/shard_map/ppermute | solution.py:242
  97.2 10.3 %collective-permute-done.2.wy_ref = bf16[2,462,256]{2,1,0:T(8,128)(2,1)S(1)} collective-permute-done((bf16[2,462,256]{2,1,0:T(8,128)(2,1)S(1)}, bf16[2,462,256]{2,1,0:T(8,128)(2,1)S(1)}, u32[]{:S(2)}, u32[]{:S(2)}) %collective-permute-start.2) | collective-permute-done | bytes 473120 | tf_op jit(solution)/shard_map/ppermute | solution.py:242
  107.5 0.0 all-to-all-done.2.h_ref
  107.5 0.0 copy-done
  107.5 0.3 out.1
  107.7 0.0 copy-start.1
  107.8 14.9 %all_to_all.40.in_ref = bf16[16,12,256]{2,1,0:T(8,128)(2,1)S(1)} all-to-all(bf16[16,12,256]{2,1,0:T(8,128)(2,1)S(1)} %out.1), channel_id=1, replica_groups=mesh['far'=8,'lo'=2,'hi'=2,'tp'=16] {'tp'}, dimensions={0} | all-to-all | bytes 196608 | tf_op jit(solution)/shard_map/all_to_all | solution.py:300
  122.7 0.0 copy-done.1
  122.7 14.0 %all_to_all.41.x_ref = bf16[32,12,256]{2,1,0:T(8,128)(2,1)S(1)} all-to-all(bf16[32,12,256]{2,1,0:T(8,128)(2,1)S(1)} %get-tuple-element.23), channel_id=1, replica_groups=mesh['far'=8,'lo'=2,'hi'=2,'tp'=16] {'hi','tp'}, dimensions={0} | all-to-all | bytes 393216 | tf_op jit(solution)/shard_map/all_to_all | solution.py:312
  136.7 0.7 project.1
  137.4 2.3 %collective-permute-start.3 = (bf16[192,1024]{1,0:T(8,128)(2,1)S(1)}, bf16[192,1024]{1,0:T(8,128)(2,1)S(1)}, u32[]{:S(2)}, u32[]{:S(2)}) collective-permute-start(bf16[192,1024]{1,0:T(8,128)(2,1)S(1)} %get-tuple-element.27), channel_id=1, source_target_pairs={{0,32},{32,0},{1,33},{33,1},{2,34},{34,2},{3,35},{35,3},{4,36},{36... | collective-permute-start | bytes 1179656 | tf_op jit(solution)/shard_map/ppermute | solution.py:327
  139.8 9.2 %collective-permute-done.3.got_ref = bf16[192,1024]{1,0:T(8,128)(2,1)S(1)} collective-permute-done((bf16[192,1024]{1,0:T(8,128)(2,1)S(1)}, bf16[192,1024]{1,0:T(8,128)(2,1)S(1)}, u32[]{:S(2)}, u32[]{:S(2)}) %collective-permute-start.3) | collective-permute-done | bytes 393248 | tf_op jit(solution)/shard_map/ppermute | solution.py:327
  149.0 0.3 join.1
  149.3 31.5 %all_to_all.42.in_ref = bf16[8,24,1024]{2,1,0:T(8,128)(2,1)S(1)} all-to-all(bf16[8,24,1024]{2,1,0:T(8,128)(2,1)S(1)} %join.1), channel_id=1, replica_groups=mesh['far'=8,'lo'=2,'hi'=2,'tp'=16] {'far'}, dimensions={0} | all-to-all | bytes 786432 | tf_op jit(solution)/shard_map/all_to_all | solution.py:336
  180.8 0.2 hidden.1
  181.0 0.0 copy-start.4
  181.0 23.3 %all_to_all.43 = bf16[8,24,462]{2,1,0:T(8,128)(2,1)S(1)} all-to-all(bf16[8,24,462]{2,1,0:T(8,128)(2,1)S(1)} %hidden.1), channel_id=1, replica_groups=mesh['far'=8,'lo'=2,'hi'=2,'tp'=16] {'far'}, dimensions={0} | all-to-all | bytes 354816 | tf_op jit(solution)/shard_map/all_to_all | solution.py:345
  204.3 1.9 collective-permute-start.4
  206.3 4.4 %collective-permute-done.4.other_ref = bf16[192,462]{1,0:T(8,128)(2,1)S(1)} collective-permute-done((bf16[192,462]{1,0:T(8,128)(2,1)S(1)}, bf16[192,462]{1,0:T(8,128)(2,1)S(1)}, u32[]{:S(2)}, u32[]{:S(2)}) %collective-permute-start.4) | collective-permute-done | bytes 177440 | tf_op jit(solution)/shard_map/ppermute | solution.py:346
  210.7 1.1 down.1
  211.8 8.1 %all-to-all-start.7 = ((bf16[32,12,256]{2,1,0:T(8,128)(2,1)}), bf16[32,12,256]{2,1,0:T(8,128)(2,1)S(1)}, u32[]{:S(2)}, u32[]{:S(2)}) async-start(bf16[32,12,256]{2,1,0:T(8,128)(2,1)} %down.1), calls=%async_computation.7 | async-start | bytes 524288 | tf_op jit(solution)/shard_map/all_to_all | solution.py:355
  219.9 0.6 reshape.13
  220.5 8.2 %all-to-all-done.7.in_ref = bf16[32,12,256]{2,1,0:T(8,128)(2,1)S(1)} async-done(((bf16[32,12,256]{2,1,0:T(8,128)(2,1)}), bf16[32,12,256]{2,1,0:T(8,128)(2,1)S(1)}, u32[]{:S(2)}, u32[]{:S(2)}) %all-to-all-start.7) | async-done | bytes 196640 | tf_op jit(solution)/shard_map/all_to_all | solution.py:355
  228.7 0.7 last.1
  (9 shorter events, 0.1 us)
Async XLA Ops:
  2.0 37.6 %all-to-all-start = ((bf16[32,24,128]{2,1,0:T(8,128)(2,1)}), bf16[32,24,128]{2,1,0:T(8,128)(2,1)S(1)}, u32[]{:S(2)}, u32[]{:S(2)}) async-start(bf16[32,24,128]{2,1,0:T(8,128)(2,1)} %broadcast_in_dim.5), calls=%async_computation | async-start | bytes 393216 | tf_op jit(solution)/shard_map/all_to_all | solution.py:253
  22.3 0.7 copy-start.7
  23.1 16.6 %collective-permute-start = (bf16[2,462,256]{2,1,0:T(8,128)(2,1)S(1)}, bf16[2,462,256]{2,1,0:T(8,128)(2,1)S(1)}, u32[]{:S(2)}, u32[]{:S(2)}) collective-permute-start(bf16[2,462,256]{2,1,0:T(8,128)(2,1)S(1)} %multiply_convert_fusion.3), channel_id=1, source_target_pairs={{0,16},{16,0},{1,17},{17,1},{2,18},{18,2},{3,19},{19,3},{4,20},{20... | collective-permute-start | bytes 1419272 | tf_op jit(solution)/shard_map/ppermute | solution.py:242
  39.7 0.7 copy-start.6
  40.3 19.7 %copy-start.2 = (bf16[256,1848]{0,1:T(8,128)(2,1)S(1)}, bf16[256,1848]{0,1:T(8,128)(2,1)}, u32[]{:S(2)}) copy-start(bf16[256,1848]{0,1:T(8,128)(2,1)} %param.22) | copy-start | bytes 2838532
  48.1 31.1 %all-to-all-start.1 = ((bf16[32,32,128]{2,1,0:T(8,128)(2,1)}), bf16[32,32,128]{2,1,0:T(8,128)(2,1)S(1)}, u32[]{:S(2)}, u32[]{:S(2)}) async-start(bf16[32,32,128]{2,1,0:T(8,128)(2,1)} %attend.1), calls=%async_computation.1 | async-start | bytes 524288 | tf_op jit(solution)/shard_map/all_to_all | solution.py:278
  60.3 31.0 %copy-start.3 = (bf16[1848,256]{1,0:T(8,128)(2,1)S(1)}, bf16[1848,256]{1,0:T(8,128)(2,1)}, u32[]{:S(2)}) copy-start(bf16[1848,256]{1,0:T(8,128)(2,1)} %param.23) | copy-start | bytes 2838532
  60.6 16.2 %collective-permute-start.1 = (bf16[2,462,256]{2,1,0:T(8,128)(2,1)S(1)}, bf16[2,462,256]{2,1,0:T(8,128)(2,1)S(1)}, u32[]{:S(2)}, u32[]{:S(2)}) collective-permute-start(bf16[2,462,256]{2,1,0:T(8,128)(2,1)S(1)} %get-tuple-element.43), channel_id=1, source_target_pairs={{0,16},{16,0},{1,17},{17,1},{2,18},{18,2},{3,19},{19,3},{4,20},{20... | collective-permute-start | bytes 1419272 | tf_op jit(solution)/shard_map/ppermute | solution.py:242
  80.3 27.2 %all-to-all-start.2 = ((bf16[32,24,128]{2,1,0:T(8,128)(2,1)}), bf16[32,24,128]{2,1,0:T(8,128)(2,1)S(1)}, u32[]{:S(2)}, u32[]{:S(2)}) async-start(bf16[32,24,128]{2,1,0:T(8,128)(2,1)} %get-tuple-element.20), calls=%async_computation.2 | async-start | bytes 393216 | tf_op jit(solution)/shard_map/all_to_all | solution.py:289
  92.3 15.1 %copy-start = (bf16[512,256]{1,0:T(8,128)(2,1)S(1)}, bf16[512,256]{1,0:T(8,128)(2,1)}, u32[]{:S(2)}) copy-start(bf16[512,256]{1,0:T(8,128)(2,1)} %w_ref.1) | copy-start | bytes 786436
  92.4 15.1 %collective-permute-start.2 = (bf16[2,462,256]{2,1,0:T(8,128)(2,1)S(1)}, bf16[2,462,256]{2,1,0:T(8,128)(2,1)S(1)}, u32[]{:S(2)}, u32[]{:S(2)}) collective-permute-start(bf16[2,462,256]{2,1,0:T(8,128)(2,1)S(1)} %pad_maximum_fusion), channel_id=1, source_target_pairs={{0,16},{16,0},{1,17},{17,1},{2,18},{18,2},{3,19},{19,3},{4,20},{20... | collective-permute-start | bytes 1419272 | tf_op jit(solution)/shard_map/ppermute | solution.py:242
  107.7 14.9 %copy-start.1 = (bf16[12,256]{1,0:T(8,128)(2,1)S(1)}, bf16[12,256]{1,0:T(8,128)(2,1)}, u32[]{:S(2)}) copy-start(bf16[12,256]{1,0:T(8,128)(2,1)} %residual_ref.1) | copy-start | bytes 18436
  137.4 11.6 %collective-permute-start.3 = (bf16[192,1024]{1,0:T(8,128)(2,1)S(1)}, bf16[192,1024]{1,0:T(8,128)(2,1)S(1)}, u32[]{:S(2)}, u32[]{:S(2)}) collective-permute-start(bf16[192,1024]{1,0:T(8,128)(2,1)S(1)} %get-tuple-element.27), channel_id=1, source_target_pairs={{0,32},{32,0},{1,33},{33,1},{2,34},{34,2},{3,35},{35,3},{4,36},{36... | collective-permute-start | bytes 1179656 | tf_op jit(solution)/shard_map/ppermute | solution.py:327
  180.8 25.4 %copy-start.5 = (bf16[1,462,256]{2,1,0:T(8,128)(2,1)S(1)}, bf16[1,462,256]{2,1,0:T(8,128)(2,1)}, u32[]{:S(2)}) copy-start(bf16[1,462,256]{2,1,0:T(8,128)(2,1)} %get-tuple-element.33) | copy-start | bytes 709636
  181.0 25.2 %copy-start.4 = (bf16[1,462,256]{2,1,0:T(8,128)(2,1)S(1)}, bf16[1,462,256]{2,1,0:T(8,128)(2,1)}, u32[]{:S(2)}) copy-start(bf16[1,462,256]{2,1,0:T(8,128)(2,1)} %get-tuple-element.30) | copy-start | bytes 709636
  204.3 6.4 %collective-permute-start.4 = (bf16[192,462]{1,0:T(8,128)(2,1)S(1)}, bf16[192,462]{1,0:T(8,128)(2,1)S(1)}, u32[]{:S(2)}, u32[]{:S(2)}) collective-permute-start(bf16[192,462]{1,0:T(8,128)(2,1)S(1)} %bitcast.43), channel_id=1, source_target_pairs={{0,32},{32,0},{1,33},{33,1},{2,34},{34,2},{3,35},{35,3},{4,36},{36... | collective-permute-start | bytes 532232 | tf_op jit(solution)/shard_map/ppermute | solution.py:346
  211.8 16.9 %all-to-all-start.7 = ((bf16[32,12,256]{2,1,0:T(8,128)(2,1)}), bf16[32,12,256]{2,1,0:T(8,128)(2,1)S(1)}, u32[]{:S(2)}, u32[]{:S(2)}) async-start(bf16[32,12,256]{2,1,0:T(8,128)(2,1)} %down.1), calls=%async_computation.7 | async-start | bytes 524288 | tf_op jit(solution)/shard_map/all_to_all | solution.py:355

commit v9 on v8

--- a/solution.py
+++ b/solution.py
@@ -135,7 +135,7 @@
     out_ref[...] = (own_ref[...].astype(F32) + jnp.sum(in_ref[...].astype(F32), axis=0)).astype(BF16)
 
 
-def project_kernel(x_ref, gate_ref, gate_y_ref, up_ref, up_y_ref, send_ref, keep_ref):
+def project_kernel(x_ref, gate_ref, gate_y_ref, up_ref, up_y0_ref, up_y1_ref, send_ref, keep_ref):
     units = gate_ref.shape[1]
     each = x_ref.shape[0] // 2
     half = keep_ref.shape[1] // 2
@@ -147,15 +147,15 @@
     parts = three_parts(squares)
     own, other = own.astype(BF16), other.astype(BF16)
 
-    def product(w_ref, w_y_ref, at):
-        y = lax.dot_general(own, w_ref[at], (((1,), (1,)), ((), ())), preferred_element_type=F32)
-        return y + lax.dot_general(other, w_y_ref[at], (((1,), (1,)), ((), ())), preferred_element_type=F32)
+    def product(w, w_y):
+        y = lax.dot_general(own, w, (((1,), (1,)), ((), ())), preferred_element_type=F32)
+        return y + lax.dot_general(other, w_y, (((1,), (1,)), ((), ())), preferred_element_type=F32)
 
     tokens = squares.shape[0]
     spare = half - units
     for at, ref in ((1 - lo, send_ref), (lo, keep_ref)):
-        gate = product(gate_ref, gate_y_ref, at)
-        up = product(up_ref, up_y_ref, at)
+        gate = product(gate_ref[at], gate_y_ref[at])
+        up = product(up_ref[at], jnp.where(at == 0, up_y0_ref[...], up_y1_ref[...]))
         ref[:, :half] = jnp.concatenate([gate, *parts, jnp.zeros((tokens, spare - 3), F32)], axis=1).astype(ref.dtype)
         ref[:, half:] = jnp.concatenate([up, jnp.zeros((tokens, spare), F32)], axis=1).astype(ref.dtype)
 
@@ -187,13 +187,13 @@
         out_ref[i] = out
 
 
-def down_kernel(mine_ref, other_ref, w_ref, wy_ref, out_ref):
+def down_kernel(h_ref, w_ref, wy_ref, out_ref):
     rows = out_ref.shape[1]
     each = out_ref.shape[0] // 2
-    lo, hi = lax.axis_index("lo"), lax.axis_index("hi")
+    hi = lax.axis_index("hi")
+    h = [jnp.concatenate([h_ref[i] for i in range(lo, h_ref.shape[0], 2)], axis=0) for lo in range(2)]
     for at, ref in ((hi, w_ref), (1 - hi, wy_ref)):
-        y = jnp.dot(mine_ref[...], ref[lo], preferred_element_type=F32)
-        y = y + jnp.dot(other_ref[...], ref[1 - lo], preferred_element_type=F32)
+        y = jnp.dot(h[0], ref[0], preferred_element_type=F32) + jnp.dot(h[1], ref[1], preferred_element_type=F32)
         for k in range(each):
             out_ref[at * each + k] = y[k * rows : (k + 1) * rows].astype(BF16)
 
@@ -226,17 +226,23 @@
 
     near = lax.axis_index(near_axes)
 
-    def chunk(w, place):
-        lows = [lax.dynamic_slice_in_dim(w, (2 * lo + (place & 1)) * units, units, 0) for lo in range(2)]
-        return jnp.stack(lows)
-
-    def scaled(w):
-        return lambda place: (chunk(w.T, place).astype(F32) * norm_gain).astype(BF16)
-
-    gate_chunk, up_chunk = scaled(gate_weight), scaled(up_weight)
+    def piece(w, lo, place):
+        return lax.dynamic_slice_in_dim(w, (2 * lo + (place & 1)) * units, units, 0)
+
+    def scaled(w, lo, place):
+        return (piece(w.T, lo, place).astype(F32) * norm_gain).astype(BF16)
+
+    def gate_chunk(place):
+        return jnp.stack([scaled(gate_weight, lo, place) for lo in range(2)])
+
+    def up_0(place):
+        return scaled(up_weight, 0, place)
+
+    def up_1(place):
+        return scaled(up_weight, 1, place)
 
     def down_chunk(place):
-        return chunk(down_weight, place)
+        return jnp.stack([piece(down_weight, lo, place) for lo in range(2)])
 
     def trade(part):
         return lambda place: lax.ppermute(part(place ^ 1), "hi", [(0, 1), (1, 0)])
@@ -276,7 +282,7 @@
         name="attend",
     )(lengths, q_all, cache_keys[0], cache_values[0], seg_keys, seg_values)
     parts = lax.all_to_all(partial, ctx, 0, 0, tiled=True)
-    parts, up_y = beside(parts, trade(up_chunk))
+    parts, up_y0 = beside(parts, trade(up_0))
     attention, copies = pl.pallas_call(
         merge_kernel,
         out_shape=(jax.ShapeDtypeStruct((each, head), BF16), jax.ShapeDtypeStruct((n_ctx, each, head), BF16)),
@@ -287,7 +293,7 @@
     )(parts)
     attention = attention.reshape(rows, width)
     heads_all = lax.all_to_all(copies, ctx, 0, 0, tiled=True)
-    heads_all, down_y = beside(heads_all, trade(down_chunk))
+    heads_all, up_y1 = beside(heads_all, trade(up_1))
     mixed = pl.pallas_call(
         out_kernel,
         out_shape=jax.ShapeDtypeStruct((n_tp, trows, feats), BF16),
@@ -319,11 +325,11 @@
             jax.ShapeDtypeStruct((tokens, 2 * half), BF16),
             jax.ShapeDtypeStruct((tokens, 2 * half), F32),
         ),
-        in_specs=[vmem] * 5,
+        in_specs=[vmem] * 6,
         out_specs=(vmem, vmem),
         compiler_params=small,
         name="project",
-    )(stream, gate_chunk(near), gate_y, up_chunk(near), up_y)
+    )(stream, gate_chunk(near), gate_y, jnp.stack([up_0(near), up_1(near)]), up_y0, up_y1)
     got = lax.ppermute(send, "lo", [(0, 1), (1, 0)])
     sums = pl.pallas_call(
         functools.partial(join_kernel, units=units),
@@ -333,25 +339,24 @@
         compiler_params=small,
         name="join",
     )(keep, got)
-    sums = lax.all_to_all(sums, "far", 0, 0, tiled=True)
+    sums, down_y = beside(lax.all_to_all(sums, "far", 0, 0, tiled=True), trade(down_chunk))
     hidden = pl.pallas_call(
         hidden_kernel,
-        out_shape=jax.ShapeDtypeStruct((n_far, block, units), BF16),
+        out_shape=jax.ShapeDtypeStruct((2 * n_far, block, units), BF16),
         in_specs=[vmem],
         out_specs=vmem,
         compiler_params=small,
         name="hidden",
     )(sums)
-    hidden = lax.all_to_all(hidden, "far", 0, 0, tiled=True).reshape(tokens, units)
-    other = lax.ppermute(hidden, "lo", [(0, 1), (1, 0)])
+    hidden = lax.all_to_all(hidden, ("far", "lo"), 0, 0, tiled=True)
     lowered = pl.pallas_call(
         down_kernel,
         out_shape=jax.ShapeDtypeStruct((2 * n_tp, trows, feats), BF16),
-        in_specs=[vmem] * 4,
+        in_specs=[vmem] * 3,
         out_specs=vmem,
         compiler_params=small,
         name="down",
-    )(hidden, other, down_chunk(near), down_y)
+    )(hidden, down_chunk(near), down_y)
     lowered = lax.all_to_all(lowered, ("hi", "tp"), 0, 0, tiled=True)
     layer_out = pl.pallas_call(
         last_kernel,

time: 230 us -> 222 us (0.965)
  blocking collectives: 83.7 us -> 15.3 us
  waiting for transfers between devices: 57.4 us -> 95.9 us
  starting transfers between devices: 67.9 us -> 87.6 us
  other arithmetic: 0.47 us -> 2.82 us
    all_to_all x3 -> x0, blocking collectives: 68.8 us -> none  [the longest x1 31.5 us: per_device(): sums = lax.all_to_all(sums, 'far', 0, 0, tiled=True)]
    all_to_all x0 -> x3, waiting for transfers between devices: none -> 31.8 us  [the longest x1 17.8 us: per_device(): hidden = lax.all_to_all(hidden, ('far', 'lo'), 0, 0, tiled=True)]
    all_to_all x0 -> x3, starting transfers between devices: none -> 19.6 us  [the longest x1 9.98 us: per_device(): hidden = lax.all_to_all(hidden, ('far', 'lo'), 0, 0, tiled=True)]
    all_to_all x1, waiting for transfers between devices: 2.35 us -> 9.23 us  [per_device(): parts = lax.all_to_all(partial, ctx, 0, 0, tiled=True)]
    all_to_all x1, waiting for transfers between devices: 0.01 us -> 5.37 us  [per_device(): heads_all = lax.all_to_all(copies, ctx, 0, 0, tiled=True)]
    all_to_all x1, starting transfers between devices: 11 us -> 6.29 us  [per_device(): heads_all = lax.all_to_all(copies, ctx, 0, 0, tiled=True)]
    ppermute x1 -> x0, waiting for transfers between devices: 4.41 us -> none  [per_device(): other = lax.ppermute(hidden, 'lo', [(0, 1), (1, 0)])]
    ppermute x3 -> x4, starting transfers between devices: 14.1 us -> 17.3 us  [trade(): return lambda place: lax.ppermute(part(place ^ 1), 'hi', [(0, 1), (1, 0)])]
  transfers between devices with their start and end apart: 9 -> 12, of which waited for: 7 -> 11; matrix products, arithmetic and copies ran while one was open for 2% -> 2% of each run, Pallas kernels for 0% -> 0%
where the time goes in v9:
time: 222 us; the launch traced here: 221 us
  waiting for transfers between devices  95.9 us (43%)
  starting transfers between devices  87.6 us (39%)
  blocking collectives  15.3 us (7%)
  Pallas kernels  13.5 us (6%)
  local copies, waits for them, and re-layouts  4.52 us (2%)
  other arithmetic  2.82 us (1%)
    ppermute x4, waiting for transfers between devices, trade(): return lambda place: lax.ppermute(part(place ^ 1), 'hi', [(0, 1), (1, 0)])  31.7 us
    all_to_all x1, starting transfers between devices, per_device(): q_all = lax.all_to_all(q_all, ctx, 0, 0, tiled=True)  18.7 us
    all_to_all x1, waiting for transfers between devices, per_device(): hidden = lax.all_to_all(hidden, ('far', 'lo'), 0, 0, tiled=True)  17.8 us
    ppermute x4, starting transfers between devices, trade(): return lambda place: lax.ppermute(part(place ^ 1), 'hi', [(0, 1), (1, 0)])  17.3 us
    all_to_all x1, blocking collectives, per_device(): mixed = lax.all_to_all(mixed, 'tp', 0, 0, tiled=True)  15.3 us
    all_to_all x1, starting transfers between devices, per_device(): parts = lax.all_to_all(partial, ctx, 0, 0, tiled=True)  12.5 us
    all_to_all x1, starting transfers between devices, per_device(): lowered = lax.all_to_all(lowered, ('hi', 'tp'), 0, 0, tiled=True)  11.3 us
    all_to_all x1, starting transfers between devices, per_device(): hidden = lax.all_to_all(hidden, ('far', 'lo'), 0, 0, tiled=True)  9.98 us
  transfers between devices with their start and end apart: 12, of which 11 were waited for; matrix products, arithmetic and copies ran while one was open for 2% of the time, Pallas kernels for 0%

profile of v9, /device:TPU:1, one launch (start us, length us, event | category | flops | bytes accessed | tf_op | source)
XLA Modules:
  0.0 221.1 jit_solution(2143682439023621121)
XLA Ops:
  0.6 0.7 broadcast_in_dim.4
  1.3 0.7 broadcast_in_dim.5
  2.0 18.7 %all-to-all-start = ((bf16[32,24,128]{2,1,0:T(8,128)(2,1)}), bf16[32,24,128]{2,1,0:T(8,128)(2,1)S(1)}, u32[]{:S(2)}, u32[]{:S(2)}) async-start(bf16[32,24,128]{2,1,0:T(8,128)(2,1)} %broadcast_in_dim.5), calls=%async_computation | async-start | bytes 393216 | tf_op jit(solution)/shard_map/all_to_all | solution.py:259
  20.7 0.0 copy-start.6
  20.7 0.7 copy-done.6
  21.4 1.6 fusion.4
  23.1 4.6 %collective-permute-start = (bf16[2,462,256]{2,1,0:T(8,128)(2,1)S(1)}, bf16[2,462,256]{2,1,0:T(8,128)(2,1)S(1)}, u32[]{:S(2)}, u32[]{:S(2)}) collective-permute-start(bf16[2,462,256]{2,1,0:T(8,128)(2,1)S(1)} %pad_maximum_fusion), channel_id=1, source_target_pairs={{0,16},{16,0},{1,17},{17,1},{2,18},{18,2},{3,19},{19,3},{4,20},{20... | collective-permute-start | bytes 1419272 | tf_op jit(solution)/shard_map/ppermute | solution.py:248
  28.4 11.3 %collective-permute-done.gate_y_ref = bf16[2,462,256]{2,1,0:T(8,128)(2,1)S(1)} collective-permute-done((bf16[2,462,256]{2,1,0:T(8,128)(2,1)S(1)}, bf16[2,462,256]{2,1,0:T(8,128)(2,1)S(1)}, u32[]{:S(2)}, u32[]{:S(2)}) %collective-permute-start) | collective-permute-done | bytes 473120 | tf_op jit(solution)/shard_map/ppermute | solution.py:248
  39.6 0.0 all-to-all-done.q_ref
  39.7 0.7 copy-done.5
  40.3 6.9 %attend.1 = bf16[32,32,128]{2,1,0:T(8,128)(2,1)} custom-call(s32[1]{0:T(128)S(6)} %copy.14.lengths, bf16[32,24,128]{2,1,0:T(8,128)(2,1)} %copy-done.5, bf16[3072,128]{1,0:T(8,128)(2,1)} %bitcast.38, bf16[3072,128]{1,0:T(8,128)(2,1)} %bitcast.39, bf16[6,128]{1,0:T(8,128)(2,1)} %sk_hbm.1, bf16[6,128]{1,0:T(8,128)(2,1)} %sv_hbm.1), custom_call_target="tpu_custom_call" | custom-call | flops 1207959552 | bytes 2097152 | tf_op jit(solution)/shard_map/attend/pallas_call | solution.py:266
  47.3 12.5 %all-to-all-start.1 = ((bf16[32,32,128]{2,1,0:T(8,128)(2,1)}), bf16[32,32,128]{2,1,0:T(8,128)(2,1)S(1)}, u32[]{:S(2)}, u32[]{:S(2)}) async-start(bf16[32,32,128]{2,1,0:T(8,128)(2,1)} %attend.1), calls=%async_computation.1 | async-start | bytes 524288 | tf_op jit(solution)/shard_map/all_to_all | solution.py:284
  59.7 0.0 copy-done.3
  59.7 0.1 fusion.2
  59.8 4.6 %collective-permute-start.1 = (bf16[462,256]{1,0:T(8,128)(2,1)S(1)}, bf16[462,256]{1,0:T(8,128)(2,1)S(1)}, u32[]{:S(2)}, u32[]{:S(2)}) collective-permute-start(bf16[462,256]{1,0:T(8,128)(2,1)S(1)} %fusion.2), channel_id=1, source_target_pairs={{0,16},{16,0},{1,17},{17,1},{2,18},{18,2},{3,19},{19,3},{4,20},{20... | collective-permute-start | bytes 709640 | tf_op jit(solution)/shard_map/ppermute | solution.py:248
  64.5 5.2 %collective-permute-done.1.up_y0_ref = bf16[462,256]{1,0:T(8,128)(2,1)S(1)} collective-permute-done((bf16[462,256]{1,0:T(8,128)(2,1)S(1)}, bf16[462,256]{1,0:T(8,128)(2,1)S(1)}, u32[]{:S(2)}, u32[]{:S(2)}) %collective-permute-start.1) | collective-permute-done | bytes 236576 | tf_op jit(solution)/shard_map/ppermute | solution.py:248
  69.7 9.2 %all-to-all-done.1.in_ref = bf16[32,32,128]{2,1,0:T(8,128)(2,1)S(1)} async-done(((bf16[32,32,128]{2,1,0:T(8,128)(2,1)}), bf16[32,32,128]{2,1,0:T(8,128)(2,1)S(1)}, u32[]{:S(2)}, u32[]{:S(2)}) %all-to-all-start.1) | async-done | bytes 262176 | tf_op jit(solution)/shard_map/all_to_all | solution.py:284
  78.9 1.1 merge.1
  80.0 6.3 %all-to-all-start.2 = ((bf16[32,24,128]{2,1,0:T(8,128)(2,1)}), bf16[32,24,128]{2,1,0:T(8,128)(2,1)S(1)}, u32[]{:S(2)}, u32[]{:S(2)}) async-start(bf16[32,24,128]{2,1,0:T(8,128)(2,1)} %get-tuple-element.23), calls=%async_computation.2 | async-start | bytes 393216 | tf_op jit(solution)/shard_map/all_to_all | solution.py:295
  86.3 0.0 copy-start
  86.3 0.9 fusion.6
  87.3 4.6 %collective-permute-start.2 = (bf16[462,256]{1,0:T(8,128)(2,1)S(1)}, bf16[462,256]{1,0:T(8,128)(2,1)S(1)}, u32[]{:S(2)}, u32[]{:S(2)}) collective-permute-start(bf16[462,256]{1,0:T(8,128)(2,1)S(1)} %get-tuple-element.37), channel_id=1, source_target_pairs={{0,16},{16,0},{1,17},{17,1},{2,18},{18,2},{3,19},{19,3},{4,20},{20... | collective-permute-start | bytes 709640 | tf_op jit(solution)/shard_map/ppermute | solution.py:248
  91.9 4.9 %collective-permute-done.2.up_y1_ref = bf16[462,256]{1,0:T(8,128)(2,1)S(1)} collective-permute-done((bf16[462,256]{1,0:T(8,128)(2,1)S(1)}, bf16[462,256]{1,0:T(8,128)(2,1)S(1)}, u32[]{:S(2)}, u32[]{:S(2)}) %collective-permute-start.2) | collective-permute-done | bytes 236576 | tf_op jit(solution)/shard_map/ppermute | solution.py:248
  96.8 5.4 %all-to-all-done.2.h_ref = bf16[32,24,128]{2,1,0:T(8,128)(2,1)S(1)} async-done(((bf16[32,24,128]{2,1,0:T(8,128)(2,1)}), bf16[32,24,128]{2,1,0:T(8,128)(2,1)S(1)}, u32[]{:S(2)}, u32[]{:S(2)}) %all-to-all-start.2) | async-done | bytes 196640 | tf_op jit(solution)/shard_map/all_to_all | solution.py:295
  102.2 0.3 out.1
  102.5 0.0 copy-start.1
  102.5 15.3 %all_to_all.40.in_ref = bf16[16,12,256]{2,1,0:T(8,128)(2,1)S(1)} all-to-all(bf16[16,12,256]{2,1,0:T(8,128)(2,1)S(1)} %out.1), channel_id=1, replica_groups=mesh['far'=8,'lo'=2,'hi'=2,'tp'=16] {'tp'}, dimensions={0} | all-to-all | bytes 196608 | tf_op jit(solution)/shard_map/all_to_all | solution.py:306
  117.8 0.7 stream.1
  118.5 5.2 %all-to-all-start.4 = ((bf16[32,12,256]{2,1,0:T(8,128)(2,1)}), bf16[32,12,256]{2,1,0:T(8,128)(2,1)S(1)}, u32[]{:S(2)}, u32[]{:S(2)}) async-start(bf16[32,12,256]{2,1,0:T(8,128)(2,1)} %get-tuple-element.26), calls=%async_computation.4 | async-start | bytes 524288 | tf_op jit(solution)/shard_map/all_to_all | solution.py:318
  123.8 0.9 copy-done.4
  124.8 7.9 %all-to-all-done.4.x_ref = bf16[32,12,256]{2,1,0:T(8,128)(2,1)S(1)} async-done(((bf16[32,12,256]{2,1,0:T(8,128)(2,1)}), bf16[32,12,256]{2,1,0:T(8,128)(2,1)S(1)}, u32[]{:S(2)}, u32[]{:S(2)}) %all-to-all-start.4) | async-done | bytes 196640 | tf_op jit(solution)/shard_map/all_to_all | solution.py:318
  132.6 0.7 project.1
  133.3 2.0 collective-permute-start.3
  135.3 9.6 %collective-permute-done.3.got_ref = bf16[192,1024]{1,0:T(8,128)(2,1)S(1)} collective-permute-done((bf16[192,1024]{1,0:T(8,128)(2,1)S(1)}, bf16[192,1024]{1,0:T(8,128)(2,1)S(1)}, u32[]{:S(2)}, u32[]{:S(2)}) %collective-permute-start.3) | collective-permute-done | bytes 393248 | tf_op jit(solution)/shard_map/ppermute | solution.py:333
  144.9 1.0 join.1
  145.9 4.4 %all-to-all-start.5 = ((bf16[8,24,1024]{2,1,0:T(8,128)(2,1)}), bf16[8,24,1024]{2,1,0:T(8,128)(2,1)S(1)}, u32[]{:S(2)}, u32[]{:S(2)}) async-start(bf16[8,24,1024]{2,1,0:T(8,128)(2,1)} %join.1), calls=%async_computation.5 | async-start | bytes 786432 | tf_op jit(solution)/shard_map/all_to_all | solution.py:342
  150.4 0.2 dynamic-slice_bitcast_fusion.1
  150.7 3.4 %collective-permute-start.4 = (bf16[2,462,256]{2,1,0:T(8,128)(2,1)S(1)}, bf16[2,462,256]{2,1,0:T(8,128)(2,1)S(1)}, u32[]{:S(2)}, u32[]{:S(2)}) collective-permute-start(bf16[2,462,256]{2,1,0:T(8,128)(2,1)S(1)} %pad_maximum_fusion.3), channel_id=1, source_target_pairs={{0,16},{16,0},{1,17},{17,1},{2,18},{18,2},{3,19},{19,3},{4,20},{20... | collective-permute-start | bytes 1419272 | tf_op jit(solution)/shard_map/ppermute | solution.py:248
  154.0 10.2 %collective-permute-done.4.wy_ref = bf16[2,462,256]{2,1,0:T(8,128)(2,1)S(1)} collective-permute-done((bf16[2,462,256]{2,1,0:T(8,128)(2,1)S(1)}, bf16[2,462,256]{2,1,0:T(8,128)(2,1)S(1)}, u32[]{:S(2)}, u32[]{:S(2)}) %collective-permute-start.4) | collective-permute-done | bytes 473120 | tf_op jit(solution)/shard_map/ppermute | solution.py:248
  164.3 6.1 %all-to-all-done.5.in_ref = bf16[8,24,1024]{2,1,0:T(8,128)(2,1)S(1)} async-done(((bf16[8,24,1024]{2,1,0:T(8,128)(2,1)}), bf16[8,24,1024]{2,1,0:T(8,128)(2,1)S(1)}, u32[]{:S(2)}, u32[]{:S(2)}) %all-to-all-start.5) | async-done | bytes 393248 | tf_op jit(solution)/shard_map/all_to_all | solution.py:342
  170.4 1.0 hidden.1
  171.4 10.0 %all-to-all-start.6 = ((bf16[16,24,462]{2,1,0:T(8,128)(2,1)}), bf16[16,24,462]{2,1,0:T(8,128)(2,1)S(1)}, u32[]{:S(2)}, u32[]{:S(2)}) async-start(bf16[16,24,462]{2,1,0:T(8,128)(2,1)} %hidden.1), calls=%async_computation.6 | async-start | bytes 786432 | tf_op jit(solution)/shard_map/all_to_all | solution.py:351
  181.4 17.8 %all-to-all-done.6.h_ref = bf16[16,24,462]{2,1,0:T(8,128)(2,1)S(1)} async-done(((bf16[16,24,462]{2,1,0:T(8,128)(2,1)}), bf16[16,24,462]{2,1,0:T(8,128)(2,1)S(1)}, u32[]{:S(2)}, u32[]{:S(2)}) %all-to-all-start.6) | async-done | bytes 354848 | tf_op jit(solution)/shard_map/all_to_all | solution.py:351
  199.2 1.1 down.1
  200.3 11.3 %all-to-all-start.7 = ((bf16[32,12,256]{2,1,0:T(8,128)(2,1)}), bf16[32,12,256]{2,1,0:T(8,128)(2,1)S(1)}, u32[]{:S(2)}, u32[]{:S(2)}) async-start(bf16[32,12,256]{2,1,0:T(8,128)(2,1)} %down.1), calls=%async_computation.7 | async-start | bytes 524288 | tf_op jit(solution)/shard_map/all_to_all | solution.py:360
  211.6 0.6 reshape.10
  212.2 8.2 %all-to-all-done.7.in_ref = bf16[32,12,256]{2,1,0:T(8,128)(2,1)S(1)} async-done(((bf16[32,12,256]{2,1,0:T(8,128)(2,1)}), bf16[32,12,256]{2,1,0:T(8,128)(2,1)S(1)}, u32[]{:S(2)}, u32[]{:S(2)}) %all-to-all-start.7) | async-done | bytes 196640 | tf_op jit(solution)/shard_map/all_to_all | solution.py:360
  220.4 0.7 last.1
  (12 shorter events, 0.2 us)
Async XLA Ops:
  2.0 37.6 %all-to-all-start = ((bf16[32,24,128]{2,1,0:T(8,128)(2,1)}), bf16[32,24,128]{2,1,0:T(8,128)(2,1)S(1)}, u32[]{:S(2)}, u32[]{:S(2)}) async-start(bf16[32,24,128]{2,1,0:T(8,128)(2,1)} %broadcast_in_dim.5), calls=%async_computation | async-start | bytes 393216 | tf_op jit(solution)/shard_map/all_to_all | solution.py:259
  20.7 0.7 copy-start.6
  23.1 16.6 %collective-permute-start = (bf16[2,462,256]{2,1,0:T(8,128)(2,1)S(1)}, bf16[2,462,256]{2,1,0:T(8,128)(2,1)S(1)}, u32[]{:S(2)}, u32[]{:S(2)}) collective-permute-start(bf16[2,462,256]{2,1,0:T(8,128)(2,1)S(1)} %pad_maximum_fusion), channel_id=1, source_target_pairs={{0,16},{16,0},{1,17},{17,1},{2,18},{18,2},{3,19},{19,3},{4,20},{20... | collective-permute-start | bytes 1419272 | tf_op jit(solution)/shard_map/ppermute | solution.py:248
  39.7 0.7 copy-start.5
  40.3 19.4 %copy-start.3 = (bf16[256,1848]{0,1:T(8,128)(2,1)S(1)}, bf16[256,1848]{0,1:T(8,128)(2,1)}, u32[]{:S(2)}) copy-start(bf16[256,1848]{0,1:T(8,128)(2,1)} %param.22) | copy-start | bytes 2838532
  47.3 31.6 %all-to-all-start.1 = ((bf16[32,32,128]{2,1,0:T(8,128)(2,1)}), bf16[32,32,128]{2,1,0:T(8,128)(2,1)S(1)}, u32[]{:S(2)}, u32[]{:S(2)}) async-start(bf16[32,32,128]{2,1,0:T(8,128)(2,1)} %attend.1), calls=%async_computation.1 | async-start | bytes 524288 | tf_op jit(solution)/shard_map/all_to_all | solution.py:284
  59.8 9.8 %collective-permute-start.1 = (bf16[462,256]{1,0:T(8,128)(2,1)S(1)}, bf16[462,256]{1,0:T(8,128)(2,1)S(1)}, u32[]{:S(2)}, u32[]{:S(2)}) collective-permute-start(bf16[462,256]{1,0:T(8,128)(2,1)S(1)} %fusion.2), channel_id=1, source_target_pairs={{0,16},{16,0},{1,17},{17,1},{2,18},{18,2},{3,19},{19,3},{4,20},{20... | collective-permute-start | bytes 709640 | tf_op jit(solution)/shard_map/ppermute | solution.py:248
  80.0 22.2 %all-to-all-start.2 = ((bf16[32,24,128]{2,1,0:T(8,128)(2,1)}), bf16[32,24,128]{2,1,0:T(8,128)(2,1)S(1)}, u32[]{:S(2)}, u32[]{:S(2)}) async-start(bf16[32,24,128]{2,1,0:T(8,128)(2,1)} %get-tuple-element.23), calls=%async_computation.2 | async-start | bytes 393216 | tf_op jit(solution)/shard_map/all_to_all | solution.py:295
  86.3 15.9 %copy-start = (bf16[512,256]{1,0:T(8,128)(2,1)S(1)}, bf16[512,256]{1,0:T(8,128)(2,1)}, u32[]{:S(2)}) copy-start(bf16[512,256]{1,0:T(8,128)(2,1)} %w_ref.1) | copy-start | bytes 786436
  87.3 9.6 %collective-permute-start.2 = (bf16[462,256]{1,0:T(8,128)(2,1)S(1)}, bf16[462,256]{1,0:T(8,128)(2,1)S(1)}, u32[]{:S(2)}, u32[]{:S(2)}) collective-permute-start(bf16[462,256]{1,0:T(8,128)(2,1)S(1)} %get-tuple-element.37), channel_id=1, source_target_pairs={{0,16},{16,0},{1,17},{17,1},{2,18},{18,2},{3,19},{19,3},{4,20},{20... | collective-permute-start | bytes 709640 | tf_op jit(solution)/shard_map/ppermute | solution.py:248
  102.5 15.3 %copy-start.1 = (bf16[12,256]{1,0:T(8,128)(2,1)S(1)}, bf16[12,256]{1,0:T(8,128)(2,1)}, u32[]{:S(2)}) copy-start(bf16[12,256]{1,0:T(8,128)(2,1)} %residual_ref.1) | copy-start | bytes 18436
  118.5 14.1 %all-to-all-start.4 = ((bf16[32,12,256]{2,1,0:T(8,128)(2,1)}), bf16[32,12,256]{2,1,0:T(8,128)(2,1)S(1)}, u32[]{:S(2)}, u32[]{:S(2)}) async-start(bf16[32,12,256]{2,1,0:T(8,128)(2,1)} %get-tuple-element.26), calls=%async_computation.4 | async-start | bytes 524288 | tf_op jit(solution)/shard_map/all_to_all | solution.py:318
  123.8 0.9 copy-start.4
  133.3 11.6 %collective-permute-start.3 = (bf16[192,1024]{1,0:T(8,128)(2,1)S(1)}, bf16[192,1024]{1,0:T(8,128)(2,1)S(1)}, u32[]{:S(2)}, u32[]{:S(2)}) collective-permute-start(bf16[192,1024]{1,0:T(8,128)(2,1)S(1)} %get-tuple-element.31), channel_id=1, source_target_pairs={{0,32},{32,0},{1,33},{33,1},{2,34},{34,2},{3,35},{35,3},{4,36},{36... | collective-permute-start | bytes 1179656 | tf_op jit(solution)/shard_map/ppermute | solution.py:333
  144.9 5.4 %copy-start.2 = (bf16[1848,256]{1,0:T(8,128)(2,1)S(1)}, bf16[1848,256]{1,0:T(8,128)(2,1)}, u32[]{:S(2)}) copy-start(bf16[1848,256]{1,0:T(8,128)(2,1)} %param.23) | copy-start | bytes 2838532
  145.9 24.5 %all-to-all-start.5 = ((bf16[8,24,1024]{2,1,0:T(8,128)(2,1)}), bf16[8,24,1024]{2,1,0:T(8,128)(2,1)S(1)}, u32[]{:S(2)}, u32[]{:S(2)}) async-start(bf16[8,24,1024]{2,1,0:T(8,128)(2,1)} %join.1), calls=%async_computation.5 | async-start | bytes 786432 | tf_op jit(solution)/shard_map/all_to_all | solution.py:342
  150.7 13.6 %collective-permute-start.4 = (bf16[2,462,256]{2,1,0:T(8,128)(2,1)S(1)}, bf16[2,462,256]{2,1,0:T(8,128)(2,1)S(1)}, u32[]{:S(2)}, u32[]{:S(2)}) collective-permute-start(bf16[2,462,256]{2,1,0:T(8,128)(2,1)S(1)} %pad_maximum_fusion.3), channel_id=1, source_target_pairs={{0,16},{16,0},{1,17},{17,1},{2,18},{18,2},{3,19},{19,3},{4,20},{20... | collective-permute-start | bytes 1419272 | tf_op jit(solution)/shard_map/ppermute | solution.py:248
  171.4 27.8 %all-to-all-start.6 = ((bf16[16,24,462]{2,1,0:T(8,128)(2,1)}), bf16[16,24,462]{2,1,0:T(8,128)(2,1)S(1)}, u32[]{:S(2)}, u32[]{:S(2)}) async-start(bf16[16,24,462]{2,1,0:T(8,128)(2,1)} %hidden.1), calls=%async_computation.6 | async-start | bytes 786432 | tf_op jit(solution)/shard_map/all_to_all | solution.py:351
  200.3 20.2 %all-to-all-start.7 = ((bf16[32,12,256]{2,1,0:T(8,128)(2,1)}), bf16[32,12,256]{2,1,0:T(8,128)(2,1)S(1)}, u32[]{:S(2)}, u32[]{:S(2)}) async-start(bf16[32,12,256]{2,1,0:T(8,128)(2,1)} %down.1), calls=%async_computation.7 | async-start | bytes 524288 | tf_op jit(solution)/shard_map/all_to_all | solution.py:360

commit v10 on v9

--- a/solution.py
+++ b/solution.py
@@ -22,18 +22,7 @@
     return one, two, (rest - two).astype(BF16).astype(F32)
 
 
-def attend_kernel(
-    lengths, q_ref, k_hbm, v_hbm, sk_hbm, sv_hbm, out_ref, k_ref, v_ref, sk_ref, sv_ref, sems,
-    *, tokens, group, head, scale
-):
-    k_copy = pltpu.make_async_copy(k_hbm, k_ref, sems.at[0])
-    v_copy = pltpu.make_async_copy(v_hbm, v_ref, sems.at[1])
-    sk_copy = pltpu.make_async_copy(sk_hbm, sk_ref, sems.at[2])
-    sv_copy = pltpu.make_async_copy(sv_hbm, sv_ref, sems.at[3])
-    sk_copy.start()
-    sv_copy.start()
-    k_copy.start()
-    v_copy.start()
+def attend_kernel(lengths, q_ref, k_ref, v_ref, sk_ref, sv_ref, out_ref, *, tokens, group, head, scale):
     length = lengths[0]
     rows = tokens * group
     own = sk_ref.shape[0]
@@ -54,8 +43,6 @@
         w = jnp.exp2((s - top_new) * unit)
         return top_new, total * fade + jnp.sum(w, axis=0, keepdims=True), numer * fade + weigh(values, w)
 
-    sk_copy.wait()
-    sv_copy.wait()
     s = scores(sk_ref[...])
     token = lax.broadcasted_iota(jnp.int32, (own, rows), 1) // group
     place = first + lax.broadcasted_iota(jnp.int32, (own, rows), 0)
@@ -65,9 +52,6 @@
     w = jnp.where(seen, jnp.exp2((s - top) * unit), 0.0)
     total = jnp.sum(w, axis=0, keepdims=True)
     numer = weigh(sv_ref[...], w)
-    k_copy.wait()
-    v_copy.wait()
-
     def whole(step, carry):
         at = pl.ds(pl.multiple_of(step * SPAN, SPAN), SPAN)
         return add(carry, scores(k_ref[at, :]), v_ref[at, :])
@@ -260,21 +244,13 @@
     q_all, gate_y = beside(q_all, trade(gate_chunk))
     vmem = pl.BlockSpec(memory_space=pltpu.VMEM)
     smem = pl.BlockSpec(memory_space=pltpu.SMEM)
-    anywhere = pl.BlockSpec(memory_space=pl.ANY)
-    params = pltpu.CompilerParams(vmem_limit_bytes=60 * 2**20)
+    params = pltpu.CompilerParams(vmem_limit_bytes=40 * 2**20)
     small = pltpu.CompilerParams(vmem_limit_bytes=24 * 2**20)
     partial = pl.pallas_call(
         functools.partial(attend_kernel, tokens=tokens, group=group, head=head, scale=1.0 / math.sqrt(head)),
         out_shape=jax.ShapeDtypeStruct((n_ctx, each + 8, head), BF16),
-        in_specs=[smem, vmem] + [anywhere] * 4,
-        out_specs=vmem,
-        scratch_shapes=[
-            pltpu.VMEM((stretch, head), BF16),
-            pltpu.VMEM((stretch, head), BF16),
-            pltpu.VMEM(seg_keys.shape, BF16),
-            pltpu.VMEM(seg_values.shape, BF16),
-            pltpu.SemaphoreType.DMA((4,)),
-        ],
+        in_specs=[smem] + [vmem] * 5,
+        out_specs=vmem,
         compiler_params=params,
         cost_estimate=pl.CostEstimate(
             flops=4 * tokens * width * stretch, bytes_accessed=2**21, transcendentals=tokens * group * stretch
@@ -282,7 +258,7 @@
         name="attend",
     )(lengths, q_all, cache_keys[0], cache_values[0], seg_keys, seg_values)
     parts = lax.all_to_all(partial, ctx, 0, 0, tiled=True)
-    parts, up_y0 = beside(parts, trade(up_0))
+    (parts,) = beside(parts)
     attention, copies = pl.pallas_call(
         merge_kernel,
         out_shape=(jax.ShapeDtypeStruct((each, head), BF16), jax.ShapeDtypeStruct((n_ctx, each, head), BF16)),
@@ -293,7 +269,7 @@
     )(parts)
     attention = attention.reshape(rows, width)
     heads_all = lax.all_to_all(copies, ctx, 0, 0, tiled=True)
-    heads_all, up_y1 = beside(heads_all, trade(up_1))
+    heads_all, up_y0 = beside(heads_all, trade(up_0))
     mixed = pl.pallas_call(
         out_kernel,
         out_shape=jax.ShapeDtypeStruct((n_tp, trows, feats), BF16),
@@ -316,6 +292,7 @@
         name="stream",
     )(mixed, residual_stream)
     stream = lax.all_to_all(stream, ("hi", "tp"), 0, 0, tiled=True)
+    stream, up_y1 = beside(stream, trade(up_1))
 
     half = -(-(units + 3) // 128) * 128
     block = tokens // n_far

time: 222 us -> 221 us (level)
  blocking collectives: 15.3 us -> 31.9 us
  waiting for transfers between devices: 95.9 us -> 81.2 us
  starting transfers between devices: 87.6 us -> 84.6 us
    all_to_all x1, blocking collectives: 15.3 us -> 31.9 us  [per_device(): parts = lax.all_to_all(partial, ctx, 0, 0, tiled=True)]
    all_to_all x1, waiting for transfers between devices: 9.23 us -> 0.36 us  [per_device(): mixed = lax.all_to_all(mixed, 'tp', 0, 0, tiled=True)]
    ppermute x4, waiting for transfers between devices: 31.7 us -> 26.1 us  [trade(): return lambda place: lax.ppermute(part(place ^ 1), 'hi', [(0, 1), (1, 0)])]
    all_to_all x1, starting transfers between devices: 12.5 us -> 8.86 us  [per_device(): mixed = lax.all_to_all(mixed, 'tp', 0, 0, tiled=True)]
  transfers between devices with their start and end apart: 12 -> 12, of which waited for: 11 -> 10; matrix products, arithmetic and copies ran while one was open for 2% -> 2% of each run, Pallas kernels for 0% -> 0%
where the time goes in v10:
time: 221 us; the launch traced here: 220 us
  starting transfers between devices  84.6 us (38%)
  waiting for transfers between devices  81.2 us (37%)
  blocking collectives  31.9 us (14%)
  Pallas kernels  12.9 us (6%)
  local copies, waits for them, and re-layouts  3.97 us (2%)
  other arithmetic  3.64 us (2%)
    all_to_all x1, blocking collectives, per_device(): parts = lax.all_to_all(partial, ctx, 0, 0, tiled=True)  31.9 us
    ppermute x4, waiting for transfers between devices, trade(): return lambda place: lax.ppermute(part(place ^ 1), 'hi', [(0, 1), (1, 0)])  26.1 us
    all_to_all x1, starting transfers between devices, per_device(): q_all = lax.all_to_all(q_all, ctx, 0, 0, tiled=True)  18.7 us
    all_to_all x1, waiting for transfers between devices, per_device(): hidden = lax.all_to_all(hidden, ('far', 'lo'), 0, 0, tiled=True)  17.6 us
    ppermute x4, starting transfers between devices, trade(): return lambda place: lax.ppermute(part(place ^ 1), 'hi', [(0, 1), (1, 0)])  17.6 us
    all_to_all x1, starting transfers between devices, per_device(): lowered = lax.all_to_all(lowered, ('hi', 'tp'), 0, 0, tiled=True)  11.5 us
    all_to_all x1, starting transfers between devices, per_device(): hidden = lax.all_to_all(hidden, ('far', 'lo'), 0, 0, tiled=True)  10.3 us
    ppermute x1, waiting for transfers between devices, per_device(): got = lax.ppermute(send, 'lo', [(0, 1), (1, 0)])  9.64 us
  transfers between devices with their start and end apart: 12, of which 10 were waited for; matrix products, arithmetic and copies ran while one was open for 2% of the time, Pallas kernels for 0%

profile of v10, /device:TPU:1, one launch (start us, length us, event | category | flops | bytes accessed | tf_op | source)
XLA Modules:
  0.0 219.8 jit_solution(15653960950318089472)
XLA Ops:
  0.6 0.7 broadcast_in_dim.4
  1.3 0.7 broadcast_in_dim.5
  2.0 18.7 %all-to-all-start = ((bf16[32,24,128]{2,1,0:T(8,128)(2,1)}), bf16[32,24,128]{2,1,0:T(8,128)(2,1)S(1)}, u32[]{:S(2)}, u32[]{:S(2)}) async-start(bf16[32,24,128]{2,1,0:T(8,128)(2,1)} %broadcast_in_dim.5), calls=%async_computation | async-start | bytes 393216 | tf_op jit(solution)/shard_map/all_to_all | solution.py:243
  20.7 0.0 copy-start.11
  20.7 0.7 copy-done.11
  21.4 2.3 %fusion.4 = (bf16[1,462,256]{2,1,0:T(8,128)(2,1)S(1)}, bf16[1,462,256]{2,1,0:T(8,128)(2,1)S(1)}, bf16[1,462,256]{2,1,0:T(8,128)(2,1)S(1)}, bf16[1,462,256]{2,1,0:T(8,128)(2,1)}) fusion(bf16[256,1848]{0,1:T(8,128)(2,1)} %param.21, s32[]{:T(128)S(6)} %select_n.32, f32[256]{0:T(256)S(1)} %copy-done.11, s32[]{:T(128)S(6)} %select_n.29, s32[]{:T(128)S(6)} %select_n.28, ...), kind=kLoop, calls=%fused_computation.17 | loop fusion | flops 1419264 | bytes 1893392 | tf_op jit(solution)/shard_map/stack | solution.py:220
  23.8 4.8 %collective-permute-start = (bf16[2,462,256]{2,1,0:T(8,128)(2,1)S(1)}, bf16[2,462,256]{2,1,0:T(8,128)(2,1)S(1)}, u32[]{:S(2)}, u32[]{:S(2)}) collective-permute-start(bf16[2,462,256]{2,1,0:T(8,128)(2,1)S(1)} %pad_maximum_fusion), channel_id=1, source_target_pairs={{0,16},{16,0},{1,17},{17,1},{2,18},{18,2},{3,19},{19,3},{4,20},{20... | collective-permute-start | bytes 1419272 | tf_op jit(solution)/shard_map/ppermute | solution.py:232
  28.6 0.0 copy-start.5
  29.2 0.0 copy-start.4
  29.3 10.9 %collective-permute-done.gate_y_ref = bf16[2,462,256]{2,1,0:T(8,128)(2,1)S(1)} collective-permute-done((bf16[2,462,256]{2,1,0:T(8,128)(2,1)S(1)}, bf16[2,462,256]{2,1,0:T(8,128)(2,1)S(1)}, u32[]{:S(2)}, u32[]{:S(2)}) %collective-permute-start) | collective-permute-done | bytes 473120 | tf_op jit(solution)/shard_map/ppermute | solution.py:232
  40.1 0.0 all-to-all-done.q_ref
  40.2 5.8 %attend.1 = bf16[32,32,128]{2,1,0:T(8,128)(2,1)S(1)} custom-call(s32[1]{0:T(128)S(6)} %copy.14.lengths, bf16[32,24,128]{2,1,0:T(8,128)(2,1)S(1)} %all-to-all-done.q_ref, bf16[3072,128]{1,0:T(8,128)(2,1)S(1)} %bitcast.38, bf16[3072,128]{1,0:T(8,128)(2,1)S(1)} %bitcast.39, bf16[6,128]{1,0:T(8,128)(2,1)S(1)} %copy-done.4, bf16[6,128]{1,0:T(8,128)(2,1)S(1)} %copy-done.5), custom_call_target="tpu_custom_call" | custom-call | flops 1207959552 | bytes 2097152 | tf_op jit(solution)/shard_map/attend/pallas_call | solution.py:249
  45.9 0.0 copy-start.7
  46.0 31.9 %all_to_all.40.in_ref = bf16[32,32,128]{2,1,0:T(8,128)(2,1)S(1)} all-to-all(bf16[32,32,128]{2,1,0:T(8,128)(2,1)S(1)} %attend.1), channel_id=1, replica_groups=mesh['far'=8,'lo'=2,'hi'=2,'tp'=16] {'far','lo','hi'}, dimensions={0} | all-to-all | bytes 524288 | tf_op jit(solution)/shard_map/all_to_all | solution.py:260
  77.9 1.1 merge.1
  79.0 6.3 %all-to-all-start.2 = ((bf16[32,24,128]{2,1,0:T(8,128)(2,1)}), bf16[32,24,128]{2,1,0:T(8,128)(2,1)S(1)}, u32[]{:S(2)}, u32[]{:S(2)}) async-start(bf16[32,24,128]{2,1,0:T(8,128)(2,1)} %get-tuple-element.25), calls=%async_computation.2 | async-start | bytes 393216 | tf_op jit(solution)/shard_map/all_to_all | solution.py:271
  85.3 0.0 copy-start
  85.4 0.1 fusion.2
  85.5 4.6 %collective-permute-start.1 = (bf16[462,256]{1,0:T(8,128)(2,1)S(1)}, bf16[462,256]{1,0:T(8,128)(2,1)S(1)}, u32[]{:S(2)}, u32[]{:S(2)}) collective-permute-start(bf16[462,256]{1,0:T(8,128)(2,1)S(1)} %fusion.2), channel_id=1, source_target_pairs={{0,16},{16,0},{1,17},{17,1},{2,18},{18,2},{3,19},{19,3},{4,20},{20... | collective-permute-start | bytes 709640 | tf_op jit(solution)/shard_map/ppermute | solution.py:232
  90.1 5.0 %collective-permute-done.1.up_y0_ref = bf16[462,256]{1,0:T(8,128)(2,1)S(1)} collective-permute-done((bf16[462,256]{1,0:T(8,128)(2,1)S(1)}, bf16[462,256]{1,0:T(8,128)(2,1)S(1)}, u32[]{:S(2)}, u32[]{:S(2)}) %collective-permute-start.1) | collective-permute-done | bytes 236576 | tf_op jit(solution)/shard_map/ppermute | solution.py:232
  95.1 6.3 %all-to-all-done.2.h_ref = bf16[32,24,128]{2,1,0:T(8,128)(2,1)S(1)} async-done(((bf16[32,24,128]{2,1,0:T(8,128)(2,1)}), bf16[32,24,128]{2,1,0:T(8,128)(2,1)S(1)}, u32[]{:S(2)}, u32[]{:S(2)}) %all-to-all-start.2) | async-done | bytes 196640 | tf_op jit(solution)/shard_map/all_to_all | solution.py:271
  101.4 0.9 out.1
  102.3 8.9 %all-to-all-start.3 = ((bf16[16,12,256]{2,1,0:T(8,128)(2,1)}), bf16[16,12,256]{2,1,0:T(8,128)(2,1)S(1)}, u32[]{:S(2)}, u32[]{:S(2)}) async-start(bf16[16,12,256]{2,1,0:T(8,128)(2,1)} %out.1), calls=%async_computation.3 | async-start | bytes 262144 | tf_op jit(solution)/shard_map/all_to_all | solution.py:282
  111.2 1.0 fusion.6
  112.2 4.8 %collective-permute-start.2 = (bf16[462,256]{1,0:T(8,128)(2,1)}, bf16[462,256]{1,0:T(8,128)(2,1)S(1)}, u32[]{:S(2)}, u32[]{:S(2)}) collective-permute-start(bf16[462,256]{1,0:T(8,128)(2,1)} %get-tuple-element.41), channel_id=1, source_target_pairs={{0,16},{16,0},{1,17},{17,1},{2,18},{18,2},{3,19},{19,3},{4,20},{20... | collective-permute-start | bytes 709640 | tf_op jit(solution)/shard_map/ppermute | solution.py:232
  117.0 0.4 all-to-all-done.3.in_ref
  117.3 0.7 stream.1
  118.1 5.7 %all-to-all-start.4 = ((bf16[32,12,256]{2,1,0:T(8,128)(2,1)}), bf16[32,12,256]{2,1,0:T(8,128)(2,1)S(1)}, u32[]{:S(2)}, u32[]{:S(2)}) async-start(bf16[32,12,256]{2,1,0:T(8,128)(2,1)} %get-tuple-element.28), calls=%async_computation.4 | async-start | bytes 524288 | tf_op jit(solution)/shard_map/all_to_all | solution.py:294
  123.9 0.9 copy-done.9
  124.8 0.1 copy-done.10
  124.9 7.7 %all-to-all-done.4.x_ref = bf16[32,12,256]{2,1,0:T(8,128)(2,1)S(1)} async-done(((bf16[32,12,256]{2,1,0:T(8,128)(2,1)}), bf16[32,12,256]{2,1,0:T(8,128)(2,1)S(1)}, u32[]{:S(2)}, u32[]{:S(2)}) %all-to-all-start.4) | async-done | bytes 196640 | tf_op jit(solution)/shard_map/all_to_all | solution.py:294
  132.7 0.7 project.1
  133.4 1.9 collective-permute-start.3
  135.3 9.6 %collective-permute-done.3.got_ref = bf16[192,1024]{1,0:T(8,128)(2,1)S(1)} collective-permute-done((bf16[192,1024]{1,0:T(8,128)(2,1)S(1)}, bf16[192,1024]{1,0:T(8,128)(2,1)S(1)}, u32[]{:S(2)}, u32[]{:S(2)}) %collective-permute-start.3) | collective-permute-done | bytes 393248 | tf_op jit(solution)/shard_map/ppermute | solution.py:310
  145.0 1.0 join.1
  146.0 3.6 %all-to-all-start.5 = ((bf16[8,24,1024]{2,1,0:T(8,128)(2,1)}), bf16[8,24,1024]{2,1,0:T(8,128)(2,1)S(1)}, u32[]{:S(2)}, u32[]{:S(2)}) async-start(bf16[8,24,1024]{2,1,0:T(8,128)(2,1)} %join.1), calls=%async_computation.5 | async-start | bytes 786432 | tf_op jit(solution)/shard_map/all_to_all | solution.py:319
  149.6 0.2 dynamic-slice_bitcast_fusion.1
  149.9 3.4 %collective-permute-start.4 = (bf16[2,462,256]{2,1,0:T(8,128)(2,1)S(1)}, bf16[2,462,256]{2,1,0:T(8,128)(2,1)S(1)}, u32[]{:S(2)}, u32[]{:S(2)}) collective-permute-start(bf16[2,462,256]{2,1,0:T(8,128)(2,1)S(1)} %pad_maximum_fusion.3), channel_id=1, source_target_pairs={{0,16},{16,0},{1,17},{17,1},{2,18},{18,2},{3,19},{19,3},{4,20},{20... | collective-permute-start | bytes 1419272 | tf_op jit(solution)/shard_map/ppermute | solution.py:232
  153.3 10.3 %collective-permute-done.4.wy_ref = bf16[2,462,256]{2,1,0:T(8,128)(2,1)S(1)} collective-permute-done((bf16[2,462,256]{2,1,0:T(8,128)(2,1)S(1)}, bf16[2,462,256]{2,1,0:T(8,128)(2,1)S(1)}, u32[]{:S(2)}, u32[]{:S(2)}) %collective-permute-start.4) | collective-permute-done | bytes 473120 | tf_op jit(solution)/shard_map/ppermute | solution.py:232
  163.5 5.2 %all-to-all-done.5.in_ref = bf16[8,24,1024]{2,1,0:T(8,128)(2,1)S(1)} async-done(((bf16[8,24,1024]{2,1,0:T(8,128)(2,1)}), bf16[8,24,1024]{2,1,0:T(8,128)(2,1)S(1)}, u32[]{:S(2)}, u32[]{:S(2)}) %all-to-all-start.5) | async-done | bytes 393248 | tf_op jit(solution)/shard_map/all_to_all | solution.py:319
  168.7 0.9 hidden.1
  169.6 10.3 %all-to-all-start.6 = ((bf16[16,24,462]{2,1,0:T(8,128)(2,1)}), bf16[16,24,462]{2,1,0:T(8,128)(2,1)S(1)}, u32[]{:S(2)}, u32[]{:S(2)}) async-start(bf16[16,24,462]{2,1,0:T(8,128)(2,1)} %hidden.1), calls=%async_computation.6 | async-start | bytes 786432 | tf_op jit(solution)/shard_map/all_to_all | solution.py:328
  180.0 17.6 %all-to-all-done.6.h_ref = bf16[16,24,462]{2,1,0:T(8,128)(2,1)S(1)} async-done(((bf16[16,24,462]{2,1,0:T(8,128)(2,1)}), bf16[16,24,462]{2,1,0:T(8,128)(2,1)S(1)}, u32[]{:S(2)}, u32[]{:S(2)}) %all-to-all-start.6) | async-done | bytes 354848 | tf_op jit(solution)/shard_map/all_to_all | solution.py:328
  197.7 1.1 down.1
  198.7 11.5 %all-to-all-start.7 = ((bf16[32,12,256]{2,1,0:T(8,128)(2,1)}), bf16[32,12,256]{2,1,0:T(8,128)(2,1)S(1)}, u32[]{:S(2)}, u32[]{:S(2)}) async-start(bf16[32,12,256]{2,1,0:T(8,128)(2,1)} %down.1), calls=%async_computation.7 | async-start | bytes 524288 | tf_op jit(solution)/shard_map/all_to_all | solution.py:337
  210.2 0.6 reshape.10
  210.9 8.2 %all-to-all-done.7.in_ref = bf16[32,12,256]{2,1,0:T(8,128)(2,1)S(1)} async-done(((bf16[32,12,256]{2,1,0:T(8,128)(2,1)}), bf16[32,12,256]{2,1,0:T(8,128)(2,1)S(1)}, u32[]{:S(2)}, u32[]{:S(2)}) %all-to-all-start.7) | async-done | bytes 196640 | tf_op jit(solution)/shard_map/all_to_all | solution.py:337
  219.1 0.7 last.1
  (22 shorter events, 0.3 us)
Async XLA Ops:
  2.0 38.1 %all-to-all-start = ((bf16[32,24,128]{2,1,0:T(8,128)(2,1)}), bf16[32,24,128]{2,1,0:T(8,128)(2,1)S(1)}, u32[]{:S(2)}, u32[]{:S(2)}) async-start(bf16[32,24,128]{2,1,0:T(8,128)(2,1)} %broadcast_in_dim.5), calls=%async_computation | async-start | bytes 393216 | tf_op jit(solution)/shard_map/all_to_all | solution.py:243
  20.7 0.7 copy-start.11
  21.4 18.7 %copy-start.3 = (bf16[1,3072,128]{2,1,0:T(8,128)(2,1)S(1)}, bf16[1,3072,128]{2,1,0:T(8,128)(2,1)}, u32[]{:S(2)}) copy-start(bf16[1,3072,128]{2,1,0:T(8,128)(2,1)} %param.14) | copy-start | bytes 2359300
  23.7 16.4 %copy-start.2 = (bf16[1,3072,128]{2,1,0:T(8,128)(2,1)S(1)}, bf16[1,3072,128]{2,1,0:T(8,128)(2,1)}, u32[]{:S(2)}) copy-start(bf16[1,3072,128]{2,1,0:T(8,128)(2,1)} %param.13) | copy-start | bytes 2359300
  23.8 16.3 %collective-permute-start = (bf16[2,462,256]{2,1,0:T(8,128)(2,1)S(1)}, bf16[2,462,256]{2,1,0:T(8,128)(2,1)S(1)}, u32[]{:S(2)}, u32[]{:S(2)}) collective-permute-start(bf16[2,462,256]{2,1,0:T(8,128)(2,1)S(1)} %pad_maximum_fusion), channel_id=1, source_target_pairs={{0,16},{16,0},{1,17},{17,1},{2,18},{18,2},{3,19},{19,3},{4,20},{20... | collective-permute-start | bytes 1419272 | tf_op jit(solution)/shard_map/ppermute | solution.py:232
  28.6 11.6 %copy-start.5 = (bf16[6,128]{1,0:T(8,128)(2,1)S(1)}, bf16[6,128]{1,0:T(8,128)(2,1)}, u32[]{:S(2)}) copy-start(bf16[6,128]{1,0:T(8,128)(2,1)} %sv_ref.1) | copy-start | bytes 4612
  29.2 10.9 %copy-start.4 = (bf16[6,128]{1,0:T(8,128)(2,1)S(1)}, bf16[6,128]{1,0:T(8,128)(2,1)}, u32[]{:S(2)}) copy-start(bf16[6,128]{1,0:T(8,128)(2,1)} %sk_ref.1) | copy-start | bytes 4612
  45.9 39.4 %copy-start.7 = (bf16[256,1848]{0,1:T(8,128)(2,1)S(1)}, bf16[256,1848]{0,1:T(8,128)(2,1)}, u32[]{:S(2)}) copy-start(bf16[256,1848]{0,1:T(8,128)(2,1)} %param.22) | copy-start | bytes 2838532
  79.0 22.4 %all-to-all-start.2 = ((bf16[32,24,128]{2,1,0:T(8,128)(2,1)}), bf16[32,24,128]{2,1,0:T(8,128)(2,1)S(1)}, u32[]{:S(2)}, u32[]{:S(2)}) async-start(bf16[32,24,128]{2,1,0:T(8,128)(2,1)} %get-tuple-element.25), calls=%async_computation.2 | async-start | bytes 393216 | tf_op jit(solution)/shard_map/all_to_all | solution.py:271
  85.3 16.0 %copy-start = (bf16[512,256]{1,0:T(8,128)(2,1)S(1)}, bf16[512,256]{1,0:T(8,128)(2,1)}, u32[]{:S(2)}) copy-start(bf16[512,256]{1,0:T(8,128)(2,1)} %w_ref.1) | copy-start | bytes 786436
  85.5 9.6 %collective-permute-start.1 = (bf16[462,256]{1,0:T(8,128)(2,1)S(1)}, bf16[462,256]{1,0:T(8,128)(2,1)S(1)}, u32[]{:S(2)}, u32[]{:S(2)}) collective-permute-start(bf16[462,256]{1,0:T(8,128)(2,1)S(1)} %fusion.2), channel_id=1, source_target_pairs={{0,16},{16,0},{1,17},{17,1},{2,18},{18,2},{3,19},{19,3},{4,20},{20... | collective-permute-start | bytes 709640 | tf_op jit(solution)/shard_map/ppermute | solution.py:232
  102.3 15.0 %all-to-all-start.3 = ((bf16[16,12,256]{2,1,0:T(8,128)(2,1)}), bf16[16,12,256]{2,1,0:T(8,128)(2,1)S(1)}, u32[]{:S(2)}, u32[]{:S(2)}) async-start(bf16[16,12,256]{2,1,0:T(8,128)(2,1)} %out.1), calls=%async_computation.3 | async-start | bytes 262144 | tf_op jit(solution)/shard_map/all_to_all | solution.py:282
  111.2 6.2 %copy-start.1 = (bf16[12,256]{1,0:T(8,128)(2,1)S(1)}, bf16[12,256]{1,0:T(8,128)(2,1)}, u32[]{:S(2)}) copy-start(bf16[12,256]{1,0:T(8,128)(2,1)} %residual_ref.1) | copy-start | bytes 18436
  112.2 12.8 %collective-permute-start.2 = (bf16[462,256]{1,0:T(8,128)(2,1)}, bf16[462,256]{1,0:T(8,128)(2,1)S(1)}, u32[]{:S(2)}, u32[]{:S(2)}) collective-permute-start(bf16[462,256]{1,0:T(8,128)(2,1)} %get-tuple-element.41), channel_id=1, source_target_pairs={{0,16},{16,0},{1,17},{17,1},{2,18},{18,2},{3,19},{19,3},{4,20},{20... | collective-permute-start | bytes 709640 | tf_op jit(solution)/shard_map/ppermute | solution.py:232
  118.1 5.8 %copy-start.8 = (bf16[1,462,256]{2,1,0:T(8,128)(2,1)S(1)}, bf16[1,462,256]{2,1,0:T(8,128)(2,1)}, u32[]{:S(2)}) copy-start(bf16[1,462,256]{2,1,0:T(8,128)(2,1)} %get-tuple-element.46) | copy-start | bytes 709636
  118.1 14.6 %all-to-all-start.4 = ((bf16[32,12,256]{2,1,0:T(8,128)(2,1)}), bf16[32,12,256]{2,1,0:T(8,128)(2,1)S(1)}, u32[]{:S(2)}, u32[]{:S(2)}) async-start(bf16[32,12,256]{2,1,0:T(8,128)(2,1)} %get-tuple-element.28), calls=%async_computation.4 | async-start | bytes 524288 | tf_op jit(solution)/shard_map/all_to_all | solution.py:294
  123.8 0.9 copy-start.9
  123.8 1.0 copy-start.10
  133.4 11.6 %collective-permute-start.3 = (bf16[192,1024]{1,0:T(8,128)(2,1)S(1)}, bf16[192,1024]{1,0:T(8,128)(2,1)S(1)}, u32[]{:S(2)}, u32[]{:S(2)}) collective-permute-start(bf16[192,1024]{1,0:T(8,128)(2,1)S(1)} %get-tuple-element.35), channel_id=1, source_target_pairs={{0,32},{32,0},{1,33},{33,1},{2,34},{34,2},{3,35},{35,3},{4,36},{36... | collective-permute-start | bytes 1179656 | tf_op jit(solution)/shard_map/ppermute | solution.py:310
  145.0 4.6 %copy-start.6 = (bf16[1848,256]{1,0:T(8,128)(2,1)S(1)}, bf16[1848,256]{1,0:T(8,128)(2,1)}, u32[]{:S(2)}) copy-start(bf16[1848,256]{1,0:T(8,128)(2,1)} %param.23) | copy-start | bytes 2838532
  146.0 22.7 %all-to-all-start.5 = ((bf16[8,24,1024]{2,1,0:T(8,128)(2,1)}), bf16[8,24,1024]{2,1,0:T(8,128)(2,1)S(1)}, u32[]{:S(2)}, u32[]{:S(2)}) async-start(bf16[8,24,1024]{2,1,0:T(8,128)(2,1)} %join.1), calls=%async_computation.5 | async-start | bytes 786432 | tf_op jit(solution)/shard_map/all_to_all | solution.py:319
  149.9 13.6 %collective-permute-start.4 = (bf16[2,462,256]{2,1,0:T(8,128)(2,1)S(1)}, bf16[2,462,256]{2,1,0:T(8,128)(2,1)S(1)}, u32[]{:S(2)}, u32[]{:S(2)}) collective-permute-start(bf16[2,462,256]{2,1,0:T(8,128)(2,1)S(1)} %pad_maximum_fusion.3), channel_id=1, source_target_pairs={{0,16},{16,0},{1,17},{17,1},{2,18},{18,2},{3,19},{19,3},{4,20},{20... | collective-permute-start | bytes 1419272 | tf_op jit(solution)/shard_map/ppermute | solution.py:232
  169.6 28.0 %all-to-all-start.6 = ((bf16[16,24,462]{2,1,0:T(8,128)(2,1)}), bf16[16,24,462]{2,1,0:T(8,128)(2,1)S(1)}, u32[]{:S(2)}, u32[]{:S(2)}) async-start(bf16[16,24,462]{2,1,0:T(8,128)(2,1)} %hidden.1), calls=%async_computation.6 | async-start | bytes 786432 | tf_op jit(solution)/shard_map/all_to_all | solution.py:328
  198.7 20.4 %all-to-all-start.7 = ((bf16[32,12,256]{2,1,0:T(8,128)(2,1)}), bf16[32,12,256]{2,1,0:T(8,128)(2,1)S(1)}, u32[]{:S(2)}, u32[]{:S(2)}) async-start(bf16[32,12,256]{2,1,0:T(8,128)(2,1)} %down.1), calls=%async_computation.7 | async-start | bytes 524288 | tf_op jit(solution)/shard_map/all_to_all | solution.py:337

commit v11 on v10

--- a/solution.py
+++ b/solution.py
@@ -119,7 +119,9 @@
     out_ref[...] = (own_ref[...].astype(F32) + jnp.sum(in_ref[...].astype(F32), axis=0)).astype(BF16)
 
 
-def project_kernel(x_ref, gate_ref, gate_y_ref, up_ref, up_y0_ref, up_y1_ref, send_ref, keep_ref):
+def project_kernel(
+    x_ref, gate_ref, gate_y0_ref, gate_y1_ref, up_ref, up_y0_ref, up_y1_ref, send_ref, keep_ref
+):
     units = gate_ref.shape[1]
     each = x_ref.shape[0] // 2
     half = keep_ref.shape[1] // 2
@@ -138,7 +140,7 @@
     tokens = squares.shape[0]
     spare = half - units
     for at, ref in ((1 - lo, send_ref), (lo, keep_ref)):
-        gate = product(gate_ref[at], gate_y_ref[at])
+        gate = product(gate_ref[at], jnp.where(at == 0, gate_y0_ref[...], gate_y1_ref[...]))
         up = product(up_ref[at], jnp.where(at == 0, up_y0_ref[...], up_y1_ref[...]))
         ref[:, :half] = jnp.concatenate([gate, *parts, jnp.zeros((tokens, spare - 3), F32)], axis=1).astype(ref.dtype)
         ref[:, half:] = jnp.concatenate([up, jnp.zeros((tokens, spare), F32)], axis=1).astype(ref.dtype)
@@ -216,8 +218,11 @@
     def scaled(w, lo, place):
         return (piece(w.T, lo, place).astype(F32) * norm_gain).astype(BF16)
 
-    def gate_chunk(place):
-        return jnp.stack([scaled(gate_weight, lo, place) for lo in range(2)])
+    def gate_0(place):
+        return scaled(gate_weight, 0, place)
+
+    def gate_1(place):
+        return scaled(gate_weight, 1, place)
 
     def up_0(place):
         return scaled(up_weight, 0, place)
@@ -241,7 +246,11 @@
     each = rows * group
     q_all = jnp.broadcast_to(queries.reshape(1, each, head), (n_ctx, each, head))
     q_all = lax.all_to_all(q_all, ctx, 0, 0, tiled=True)
-    q_all, gate_y = beside(q_all, trade(gate_chunk))
+    own_gate = jnp.stack([gate_0(near), gate_1(near)])
+    own_up = jnp.stack([up_0(near), up_1(near)])
+    own_gate, own_up, gate_y0, q_all, place = lax.optimization_barrier(
+        (own_gate, own_up, trade(gate_0)(place), q_all, place)
+    )
     vmem = pl.BlockSpec(memory_space=pltpu.VMEM)
     smem = pl.BlockSpec(memory_space=pltpu.SMEM)
     params = pltpu.CompilerParams(vmem_limit_bytes=40 * 2**20)
@@ -258,7 +267,7 @@
         name="attend",
     )(lengths, q_all, cache_keys[0], cache_values[0], seg_keys, seg_values)
     parts = lax.all_to_all(partial, ctx, 0, 0, tiled=True)
-    (parts,) = beside(parts)
+    parts, up_y1 = beside(parts, trade(up_1))
     attention, copies = pl.pallas_call(
         merge_kernel,
         out_shape=(jax.ShapeDtypeStruct((each, head), BF16), jax.ShapeDtypeStruct((n_ctx, each, head), BF16)),
@@ -269,7 +278,7 @@
     )(parts)
     attention = attention.reshape(rows, width)
     heads_all = lax.all_to_all(copies, ctx, 0, 0, tiled=True)
-    heads_all, up_y0 = beside(heads_all, trade(up_0))
+    heads_all, gate_y1 = beside(heads_all, trade(gate_1))
     mixed = pl.pallas_call(
         out_kernel,
         out_shape=jax.ShapeDtypeStruct((n_tp, trows, feats), BF16),
@@ -292,7 +301,7 @@
         name="stream",
     )(mixed, residual_stream)
     stream = lax.all_to_all(stream, ("hi", "tp"), 0, 0, tiled=True)
-    stream, up_y1 = beside(stream, trade(up_1))
+    stream, up_y0 = beside(stream, trade(up_0))
 
     half = -(-(units + 3) // 128) * 128
     block = tokens // n_far
@@ -302,11 +311,11 @@
             jax.ShapeDtypeStruct((tokens, 2 * half), BF16),
             jax.ShapeDtypeStruct((tokens, 2 * half), F32),
         ),
-        in_specs=[vmem] * 6,
+        in_specs=[vmem] * 7,
         out_specs=(vmem, vmem),
         compiler_params=small,
         name="project",
-    )(stream, gate_chunk(near), gate_y, jnp.stack([up_0(near), up_1(near)]), up_y0, up_y1)
+    )(stream, own_gate, gate_y0, gate_y1, own_up, up_y0, up_y1)
     got = lax.ppermute(send, "lo", [(0, 1), (1, 0)])
     sums = pl.pallas_call(
         functools.partial(join_kernel, units=units),

time: 221 us -> 216 us (0.977)
  blocking collectives: 31.9 us -> 0 us
  starting transfers between devices: 84.6 us -> 99.3 us
  waiting for transfers between devices: 81.2 us -> 94 us
    all_to_all x1 -> x0, blocking collectives: 31.9 us -> none  [per_device(): parts = lax.all_to_all(partial, ctx, 0, 0, tiled=True)]
    all_to_all x0 -> x1, starting transfers between devices: none -> 9.65 us  [per_device(): parts = lax.all_to_all(partial, ctx, 0, 0, tiled=True)]
    all_to_all x0 -> x1, waiting for transfers between devices: none -> 8.4 us  [per_device(): parts = lax.all_to_all(partial, ctx, 0, 0, tiled=True)]
    convert_element_type x1 -> x4, other arithmetic: 0.08 us -> 4.84 us  [scaled(): return (piece(w.T, lo, place).astype(F32) * norm_gain).astype(BF16)]
    ppermute x4 -> x5, starting transfers between devices: 17.6 us -> 21.8 us  [trade(): return lambda place: lax.ppermute(part(place ^ 1), 'hi', [(0, 1), (1, 0)])]
    all_to_all x1, waiting for transfers between devices: 0.01 us -> 3.82 us  [per_device(): q_all = lax.all_to_all(q_all, ctx, 0, 0, tiled=True)]
    another operation x5 -> x1, other arithmetic: 3.47 us -> 0.09 us  [per_device(): own_gate = jnp.stack([gate_0(near), gate_1(near)])]
    ppermute x4 -> x5, waiting for transfers between devices: 26.1 us -> 25.3 us  [trade(): return lambda place: lax.ppermute(part(place ^ 1), 'hi', [(0, 1), (1, 0)])]
  transfers between devices with their start and end apart: 12 -> 14, of which waited for: 10 -> 14; matrix products, arithmetic and copies ran while one was open for 2% -> 3% of each run, Pallas kernels for 0% -> 0%
where the time goes in v11:
time: 216 us; the launch traced here: 215 us
  starting transfers between devices  99.3 us (46%)
  waiting for transfers between devices  94 us (44%)
  Pallas kernels  11.1 us (5%)
  other arithmetic  5.02 us (2%)
  local copies, waits for them, and re-layouts  3.65 us (2%)
    ppermute x5, waiting for transfers between devices, trade(): return lambda place: lax.ppermute(part(place ^ 1), 'hi', [(0, 1), (1, 0)])  25.3 us
    ppermute x5, starting transfers between devices, trade(): return lambda place: lax.ppermute(part(place ^ 1), 'hi', [(0, 1), (1, 0)])  21.8 us
    all_to_all x1, starting transfers between devices, per_device(): q_all = lax.all_to_all(q_all, ctx, 0, 0, tiled=True)  18.7 us
    all_to_all x1, waiting for transfers between devices, per_device(): hidden = lax.all_to_all(hidden, ('far', 'lo'), 0, 0, tiled=True)  17.8 us
    all_to_all x1, starting transfers between devices, per_device(): lowered = lax.all_to_all(lowered, ('hi', 'tp'), 0, 0, tiled=True)  11.3 us
    all_to_all x1, starting transfers between devices, per_device(): hidden = lax.all_to_all(hidden, ('far', 'lo'), 0, 0, tiled=True)  9.95 us
    all_to_all x1, starting transfers between devices, per_device(): parts = lax.all_to_all(partial, ctx, 0, 0, tiled=True)  9.65 us
    ppermute x1, waiting for transfers between devices, per_device(): got = lax.ppermute(send, 'lo', [(0, 1), (1, 0)])  9.64 us
  transfers between devices with their start and end apart: 14, of which 14 were waited for; matrix products, arithmetic and copies ran while one was open for 3% of the time, Pallas kernels for 0%

profile of v11, /device:TPU:1, one launch (start us, length us, event | category | flops | bytes accessed | tf_op | source)
XLA Modules:
  0.0 214.6 jit_solution(14533204901864350104)
XLA Ops:
  0.6 0.7 broadcast_in_dim.4
  1.3 0.7 broadcast_in_dim.5
  2.0 18.7 %all-to-all-start = ((bf16[32,24,128]{2,1,0:T(8,128)(2,1)}), bf16[32,24,128]{2,1,0:T(8,128)(2,1)S(1)}, u32[]{:S(2)}, u32[]{:S(2)}) async-start(bf16[32,24,128]{2,1,0:T(8,128)(2,1)} %broadcast_in_dim.5), calls=%async_computation | async-start | bytes 393216 | tf_op jit(solution)/shard_map/all_to_all | solution.py:248
  20.7 0.7 copy-done.7
  21.4 1.7 fusion.4
  23.1 4.6 %collective-permute-start = (bf16[462,256]{1,0:T(8,128)(2,1)S(1)}, bf16[462,256]{1,0:T(8,128)(2,1)S(1)}, u32[]{:S(2)}, u32[]{:S(2)}) collective-permute-start(bf16[462,256]{1,0:T(8,128)(2,1)S(1)} %get-tuple-element.46), channel_id=1, source_target_pairs={{0,16},{16,0},{1,17},{17,1},{2,18},{18,2},{3,19},{19,3},{4,20},{20... | collective-permute-start | bytes 709640 | tf_op jit(solution)/shard_map/ppermute | solution.py:237
  28.5 0.1 pad_maximum_fusion
  28.6 5.5 %collective-permute-done.gate_y0_ref = bf16[462,256]{1,0:T(8,128)(2,1)S(1)} collective-permute-done((bf16[462,256]{1,0:T(8,128)(2,1)S(1)}, bf16[462,256]{1,0:T(8,128)(2,1)S(1)}, u32[]{:S(2)}, u32[]{:S(2)}) %collective-permute-start) | collective-permute-done | bytes 236576 | tf_op jit(solution)/shard_map/ppermute | solution.py:237
  34.0 3.8 %all-to-all-done.q_ref = bf16[32,24,128]{2,1,0:T(8,128)(2,1)S(1)} async-done(((bf16[32,24,128]{2,1,0:T(8,128)(2,1)}), bf16[32,24,128]{2,1,0:T(8,128)(2,1)S(1)}, u32[]{:S(2)}, u32[]{:S(2)}) %all-to-all-start) | async-done | bytes 196640 | tf_op jit(solution)/shard_map/all_to_all | solution.py:248
  37.9 0.7 copy-done.4
  38.6 4.0 %attend.1 = bf16[32,32,128]{2,1,0:T(8,128)(2,1)} custom-call(s32[1]{0:T(128)S(6)} %copy.14.lengths, bf16[32,24,128]{2,1,0:T(8,128)(2,1)S(1)} %all-to-all-done.q_ref, bf16[3072,128]{1,0:T(8,128)(2,1)S(1)} %bitcast.34, bf16[3072,128]{1,0:T(8,128)(2,1)S(1)} %bitcast.35, bf16[6,128]{1,0:T(8,128)(2,1)S(1)} %copy-done.4, bf16[6,128]{1,0:T(8,128)(2,1)S(1)} %copy-done.5), custom_call_target="tpu_custom_call" | custom-call | flops 1207959552 | bytes 2097152 | tf_op jit(solution)/shard_map/attend/pallas_call | solution.py:258
  42.5 9.6 %all-to-all-start.1 = ((bf16[32,32,128]{2,1,0:T(8,128)(2,1)}), bf16[32,32,128]{2,1,0:T(8,128)(2,1)S(1)}, u32[]{:S(2)}, u32[]{:S(2)}) async-start(bf16[32,32,128]{2,1,0:T(8,128)(2,1)} %attend.1), calls=%async_computation.1 | async-start | bytes 524288 | tf_op jit(solution)/shard_map/all_to_all | solution.py:269
  52.2 1.0 fusion.5
  53.2 4.6 %collective-permute-start.1 = (bf16[462,256]{1,0:T(8,128)(2,1)S(1)}, bf16[462,256]{1,0:T(8,128)(2,1)S(1)}, u32[]{:S(2)}, u32[]{:S(2)}) collective-permute-start(bf16[462,256]{1,0:T(8,128)(2,1)S(1)} %fusion.5), channel_id=1, source_target_pairs={{0,16},{16,0},{1,17},{17,1},{2,18},{18,2},{3,19},{19,3},{4,20},{20... | collective-permute-start | bytes 709640 | tf_op jit(solution)/shard_map/ppermute | solution.py:237
  57.8 4.9 %collective-permute-done.1.up_y1_ref = bf16[462,256]{1,0:T(8,128)(2,1)S(1)} collective-permute-done((bf16[462,256]{1,0:T(8,128)(2,1)S(1)}, bf16[462,256]{1,0:T(8,128)(2,1)S(1)}, u32[]{:S(2)}, u32[]{:S(2)}) %collective-permute-start.1) | collective-permute-done | bytes 236576 | tf_op jit(solution)/shard_map/ppermute | solution.py:237
  62.8 8.4 %all-to-all-done.1.in_ref = bf16[32,32,128]{2,1,0:T(8,128)(2,1)S(1)} async-done(((bf16[32,32,128]{2,1,0:T(8,128)(2,1)}), bf16[32,32,128]{2,1,0:T(8,128)(2,1)S(1)}, u32[]{:S(2)}, u32[]{:S(2)}) %all-to-all-start.1) | async-done | bytes 262176 | tf_op jit(solution)/shard_map/all_to_all | solution.py:269
  71.2 1.1 merge.1
  72.3 6.5 %all-to-all-start.2 = ((bf16[32,24,128]{2,1,0:T(8,128)(2,1)}), bf16[32,24,128]{2,1,0:T(8,128)(2,1)S(1)}, u32[]{:S(2)}, u32[]{:S(2)}) async-start(bf16[32,24,128]{2,1,0:T(8,128)(2,1)} %get-tuple-element.28), calls=%async_computation.2 | async-start | bytes 393216 | tf_op jit(solution)/shard_map/all_to_all | solution.py:280
  78.8 1.1 fusion.6
  79.9 4.6 %collective-permute-start.2 = (bf16[462,256]{1,0:T(8,128)(2,1)S(1)}, bf16[462,256]{1,0:T(8,128)(2,1)S(1)}, u32[]{:S(2)}, u32[]{:S(2)}) collective-permute-start(bf16[462,256]{1,0:T(8,128)(2,1)S(1)} %fusion.6), channel_id=1, source_target_pairs={{0,16},{16,0},{1,17},{17,1},{2,18},{18,2},{3,19},{19,3},{4,20},{20... | collective-permute-start | bytes 709640 | tf_op jit(solution)/shard_map/ppermute | solution.py:237
  84.5 4.6 %collective-permute-done.2.gate_y1_ref = bf16[462,256]{1,0:T(8,128)(2,1)S(1)} collective-permute-done((bf16[462,256]{1,0:T(8,128)(2,1)S(1)}, bf16[462,256]{1,0:T(8,128)(2,1)S(1)}, u32[]{:S(2)}, u32[]{:S(2)}) %collective-permute-start.2) | collective-permute-done | bytes 236576 | tf_op jit(solution)/shard_map/ppermute | solution.py:237
  89.1 5.3 %all-to-all-done.2.h_ref = bf16[32,24,128]{2,1,0:T(8,128)(2,1)S(1)} async-done(((bf16[32,24,128]{2,1,0:T(8,128)(2,1)}), bf16[32,24,128]{2,1,0:T(8,128)(2,1)S(1)}, u32[]{:S(2)}, u32[]{:S(2)}) %all-to-all-start.2) | async-done | bytes 196640 | tf_op jit(solution)/shard_map/all_to_all | solution.py:280
  94.4 0.9 out.1
  95.3 9.6 %all-to-all-start.3 = ((bf16[16,12,256]{2,1,0:T(8,128)(2,1)}), bf16[16,12,256]{2,1,0:T(8,128)(2,1)S(1)}, u32[]{:S(2)}, u32[]{:S(2)}) async-start(bf16[16,12,256]{2,1,0:T(8,128)(2,1)} %out.1), calls=%async_computation.3 | async-start | bytes 262144 | tf_op jit(solution)/shard_map/all_to_all | solution.py:291
  104.9 1.0 fusion.7
  105.9 4.5 %collective-permute-start.3 = (bf16[462,256]{1,0:T(8,128)(2,1)S(1)}, bf16[462,256]{1,0:T(8,128)(2,1)S(1)}, u32[]{:S(2)}, u32[]{:S(2)}) collective-permute-start(bf16[462,256]{1,0:T(8,128)(2,1)S(1)} %fusion.7), channel_id=1, source_target_pairs={{0,16},{16,0},{1,17},{17,1},{2,18},{18,2},{3,19},{19,3},{4,20},{20... | collective-permute-start | bytes 709640 | tf_op jit(solution)/shard_map/ppermute | solution.py:237
  110.4 0.6 all-to-all-done.3.in_ref
  111.0 0.7 stream.1
  111.7 5.3 %all-to-all-start.4 = ((bf16[32,12,256]{2,1,0:T(8,128)(2,1)}), bf16[32,12,256]{2,1,0:T(8,128)(2,1)S(1)}, u32[]{:S(2)}, u32[]{:S(2)}) async-start(bf16[32,12,256]{2,1,0:T(8,128)(2,1)} %get-tuple-element.31), calls=%async_computation.4 | async-start | bytes 524288 | tf_op jit(solution)/shard_map/all_to_all | solution.py:303
  117.1 0.1 collective-permute-done.3.up_y0_ref
  117.2 8.8 %all-to-all-done.4.x_ref = bf16[32,12,256]{2,1,0:T(8,128)(2,1)S(1)} async-done(((bf16[32,12,256]{2,1,0:T(8,128)(2,1)}), bf16[32,12,256]{2,1,0:T(8,128)(2,1)S(1)}, u32[]{:S(2)}, u32[]{:S(2)}) %all-to-all-start.4) | async-done | bytes 196640 | tf_op jit(solution)/shard_map/all_to_all | solution.py:303
  125.9 0.7 project.1
  126.7 1.9 collective-permute-start.4
  128.6 9.6 %collective-permute-done.4.got_ref = bf16[192,1024]{1,0:T(8,128)(2,1)S(1)} collective-permute-done((bf16[192,1024]{1,0:T(8,128)(2,1)S(1)}, bf16[192,1024]{1,0:T(8,128)(2,1)S(1)}, u32[]{:S(2)}, u32[]{:S(2)}) %collective-permute-start.4) | collective-permute-done | bytes 393248 | tf_op jit(solution)/shard_map/ppermute | solution.py:319
  138.2 1.0 join.1
  139.3 4.7 %all-to-all-start.5 = ((bf16[8,24,1024]{2,1,0:T(8,128)(2,1)}), bf16[8,24,1024]{2,1,0:T(8,128)(2,1)S(1)}, u32[]{:S(2)}, u32[]{:S(2)}) async-start(bf16[8,24,1024]{2,1,0:T(8,128)(2,1)} %join.1), calls=%async_computation.5 | async-start | bytes 786432 | tf_op jit(solution)/shard_map/all_to_all | solution.py:328
  144.0 0.2 dynamic-slice_bitcast_fusion.1
  144.3 3.4 %collective-permute-start.5 = (bf16[2,462,256]{2,1,0:T(8,128)(2,1)S(1)}, bf16[2,462,256]{2,1,0:T(8,128)(2,1)S(1)}, u32[]{:S(2)}, u32[]{:S(2)}) collective-permute-start(bf16[2,462,256]{2,1,0:T(8,128)(2,1)S(1)} %pad_maximum_fusion.2), channel_id=1, source_target_pairs={{0,16},{16,0},{1,17},{17,1},{2,18},{18,2},{3,19},{19,3},{4,20},{20... | collective-permute-start | bytes 1419272 | tf_op jit(solution)/shard_map/ppermute | solution.py:237
  147.6 10.3 %collective-permute-done.5.wy_ref = bf16[2,462,256]{2,1,0:T(8,128)(2,1)S(1)} collective-permute-done((bf16[2,462,256]{2,1,0:T(8,128)(2,1)S(1)}, bf16[2,462,256]{2,1,0:T(8,128)(2,1)S(1)}, u32[]{:S(2)}, u32[]{:S(2)}) %collective-permute-start.5) | collective-permute-done | bytes 473120 | tf_op jit(solution)/shard_map/ppermute | solution.py:237
  157.9 6.1 %all-to-all-done.5.in_ref = bf16[8,24,1024]{2,1,0:T(8,128)(2,1)S(1)} async-done(((bf16[8,24,1024]{2,1,0:T(8,128)(2,1)}), bf16[8,24,1024]{2,1,0:T(8,128)(2,1)S(1)}, u32[]{:S(2)}, u32[]{:S(2)}) %all-to-all-start.5) | async-done | bytes 393248 | tf_op jit(solution)/shard_map/all_to_all | solution.py:328
  164.0 1.0 hidden.1
  165.0 10.0 %all-to-all-start.6 = ((bf16[16,24,462]{2,1,0:T(8,128)(2,1)}), bf16[16,24,462]{2,1,0:T(8,128)(2,1)S(1)}, u32[]{:S(2)}, u32[]{:S(2)}) async-start(bf16[16,24,462]{2,1,0:T(8,128)(2,1)} %hidden.1), calls=%async_computation.6 | async-start | bytes 786432 | tf_op jit(solution)/shard_map/all_to_all | solution.py:337
  175.0 17.8 %all-to-all-done.6.h_ref = bf16[16,24,462]{2,1,0:T(8,128)(2,1)S(1)} async-done(((bf16[16,24,462]{2,1,0:T(8,128)(2,1)}), bf16[16,24,462]{2,1,0:T(8,128)(2,1)S(1)}, u32[]{:S(2)}, u32[]{:S(2)}) %all-to-all-start.6) | async-done | bytes 354848 | tf_op jit(solution)/shard_map/all_to_all | solution.py:337
  192.8 1.1 down.1
  193.9 11.3 %all-to-all-start.7 = ((bf16[32,12,256]{2,1,0:T(8,128)(2,1)}), bf16[32,12,256]{2,1,0:T(8,128)(2,1)S(1)}, u32[]{:S(2)}, u32[]{:S(2)}) async-start(bf16[32,12,256]{2,1,0:T(8,128)(2,1)} %down.1), calls=%async_computation.7 | async-start | bytes 524288 | tf_op jit(solution)/shard_map/all_to_all | solution.py:346
  205.1 0.6 reshape.10
  205.7 8.2 %all-to-all-done.7.in_ref = bf16[32,12,256]{2,1,0:T(8,128)(2,1)S(1)} async-done(((bf16[32,12,256]{2,1,0:T(8,128)(2,1)}), bf16[32,12,256]{2,1,0:T(8,128)(2,1)S(1)}, u32[]{:S(2)}, u32[]{:S(2)}) %all-to-all-start.7) | async-done | bytes 196640 | tf_op jit(solution)/shard_map/all_to_all | solution.py:346
  214.0 0.7 last.1
  (16 shorter events, 0.1 us)
Async XLA Ops:
  2.0 35.8 %all-to-all-start = ((bf16[32,24,128]{2,1,0:T(8,128)(2,1)}), bf16[32,24,128]{2,1,0:T(8,128)(2,1)S(1)}, u32[]{:S(2)}, u32[]{:S(2)}) async-start(bf16[32,24,128]{2,1,0:T(8,128)(2,1)} %broadcast_in_dim.5), calls=%async_computation | async-start | bytes 393216 | tf_op jit(solution)/shard_map/all_to_all | solution.py:248
  20.7 0.7 copy-start.7
  23.1 10.9 %collective-permute-start = (bf16[462,256]{1,0:T(8,128)(2,1)S(1)}, bf16[462,256]{1,0:T(8,128)(2,1)S(1)}, u32[]{:S(2)}, u32[]{:S(2)}) collective-permute-start(bf16[462,256]{1,0:T(8,128)(2,1)S(1)} %get-tuple-element.46), channel_id=1, source_target_pairs={{0,16},{16,0},{1,17},{17,1},{2,18},{18,2},{3,19},{19,3},{4,20},{20... | collective-permute-start | bytes 709640 | tf_op jit(solution)/shard_map/ppermute | solution.py:237
  28.4 9.4 %copy-start.2 = (bf16[1,3072,128]{2,1,0:T(8,128)(2,1)S(1)}, bf16[1,3072,128]{2,1,0:T(8,128)(2,1)}, u32[]{:S(2)}) copy-start(bf16[1,3072,128]{2,1,0:T(8,128)(2,1)} %param.13) | copy-start | bytes 2359300
  28.4 9.4 %copy-start.3 = (bf16[1,3072,128]{2,1,0:T(8,128)(2,1)S(1)}, bf16[1,3072,128]{2,1,0:T(8,128)(2,1)}, u32[]{:S(2)}) copy-start(bf16[1,3072,128]{2,1,0:T(8,128)(2,1)} %param.14) | copy-start | bytes 2359300
  28.5 9.4 %copy-start.5 = (bf16[6,128]{1,0:T(8,128)(2,1)S(1)}, bf16[6,128]{1,0:T(8,128)(2,1)}, u32[]{:S(2)}) copy-start(bf16[6,128]{1,0:T(8,128)(2,1)} %sv_ref.1) | copy-start | bytes 4612
  37.9 0.7 copy-start.4
  42.5 28.6 %all-to-all-start.1 = ((bf16[32,32,128]{2,1,0:T(8,128)(2,1)}), bf16[32,32,128]{2,1,0:T(8,128)(2,1)S(1)}, u32[]{:S(2)}, u32[]{:S(2)}) async-start(bf16[32,32,128]{2,1,0:T(8,128)(2,1)} %attend.1), calls=%async_computation.1 | async-start | bytes 524288 | tf_op jit(solution)/shard_map/all_to_all | solution.py:269
  53.2 9.6 %collective-permute-start.1 = (bf16[462,256]{1,0:T(8,128)(2,1)S(1)}, bf16[462,256]{1,0:T(8,128)(2,1)S(1)}, u32[]{:S(2)}, u32[]{:S(2)}) collective-permute-start(bf16[462,256]{1,0:T(8,128)(2,1)S(1)} %fusion.5), channel_id=1, source_target_pairs={{0,16},{16,0},{1,17},{17,1},{2,18},{18,2},{3,19},{19,3},{4,20},{20... | collective-permute-start | bytes 709640 | tf_op jit(solution)/shard_map/ppermute | solution.py:237
  72.3 22.1 %all-to-all-start.2 = ((bf16[32,24,128]{2,1,0:T(8,128)(2,1)}), bf16[32,24,128]{2,1,0:T(8,128)(2,1)S(1)}, u32[]{:S(2)}, u32[]{:S(2)}) async-start(bf16[32,24,128]{2,1,0:T(8,128)(2,1)} %get-tuple-element.28), calls=%async_computation.2 | async-start | bytes 393216 | tf_op jit(solution)/shard_map/all_to_all | solution.py:280
  78.8 15.6 %copy-start = (bf16[512,256]{1,0:T(8,128)(2,1)S(1)}, bf16[512,256]{1,0:T(8,128)(2,1)}, u32[]{:S(2)}) copy-start(bf16[512,256]{1,0:T(8,128)(2,1)} %w_ref.1) | copy-start | bytes 786436
  79.9 9.2 %collective-permute-start.2 = (bf16[462,256]{1,0:T(8,128)(2,1)S(1)}, bf16[462,256]{1,0:T(8,128)(2,1)S(1)}, u32[]{:S(2)}, u32[]{:S(2)}) collective-permute-start(bf16[462,256]{1,0:T(8,128)(2,1)S(1)} %fusion.6), channel_id=1, source_target_pairs={{0,16},{16,0},{1,17},{17,1},{2,18},{18,2},{3,19},{19,3},{4,20},{20... | collective-permute-start | bytes 709640 | tf_op jit(solution)/shard_map/ppermute | solution.py:237
  95.3 15.7 %all-to-all-start.3 = ((bf16[16,12,256]{2,1,0:T(8,128)(2,1)}), bf16[16,12,256]{2,1,0:T(8,128)(2,1)S(1)}, u32[]{:S(2)}, u32[]{:S(2)}) async-start(bf16[16,12,256]{2,1,0:T(8,128)(2,1)} %out.1), calls=%async_computation.3 | async-start | bytes 262144 | tf_op jit(solution)/shard_map/all_to_all | solution.py:291
  104.8 6.2 %copy-start.1 = (bf16[12,256]{1,0:T(8,128)(2,1)S(1)}, bf16[12,256]{1,0:T(8,128)(2,1)}, u32[]{:S(2)}) copy-start(bf16[12,256]{1,0:T(8,128)(2,1)} %residual_ref.1) | copy-start | bytes 18436
  105.9 11.3 %collective-permute-start.3 = (bf16[462,256]{1,0:T(8,128)(2,1)S(1)}, bf16[462,256]{1,0:T(8,128)(2,1)S(1)}, u32[]{:S(2)}, u32[]{:S(2)}) collective-permute-start(bf16[462,256]{1,0:T(8,128)(2,1)S(1)} %fusion.7), channel_id=1, source_target_pairs={{0,16},{16,0},{1,17},{17,1},{2,18},{18,2},{3,19},{19,3},{4,20},{20... | collective-permute-start | bytes 709640 | tf_op jit(solution)/shard_map/ppermute | solution.py:237
  111.7 14.2 %all-to-all-start.4 = ((bf16[32,12,256]{2,1,0:T(8,128)(2,1)}), bf16[32,12,256]{2,1,0:T(8,128)(2,1)S(1)}, u32[]{:S(2)}, u32[]{:S(2)}) async-start(bf16[32,12,256]{2,1,0:T(8,128)(2,1)} %get-tuple-element.31), calls=%async_computation.4 | async-start | bytes 524288 | tf_op jit(solution)/shard_map/all_to_all | solution.py:303
  126.7 11.6 %collective-permute-start.4 = (bf16[192,1024]{1,0:T(8,128)(2,1)S(1)}, bf16[192,1024]{1,0:T(8,128)(2,1)S(1)}, u32[]{:S(2)}, u32[]{:S(2)}) collective-permute-start(bf16[192,1024]{1,0:T(8,128)(2,1)S(1)} %get-tuple-element.41), channel_id=1, source_target_pairs={{0,32},{32,0},{1,33},{33,1},{2,34},{34,2},{3,35},{35,3},{4,36},{36... | collective-permute-start | bytes 1179656 | tf_op jit(solution)/shard_map/ppermute | solution.py:319
  138.2 5.7 %copy-start.6 = (bf16[1848,256]{1,0:T(8,128)(2,1)S(1)}, bf16[1848,256]{1,0:T(8,128)(2,1)}, u32[]{:S(2)}) copy-start(bf16[1848,256]{1,0:T(8,128)(2,1)} %param.23) | copy-start | bytes 2838532
  139.3 24.7 %all-to-all-start.5 = ((bf16[8,24,1024]{2,1,0:T(8,128)(2,1)}), bf16[8,24,1024]{2,1,0:T(8,128)(2,1)S(1)}, u32[]{:S(2)}, u32[]{:S(2)}) async-start(bf16[8,24,1024]{2,1,0:T(8,128)(2,1)} %join.1), calls=%async_computation.5 | async-start | bytes 786432 | tf_op jit(solution)/shard_map/all_to_all | solution.py:328
  144.3 13.6 %collective-permute-start.5 = (bf16[2,462,256]{2,1,0:T(8,128)(2,1)S(1)}, bf16[2,462,256]{2,1,0:T(8,128)(2,1)S(1)}, u32[]{:S(2)}, u32[]{:S(2)}) collective-permute-start(bf16[2,462,256]{2,1,0:T(8,128)(2,1)S(1)} %pad_maximum_fusion.2), channel_id=1, source_target_pairs={{0,16},{16,0},{1,17},{17,1},{2,18},{18,2},{3,19},{19,3},{4,20},{20... | collective-permute-start | bytes 1419272 | tf_op jit(solution)/shard_map/ppermute | solution.py:237
  165.0 27.8 %all-to-all-start.6 = ((bf16[16,24,462]{2,1,0:T(8,128)(2,1)}), bf16[16,24,462]{2,1,0:T(8,128)(2,1)S(1)}, u32[]{:S(2)}, u32[]{:S(2)}) async-start(bf16[16,24,462]{2,1,0:T(8,128)(2,1)} %hidden.1), calls=%async_computation.6 | async-start | bytes 786432 | tf_op jit(solution)/shard_map/all_to_all | solution.py:337
  193.9 20.1 %all-to-all-start.7 = ((bf16[32,12,256]{2,1,0:T(8,128)(2,1)}), bf16[32,12,256]{2,1,0:T(8,128)(2,1)S(1)}, u32[]{:S(2)}, u32[]{:S(2)}) async-start(bf16[32,12,256]{2,1,0:T(8,128)(2,1)} %down.1), calls=%async_computation.7 | async-start | bytes 524288 | tf_op jit(solution)/shard_map/all_to_all | solution.py:346

commit v12 on v11

--- a/solution.py
+++ b/solution.py
@@ -11,8 +11,7 @@
 D = 8192
 F32 = jnp.float32
 BF16 = jnp.bfloat16
-LOW = -1e30
-SPAN = 512
+LOW = float("-inf")
 
 
 def three_parts(x):
@@ -36,36 +35,17 @@
     def weigh(values, w):
         return lax.dot_general(values, w.astype(BF16), (((0,), (0,)), ((), ())), preferred_element_type=F32)
 
-    def add(carry, s, values):
-        top, total, numer = carry
-        top_new = jnp.maximum(top, jnp.max(s, axis=0, keepdims=True))
-        fade = jnp.exp2((top - top_new) * unit)
-        w = jnp.exp2((s - top_new) * unit)
-        return top_new, total * fade + jnp.sum(w, axis=0, keepdims=True), numer * fade + weigh(values, w)
-
-    s = scores(sk_ref[...])
+    own_s = scores(sk_ref[...])
     token = lax.broadcasted_iota(jnp.int32, (own, rows), 1) // group
-    place = first + lax.broadcasted_iota(jnp.int32, (own, rows), 0)
-    seen = place <= token
-    s = jnp.where(seen, s, LOW)
-    top = jnp.max(s, axis=0, keepdims=True)
-    w = jnp.where(seen, jnp.exp2((s - top) * unit), 0.0)
-    total = jnp.sum(w, axis=0, keepdims=True)
-    numer = weigh(sv_ref[...], w)
-    def whole(step, carry):
-        at = pl.ds(pl.multiple_of(step * SPAN, SPAN), SPAN)
-        return add(carry, scores(k_ref[at, :]), v_ref[at, :])
-
-    full = length // SPAN
-    carry = lax.fori_loop(0, full, whole, (top, total, numer))
-
-    def part(step, carry):
-        at = pl.ds(pl.multiple_of(step * SPAN, SPAN), SPAN)
-        s = scores(k_ref[at, :])
-        live = step * SPAN + lax.broadcasted_iota(jnp.int32, s.shape, 0) < length
-        return add(carry, jnp.where(live, s, LOW), v_ref[at, :])
-
-    top, total, numer = lax.fori_loop(full, (length + SPAN - 1) // SPAN, part, carry)
+    seen = first + lax.broadcasted_iota(jnp.int32, (own, rows), 0) <= token
+    own_s = jnp.where(seen, own_s, LOW)
+    s = scores(k_ref[...])
+    s = jnp.where(lax.broadcasted_iota(jnp.int32, s.shape, 0) < length, s, LOW)
+    top = jnp.maximum(jnp.max(own_s, axis=0, keepdims=True), jnp.max(s, axis=0, keepdims=True))
+    own_w = jnp.exp2((own_s - top) * unit)
+    w = jnp.exp2((s - top) * unit)
+    total = jnp.sum(own_w, axis=0, keepdims=True) + jnp.sum(w, axis=0, keepdims=True)
+    numer = weigh(sv_ref[...], own_w) + weigh(v_ref[...], w)
     blocks = out_ref.shape[0]
     each = rows // blocks
     out_ref[:, :each, :] = (numer / total).T.astype(BF16).reshape(blocks, each, head)
@@ -120,7 +100,7 @@
 
 
 def project_kernel(
-    x_ref, gate_ref, gate_y0_ref, gate_y1_ref, up_ref, up_y0_ref, up_y1_ref, send_ref, keep_ref
+    x_ref, gate_ref, gate_y0_ref, gate_y1_ref, up_ref, up_y0_ref, up_y1_ref, send_g_ref, send_u_ref, keep_ref
 ):
     units = gate_ref.shape[1]
     each = x_ref.shape[0] // 2
@@ -139,15 +119,16 @@
 
     tokens = squares.shape[0]
     spare = half - units
-    for at, ref in ((1 - lo, send_ref), (lo, keep_ref)):
+    keep_refs = (keep_ref.at[:, :half], keep_ref.at[:, half:])
+    for at, (g_ref, u_ref) in ((1 - lo, (send_g_ref, send_u_ref)), (lo, keep_refs)):
         gate = product(gate_ref[at], jnp.where(at == 0, gate_y0_ref[...], gate_y1_ref[...]))
         up = product(up_ref[at], jnp.where(at == 0, up_y0_ref[...], up_y1_ref[...]))
-        ref[:, :half] = jnp.concatenate([gate, *parts, jnp.zeros((tokens, spare - 3), F32)], axis=1).astype(ref.dtype)
-        ref[:, half:] = jnp.concatenate([up, jnp.zeros((tokens, spare), F32)], axis=1).astype(ref.dtype)
-
-
-def join_kernel(keep_ref, got_ref, out_ref, *, units):
-    total = keep_ref[...] + got_ref[...].astype(F32)
+        g_ref[...] = jnp.concatenate([gate, *parts, jnp.zeros((tokens, spare - 3), F32)], axis=1).astype(g_ref.dtype)
+        u_ref[...] = jnp.concatenate([up, jnp.zeros((tokens, spare), F32)], axis=1).astype(u_ref.dtype)
+
+
+def join_kernel(keep_ref, got_g_ref, got_u_ref, out_ref, *, units):
+    total = keep_ref[...] + jnp.concatenate([got_g_ref[...], got_u_ref[...]], axis=1).astype(F32)
     cut = units // 128 * 128
     at = units - cut
     tail = total[:, cut : cut + 128]
@@ -305,26 +286,29 @@
 
     half = -(-(units + 3) // 128) * 128
     block = tokens // n_far
-    send, keep = pl.pallas_call(
+    send_g, send_u, keep = pl.pallas_call(
         project_kernel,
         out_shape=(
-            jax.ShapeDtypeStruct((tokens, 2 * half), BF16),
+            jax.ShapeDtypeStruct((tokens, half), BF16),
+            jax.ShapeDtypeStruct((tokens, half), BF16),
             jax.ShapeDtypeStruct((tokens, 2 * half), F32),
         ),
         in_specs=[vmem] * 7,
-        out_specs=(vmem, vmem),
+        out_specs=(vmem, vmem, vmem),
         compiler_params=small,
         name="project",
     )(stream, own_gate, gate_y0, gate_y1, own_up, up_y0, up_y1)
-    got = lax.ppermute(send, "lo", [(0, 1), (1, 0)])
+    n_z = 2 * n_far
+    got_g = lax.ppermute(send_g, ("far", "lo"), [(z, z ^ 1) for z in range(n_z)])
+    got_u = lax.ppermute(send_u, ("far", "lo"), [(z, (z + 2 * (z % 2) - 1) % n_z) for z in range(n_z)])
     sums = pl.pallas_call(
         functools.partial(join_kernel, units=units),
         out_shape=jax.ShapeDtypeStruct((n_far, block, 2 * half), BF16),
-        in_specs=[vmem] * 2,
+        in_specs=[vmem] * 3,
         out_specs=vmem,
         compiler_params=small,
         name="join",
-    )(keep, got)
+    )(keep, got_g, got_u)
     sums, down_y = beside(lax.all_to_all(sums, "far", 0, 0, tiled=True), trade(down_chunk))
     hidden = pl.pallas_call(
         hidden_kernel,

time: 216 us -> 216 us (level)
  waiting for transfers between devices: 94 us -> 91 us
  starting transfers between devices: 99.3 us -> 102 us
    ppermute x1 -> x2, waiting for transfers between devices: 9.64 us -> 4.8 us  [the longest x1 2.9 us: per_device(): lax.ppermute(send_u, ('far', 'lo'), [(z, (z + 2 * (z % 2) - 1) % n_z) for...]
    ppermute x1 -> x2, starting transfers between devices: 1.92 us -> 5.44 us  [the longest x1 3.52 us: per_device(): lax.ppermute(send_u, ('far', 'lo'), [(z, (z + 2 * (z % 2) - 1) % n_z) for...]
  transfers between devices with their start and end apart: 14 -> 15, of which waited for: 14 -> 15; matrix products, arithmetic and copies ran while one was open for 3% -> 3% of each run, Pallas kernels for 0% -> 0%
where the time goes in v12:
time: 216 us; the launch traced here: 214 us
  starting transfers between devices  102 us (47%)
  waiting for transfers between devices  91 us (42%)
  Pallas kernels  11.7 us (5%)
  other arithmetic  5.02 us (2%)
  local copies, waits for them, and re-layouts  3.65 us (2%)
    ppermute x5, waiting for transfers between devices, trade(): return lambda place: lax.ppermute(part(place ^ 1), 'hi', [(0, 1), (1, 0)])  25.1 us
    ppermute x5, starting transfers between devices, trade(): return lambda place: lax.ppermute(part(place ^ 1), 'hi', [(0, 1), (1, 0)])  21.8 us
    all_to_all x1, starting transfers between devices, per_device(): q_all = lax.all_to_all(q_all, ctx, 0, 0, tiled=True)  18.7 us
    all_to_all x1, waiting for transfers between devices, per_device(): hidden = lax.all_to_all(hidden, ('far', 'lo'), 0, 0, tiled=True)  18 us
    all_to_all x1, starting transfers between devices, per_device(): lowered = lax.all_to_all(lowered, ('hi', 'tp'), 0, 0, tiled=True)  11.5 us
    all_to_all x1, starting transfers between devices, per_device(): mixed = lax.all_to_all(mixed, 'tp', 0, 0, tiled=True)  9.69 us
    all_to_all x1, starting transfers between devices, per_device(): parts = lax.all_to_all(partial, ctx, 0, 0, tiled=True)  9.64 us
    all_to_all x1, waiting for transfers between devices, per_device(): stream = lax.all_to_all(stream, ('hi', 'tp'), 0, 0, tiled=True)  8.77 us
  transfers between devices with their start and end apart: 15, of which 15 were waited for; matrix products, arithmetic and copies ran while one was open for 3% of the time, Pallas kernels for 0%

profile of v12, /device:TPU:1, one launch (start us, length us, event | category | flops | bytes accessed | tf_op | source)
XLA Modules:
  0.0 214.4 jit_solution(14373248251602645632)
XLA Ops:
  0.6 0.7 broadcast_in_dim.4
  1.3 0.7 broadcast_in_dim.5
  2.0 18.7 %all-to-all-start = ((bf16[32,24,128]{2,1,0:T(8,128)(2,1)}), bf16[32,24,128]{2,1,0:T(8,128)(2,1)S(1)}, u32[]{:S(2)}, u32[]{:S(2)}) async-start(bf16[32,24,128]{2,1,0:T(8,128)(2,1)} %broadcast_in_dim.5), calls=%async_computation | async-start | bytes 393216 | tf_op jit(solution)/shard_map/all_to_all | solution.py:229
  20.7 0.7 copy-done.7
  21.4 1.7 fusion.4
  23.1 4.6 %collective-permute-start = (bf16[462,256]{1,0:T(8,128)(2,1)S(1)}, bf16[462,256]{1,0:T(8,128)(2,1)S(1)}, u32[]{:S(2)}, u32[]{:S(2)}) collective-permute-start(bf16[462,256]{1,0:T(8,128)(2,1)S(1)} %get-tuple-element.48), channel_id=1, source_target_pairs={{0,16},{16,0},{1,17},{17,1},{2,18},{18,2},{3,19},{19,3},{4,20},{20... | collective-permute-start | bytes 709640 | tf_op jit(solution)/shard_map/ppermute | solution.py:218
  28.6 5.5 %collective-permute-done.gate_y0_ref = bf16[462,256]{1,0:T(8,128)(2,1)S(1)} collective-permute-done((bf16[462,256]{1,0:T(8,128)(2,1)S(1)}, bf16[462,256]{1,0:T(8,128)(2,1)S(1)}, u32[]{:S(2)}, u32[]{:S(2)}) %collective-permute-start) | collective-permute-done | bytes 236576 | tf_op jit(solution)/shard_map/ppermute | solution.py:218
  34.0 3.8 %all-to-all-done.q_ref = bf16[32,24,128]{2,1,0:T(8,128)(2,1)S(1)} async-done(((bf16[32,24,128]{2,1,0:T(8,128)(2,1)}), bf16[32,24,128]{2,1,0:T(8,128)(2,1)S(1)}, u32[]{:S(2)}, u32[]{:S(2)}) %all-to-all-start) | async-done | bytes 196640 | tf_op jit(solution)/shard_map/all_to_all | solution.py:229
  37.9 0.7 copy-done.4
  38.5 4.6 %attend.1 = bf16[32,32,128]{2,1,0:T(8,128)(2,1)} custom-call(s32[1]{0:T(128)S(6)} %copy.14.lengths, bf16[32,24,128]{2,1,0:T(8,128)(2,1)S(1)} %all-to-all-done.q_ref, bf16[3072,128]{1,0:T(8,128)(2,1)S(1)} %bitcast.34, bf16[3072,128]{1,0:T(8,128)(2,1)S(1)} %bitcast.35, bf16[6,128]{1,0:T(8,128)(2,1)S(1)} %copy-done.4, bf16[6,128]{1,0:T(8,128)(2,1)S(1)} %copy-done.5), custom_call_target="tpu_custom_call" | custom-call | flops 1207959552 | bytes 2097152 | tf_op jit(solution)/shard_map/attend/pallas_call | solution.py:239
  43.1 9.6 %all-to-all-start.1 = ((bf16[32,32,128]{2,1,0:T(8,128)(2,1)}), bf16[32,32,128]{2,1,0:T(8,128)(2,1)S(1)}, u32[]{:S(2)}, u32[]{:S(2)}) async-start(bf16[32,32,128]{2,1,0:T(8,128)(2,1)} %attend.1), calls=%async_computation.1 | async-start | bytes 524288 | tf_op jit(solution)/shard_map/all_to_all | solution.py:250
  52.8 1.0 fusion.5
  53.8 4.6 %collective-permute-start.1 = (bf16[462,256]{1,0:T(8,128)(2,1)S(1)}, bf16[462,256]{1,0:T(8,128)(2,1)S(1)}, u32[]{:S(2)}, u32[]{:S(2)}) collective-permute-start(bf16[462,256]{1,0:T(8,128)(2,1)S(1)} %fusion.5), channel_id=1, source_target_pairs={{0,16},{16,0},{1,17},{17,1},{2,18},{18,2},{3,19},{19,3},{4,20},{20... | collective-permute-start | bytes 709640 | tf_op jit(solution)/shard_map/ppermute | solution.py:218
  58.4 4.9 %collective-permute-done.1.up_y1_ref = bf16[462,256]{1,0:T(8,128)(2,1)S(1)} collective-permute-done((bf16[462,256]{1,0:T(8,128)(2,1)S(1)}, bf16[462,256]{1,0:T(8,128)(2,1)S(1)}, u32[]{:S(2)}, u32[]{:S(2)}) %collective-permute-start.1) | collective-permute-done | bytes 236576 | tf_op jit(solution)/shard_map/ppermute | solution.py:218
  63.4 8.4 %all-to-all-done.1.in_ref = bf16[32,32,128]{2,1,0:T(8,128)(2,1)S(1)} async-done(((bf16[32,32,128]{2,1,0:T(8,128)(2,1)}), bf16[32,32,128]{2,1,0:T(8,128)(2,1)S(1)}, u32[]{:S(2)}, u32[]{:S(2)}) %all-to-all-start.1) | async-done | bytes 262176 | tf_op jit(solution)/shard_map/all_to_all | solution.py:250
  71.8 1.1 merge.1
  72.9 6.5 %all-to-all-start.2 = ((bf16[32,24,128]{2,1,0:T(8,128)(2,1)}), bf16[32,24,128]{2,1,0:T(8,128)(2,1)S(1)}, u32[]{:S(2)}, u32[]{:S(2)}) async-start(bf16[32,24,128]{2,1,0:T(8,128)(2,1)} %get-tuple-element.29), calls=%async_computation.2 | async-start | bytes 393216 | tf_op jit(solution)/shard_map/all_to_all | solution.py:261
  79.4 1.1 fusion.6
  80.5 4.6 %collective-permute-start.2 = (bf16[462,256]{1,0:T(8,128)(2,1)S(1)}, bf16[462,256]{1,0:T(8,128)(2,1)S(1)}, u32[]{:S(2)}, u32[]{:S(2)}) collective-permute-start(bf16[462,256]{1,0:T(8,128)(2,1)S(1)} %fusion.6), channel_id=1, source_target_pairs={{0,16},{16,0},{1,17},{17,1},{2,18},{18,2},{3,19},{19,3},{4,20},{20... | collective-permute-start | bytes 709640 | tf_op jit(solution)/shard_map/ppermute | solution.py:218
  85.1 4.6 %collective-permute-done.2.gate_y1_ref = bf16[462,256]{1,0:T(8,128)(2,1)S(1)} collective-permute-done((bf16[462,256]{1,0:T(8,128)(2,1)S(1)}, bf16[462,256]{1,0:T(8,128)(2,1)S(1)}, u32[]{:S(2)}, u32[]{:S(2)}) %collective-permute-start.2) | collective-permute-done | bytes 236576 | tf_op jit(solution)/shard_map/ppermute | solution.py:218
  89.7 5.1 %all-to-all-done.2.h_ref = bf16[32,24,128]{2,1,0:T(8,128)(2,1)S(1)} async-done(((bf16[32,24,128]{2,1,0:T(8,128)(2,1)}), bf16[32,24,128]{2,1,0:T(8,128)(2,1)S(1)}, u32[]{:S(2)}, u32[]{:S(2)}) %all-to-all-start.2) | async-done | bytes 196640 | tf_op jit(solution)/shard_map/all_to_all | solution.py:261
  94.8 0.9 out.1
  95.8 9.7 %all-to-all-start.3 = ((bf16[16,12,256]{2,1,0:T(8,128)(2,1)}), bf16[16,12,256]{2,1,0:T(8,128)(2,1)S(1)}, u32[]{:S(2)}, u32[]{:S(2)}) async-start(bf16[16,12,256]{2,1,0:T(8,128)(2,1)} %out.1), calls=%async_computation.3 | async-start | bytes 262144 | tf_op jit(solution)/shard_map/all_to_all | solution.py:272
  105.5 1.0 fusion.7
  106.5 4.5 %collective-permute-start.3 = (bf16[462,256]{1,0:T(8,128)(2,1)S(1)}, bf16[462,256]{1,0:T(8,128)(2,1)S(1)}, u32[]{:S(2)}, u32[]{:S(2)}) collective-permute-start(bf16[462,256]{1,0:T(8,128)(2,1)S(1)} %fusion.7), channel_id=1, source_target_pairs={{0,16},{16,0},{1,17},{17,1},{2,18},{18,2},{3,19},{19,3},{4,20},{20... | collective-permute-start | bytes 709640 | tf_op jit(solution)/shard_map/ppermute | solution.py:218
  111.0 0.6 all-to-all-done.3.in_ref
  111.6 0.7 stream.1
  112.4 5.3 %all-to-all-start.4 = ((bf16[32,12,256]{2,1,0:T(8,128)(2,1)}), bf16[32,12,256]{2,1,0:T(8,128)(2,1)S(1)}, u32[]{:S(2)}, u32[]{:S(2)}) async-start(bf16[32,12,256]{2,1,0:T(8,128)(2,1)} %get-tuple-element.32), calls=%async_computation.4 | async-start | bytes 524288 | tf_op jit(solution)/shard_map/all_to_all | solution.py:284
  117.8 8.8 %all-to-all-done.4.x_ref = bf16[32,12,256]{2,1,0:T(8,128)(2,1)S(1)} async-done(((bf16[32,12,256]{2,1,0:T(8,128)(2,1)}), bf16[32,12,256]{2,1,0:T(8,128)(2,1)S(1)}, u32[]{:S(2)}, u32[]{:S(2)}) %all-to-all-start.4) | async-done | bytes 196640 | tf_op jit(solution)/shard_map/all_to_all | solution.py:284
  126.6 0.7 project.1
  127.3 1.9 collective-permute-start.4
  129.2 3.5 %collective-permute-start.5 = (bf16[192,512]{1,0:T(8,128)(2,1)S(1)}, bf16[192,512]{1,0:T(8,128)(2,1)S(1)}, u32[]{:S(2)}, u32[]{:S(2)}) collective-permute-start(bf16[192,512]{1,0:T(8,128)(2,1)S(1)} %get-tuple-element.43), channel_id=1, source_target_pairs={{0,480},{32,64},{64,32},{96,128},{128,96},{160,192},{192,160},{224... | collective-permute-start | bytes 589832 | tf_op jit(solution)/shard_map/ppermute | solution.py:303
  132.7 1.9 collective-permute-done.4.got_g_ref
  134.6 2.9 %collective-permute-done.5.got_u_ref = bf16[192,512]{1,0:T(8,128)(2,1)S(1)} collective-permute-done((bf16[192,512]{1,0:T(8,128)(2,1)S(1)}, bf16[192,512]{1,0:T(8,128)(2,1)S(1)}, u32[]{:S(2)}, u32[]{:S(2)}) %collective-permute-start.5) | collective-permute-done | bytes 196640 | tf_op jit(solution)/shard_map/ppermute | solution.py:303
  137.5 1.0 join.1
  138.5 5.0 %all-to-all-start.5 = ((bf16[8,24,1024]{2,1,0:T(8,128)(2,1)}), bf16[8,24,1024]{2,1,0:T(8,128)(2,1)S(1)}, u32[]{:S(2)}, u32[]{:S(2)}) async-start(bf16[8,24,1024]{2,1,0:T(8,128)(2,1)} %join.1), calls=%async_computation.5 | async-start | bytes 786432 | tf_op jit(solution)/shard_map/all_to_all | solution.py:312
  143.5 0.2 dynamic-slice_bitcast_fusion.1
  143.8 3.3 %collective-permute-start.6 = (bf16[2,462,256]{2,1,0:T(8,128)(2,1)S(1)}, bf16[2,462,256]{2,1,0:T(8,128)(2,1)S(1)}, u32[]{:S(2)}, u32[]{:S(2)}) collective-permute-start(bf16[2,462,256]{2,1,0:T(8,128)(2,1)S(1)} %pad_maximum_fusion.2), channel_id=1, source_target_pairs={{0,16},{16,0},{1,17},{17,1},{2,18},{18,2},{3,19},{19,3},{4,20},{20... | collective-permute-start | bytes 1419272 | tf_op jit(solution)/shard_map/ppermute | solution.py:218
  147.2 10.0 %collective-permute-done.6.wy_ref = bf16[2,462,256]{2,1,0:T(8,128)(2,1)S(1)} collective-permute-done((bf16[2,462,256]{2,1,0:T(8,128)(2,1)S(1)}, bf16[2,462,256]{2,1,0:T(8,128)(2,1)S(1)}, u32[]{:S(2)}, u32[]{:S(2)}) %collective-permute-start.6) | collective-permute-done | bytes 473120 | tf_op jit(solution)/shard_map/ppermute | solution.py:218
  157.2 8.1 %all-to-all-done.5.in_ref = bf16[8,24,1024]{2,1,0:T(8,128)(2,1)S(1)} async-done(((bf16[8,24,1024]{2,1,0:T(8,128)(2,1)}), bf16[8,24,1024]{2,1,0:T(8,128)(2,1)S(1)}, u32[]{:S(2)}, u32[]{:S(2)}) %all-to-all-start.5) | async-done | bytes 393248 | tf_op jit(solution)/shard_map/all_to_all | solution.py:312
  165.3 0.9 hidden.1
  166.3 8.0 %all-to-all-start.6 = ((bf16[16,24,462]{2,1,0:T(8,128)(2,1)}), bf16[16,24,462]{2,1,0:T(8,128)(2,1)S(1)}, u32[]{:S(2)}, u32[]{:S(2)}) async-start(bf16[16,24,462]{2,1,0:T(8,128)(2,1)} %hidden.1), calls=%async_computation.6 | async-start | bytes 786432 | tf_op jit(solution)/shard_map/all_to_all | solution.py:321
  174.3 18.0 %all-to-all-done.6.h_ref = bf16[16,24,462]{2,1,0:T(8,128)(2,1)S(1)} async-done(((bf16[16,24,462]{2,1,0:T(8,128)(2,1)}), bf16[16,24,462]{2,1,0:T(8,128)(2,1)S(1)}, u32[]{:S(2)}, u32[]{:S(2)}) %all-to-all-start.6) | async-done | bytes 354848 | tf_op jit(solution)/shard_map/all_to_all | solution.py:321
  192.3 1.1 down.1
  193.3 11.5 %all-to-all-start.7 = ((bf16[32,12,256]{2,1,0:T(8,128)(2,1)}), bf16[32,12,256]{2,1,0:T(8,128)(2,1)S(1)}, u32[]{:S(2)}, u32[]{:S(2)}) async-start(bf16[32,12,256]{2,1,0:T(8,128)(2,1)} %down.1), calls=%async_computation.7 | async-start | bytes 524288 | tf_op jit(solution)/shard_map/all_to_all | solution.py:330
  204.9 0.6 reshape.10
  205.5 8.2 %all-to-all-done.7.in_ref = bf16[32,12,256]{2,1,0:T(8,128)(2,1)S(1)} async-done(((bf16[32,12,256]{2,1,0:T(8,128)(2,1)}), bf16[32,12,256]{2,1,0:T(8,128)(2,1)S(1)}, u32[]{:S(2)}, u32[]{:S(2)}) %all-to-all-start.7) | async-done | bytes 196640 | tf_op jit(solution)/shard_map/all_to_all | solution.py:330
  213.7 0.7 last.1
  (18 shorter events, 0.3 us)
Async XLA Ops:
  2.0 35.8 %all-to-all-start = ((bf16[32,24,128]{2,1,0:T(8,128)(2,1)}), bf16[32,24,128]{2,1,0:T(8,128)(2,1)S(1)}, u32[]{:S(2)}, u32[]{:S(2)}) async-start(bf16[32,24,128]{2,1,0:T(8,128)(2,1)} %broadcast_in_dim.5), calls=%async_computation | async-start | bytes 393216 | tf_op jit(solution)/shard_map/all_to_all | solution.py:229
  20.7 0.7 copy-start.7
  23.1 10.9 %collective-permute-start = (bf16[462,256]{1,0:T(8,128)(2,1)S(1)}, bf16[462,256]{1,0:T(8,128)(2,1)S(1)}, u32[]{:S(2)}, u32[]{:S(2)}) collective-permute-start(bf16[462,256]{1,0:T(8,128)(2,1)S(1)} %get-tuple-element.48), channel_id=1, source_target_pairs={{0,16},{16,0},{1,17},{17,1},{2,18},{18,2},{3,19},{19,3},{4,20},{20... | collective-permute-start | bytes 709640 | tf_op jit(solution)/shard_map/ppermute | solution.py:218
  28.4 9.4 %copy-start.2 = (bf16[1,3072,128]{2,1,0:T(8,128)(2,1)S(1)}, bf16[1,3072,128]{2,1,0:T(8,128)(2,1)}, u32[]{:S(2)}) copy-start(bf16[1,3072,128]{2,1,0:T(8,128)(2,1)} %param.13) | copy-start | bytes 2359300
  28.4 9.4 %copy-start.3 = (bf16[1,3072,128]{2,1,0:T(8,128)(2,1)S(1)}, bf16[1,3072,128]{2,1,0:T(8,128)(2,1)}, u32[]{:S(2)}) copy-start(bf16[1,3072,128]{2,1,0:T(8,128)(2,1)} %param.14) | copy-start | bytes 2359300
  28.5 9.4 %copy-start.5 = (bf16[6,128]{1,0:T(8,128)(2,1)S(1)}, bf16[6,128]{1,0:T(8,128)(2,1)}, u32[]{:S(2)}) copy-start(bf16[6,128]{1,0:T(8,128)(2,1)} %sv_ref.1) | copy-start | bytes 4612
  37.9 0.7 copy-start.4
  43.1 28.7 %all-to-all-start.1 = ((bf16[32,32,128]{2,1,0:T(8,128)(2,1)}), bf16[32,32,128]{2,1,0:T(8,128)(2,1)S(1)}, u32[]{:S(2)}, u32[]{:S(2)}) async-start(bf16[32,32,128]{2,1,0:T(8,128)(2,1)} %attend.1), calls=%async_computation.1 | async-start | bytes 524288 | tf_op jit(solution)/shard_map/all_to_all | solution.py:250
  53.8 9.6 %collective-permute-start.1 = (bf16[462,256]{1,0:T(8,128)(2,1)S(1)}, bf16[462,256]{1,0:T(8,128)(2,1)S(1)}, u32[]{:S(2)}, u32[]{:S(2)}) collective-permute-start(bf16[462,256]{1,0:T(8,128)(2,1)S(1)} %fusion.5), channel_id=1, source_target_pairs={{0,16},{16,0},{1,17},{17,1},{2,18},{18,2},{3,19},{19,3},{4,20},{20... | collective-permute-start | bytes 709640 | tf_op jit(solution)/shard_map/ppermute | solution.py:218
  72.9 21.9 %all-to-all-start.2 = ((bf16[32,24,128]{2,1,0:T(8,128)(2,1)}), bf16[32,24,128]{2,1,0:T(8,128)(2,1)S(1)}, u32[]{:S(2)}, u32[]{:S(2)}) async-start(bf16[32,24,128]{2,1,0:T(8,128)(2,1)} %get-tuple-element.29), calls=%async_computation.2 | async-start | bytes 393216 | tf_op jit(solution)/shard_map/all_to_all | solution.py:261
  79.4 15.5 %copy-start = (bf16[512,256]{1,0:T(8,128)(2,1)S(1)}, bf16[512,256]{1,0:T(8,128)(2,1)}, u32[]{:S(2)}) copy-start(bf16[512,256]{1,0:T(8,128)(2,1)} %w_ref.1) | copy-start | bytes 786436
  80.5 9.2 %collective-permute-start.2 = (bf16[462,256]{1,0:T(8,128)(2,1)S(1)}, bf16[462,256]{1,0:T(8,128)(2,1)S(1)}, u32[]{:S(2)}, u32[]{:S(2)}) collective-permute-start(bf16[462,256]{1,0:T(8,128)(2,1)S(1)} %fusion.6), channel_id=1, source_target_pairs={{0,16},{16,0},{1,17},{17,1},{2,18},{18,2},{3,19},{19,3},{4,20},{20... | collective-permute-start | bytes 709640 | tf_op jit(solution)/shard_map/ppermute | solution.py:218
  95.8 15.9 %all-to-all-start.3 = ((bf16[16,12,256]{2,1,0:T(8,128)(2,1)}), bf16[16,12,256]{2,1,0:T(8,128)(2,1)S(1)}, u32[]{:S(2)}, u32[]{:S(2)}) async-start(bf16[16,12,256]{2,1,0:T(8,128)(2,1)} %out.1), calls=%async_computation.3 | async-start | bytes 262144 | tf_op jit(solution)/shard_map/all_to_all | solution.py:272
  105.5 6.2 %copy-start.1 = (bf16[12,256]{1,0:T(8,128)(2,1)S(1)}, bf16[12,256]{1,0:T(8,128)(2,1)}, u32[]{:S(2)}) copy-start(bf16[12,256]{1,0:T(8,128)(2,1)} %residual_ref.1) | copy-start | bytes 18436
  106.5 11.3 %collective-permute-start.3 = (bf16[462,256]{1,0:T(8,128)(2,1)S(1)}, bf16[462,256]{1,0:T(8,128)(2,1)S(1)}, u32[]{:S(2)}, u32[]{:S(2)}) collective-permute-start(bf16[462,256]{1,0:T(8,128)(2,1)S(1)} %fusion.7), channel_id=1, source_target_pairs={{0,16},{16,0},{1,17},{17,1},{2,18},{18,2},{3,19},{19,3},{4,20},{20... | collective-permute-start | bytes 709640 | tf_op jit(solution)/shard_map/ppermute | solution.py:218
  112.4 14.2 %all-to-all-start.4 = ((bf16[32,12,256]{2,1,0:T(8,128)(2,1)}), bf16[32,12,256]{2,1,0:T(8,128)(2,1)S(1)}, u32[]{:S(2)}, u32[]{:S(2)}) async-start(bf16[32,12,256]{2,1,0:T(8,128)(2,1)} %get-tuple-element.32), calls=%async_computation.4 | async-start | bytes 524288 | tf_op jit(solution)/shard_map/all_to_all | solution.py:284
  127.3 7.4 %collective-permute-start.4 = (bf16[192,512]{1,0:T(8,128)(2,1)S(1)}, bf16[192,512]{1,0:T(8,128)(2,1)S(1)}, u32[]{:S(2)}, u32[]{:S(2)}) collective-permute-start(bf16[192,512]{1,0:T(8,128)(2,1)S(1)} %get-tuple-element.42), channel_id=1, source_target_pairs={{0,32},{32,0},{64,96},{96,64},{128,160},{160,128},{192,224},{224,1... | collective-permute-start | bytes 589832 | tf_op jit(solution)/shard_map/ppermute | solution.py:302
  129.2 8.3 %collective-permute-start.5 = (bf16[192,512]{1,0:T(8,128)(2,1)S(1)}, bf16[192,512]{1,0:T(8,128)(2,1)S(1)}, u32[]{:S(2)}, u32[]{:S(2)}) collective-permute-start(bf16[192,512]{1,0:T(8,128)(2,1)S(1)} %get-tuple-element.43), channel_id=1, source_target_pairs={{0,480},{32,64},{64,32},{96,128},{128,96},{160,192},{192,160},{224... | collective-permute-start | bytes 589832 | tf_op jit(solution)/shard_map/ppermute | solution.py:303
  137.5 6.0 %copy-start.6 = (bf16[1848,256]{1,0:T(8,128)(2,1)S(1)}, bf16[1848,256]{1,0:T(8,128)(2,1)}, u32[]{:S(2)}) copy-start(bf16[1848,256]{1,0:T(8,128)(2,1)} %param.23) | copy-start | bytes 2838532
  138.5 26.8 %all-to-all-start.5 = ((bf16[8,24,1024]{2,1,0:T(8,128)(2,1)}), bf16[8,24,1024]{2,1,0:T(8,128)(2,1)S(1)}, u32[]{:S(2)}, u32[]{:S(2)}) async-start(bf16[8,24,1024]{2,1,0:T(8,128)(2,1)} %join.1), calls=%async_computation.5 | async-start | bytes 786432 | tf_op jit(solution)/shard_map/all_to_all | solution.py:312
  143.8 13.3 %collective-permute-start.6 = (bf16[2,462,256]{2,1,0:T(8,128)(2,1)S(1)}, bf16[2,462,256]{2,1,0:T(8,128)(2,1)S(1)}, u32[]{:S(2)}, u32[]{:S(2)}) collective-permute-start(bf16[2,462,256]{2,1,0:T(8,128)(2,1)S(1)} %pad_maximum_fusion.2), channel_id=1, source_target_pairs={{0,16},{16,0},{1,17},{17,1},{2,18},{18,2},{3,19},{19,3},{4,20},{20... | collective-permute-start | bytes 1419272 | tf_op jit(solution)/shard_map/ppermute | solution.py:218
  166.3 26.0 %all-to-all-start.6 = ((bf16[16,24,462]{2,1,0:T(8,128)(2,1)}), bf16[16,24,462]{2,1,0:T(8,128)(2,1)S(1)}, u32[]{:S(2)}, u32[]{:S(2)}) async-start(bf16[16,24,462]{2,1,0:T(8,128)(2,1)} %hidden.1), calls=%async_computation.6 | async-start | bytes 786432 | tf_op jit(solution)/shard_map/all_to_all | solution.py:321
  193.3 20.4 %all-to-all-start.7 = ((bf16[32,12,256]{2,1,0:T(8,128)(2,1)}), bf16[32,12,256]{2,1,0:T(8,128)(2,1)S(1)}, u32[]{:S(2)}, u32[]{:S(2)}) async-start(bf16[32,12,256]{2,1,0:T(8,128)(2,1)} %down.1), calls=%async_computation.7 | async-start | bytes 524288 | tf_op jit(solution)/shard_map/all_to_all | solution.py:330

commit v13 on v12

--- a/solution.py
+++ b/solution.py
@@ -57,7 +57,7 @@
         out_ref[i, each:, :] = jnp.concatenate([tail, spare], axis=1).astype(BF16)
 
 
-def merge_kernel(in_ref, out_ref, copies_ref):
+def merge_kernel(in_ref, out_ref, copies_ref, wide_ref):
     blocks, rows, head = copies_ref.shape
     stat = [in_ref[:, rows + i, :].astype(F32) for i in range(6)]
     top = stat[0] + stat[1] + stat[2]
@@ -67,8 +67,12 @@
     out = jnp.zeros((rows, head), F32)
     for i in range(blocks):
         out = out + in_ref[i, :rows, :].astype(F32) * w[:rows, i : i + 1]
+    wide_ref[...] = out
+    tokens = out_ref.shape[0]
+    group = rows // tokens
+    for g in range(group):
+        out_ref[:, g * head : (g + 1) * head] = wide_ref[pl.ds(g, tokens, stride=group), :].astype(BF16)
     out = out.astype(BF16)
-    out_ref[...] = out
     for i in range(blocks):
         copies_ref[i] = out
 
@@ -251,13 +255,13 @@
     parts, up_y1 = beside(parts, trade(up_1))
     attention, copies = pl.pallas_call(
         merge_kernel,
-        out_shape=(jax.ShapeDtypeStruct((each, head), BF16), jax.ShapeDtypeStruct((n_ctx, each, head), BF16)),
+        out_shape=(jax.ShapeDtypeStruct((rows, width), BF16), jax.ShapeDtypeStruct((n_ctx, each, head), BF16)),
         in_specs=[vmem],
         out_specs=(vmem, vmem),
+        scratch_shapes=[pltpu.VMEM((each, head), F32)],
         compiler_params=small,
         name="merge",
     )(parts)
-    attention = attention.reshape(rows, width)
     heads_all = lax.all_to_all(copies, ctx, 0, 0, tiled=True)
     heads_all, gate_y1 = beside(heads_all, trade(gate_1))
     mixed = pl.pallas_call(
@@ -309,7 +313,9 @@
         compiler_params=small,
         name="join",
     )(keep, got_g, got_u)
-    sums, down_y = beside(lax.all_to_all(sums, "far", 0, 0, tiled=True), trade(down_chunk))
+    sums, down_y, own_down = beside(
+        lax.all_to_all(sums, "far", 0, 0, tiled=True), trade(down_chunk), lambda place: down_chunk(place)
+    )
     hidden = pl.pallas_call(
         hidden_kernel,
         out_shape=jax.ShapeDtypeStruct((2 * n_far, block, units), BF16),
@@ -326,7 +332,7 @@
         out_specs=vmem,
         compiler_params=small,
         name="down",
-    )(hidden, down_chunk(near), down_y)
+    )(hidden, own_down, down_y)
     lowered = lax.all_to_all(lowered, ("hi", "tp"), 0, 0, tiled=True)
     layer_out = pl.pallas_call(
         last_kernel,

time: 216 us -> 214 us (level)
  blocking collectives: 0 us -> 46 us
  waiting for transfers between devices: 91 us -> 64.8 us
  starting transfers between devices: 102 us -> 82 us
    all_to_all x0 -> x2, blocking collectives: none -> 46 us  [the longest x1 25.8 us: per_device(): hidden = lax.all_to_all(hidden, ('far', 'lo'), 0, 0, tiled=True)]
    all_to_all x2 -> x0, waiting for transfers between devices: 26.2 us -> none  [the longest x1 18 us: per_device(): hidden = lax.all_to_all(hidden, ('far', 'lo'), 0, 0, tiled=True)]
    all_to_all x2 -> x0, starting transfers between devices: 19.5 us -> none  [the longest x1 11.5 us: per_device(): lowered = lax.all_to_all(lowered, ('hi', 'tp'), 0, 0, tiled=True)]
  transfers between devices with their start and end apart: 15 -> 13, of which waited for: 15 -> 13; matrix products, arithmetic and copies ran while one was open for 3% -> 2% of each run, Pallas kernels for 0% -> 0%
where the time goes in v13:
time: 214 us; the launch traced here: 213 us
  starting transfers between devices  82 us (38%)
  waiting for transfers between devices  64.8 us (30%)
  blocking collectives  46 us (21%)
  Pallas kernels  10.4 us (5%)
  other arithmetic  5.02 us (2%)
  local copies, waits for them, and re-layouts  3.03 us (1%)
    all_to_all x1, blocking collectives, per_device(): hidden = lax.all_to_all(hidden, ('far', 'lo'), 0, 0, tiled=True)  25.8 us
    ppermute x5, waiting for transfers between devices, trade(): return lambda place: lax.ppermute(part(place ^ 1), 'hi', [(0, 1), (1, 0)])  25 us
    ppermute x5, starting transfers between devices, trade(): return lambda place: lax.ppermute(part(place ^ 1), 'hi', [(0, 1), (1, 0)])  21.8 us
    all_to_all x1, blocking collectives, per_device(): lowered = lax.all_to_all(lowered, ('hi', 'tp'), 0, 0, tiled=True)  20.2 us
    all_to_all x1, starting transfers between devices, per_device(): q_all = lax.all_to_all(q_all, ctx, 0, 0, tiled=True)  18.7 us
    all_to_all x1, starting transfers between devices, per_device(): parts = lax.all_to_all(partial, ctx, 0, 0, tiled=True)  9.64 us
    all_to_all x1, starting transfers between devices, per_device(): mixed = lax.all_to_all(mixed, 'tp', 0, 0, tiled=True)  9.62 us
    all_to_all x1, waiting for transfers between devices, per_device(): stream = lax.all_to_all(stream, ('hi', 'tp'), 0, 0, tiled=True)  8.77 us
  transfers between devices with their start and end apart: 13, of which 13 were waited for; matrix products, arithmetic and copies ran while one was open for 2% of the time, Pallas kernels for 0%

profile of v13, /device:TPU:1, one launch (start us, length us, event | category | flops | bytes accessed | tf_op | source)
XLA Modules:
  0.0 212.7 jit_solution(12881394438956059652)
XLA Ops:
  0.6 0.7 broadcast_in_dim.4
  1.3 0.7 broadcast_in_dim.5
  2.0 18.7 %all-to-all-start = ((bf16[32,24,128]{2,1,0:T(8,128)(2,1)}), bf16[32,24,128]{2,1,0:T(8,128)(2,1)S(1)}, u32[]{:S(2)}, u32[]{:S(2)}) async-start(bf16[32,24,128]{2,1,0:T(8,128)(2,1)} %broadcast_in_dim.5), calls=%async_computation | async-start | bytes 393216 | tf_op jit(solution)/shard_map/all_to_all | solution.py:233
  20.7 0.0 copy-start.7
  20.7 0.7 copy-done.7
  21.4 1.7 fusion.4
  23.1 4.6 %collective-permute-start = (bf16[462,256]{1,0:T(8,128)(2,1)S(1)}, bf16[462,256]{1,0:T(8,128)(2,1)S(1)}, u32[]{:S(2)}, u32[]{:S(2)}) collective-permute-start(bf16[462,256]{1,0:T(8,128)(2,1)S(1)} %get-tuple-element.50), channel_id=1, source_target_pairs={{0,16},{16,0},{1,17},{17,1},{2,18},{18,2},{3,19},{19,3},{4,20},{20... | collective-permute-start | bytes 709640 | tf_op jit(solution)/shard_map/ppermute | solution.py:222
  28.5 0.1 pad_maximum_fusion
  28.6 5.5 %collective-permute-done.gate_y0_ref = bf16[462,256]{1,0:T(8,128)(2,1)S(1)} collective-permute-done((bf16[462,256]{1,0:T(8,128)(2,1)S(1)}, bf16[462,256]{1,0:T(8,128)(2,1)S(1)}, u32[]{:S(2)}, u32[]{:S(2)}) %collective-permute-start) | collective-permute-done | bytes 236576 | tf_op jit(solution)/shard_map/ppermute | solution.py:222
  34.0 3.8 %all-to-all-done.q_ref = bf16[32,24,128]{2,1,0:T(8,128)(2,1)S(1)} async-done(((bf16[32,24,128]{2,1,0:T(8,128)(2,1)}), bf16[32,24,128]{2,1,0:T(8,128)(2,1)S(1)}, u32[]{:S(2)}, u32[]{:S(2)}) %all-to-all-start) | async-done | bytes 196640 | tf_op jit(solution)/shard_map/all_to_all | solution.py:233
  37.9 0.7 copy-done.4
  38.6 4.6 %attend.1 = bf16[32,32,128]{2,1,0:T(8,128)(2,1)} custom-call(s32[1]{0:T(128)S(6)} %copy.14.lengths, bf16[32,24,128]{2,1,0:T(8,128)(2,1)S(1)} %all-to-all-done.q_ref, bf16[3072,128]{1,0:T(8,128)(2,1)S(1)} %bitcast.34, bf16[3072,128]{1,0:T(8,128)(2,1)S(1)} %bitcast.35, bf16[6,128]{1,0:T(8,128)(2,1)S(1)} %copy-done.4, bf16[6,128]{1,0:T(8,128)(2,1)S(1)} %copy-done.5), custom_call_target="tpu_custom_call" | custom-call | flops 1207959552 | bytes 2097152 | tf_op jit(solution)/shard_map/attend/pallas_call | solution.py:243
  43.2 9.6 %all-to-all-start.1 = ((bf16[32,32,128]{2,1,0:T(8,128)(2,1)}), bf16[32,32,128]{2,1,0:T(8,128)(2,1)S(1)}, u32[]{:S(2)}, u32[]{:S(2)}) async-start(bf16[32,32,128]{2,1,0:T(8,128)(2,1)} %attend.1), calls=%async_computation.1 | async-start | bytes 524288 | tf_op jit(solution)/shard_map/all_to_all | solution.py:254
  52.8 1.0 fusion.5
  53.9 4.6 %collective-permute-start.1 = (bf16[462,256]{1,0:T(8,128)(2,1)S(1)}, bf16[462,256]{1,0:T(8,128)(2,1)S(1)}, u32[]{:S(2)}, u32[]{:S(2)}) collective-permute-start(bf16[462,256]{1,0:T(8,128)(2,1)S(1)} %fusion.5), channel_id=1, source_target_pairs={{0,16},{16,0},{1,17},{17,1},{2,18},{18,2},{3,19},{19,3},{4,20},{20... | collective-permute-start | bytes 709640 | tf_op jit(solution)/shard_map/ppermute | solution.py:222
  58.5 4.9 %collective-permute-done.1.up_y1_ref = bf16[462,256]{1,0:T(8,128)(2,1)S(1)} collective-permute-done((bf16[462,256]{1,0:T(8,128)(2,1)S(1)}, bf16[462,256]{1,0:T(8,128)(2,1)S(1)}, u32[]{:S(2)}, u32[]{:S(2)}) %collective-permute-start.1) | collective-permute-done | bytes 236576 | tf_op jit(solution)/shard_map/ppermute | solution.py:222
  63.4 8.4 %all-to-all-done.1.in_ref = bf16[32,32,128]{2,1,0:T(8,128)(2,1)S(1)} async-done(((bf16[32,32,128]{2,1,0:T(8,128)(2,1)}), bf16[32,32,128]{2,1,0:T(8,128)(2,1)S(1)}, u32[]{:S(2)}, u32[]{:S(2)}) %all-to-all-start.1) | async-done | bytes 262176 | tf_op jit(solution)/shard_map/all_to_all | solution.py:254
  71.8 1.1 merge.1
  73.0 6.5 %all-to-all-start.2 = ((bf16[32,24,128]{2,1,0:T(8,128)(2,1)}), bf16[32,24,128]{2,1,0:T(8,128)(2,1)S(1)}, u32[]{:S(2)}, u32[]{:S(2)}) async-start(bf16[32,24,128]{2,1,0:T(8,128)(2,1)} %get-tuple-element.30), calls=%async_computation.2 | async-start | bytes 393216 | tf_op jit(solution)/shard_map/all_to_all | solution.py:265
  79.5 1.1 fusion.6
  80.5 4.6 %collective-permute-start.2 = (bf16[462,256]{1,0:T(8,128)(2,1)S(1)}, bf16[462,256]{1,0:T(8,128)(2,1)S(1)}, u32[]{:S(2)}, u32[]{:S(2)}) collective-permute-start(bf16[462,256]{1,0:T(8,128)(2,1)S(1)} %fusion.6), channel_id=1, source_target_pairs={{0,16},{16,0},{1,17},{17,1},{2,18},{18,2},{3,19},{19,3},{4,20},{20... | collective-permute-start | bytes 709640 | tf_op jit(solution)/shard_map/ppermute | solution.py:222
  85.2 4.6 %collective-permute-done.2.gate_y1_ref = bf16[462,256]{1,0:T(8,128)(2,1)S(1)} collective-permute-done((bf16[462,256]{1,0:T(8,128)(2,1)S(1)}, bf16[462,256]{1,0:T(8,128)(2,1)S(1)}, u32[]{:S(2)}, u32[]{:S(2)}) %collective-permute-start.2) | collective-permute-done | bytes 236576 | tf_op jit(solution)/shard_map/ppermute | solution.py:222
  89.8 5.2 %all-to-all-done.2.h_ref = bf16[32,24,128]{2,1,0:T(8,128)(2,1)S(1)} async-done(((bf16[32,24,128]{2,1,0:T(8,128)(2,1)}), bf16[32,24,128]{2,1,0:T(8,128)(2,1)S(1)}, u32[]{:S(2)}, u32[]{:S(2)}) %all-to-all-start.2) | async-done | bytes 196640 | tf_op jit(solution)/shard_map/all_to_all | solution.py:265
  95.0 0.9 out.1
  95.9 9.6 %all-to-all-start.3 = ((bf16[16,12,256]{2,1,0:T(8,128)(2,1)}), bf16[16,12,256]{2,1,0:T(8,128)(2,1)S(1)}, u32[]{:S(2)}, u32[]{:S(2)}) async-start(bf16[16,12,256]{2,1,0:T(8,128)(2,1)} %out.1), calls=%async_computation.3 | async-start | bytes 262144 | tf_op jit(solution)/shard_map/all_to_all | solution.py:276
  105.5 1.0 fusion.7
  106.6 4.5 %collective-permute-start.3 = (bf16[462,256]{1,0:T(8,128)(2,1)S(1)}, bf16[462,256]{1,0:T(8,128)(2,1)S(1)}, u32[]{:S(2)}, u32[]{:S(2)}) collective-permute-start(bf16[462,256]{1,0:T(8,128)(2,1)S(1)} %fusion.7), channel_id=1, source_target_pairs={{0,16},{16,0},{1,17},{17,1},{2,18},{18,2},{3,19},{19,3},{4,20},{20... | collective-permute-start | bytes 709640 | tf_op jit(solution)/shard_map/ppermute | solution.py:222
  111.1 0.6 all-to-all-done.3.in_ref
  111.7 0.7 stream.1
  112.4 5.3 %all-to-all-start.4 = ((bf16[32,12,256]{2,1,0:T(8,128)(2,1)}), bf16[32,12,256]{2,1,0:T(8,128)(2,1)S(1)}, u32[]{:S(2)}, u32[]{:S(2)}) async-start(bf16[32,12,256]{2,1,0:T(8,128)(2,1)} %get-tuple-element.33), calls=%async_computation.4 | async-start | bytes 524288 | tf_op jit(solution)/shard_map/all_to_all | solution.py:288
  117.8 0.1 collective-permute-done.3.up_y0_ref
  117.9 8.8 %all-to-all-done.4.x_ref = bf16[32,12,256]{2,1,0:T(8,128)(2,1)S(1)} async-done(((bf16[32,12,256]{2,1,0:T(8,128)(2,1)}), bf16[32,12,256]{2,1,0:T(8,128)(2,1)S(1)}, u32[]{:S(2)}, u32[]{:S(2)}) %all-to-all-start.4) | async-done | bytes 196640 | tf_op jit(solution)/shard_map/all_to_all | solution.py:288
  126.6 0.7 project.1
  127.4 1.9 collective-permute-start.4
  129.3 3.5 %collective-permute-start.5 = (bf16[192,512]{1,0:T(8,128)(2,1)S(1)}, bf16[192,512]{1,0:T(8,128)(2,1)S(1)}, u32[]{:S(2)}, u32[]{:S(2)}) collective-permute-start(bf16[192,512]{1,0:T(8,128)(2,1)S(1)} %get-tuple-element.44), channel_id=1, source_target_pairs={{0,480},{32,64},{64,32},{96,128},{128,96},{160,192},{192,160},{224... | collective-permute-start | bytes 589832 | tf_op jit(solution)/shard_map/ppermute | solution.py:307
  132.8 1.9 collective-permute-done.4.got_g_ref
  134.7 2.9 %collective-permute-done.5.got_u_ref = bf16[192,512]{1,0:T(8,128)(2,1)S(1)} collective-permute-done((bf16[192,512]{1,0:T(8,128)(2,1)S(1)}, bf16[192,512]{1,0:T(8,128)(2,1)S(1)}, u32[]{:S(2)}, u32[]{:S(2)}) %collective-permute-start.5) | collective-permute-done | bytes 196640 | tf_op jit(solution)/shard_map/ppermute | solution.py:307
  137.6 1.0 join.1
  138.6 5.0 %all-to-all-start.5 = ((bf16[8,24,1024]{2,1,0:T(8,128)(2,1)}), bf16[8,24,1024]{2,1,0:T(8,128)(2,1)S(1)}, u32[]{:S(2)}, u32[]{:S(2)}) async-start(bf16[8,24,1024]{2,1,0:T(8,128)(2,1)} %join.1), calls=%async_computation.5 | async-start | bytes 786432 | tf_op jit(solution)/shard_map/all_to_all | solution.py:317
  143.6 0.2 dynamic-slice_bitcast_fusion.1
  143.9 3.3 %collective-permute-start.6 = (bf16[2,462,256]{2,1,0:T(8,128)(2,1)S(1)}, bf16[2,462,256]{2,1,0:T(8,128)(2,1)S(1)}, u32[]{:S(2)}, u32[]{:S(2)}) collective-permute-start(bf16[2,462,256]{2,1,0:T(8,128)(2,1)S(1)} %pad_maximum_fusion.2), channel_id=1, source_target_pairs={{0,16},{16,0},{1,17},{17,1},{2,18},{18,2},{3,19},{19,3},{4,20},{20... | collective-permute-start | bytes 1419272 | tf_op jit(solution)/shard_map/ppermute | solution.py:222
  147.3 9.9 %collective-permute-done.6.wy_ref = bf16[2,462,256]{2,1,0:T(8,128)(2,1)S(1)} collective-permute-done((bf16[2,462,256]{2,1,0:T(8,128)(2,1)S(1)}, bf16[2,462,256]{2,1,0:T(8,128)(2,1)S(1)}, u32[]{:S(2)}, u32[]{:S(2)}) %collective-permute-start.6) | collective-permute-done | bytes 473120 | tf_op jit(solution)/shard_map/ppermute | solution.py:222
  157.3 8.2 %all-to-all-done.5.in_ref = bf16[8,24,1024]{2,1,0:T(8,128)(2,1)S(1)} async-done(((bf16[8,24,1024]{2,1,0:T(8,128)(2,1)}), bf16[8,24,1024]{2,1,0:T(8,128)(2,1)S(1)}, u32[]{:S(2)}, u32[]{:S(2)}) %all-to-all-start.5) | async-done | bytes 393248 | tf_op jit(solution)/shard_map/all_to_all | solution.py:317
  165.4 0.2 hidden.1
  165.6 25.8 %all_to_all.40.h_ref = bf16[16,24,462]{2,1,0:T(8,128)(2,1)S(1)} all-to-all(bf16[16,24,462]{2,1,0:T(8,128)(2,1)S(1)} %hidden.1), channel_id=1, replica_groups=mesh['far'=8,'lo'=2,'hi'=2,'tp'=16] {'far','lo'}, dimensions={0} | all-to-all | bytes 709632 | tf_op jit(solution)/shard_map/all_to_all | solution.py:327
  191.4 0.4 down.1
  191.8 20.2 %all_to_all.41.in_ref = bf16[32,12,256]{2,1,0:T(8,128)(2,1)S(1)} all-to-all(bf16[32,12,256]{2,1,0:T(8,128)(2,1)S(1)} %down.1), channel_id=1, replica_groups=mesh['far'=8,'lo'=2,'hi'=2,'tp'=16] {'hi','tp'}, dimensions={0} | all-to-all | bytes 393216 | tf_op jit(solution)/shard_map/all_to_all | solution.py:336
  212.0 0.7 last.1
  (15 shorter events, 0.1 us)
Async XLA Ops:
  2.0 35.8 %all-to-all-start = ((bf16[32,24,128]{2,1,0:T(8,128)(2,1)}), bf16[32,24,128]{2,1,0:T(8,128)(2,1)S(1)}, u32[]{:S(2)}, u32[]{:S(2)}) async-start(bf16[32,24,128]{2,1,0:T(8,128)(2,1)} %broadcast_in_dim.5), calls=%async_computation | async-start | bytes 393216 | tf_op jit(solution)/shard_map/all_to_all | solution.py:233
  20.7 0.7 copy-start.7
  23.1 10.9 %collective-permute-start = (bf16[462,256]{1,0:T(8,128)(2,1)S(1)}, bf16[462,256]{1,0:T(8,128)(2,1)S(1)}, u32[]{:S(2)}, u32[]{:S(2)}) collective-permute-start(bf16[462,256]{1,0:T(8,128)(2,1)S(1)} %get-tuple-element.50), channel_id=1, source_target_pairs={{0,16},{16,0},{1,17},{17,1},{2,18},{18,2},{3,19},{19,3},{4,20},{20... | collective-permute-start | bytes 709640 | tf_op jit(solution)/shard_map/ppermute | solution.py:222
  28.4 9.4 %copy-start.2 = (bf16[1,3072,128]{2,1,0:T(8,128)(2,1)S(1)}, bf16[1,3072,128]{2,1,0:T(8,128)(2,1)}, u32[]{:S(2)}) copy-start(bf16[1,3072,128]{2,1,0:T(8,128)(2,1)} %param.13) | copy-start | bytes 2359300
  28.4 9.4 %copy-start.3 = (bf16[1,3072,128]{2,1,0:T(8,128)(2,1)S(1)}, bf16[1,3072,128]{2,1,0:T(8,128)(2,1)}, u32[]{:S(2)}) copy-start(bf16[1,3072,128]{2,1,0:T(8,128)(2,1)} %param.14) | copy-start | bytes 2359300
  28.5 9.4 %copy-start.5 = (bf16[6,128]{1,0:T(8,128)(2,1)S(1)}, bf16[6,128]{1,0:T(8,128)(2,1)}, u32[]{:S(2)}) copy-start(bf16[6,128]{1,0:T(8,128)(2,1)} %sv_ref.1) | copy-start | bytes 4612
  37.9 0.7 copy-start.4
  43.2 28.7 %all-to-all-start.1 = ((bf16[32,32,128]{2,1,0:T(8,128)(2,1)}), bf16[32,32,128]{2,1,0:T(8,128)(2,1)S(1)}, u32[]{:S(2)}, u32[]{:S(2)}) async-start(bf16[32,32,128]{2,1,0:T(8,128)(2,1)} %attend.1), calls=%async_computation.1 | async-start | bytes 524288 | tf_op jit(solution)/shard_map/all_to_all | solution.py:254
  53.9 9.6 %collective-permute-start.1 = (bf16[462,256]{1,0:T(8,128)(2,1)S(1)}, bf16[462,256]{1,0:T(8,128)(2,1)S(1)}, u32[]{:S(2)}, u32[]{:S(2)}) collective-permute-start(bf16[462,256]{1,0:T(8,128)(2,1)S(1)} %fusion.5), channel_id=1, source_target_pairs={{0,16},{16,0},{1,17},{17,1},{2,18},{18,2},{3,19},{19,3},{4,20},{20... | collective-permute-start | bytes 709640 | tf_op jit(solution)/shard_map/ppermute | solution.py:222
  73.0 22.0 %all-to-all-start.2 = ((bf16[32,24,128]{2,1,0:T(8,128)(2,1)}), bf16[32,24,128]{2,1,0:T(8,128)(2,1)S(1)}, u32[]{:S(2)}, u32[]{:S(2)}) async-start(bf16[32,24,128]{2,1,0:T(8,128)(2,1)} %get-tuple-element.30), calls=%async_computation.2 | async-start | bytes 393216 | tf_op jit(solution)/shard_map/all_to_all | solution.py:265
  79.5 15.5 %copy-start = (bf16[512,256]{1,0:T(8,128)(2,1)S(1)}, bf16[512,256]{1,0:T(8,128)(2,1)}, u32[]{:S(2)}) copy-start(bf16[512,256]{1,0:T(8,128)(2,1)} %w_ref.1) | copy-start | bytes 786436
  80.5 9.2 %collective-permute-start.2 = (bf16[462,256]{1,0:T(8,128)(2,1)S(1)}, bf16[462,256]{1,0:T(8,128)(2,1)S(1)}, u32[]{:S(2)}, u32[]{:S(2)}) collective-permute-start(bf16[462,256]{1,0:T(8,128)(2,1)S(1)} %fusion.6), channel_id=1, source_target_pairs={{0,16},{16,0},{1,17},{17,1},{2,18},{18,2},{3,19},{19,3},{4,20},{20... | collective-permute-start | bytes 709640 | tf_op jit(solution)/shard_map/ppermute | solution.py:222
  95.9 15.8 %all-to-all-start.3 = ((bf16[16,12,256]{2,1,0:T(8,128)(2,1)}), bf16[16,12,256]{2,1,0:T(8,128)(2,1)S(1)}, u32[]{:S(2)}, u32[]{:S(2)}) async-start(bf16[16,12,256]{2,1,0:T(8,128)(2,1)} %out.1), calls=%async_computation.3 | async-start | bytes 262144 | tf_op jit(solution)/shard_map/all_to_all | solution.py:276
  105.5 6.2 %copy-start.1 = (bf16[12,256]{1,0:T(8,128)(2,1)S(1)}, bf16[12,256]{1,0:T(8,128)(2,1)}, u32[]{:S(2)}) copy-start(bf16[12,256]{1,0:T(8,128)(2,1)} %residual_ref.1) | copy-start | bytes 18436
  106.6 11.3 %collective-permute-start.3 = (bf16[462,256]{1,0:T(8,128)(2,1)S(1)}, bf16[462,256]{1,0:T(8,128)(2,1)S(1)}, u32[]{:S(2)}, u32[]{:S(2)}) collective-permute-start(bf16[462,256]{1,0:T(8,128)(2,1)S(1)} %fusion.7), channel_id=1, source_target_pairs={{0,16},{16,0},{1,17},{17,1},{2,18},{18,2},{3,19},{19,3},{4,20},{20... | collective-permute-start | bytes 709640 | tf_op jit(solution)/shard_map/ppermute | solution.py:222
  112.4 14.2 %all-to-all-start.4 = ((bf16[32,12,256]{2,1,0:T(8,128)(2,1)}), bf16[32,12,256]{2,1,0:T(8,128)(2,1)S(1)}, u32[]{:S(2)}, u32[]{:S(2)}) async-start(bf16[32,12,256]{2,1,0:T(8,128)(2,1)} %get-tuple-element.33), calls=%async_computation.4 | async-start | bytes 524288 | tf_op jit(solution)/shard_map/all_to_all | solution.py:288
  127.4 7.4 %collective-permute-start.4 = (bf16[192,512]{1,0:T(8,128)(2,1)S(1)}, bf16[192,512]{1,0:T(8,128)(2,1)S(1)}, u32[]{:S(2)}, u32[]{:S(2)}) collective-permute-start(bf16[192,512]{1,0:T(8,128)(2,1)S(1)} %get-tuple-element.43), channel_id=1, source_target_pairs={{0,32},{32,0},{64,96},{96,64},{128,160},{160,128},{192,224},{224,1... | collective-permute-start | bytes 589832 | tf_op jit(solution)/shard_map/ppermute | solution.py:306
  129.3 8.3 %collective-permute-start.5 = (bf16[192,512]{1,0:T(8,128)(2,1)S(1)}, bf16[192,512]{1,0:T(8,128)(2,1)S(1)}, u32[]{:S(2)}, u32[]{:S(2)}) collective-permute-start(bf16[192,512]{1,0:T(8,128)(2,1)S(1)} %get-tuple-element.44), channel_id=1, source_target_pairs={{0,480},{32,64},{64,32},{96,128},{128,96},{160,192},{192,160},{224... | collective-permute-start | bytes 589832 | tf_op jit(solution)/shard_map/ppermute | solution.py:307
  137.6 6.0 %copy-start.6 = (bf16[1848,256]{1,0:T(8,128)(2,1)S(1)}, bf16[1848,256]{1,0:T(8,128)(2,1)}, u32[]{:S(2)}) copy-start(bf16[1848,256]{1,0:T(8,128)(2,1)} %param.23) | copy-start | bytes 2838532
  138.6 26.8 %all-to-all-start.5 = ((bf16[8,24,1024]{2,1,0:T(8,128)(2,1)}), bf16[8,24,1024]{2,1,0:T(8,128)(2,1)S(1)}, u32[]{:S(2)}, u32[]{:S(2)}) async-start(bf16[8,24,1024]{2,1,0:T(8,128)(2,1)} %join.1), calls=%async_computation.5 | async-start | bytes 786432 | tf_op jit(solution)/shard_map/all_to_all | solution.py:317
  143.9 13.3 %collective-permute-start.6 = (bf16[2,462,256]{2,1,0:T(8,128)(2,1)S(1)}, bf16[2,462,256]{2,1,0:T(8,128)(2,1)S(1)}, u32[]{:S(2)}, u32[]{:S(2)}) collective-permute-start(bf16[2,462,256]{2,1,0:T(8,128)(2,1)S(1)} %pad_maximum_fusion.2), channel_id=1, source_target_pairs={{0,16},{16,0},{1,17},{17,1},{2,18},{18,2},{3,19},{19,3},{4,20},{20... | collective-permute-start | bytes 1419272 | tf_op jit(solution)/shard_map/ppermute | solution.py:222
